TPU v7x, 32 devices: a whole 2x2x4 slice. The times are simulated.
32 devices in a mesh: blk: 4 (over y, x), grp: 8 (over z, core).
Axes of the slice: x: 2, y: 2, z: 4, core: 2. Of those that a mesh axis runs over, the one named last changes fastest.
Arguments:
- incident: float32 [4, 8192, 240], P('blk', 'grp'), may hold values from -6 to 6
- mie_coef: float32 [4, 8192, 240], P('blk', 'grp'), may hold values from 0.15 to 0.45
- owner_dev: int32 [4, 24576, 1], P('blk', 'grp'), may hold values from 0 to 7; in each aligned block of 3072 rows (0 to 3071, 3072 to 6143, ..., all dimensions but the last counted through in order) at most 512 rows name the same one
- near_row: int32 [4, 24576], P('blk', 'grp'), may hold values from 0 to 1023
- table_id: int32 [4, 24576], P('blk', 'grp'), may hold values from 0 to 7
- tables: bfloat16 [8, 240, 240], replicated, may hold values from -0.4 to 0.6
- wave_out: bfloat16 [240, 512], replicated, may hold values from -0.375 to 0.375
- wave_in: bfloat16 [512, 240], replicated, may hold values from -0.25 to 0.25
- plane_angle: bfloat16 [4, 8192, 512], P('blk', 'grp'), may hold values from -3.140625 to 3.140625
- far_trans: float32 [4, 8, 4, 512], P('blk', 'grp'), may hold values from -0.109375 to 0.109375
Outputs:
- solution: float32 [4, 8192, 240], P('blk', 'grp')
- residual: float32 [4, 8192, 240], P('blk', 'grp')
- hessenberg: float32 [3, 2], replicated
Inputs may be any that keep to these rules, and one draw needn't show every extreme that they name: `owner_dev`: among the 3072 requests of one device, at most 512 name the same owner, and some device reaches 512.
All inputs are finite; a program needn't handle non-finite values.
Results may differ from a plain program's by a relative error of at most 0.0075.
Values may be sent and summed in bfloat16 or wider, within the bound.
No kernel may reach another device: no remote copies, remote signals or barrier semaphores. Data moves between devices by JAX's collectives and lax.ppermute only.
A program may use at most 128 MiB of HBM per device.

v0:
```python
import jax
import jax.numpy as jnp
from jax import lax
from jax.sharding import PartitionSpec as P

epsilon = 1e-06


def from_behind(block, axis, distance):
    devices = range(lax.axis_size(axis))
    route = [((i - distance) % len(devices), i) for i in devices]
    return lax.ppermute(block, axis, route)


def slot_numbers(owner_ids, group_size):
    onehot = (owner_ids[:, None] == jnp.arange(group_size, dtype=jnp.int32)[None, :]).astype(
        jnp.int32
    )
    earlier = jnp.cumsum(onehot, axis=0) - onehot
    return jnp.sum(earlier * onehot, axis=1)


def masked_products(requested, table_ids, tables):
    table_count = tables.shape[0]

    def add_table(table_index, running):
        chosen = jnp.where(
            (table_ids == table_index)[:, None], requested, jnp.zeros_like(requested)
        )
        return running + jnp.dot(chosen, tables[table_index], preferred_element_type=jnp.float32)

    total = lax.fori_loop(0, table_count, add_table, jnp.zeros(requested.shape, jnp.float32))
    return total.astype(jnp.bfloat16)


def squared_norm(field):
    return lax.psum(jnp.sum(field * field), ("blk", "grp"))


def body(
    incident,
    mie_coef,
    owner_dev,
    near_row,
    table_id,
    tables,
    wave_out,
    wave_in,
    plane_angle,
    far_trans,
):
    source = incident[0]
    scatter_coef = mie_coef[0]
    owner_ids = owner_dev[0, :, 0]
    row_ids = near_row[0]
    table_ids = table_id[0]
    local_rows, coef_count = source.shape
    group_size = lax.axis_size("grp")
    blocks = lax.axis_size("blk")
    capacity = local_rows // 2
    per_row = owner_ids.shape[0] // local_rows
    cosine = jnp.cos(plane_angle[0].astype(jnp.float32))
    trans_rows = far_trans[0, 0]
    slot_ids = slot_numbers(owner_ids, group_size)
    my_block = lax.axis_index("blk")
    send_rows = jnp.zeros((group_size, capacity), jnp.int32).at[owner_ids, slot_ids].set(row_ids)
    wanted_rows = lax.all_to_all(send_rows, "grp", split_axis=0, concat_axis=0, tiled=True)

    def apply_operator(vector):
        coded_vec = vector.astype(jnp.bfloat16)
        picked = coded_vec[wanted_rows]
        answered = lax.all_to_all(picked, "grp", split_axis=0, concat_axis=0, tiled=True)
        near_terms = masked_products(answered[owner_ids, slot_ids], table_ids, tables)
        near_field = (
            near_terms.astype(jnp.float32).reshape(local_rows, per_row, coef_count).sum(axis=1)
        )
        outgoing = jnp.dot(coded_vec, wave_out, preferred_element_type=jnp.float32)
        own_wave = jnp.sum(cosine * outgoing, axis=0)

        def cycle_turn(turn_index, state_pair):
            moving, incoming = state_pair
            moving = from_behind(moving, "blk", 1)
            source_block = (my_block - turn_index) % blocks
            weights = lax.dynamic_index_in_dim(trans_rows, source_block, 0, keepdims=False)
            return (moving, incoming + weights * moving)

        moved_wave, incoming = lax.fori_loop(
            1, blocks, cycle_turn, (own_wave, jnp.zeros_like(own_wave))
        )
        spread = (cosine * incoming[None, :]).astype(jnp.bfloat16)
        far_field = jnp.dot(spread, wave_in, preferred_element_type=jnp.float32)
        return vector - scatter_coef * (near_field + far_field)

    initial_norm = jnp.sqrt(squared_norm(source) + epsilon)
    first_basis = source / initial_norm
    first_image = apply_operator(first_basis)
    diag_first, length_first = lax.psum(
        (jnp.sum(first_basis * first_image), jnp.sum(first_image * first_image)), ("blk", "grp")
    )
    below_first = jnp.sqrt(jnp.maximum(length_first - diag_first * diag_first, 0.0) + epsilon)
    second_basis = (first_image - diag_first * first_basis) / below_first
    second_image = apply_operator(second_basis)
    upper_second, diag_second, length_second = lax.psum(
        (
            jnp.sum(first_basis * second_image),
            jnp.sum(second_basis * second_image),
            jnp.sum(second_image * second_image),
        ),
        ("blk", "grp"),
    )
    below_second = jnp.sqrt(
        jnp.maximum(length_second - upper_second * upper_second - diag_second * diag_second, 0.0)
        + epsilon
    )
    gram_aa = diag_first * diag_first + below_first * below_first
    gram_ab = diag_first * upper_second + below_first * diag_second
    gram_bb = upper_second * upper_second + diag_second * diag_second + below_second * below_second
    rhs_first = initial_norm * diag_first
    rhs_second = initial_norm * upper_second
    determinant = gram_aa * gram_bb - gram_ab * gram_ab
    coef_first = (gram_bb * rhs_first - gram_ab * rhs_second) / determinant
    coef_second = (gram_aa * rhs_second - gram_ab * rhs_first) / determinant
    solution = coef_first * first_basis + coef_second * second_basis
    residual = source - coef_first * first_image - coef_second * second_image
    zero_entry = jnp.zeros((), jnp.float32)
    hessenberg = jnp.stack(
        [
            jnp.stack([diag_first, upper_second]),
            jnp.stack([below_first, diag_second]),
            jnp.stack([zero_entry, below_second]),
        ]
    )
    return (solution[None], residual[None], hessenberg)


def solution(mesh):
    return jax.shard_map(
        body,
        mesh=mesh,
        in_specs=(
            P("blk", "grp", None),
            P("blk", "grp", None),
            P("blk", "grp", None),
            P("blk", "grp"),
            P("blk", "grp"),
            P(),
            P(),
            P(),
            P("blk", "grp", None),
            P("blk", "grp", None, None),
        ),
        out_specs=(P("blk", "grp", None), P("blk", "grp", None), P()),
        check_vma=False,
    )
```

profile of v0, /device:TPU:0, one launch (start us, length us, event | category | flops | bytes accessed | tf_op | source)
XLA Modules:
  0.0 538.6 jit_solution(11833609244774849935)
XLA Ops:
  9.5 12.5 %scatter_custom_fusion = s32[4096]{0:T(1024)} fusion(s32[3072]{0:T(1024)S(1)} %broadcast_select_fusion, s32[3072]{0:T(1024)} %bitcast.131, s32[]{:T(128)} %constant.174.clone.1), kind=kCustom, calls=%fused_computation.76 | custom fusion | bytes 16896
  22.0 6.3 %all-to-all-start = ((s32[8,1,512]{2,1,0:T(1,128)}), s32[8,1,512]{2,1,0:T(1,128)S(1)}, u32[]{:S(2)}, u32[]{:S(2)}) async-start(s32[8,1,512]{2,1,0:T(1,128)} %bitcast.9), calls=%async_computation | async-start | bytes 32768 | tf_op jit(solution)/shard_map/all_to_all | solution.py:67
  28.3 41.0 %psum.42 = f32[]{:T(128)} all-reduce(f32[]{:T(128)} %fusion.26), channel_id=1, replica_groups=mesh['blk'=4,'grp'=8] {'blk','grp'}, use_global_device_ids=true, to_apply=%region_1.2 | all-reduce | flops 1 | bytes 8 | tf_op jit(solution)/shard_map/psum | solution.py:37
  70.9 14.6 %gather_fusion = bf16[4096,240]{1,0:T(8,128)(2,1)S(1)} fusion(bf16[1024,240]{1,0:T(8,128)(2,1)S(1)} %copy.21, s32[4096]{0:T(1024)S(1)} %broadcast_clamp_fusion), kind=kCustom, calls=%fused_computation | custom fusion | bytes 3948544 | tf_op jit(solution)/shard_map/gather | solution.py:71
  87.9 4.5 all-to-all-start.1
  92.4 8.3 %fusion.14 = f32[512]{0:T(512)S(1)} fusion(bf16[1,1024,512]{2,1,0:T(8,128)(2,1)} %param.26, bf16[1024,240]{0,1:T(8,128)(2,1)} %copy-done.8, bf16[240,512]{1,0:T(8,128)(2,1)} %param.24), kind=kOutput, calls=%fused_computation.31 | convolution fusion | flops 253230592 | bytes 1787904 | tf_op jit(solution)/shard_map/dot_general | solution.py:77
  100.7 37.8 %all-to-all-done.1 = bf16[8,512,240]{1,2,0:T(8,128)(2,1)} async-done(((bf16[8,512,240]{1,2,0:T(8,128)(2,1)}), bf16[8,512,240]{1,2,0:T(8,128)(2,1)}, u32[]{:S(2)}, u32[]{:S(2)}) %all-to-all-start.1) | async-done | bytes 1966112 | tf_op jit(solution)/shard_map/all_to_all | solution.py:72
  138.5 3.9 copy.23
  142.4 52.5 %gather_fusion.1 = bf16[3072,240]{1,0:T(8,128)(2,1)} fusion(bf16[8,512,240]{2,1,0:T(8,128)(2,1)} %copy.23, s32[3072]{0:T(1024)S(1)} %bitcast.118), kind=kCustom, calls=%fused_computation.1 | custom fusion | bytes 2973696 | tf_op jit(solution)/shard_map/gather | solution.py:73
  194.9 27.2 %while.64 = (s32[]{:T(128)}, f32[3072,240]{0,1:T(8,128)S(1)}, s32[3072]{0:T(1024)S(1)}, bf16[3072,240]{1,0:T(8,128)(2,1)}, bf16[8,240,240]{2,1,0:T(8,128)(2,1)}, /*index=5*/s32[]{:T(128)}, s32[]{:T(128)}) while((s32[]{:T(128)}, f32[3072,240]{0,1:T(8,128)S(1)}, s32[3072]{0:T(1024)S(1)}, bf16[3072,240]{1,0:T(8,128)(2,1)}, ...), condition=%wide.region_7.8_spmd.clone, body=%wide.region_6.7_spmd.clone.sunk | while | flops 356109312 | bytes 7613019 | solution.py:32
  194.9 3.4 convolution_add_fusion.6
  198.3 3.4 convolution_add_fusion.6
  201.7 3.4 convolution_add_fusion.6
  205.1 3.4 convolution_add_fusion.6
  208.5 3.4 convolution_add_fusion.6
  211.9 3.4 convolution_add_fusion.6
  215.3 3.4 convolution_add_fusion.6
  218.7 3.4 convolution_add_fusion.6
  226.2 3.1 reshape.131
  229.3 4.7 reduce_sum.104
  234.4 13.7 %while.65 = (s32[]{:T(128)}, f32[512]{0:T(512)S(1)}, f32[512]{0:T(512)S(1)}, s32[]{:T(128)}, f32[4,512]{1,0:T(4,128)S(1)}, /*index=5*/s32[]{:T(128)}, s32[]{:T(128)}, s32[]{:T(128)}, s32[]{:T(128)}) while((s32[]{:T(128)}, f32[512]{0:T(512)S(1)}, f32[512]{0:T(512)S(1)}, s32[]{:T(128)}, f32[4,512]{1,0:T(4,128)S(1)}, ...), condition=%wide.region_11.12_spmd.clone, body=%wide.region_10.11_spmd.clone.sunk | while | flops 1554 | bytes 24886 | solution.py:87
  240.3 3.2 collective-permute-done
  244.2 3.9 collective-permute-done
  248.1 10.0 %multiply_reduce_fusion.4 = (f32[]{:T(128)}, f32[]{:T(128)}, f32[1024,240]{0,1:T(8,128)S(1)}) fusion(f32[]{:T(128)S(6)} %sqrt.9, f32[1,1024,240]{1,2,0:T(8,128)S(1)} %copy-done.2, f32[1024,240]{0,1:T(8,128)S(1)} %copy.25, bf16[512,240]{0,1:T(8,128)(2,1)S(1)} %copy-done, bf16[1,1024,512]{2,1,0:T(8,128)(2,1)} %param.26, f32[512]{0:T(512)S(1)} %get-tuple-element.458, ...), kind=kOutput, calls=%fused_computation.58 | convolution fusion | flops 255197184 | bytes 5228556 | tf_op jit(solution)/shard_map/dot_general | solution.py:91
  258.1 37.5 %all-reduce.1 = (f32[]{:T(128)}, f32[]{:T(128)}) all-reduce(f32[]{:T(128)} %get-tuple-element.546, f32[]{:T(128)} %get-tuple-element.545), channel_id=1, replica_groups=mesh['blk'=4,'grp'=8] {'blk','grp'}, use_global_device_ids=true, to_apply=%region_15.16 | all-reduce | flops 2 | bytes 16 | tf_op jit(solution)/shard_map/psum | solution.py:97
  300.4 14.6 %gather_fusion.2 = bf16[4096,240]{1,0:T(8,128)(2,1)S(1)} fusion(bf16[1024,240]{1,0:T(8,128)(2,1)S(1)} %copy.26, s32[4096]{0:T(1024)S(1)} %broadcast_clamp_fusion), kind=kCustom, calls=%fused_computation.2 | custom fusion | bytes 3948544 | tf_op jit(solution)/shard_map/gather | solution.py:71
  317.4 4.6 all-to-all-start.2
  322.6 8.3 %fusion.16 = f32[512]{0:T(512)S(1)} fusion(bf16[1,1024,512]{2,1,0:T(8,128)(2,1)} %param.26, bf16[1024,240]{0,1:T(8,128)(2,1)} %copy-done.7, bf16[240,512]{1,0:T(8,128)(2,1)} %param.24), kind=kOutput, calls=%fused_computation.33 | convolution fusion | flops 253230592 | bytes 1787904 | tf_op jit(solution)/shard_map/dot_general | solution.py:77
  330.9 37.2 %all-to-all-done.2 = bf16[8,512,240]{1,2,0:T(8,128)(2,1)} async-done(((bf16[8,512,240]{1,2,0:T(8,128)(2,1)}), bf16[8,512,240]{1,2,0:T(8,128)(2,1)}, u32[]{:S(2)}, u32[]{:S(2)}) %all-to-all-start.2) | async-done | bytes 1966112 | tf_op jit(solution)/shard_map/all_to_all | solution.py:72
  368.1 3.9 copy.28
  371.9 52.5 %gather_fusion.3 = bf16[3072,240]{1,0:T(8,128)(2,1)} fusion(bf16[8,512,240]{2,1,0:T(8,128)(2,1)} %copy.28, s32[3072]{0:T(1024)S(1)} %bitcast.119), kind=kCustom, calls=%fused_computation.3 | custom fusion | bytes 2973696 | tf_op jit(solution)/shard_map/gather | solution.py:73
  424.5 27.2 %while.66 = (s32[]{:T(128)}, f32[3072,240]{0,1:T(8,128)S(1)}, s32[3072]{0:T(1024)S(1)}, bf16[3072,240]{1,0:T(8,128)(2,1)}, bf16[8,240,240]{2,1,0:T(8,128)(2,1)}, /*index=5*/s32[]{:T(128)}, s32[]{:T(128)}) while((s32[]{:T(128)}, f32[3072,240]{0,1:T(8,128)S(1)}, s32[3072]{0:T(1024)S(1)}, bf16[3072,240]{1,0:T(8,128)(2,1)}, ...), condition=%wide.region_17.18_spmd.clone, body=%wide.region_16.17_spmd.clone.sunk | while | flops 356109312 | bytes 7613019 | solution.py:32
  424.5 3.3 convolution_add_fusion.7
  427.8 3.4 convolution_add_fusion.7
  431.3 3.4 convolution_add_fusion.7
  434.6 3.4 convolution_add_fusion.7
  438.0 3.4 convolution_add_fusion.7
  441.4 3.4 convolution_add_fusion.7
  444.8 3.4 convolution_add_fusion.7
  448.2 3.4 convolution_add_fusion.7
  455.8 3.1 reshape.133
  458.8 4.7 reduce_sum.108
  464.9 14.4 %while.67 = (s32[]{:T(128)}, f32[512]{0:T(512)S(1)}, f32[512]{0:T(512)S(1)}, s32[]{:T(128)}, f32[4,512]{1,0:T(4,128)S(1)}, /*index=5*/s32[]{:T(128)}, s32[]{:T(128)}, s32[]{:T(128)}, s32[]{:T(128)}) while((s32[]{:T(128)}, f32[512]{0:T(512)S(1)}, f32[512]{0:T(512)S(1)}, s32[]{:T(128)}, f32[4,512]{1,0:T(4,128)S(1)}, ...), condition=%wide.region_21.22_spmd.clone, body=%wide.region_20.21_spmd.clone.sunk | while | flops 1554 | bytes 24886 | solution.py:87
  467.1 3.0 collective-permute-done.1
  470.7 3.9 collective-permute-done.1
  474.8 4.4 collective-permute-done.1
  479.3 10.3 %multiply_reduce_fusion = (f32[]{:T(128)}, f32[]{:T(128)}, f32[]{:T(128)}, f32[1024,240]{0,1:T(8,128)}) fusion(f32[1024,240]{0,1:T(8,128)S(1)} %copy-done.6, f32[]{:T(128)S(6)} %sqrt.9, f32[1,1024,240]{1,2,0:T(8,128)S(1)} %copy-done.3, f32[1024,240]{0,1:T(8,128)} %copy.30, bf16[512,240]{0,1:T(8,128)(2,1)S(1)} %copy-done, bf16[1,1024,512]{2,1,0:T(8,128)(2,1)} %param.26, ...), kind=kOutput, calls=%fused_computation.53 | convolution fusion | flops 255688704 | bytes 6211600 | tf_op jit(solution)/shard_map/dot_general | solution.py:91
  489.6 37.2 %all-reduce = (f32[]{:T(128)}, f32[]{:T(128)}, f32[]{:T(128)}) all-reduce(f32[]{:T(128)} %get-tuple-element.544, f32[]{:T(128)} %get-tuple-element.543, f32[]{:T(128)} %get-tuple-element.542), channel_id=1, replica_groups=mesh['blk'=4,'grp'=8] {'blk','grp'}, use_global_device_ids=true, to_apply=%region_23.24 | all-reduce | flops 3 | bytes 24 | tf_op jit(solution)/shard_map/psum | solution.py:103
  (98 shorter events, 42.4 us)
Async XLA Ops:
  0.6 247.5 %copy-start = (bf16[512,240]{0,1:T(8,128)(2,1)S(1)}, bf16[512,240]{0,1:T(8,128)(2,1)}, u32[]{:S(2)}) copy-start(bf16[512,240]{0,1:T(8,128)(2,1)} %param.25) | copy-start | bytes 737284
  0.6 69.4 %copy-start.1 = (f32[1,1024,240]{1,2,0:T(8,128)S(1)}, f32[1,1024,240]{1,2,0:T(8,128)}, u32[]{:S(2)}) copy-start(f32[1,1024,240]{1,2,0:T(8,128)} %param.18) | copy-start | bytes 2949124
  22.0 48.3 %all-to-all-start = ((s32[8,1,512]{2,1,0:T(1,128)}), s32[8,1,512]{2,1,0:T(1,128)S(1)}, u32[]{:S(2)}, u32[]{:S(2)}) async-start(s32[8,1,512]{2,1,0:T(1,128)} %bitcast.9), calls=%async_computation | async-start | bytes 32768 | tf_op jit(solution)/shard_map/all_to_all | solution.py:67
  70.1 0.8 copy-start.8
  87.9 50.6 %all-to-all-start.1 = ((bf16[8,512,240]{1,2,0:T(8,128)(2,1)}), bf16[8,512,240]{1,2,0:T(8,128)(2,1)}, u32[]{:S(2)}, u32[]{:S(2)}) async-start(bf16[8,512,240]{1,2,0:T(8,128)(2,1)} %copy.22), calls=%async_computation.1 | async-start | bytes 3932160 | tf_op jit(solution)/shard_map/all_to_all | solution.py:72
  142.4 52.5 %copy-start.9 = (s32[1,3072]{1,0:T(1,128)S(1)}, s32[1,3072]{1,0:T(1,128)}, u32[]{:S(2)}) copy-start(s32[1,3072]{1,0:T(1,128)} %param.22) | copy-start | bytes 36868
  229.3 5.1 copy-start.10
  234.0 14.1 %copy-start.2 = (f32[1,1024,240]{1,2,0:T(8,128)S(1)}, f32[1,1024,240]{1,2,0:T(8,128)}, u32[]{:S(2)}) copy-start(f32[1,1024,240]{1,2,0:T(8,128)} %param.18) | copy-start | bytes 2949124
  234.4 4.5 collective-permute-start
  239.0 4.5 collective-permute-start
  243.5 4.5 collective-permute-start
  258.1 41.3 %copy-start.4 = (f32[1024,240]{0,1:T(8,128)}, f32[1024,240]{0,1:T(8,128)S(1)}, u32[]{:S(2)}) copy-start(f32[1024,240]{0,1:T(8,128)S(1)} %get-tuple-element.599) | copy-start | bytes 2949124
  299.4 0.8 copy-start.7
  317.4 50.7 %all-to-all-start.2 = ((bf16[8,512,240]{1,2,0:T(8,128)(2,1)}), bf16[8,512,240]{1,2,0:T(8,128)(2,1)}, u32[]{:S(2)}, u32[]{:S(2)}) async-start(bf16[8,512,240]{1,2,0:T(8,128)(2,1)} %copy.27), calls=%async_computation.2 | async-start | bytes 3932160 | tf_op jit(solution)/shard_map/all_to_all | solution.py:72
  463.6 15.7 %copy-start.3 = (f32[1,1024,240]{1,2,0:T(8,128)S(1)}, f32[1,1024,240]{1,2,0:T(8,128)}, u32[]{:S(2)}) copy-start(f32[1,1024,240]{1,2,0:T(8,128)} %param.18) | copy-start | bytes 2949124
  463.6 15.7 %copy-start.6 = (f32[1024,240]{0,1:T(8,128)S(1)}, f32[1024,240]{0,1:T(8,128)}, u32[]{:S(2)}) copy-start(f32[1024,240]{0,1:T(8,128)} %get-tuple-element.593) | copy-start | bytes 2949124
  464.9 5.3 collective-permute-start.1
  470.2 4.5 collective-permute-start.1
  474.7 4.5 collective-permute-start.1
  479.3 56.4 %copy-start.5 = (f32[1024,240]{0,1:T(8,128)S(1)}, f32[1024,240]{0,1:T(8,128)}, u32[]{:S(2)}) copy-start(f32[1024,240]{0,1:T(8,128)} %copy-done.4) | copy-start | bytes 2949124
where the time goes:
time: 542 us; the launch traced here: 539 us
  local copies, waits for them, and re-layouts  174 us (32%)
  blocking collectives  116 us (21%)
  waiting for transfers between devices  95.8 us (18%)
  matrix products  90.6 us (17%)
  other arithmetic  28.7 us (5%)
  starting transfers between devices  22.5 us (4%)
  between operations  10.3 us (2%)
    gather x2, local copies, waits for them, and re-layouts, apply_operator(): answered[owner_ids, slot_ids]  105 us
    all_to_all x2, waiting for transfers between devices, apply_operator(): lax.all_to_all(picked, 'grp', split_axis=0, concat_axis=0, tiled=True)  75 us
    dot_general x16, matrix products, add_table(): jnp.dot(chosen, tables[table_index], preferred_element_type=jnp.float32)  53.7 us
    psum x1, blocking collectives, squared_norm(): return lax.psum(jnp.sum(field * field), ('blk', 'grp'))  41 us
    psum x1, blocking collectives, body(): lax.psum((jnp.sum(first_basis * first_image), jnp.sum(first_image * first...  37.5 us
    psum x1, blocking collectives, body(): lax.psum((jnp.sum(first_basis * second_image), jnp.sum(second_basis * sec...  37.2 us
    gather x4, local copies, waits for them, and re-layouts, apply_operator(): picked = coded_vec[wanted_rows]  34 us
    ppermute x6, waiting for transfers between devices, from_behind(): return lax.ppermute(block, axis, route)  20.8 us
  transfers between devices with their start and end apart: 9, of which 8 were waited for; matrix products, arithmetic and copies ran while one was open for 3% of the time, Pallas kernels for 0%

commit v1 on v0

v1 whole, which is shorter than its diff:
```python
import functools

import jax
import jax.numpy as jnp
import numpy as np
from jax import lax
from jax.experimental import pallas as pl
from jax.experimental.pallas import tpu as pltpu
from jax.sharding import PartitionSpec as P

epsilon = 1e-06
LANES = 128
CHUNK = 256
BATCH = 32
VMEM_LIMIT = 56 * 2**20


def cosine_coefficients():
    top = 3.1416**2
    nodes = (np.cos((np.arange(400) + 0.5) * np.pi / 400) + 1.0) * top / 2.0
    fit = np.polynomial.chebyshev.Chebyshev.fit(nodes, np.cos(np.sqrt(nodes)), 8, domain=[0.0, top])
    return [float(c) for c in fit.convert(kind=np.polynomial.Polynomial).coef]


COS = cosine_coefficients()


def cosine(angle):
    square = angle * angle
    value = jnp.full_like(square, COS[-1])
    for coef in COS[-2::-1]:
        value = value * square + coef
    return value


def whole(memory=pltpu.VMEM):
    return pl.BlockSpec(memory_space=memory)


def params():
    return pltpu.CompilerParams(vmem_limit_bytes=VMEM_LIMIT)


def pad_lanes(value, width):
    rows, cols = value.shape
    return jnp.concatenate([value, jnp.zeros((rows, width - cols), value.dtype)], axis=1)


def code_kernel(field_ref, coded_ref):
    coefs, rows = field_ref.shape
    width = coded_ref.shape[1]
    for start in range(0, rows, CHUNK):
        part = field_ref[:, pl.ds(start, CHUNK)]
        part = jnp.concatenate([part, jnp.zeros((width - coefs, CHUNK), part.dtype)], axis=0)
        coded_ref[pl.ds(start, CHUNK), :] = part.T.astype(jnp.bfloat16)


def code(field_t, width):
    rows = field_t.shape[1]
    return pl.pallas_call(
        code_kernel,
        out_shape=jax.ShapeDtypeStruct((rows, width), jnp.bfloat16),
        in_specs=[whole()],
        out_specs=whole(),
        compiler_params=params(),
        name="code_rows",
    )(field_t)


def wave_kernel(coded_ref, out_ref, angle_ref, sum_ref):
    coefs, samples = out_ref.shape
    rows = coded_ref.shape[0]

    def part(index, total):
        at = pl.ds(pl.multiple_of(index * CHUNK, CHUNK), CHUNK)
        outgoing = jnp.dot(
            coded_ref[at, :][:, :coefs], out_ref[...], preferred_element_type=jnp.float32
        )
        weighted = cosine(angle_ref[at, :].astype(jnp.float32)) * outgoing
        return total + jnp.sum(weighted, axis=0, keepdims=True)

    sum_ref[...] = lax.fori_loop(0, rows // CHUNK, part, jnp.zeros((1, samples), jnp.float32))


def gather_wave(coded, wave_out, angle):
    rows, samples = angle.shape
    return pl.pallas_call(
        wave_kernel,
        out_shape=jax.ShapeDtypeStruct((1, samples), jnp.float32),
        in_specs=[whole()] * 3,
        out_specs=whole(),
        compiler_params=params(),
        cost_estimate=pl.CostEstimate(
            flops=2 * rows * samples * 256, bytes_accessed=2 * 2**20, transcendentals=0
        ),
        name="gather_wave",
    )(coded, wave_out, angle)


def spread_kernel(incoming_ref, in_ref, angle_ref, far_ref):
    rows = angle_ref.shape[0]

    def part(index, carry):
        at = pl.ds(pl.multiple_of(index * CHUNK, CHUNK), CHUNK)
        spread = cosine(angle_ref[at, :].astype(jnp.float32)) * incoming_ref[...]
        far_ref[at, :] = lax.dot_general(
            spread.astype(jnp.bfloat16),
            in_ref[...],
            (((1,), (1,)), ((), ())),
            preferred_element_type=jnp.float32,
        )
        return carry

    lax.fori_loop(0, rows // CHUNK, part, 0)


def spread_wave(incoming, wave_in_t, angle):
    rows, samples = angle.shape
    coefs = wave_in_t.shape[0]
    return pl.pallas_call(
        spread_kernel,
        out_shape=jax.ShapeDtypeStruct((rows, coefs), jnp.float32),
        in_specs=[whole()] * 3,
        out_specs=whole(),
        compiler_params=params(),
        cost_estimate=pl.CostEstimate(
            flops=2 * rows * samples * 256, bytes_accessed=3 * 2**20, transcendentals=0
        ),
        name="spread_wave",
    )(incoming, wave_in_t, angle)


def near_kernel(groups, second, slot_ref, table_ref, tables_ref, vec_ref, mie_ref, far_ref, *rest):
    if second:
        first_ref, sums_in_ref, *rest = rest
    count = sum(groups)
    shards, (image_ref, other_ref, sums_ref, source, picked) = rest[:count], rest[count:]
    rows, coefs = vec_ref.shape
    requests = slot_ref.shape[0]
    per_row = requests // rows
    width = 2 * LANES
    first = 0
    for place, members in enumerate(groups):
        value = shards[first][...].astype(jnp.float32)
        for member in range(1, members):
            value = value + shards[first + member][...].astype(jnp.float32)
        first += members
        base = place * 2 * rows
        source[pl.ds(base, rows, stride=2), :] = value[:, :LANES]
        source[pl.ds(base + 1, rows, stride=2), :] = value[:, LANES:]

    def pick(step, carry):
        start = pl.multiple_of(step * BATCH, BATCH)
        got = [
            source[pl.ds(pl.multiple_of(slot_ref[start + k], 2), 2), :] for k in range(BATCH)
        ]
        for k in range(0, BATCH, 4):
            picked[pl.ds(pl.multiple_of(2 * (start + k), 8), 8), :] = jnp.concatenate(
                got[k : k + 4], axis=0
            )
        return carry

    lax.fori_loop(0, requests // BATCH, pick, 0)

    def part(index, sums):
        start = pl.multiple_of(index * CHUNK, CHUNK)
        at = pl.ds(start, CHUNK)
        stride = 2 * per_row
        halves = [
            [
                picked[pl.ds(start * stride + 2 * k + h, CHUNK, stride=stride), :].astype(
                    jnp.bfloat16
                )
                for h in range(2)
            ]
            for k in range(per_row)
        ]
        named = [
            jnp.broadcast_to(table_ref[at, k : k + 1], (CHUNK, LANES)).astype(jnp.bfloat16)
            for k in range(per_row)
        ]
        zero = jnp.zeros((CHUNK, LANES), jnp.bfloat16)
        near = jnp.zeros((CHUNK, coefs), jnp.float32)
        for t in range(tables_ref.shape[0]):
            chosen = [named[k] == jnp.bfloat16(t) for k in range(per_row)]
            mixed = []
            for h in range(2):
                value = jnp.where(chosen[0], halves[0][h], zero)
                for k in range(1, per_row):
                    value = value + jnp.where(chosen[k], halves[k][h], zero)
                mixed.append(value)
            near = near + jnp.dot(
                jnp.concatenate(mixed, axis=1)[:, :coefs],
                tables_ref[t],
                preferred_element_type=jnp.float32,
            )
        vec = vec_ref[at, :]
        image = vec - mie_ref[at, :] * (near + far_ref[at, :])

        def dot(a, b):
            return jnp.sum(a * b, axis=0, keepdims=True)

        if second:
            image_ref[:, at] = pad_lanes(image, width).T[:coefs, :]
            new = [dot(first_ref[at, :], image), dot(vec, image), dot(image, image)]
        else:
            image_ref[at, :] = image
            other_ref[at, :] = pad_lanes(image, width).astype(jnp.bfloat16)
            new = [dot(vec, vec), dot(vec, image), dot(image, image)]
        return tuple(a + b for a, b in zip(sums, new, strict=True))

    sums = lax.fori_loop(
        0, rows // CHUNK, part, tuple(jnp.zeros((1, coefs), jnp.float32) for _ in range(3))
    )
    lane = lax.broadcasted_iota(jnp.int32, (1, LANES), 1)
    packed = sums_in_ref[...] if second else jnp.zeros((1, LANES), jnp.float32)
    for k, value in enumerate(sums):
        total = jnp.sum(value, axis=1, keepdims=True)
        packed = jnp.where(lane == k + (3 if second else 0), total, packed)
    sums_ref[...] = jnp.broadcast_to(packed, sums_ref.shape)


def near_field(groups, slots, table_ids, tables, vec, mie, far, shards, second=None, devices=1):
    rows, coefs = vec.shape
    requests = slots.shape[0]
    width = 2 * LANES
    extra = () if second is None else second
    if second is None:
        outs = (
            jax.ShapeDtypeStruct((rows, coefs), jnp.float32),
            jax.ShapeDtypeStruct((rows, width), jnp.bfloat16),
            jax.ShapeDtypeStruct((1, LANES), jnp.float32),
        )
    else:
        outs = (
            jax.ShapeDtypeStruct((coefs, rows), jnp.float32),
            jax.ShapeDtypeStruct((8, LANES), jnp.float32),
            jax.ShapeDtypeStruct((devices, LANES), jnp.float32),
        )
    return pl.pallas_call(
        functools.partial(near_kernel, groups, second is not None),
        out_shape=outs,
        in_specs=[whole(pltpu.SMEM)] + [whole()] * (5 + len(extra) + len(shards)),
        out_specs=(whole(),) * 3,
        scratch_shapes=[
            pltpu.VMEM((len(groups) * rows * 2, LANES), jnp.float32),
            pltpu.VMEM((requests * 2, LANES), jnp.float32),
        ],
        compiler_params=params(),
        cost_estimate=pl.CostEstimate(
            flops=2 * rows * 8 * 256 * 256, bytes_accessed=10 * 2**20, transcendentals=0
        ),
        name="near_second" if second is not None else "near_first",
    )(slots, table_ids, tables, vec, mie, far, *extra, *shards)


def finish_kernel(sums_ref, x_ref, u_ref, v_ref, solution_ref, residual_ref, hess_ref):
    sums = jnp.sum(sums_ref[...], axis=0, keepdims=True)
    xx, xu, uu, xv, uv, vv = [sums[:, k : k + 1] for k in range(6)]
    norm = jnp.sqrt(xx + epsilon)
    inverse = 1.0 / norm
    squared = inverse * inverse
    h11 = xu * squared
    ones = xx * squared
    size1 = uu * squared - 2.0 * h11 * h11 + h11 * h11 * ones
    h21 = jnp.sqrt(jnp.maximum(size1, 0.0) + epsilon)
    q = inverse / h21
    h12 = q * inverse * (xv - h11 * xu)
    h22 = q * q * (uv - h11 * uu - h11 * xv + h11 * h11 * xu)
    size2 = q * q * (vv - 2.0 * h11 * uv + h11 * h11 * uu)
    cross = q * inverse * (xu - h11 * xx)
    twos = size1 / (h21 * h21)
    left = (
        size2
        - 2.0 * h12 * h12
        - 2.0 * h22 * h22
        + h12 * h12 * ones
        + h22 * h22 * twos
        + 2.0 * h12 * h22 * cross
    )
    h32 = jnp.sqrt(jnp.maximum(left, 0.0) + epsilon)
    gram00 = h11 * h11 + h21 * h21
    gram01 = h11 * h12 + h21 * h22
    gram11 = h12 * h12 + h22 * h22 + h32 * h32
    rhs0, rhs1 = norm * h11, norm * h12
    det = gram00 * gram11 - gram01 * gram01
    y1 = (gram11 * rhs0 - gram01 * rhs1) / det
    y2 = (gram00 * rhs1 - gram01 * rhs0) / det
    x, u, v = x_ref[...], u_ref[...], v_ref[...]
    a1, a2 = y1 * inverse, y2 * q
    solution_ref[...] = (a1 - h11 * a2) * x + a2 * u
    residual_ref[...] = x - (a1 - h11 * a2) * u - a2 * v
    hess_ref[0:1, 0:1] = h11
    hess_ref[0:1, 1:2] = h21
    hess_ref[0:1, 2:3] = jnp.zeros_like(h11)
    hess_ref[1:2, 0:1] = h12
    hess_ref[1:2, 1:2] = h22
    hess_ref[1:2, 2:3] = h32


def finish(sums, x_t, u_t, v_t):
    coefs, rows = x_t.shape
    part = 48 if coefs % 48 == 0 else coefs
    block = pl.BlockSpec((part, rows), lambda i: (i, 0))
    return pl.pallas_call(
        finish_kernel,
        grid=(coefs // part,),
        out_shape=(
            jax.ShapeDtypeStruct((coefs, rows), jnp.float32),
            jax.ShapeDtypeStruct((coefs, rows), jnp.float32),
            jax.ShapeDtypeStruct((2, 3), jnp.float32),
        ),
        in_specs=[pl.BlockSpec(sums.shape, lambda i: (0, 0)), block, block, block],
        out_specs=(block, block, pl.BlockSpec((2, 3), lambda i: (0, 0))),
        compiler_params=params(),
        name="finish",
    )(sums, x_t, u_t, v_t)


def along_chips(block, moves):
    return lax.ppermute(block, "grp", [(2 * a + c, 2 * b + c) for a, b in moves for c in range(2)])


def other_core(block):
    return lax.ppermute(block, "grp", [(i, i ^ 1) for i in range(lax.axis_size("grp"))])


def exchange(coded):
    chips = lax.axis_size("grp") // 2
    everyone = [[coded]]
    ring = {
        m: along_chips(coded, [((z + m) % chips, z) for z in range(chips)])
        for m in range(1, chips)
        if not (chips == 4 and m == 2)
    }
    for m in range(1, chips):
        if m in ring:
            everyone.append([ring[m]])
        else:
            everyone.append(
                [along_chips(ring[1], [(1, 0), (2, 1)]), along_chips(ring[3], [(1, 2), (2, 3)])]
            )
    groups, blocks = [], []
    for members in everyone:
        groups += [len(members)] * 2
        blocks += members + [other_core(block) for block in members]
    return tuple(groups), blocks


def far_field(coded, wave_out, wave_in_t, angle, trans_rows):
    blocks = lax.axis_size("blk")
    own = gather_wave(coded, wave_out, angle)
    here = lax.axis_index("blk")
    incoming = jnp.zeros_like(own)
    for turn in range(1, blocks):
        moved = lax.ppermute(own, "blk", [((i - turn) % blocks, i) for i in range(blocks)])
        weights = lax.dynamic_slice_in_dim(trans_rows, (here - turn) % blocks, 1, 0)
        incoming = incoming + weights * moved
    return spread_wave(incoming, wave_in_t, angle)


def body(
    incident,
    mie_coef,
    owner_dev,
    near_row,
    table_id,
    tables,
    wave_out,
    wave_in,
    plane_angle,
    far_trans,
):
    x = incident[0]
    mie = mie_coef[0]
    angle = plane_angle[0]
    rows, coefs = x.shape
    width = -(-coefs // LANES) * LANES
    chips = lax.axis_size("grp") // 2
    devices = lax.axis_size("grp") * lax.axis_size("blk")
    me = lax.axis_index("grp")
    owner = owner_dev[0, :, 0]
    away = ((owner // 2 - me // 2) % chips) * 2 + ((owner % 2) ^ (me % 2))
    slots = 2 * (away * rows + near_row[0])
    table_ids = table_id[0].reshape(rows, -1)
    wave_in_t = wave_in.T

    x_t = x.T
    coded = code(x_t, width)
    groups, shards = exchange(coded)
    far = far_field(coded, wave_out, wave_in_t, angle, far_trans[0, 0])
    image, coded, sums = near_field(groups, slots, table_ids, tables, x, mie, far, shards)

    groups, shards = exchange(coded)
    far = far_field(coded, wave_out, wave_in_t, angle, far_trans[0, 0])
    second_t, _, sums = near_field(
        groups, slots, table_ids, tables, image, mie, far, shards, (x, sums), devices
    )
    sums = lax.all_to_all(sums, ("blk", "grp"), 0, 0, tiled=True)
    solution_t, residual_t, hess_t = finish(sums, x_t, image.T, second_t)
    return solution_t.T[None], residual_t.T[None], hess_t.T


def solution(mesh):
    return jax.shard_map(
        body,
        mesh=mesh,
        in_specs=(
            P("blk", "grp", None),
            P("blk", "grp", None),
            P("blk", "grp", None),
            P("blk", "grp"),
            P("blk", "grp"),
            P(),
            P(),
            P(),
            P("blk", "grp", None),
            P("blk", "grp", None, None),
        ),
        out_specs=(P("blk", "grp", None), P("blk", "grp", None), P()),
        check_vma=False,
    )
```

time: 542 us -> 148 us (0.27)
  local copies, waits for them, and re-layouts: 174 us -> 8.45 us
  blocking collectives: 116 us -> 0 us
  matrix products: 90.6 us -> 0 us
  Pallas kernels: 0 us -> 47.4 us
  waiting for transfers between devices: 95.8 us -> 61.6 us
  other arithmetic: 28.7 us -> 2.51 us
  between operations: 10.3 us -> 0.85 us
    gather x6 -> x0, local copies, waits for them, and re-layouts: 139 us -> none  [the longest x2 105 us: apply_operator(): answered[owner_ids, slot_ids]]
    psum x3 -> x0, blocking collectives: 116 us -> none  [the longest x1 41 us: squared_norm(): return lax.psum(jnp.sum(field * field), ('blk', 'grp'))]
    dot_general x20 -> x0, matrix products: 90.6 us -> none  [the longest x16 53.7 us: add_table(): jnp.dot(chosen, tables[table_index], preferred_element_type=jnp.float32)]
    all_to_all x3 -> x1, waiting for transfers between devices: 75 us -> 5.82 us  [body(): sums = lax.all_to_all(sums, ('blk', 'grp'), 0, 0, tiled=True)]
    pallas_call x0 -> x8, Pallas kernels: none -> 47.4 us  [the longest x2 22.8 us: near_field(): pl.pallas_call(functools.partial(near_kernel, groups, second is not None)...]
    ppermute x6 -> x24, waiting for transfers between devices: 20.8 us -> 55.8 us  [the longest x8 50.2 us: along_chips(): lax.ppermute(block, 'grp', [(2 * a + c, 2 * b + c) for a, b in moves for...]
    ppermute x6 -> x24, starting transfers between devices: 7.05 us -> 21.5 us  [the longest x8 12.5 us: along_chips(): lax.ppermute(block, 'grp', [(2 * a + c, 2 * b + c) for a, b in moves for...]
    reduce_sum x4 -> x0, other arithmetic: 12.3 us -> none  [the longest x2 9.49 us: apply_operator(): near_terms.astype(jnp.float32).reshape(local_rows, per_row, coef_count)]
  transfers between devices with their start and end apart: 9 -> 25, of which waited for: 8 -> 12; matrix products, arithmetic and copies ran while one was open for 3% -> 5% of each run, Pallas kernels for 0% -> 11%
where the time goes in v1:
time: 148 us
  waiting for transfers between devices  61.6 us (42%)
  Pallas kernels  47.4 us (32%)
  starting transfers between devices  26.7 us (18%)
  local copies, waits for them, and re-layouts  8.45 us (6%)
  other arithmetic  2.51 us (2%)
    ppermute x8, waiting for transfers between devices, along_chips(): lax.ppermute(block, 'grp', [(2 * a + c, 2 * b + c) for a, b in moves for...  50.2 us
    pallas_call x2, Pallas kernels, near_field(): pl.pallas_call(functools.partial(near_kernel, groups, second is not None)...  22.8 us
    ppermute x8, starting transfers between devices, along_chips(): lax.ppermute(block, 'grp', [(2 * a + c, 2 * b + c) for a, b in moves for...  12.5 us
    pallas_call x2, Pallas kernels, spread_wave(): pl.pallas_call(spread_kernel, out_shape=jax.ShapeDtypeStruct((rows, coefs...  8.58 us
    ppermute x6, starting transfers between devices, far_field(): lax.ppermute(own, 'blk', [((i - turn) % blocks, i) for i in range(blocks)])  7.87 us
    pallas_call x2, Pallas kernels, gather_wave(): pl.pallas_call(wave_kernel, out_shape=jax.ShapeDtypeStruct((1, samples),...  7.76 us
    pallas_call x1, Pallas kernels, finish(): pl.pallas_call(finish_kernel, grid=(coefs // part,), out_shape=(jax.Shape...  6.04 us
    all_to_all x1, waiting for transfers between devices, body(): sums = lax.all_to_all(sums, ('blk', 'grp'), 0, 0, tiled=True)  5.82 us
  transfers between devices with their start and end apart: 25, of which 12 were waited for; matrix products, arithmetic and copies ran while one was open for 5% of the time, Pallas kernels for 11%

profile of v1, /device:TPU:0, one launch (start us, length us, event | category | flops | bytes accessed | tf_op | source)
XLA Modules:
  0.0 147.5 jit_solution(7779364450536268781)
XLA Ops:
  0.6 2.2 %code_rows.1.coded_ref.rest_0_ = bf16[1024,256]{1,0:T(8,128)(2,1)} custom-call(f32[240,1024]{1,0:T(8,128)} %bitcast.51), custom_call_target="tpu_custom_call" | custom-call | tf_op jit(solution)/shard_map/code_rows/pallas_call | solution.py:60
  2.8 3.0 %collective-permute-start.7 = (bf16[1024,256]{1,0:T(8,128)(2,1)}, bf16[1024,256]{1,0:T(8,128)(2,1)S(1)}, u32[]{:S(2)}, u32[]{:S(2)}) collective-permute-start(bf16[1024,256]{1,0:T(8,128)(2,1)} %code_rows.1.coded_ref.rest_0_), channel_id=1, source_target_pairs={{6,0},{7,1},{0,2},{1,3},{2,4},{3,5},{4,6},{5,7},{14,8},{15,9},{8,1... | collective-permute-start | bytes 1572872 | tf_op jit(solution)/shard_map/ppermute | solution.py:321
  5.9 2.0 %collective-permute-start.4 = (bf16[1024,256]{1,0:T(8,128)(2,1)}, bf16[1024,256]{1,0:T(8,128)(2,1)S(1)}, u32[]{:S(2)}, u32[]{:S(2)}) collective-permute-start(bf16[1024,256]{1,0:T(8,128)(2,1)} %code_rows.1.coded_ref.rest_0_), channel_id=1, source_target_pairs={{2,0},{3,1},{4,2},{5,3},{6,4},{7,5},{0,6},{1,7},{10,8},{11,9},{12,... | collective-permute-start | bytes 1572872 | tf_op jit(solution)/shard_map/ppermute | solution.py:321
  7.9 13.0 %collective-permute-done.7.rest_8_ = bf16[1024,256]{1,0:T(8,128)(2,1)S(1)} collective-permute-done((bf16[1024,256]{1,0:T(8,128)(2,1)}, bf16[1024,256]{1,0:T(8,128)(2,1)S(1)}, u32[]{:S(2)}, u32[]{:S(2)}) %collective-permute-start.7) | collective-permute-done | bytes 524320 | tf_op jit(solution)/shard_map/ppermute | solution.py:321
  20.9 1.5 %collective-permute-start.8 = (bf16[1024,256]{1,0:T(8,128)(2,1)S(1)}, bf16[1024,256]{1,0:T(8,128)(2,1)}, u32[]{:S(2)}, u32[]{:S(2)}) collective-permute-start(bf16[1024,256]{1,0:T(8,128)(2,1)S(1)} %collective-permute-done.7.rest_8_), channel_id=1, source_target_pairs={{2,4},{3,5},{4,6},{5,7},{10,12},{11,13},{12,14},{13,15},{18,20},{1... | collective-permute-start | bytes 1572872 | tf_op jit(solution)/shard_map/ppermute | solution.py:321
  22.4 8.3 %collective-permute-done.4.rest_2_ = bf16[1024,256]{1,0:T(8,128)(2,1)S(1)} collective-permute-done((bf16[1024,256]{1,0:T(8,128)(2,1)}, bf16[1024,256]{1,0:T(8,128)(2,1)S(1)}, u32[]{:S(2)}, u32[]{:S(2)}) %collective-permute-start.4) | collective-permute-done | bytes 524320 | tf_op jit(solution)/shard_map/ppermute | solution.py:321
  30.7 1.3 collective-permute-start.6
  32.0 3.9 %gather_wave.2 = f32[1,512]{1,0:T(1,128)} custom-call(bf16[1024,256]{1,0:T(8,128)(2,1)} %code_rows.1.coded_ref.rest_0_, bf16[240,512]{1,0:T(8,128)(2,1)} %out_ref.3, bf16[1024,512]{1,0:T(8,128)(2,1)} %bitcast.45), custom_call_target="tpu_custom_call" | custom-call | flops 268435456 | bytes 2097152 | tf_op jit(solution)/shard_map/gather_wave/pallas_call | solution.py:87
  35.9 1.5 %collective-permute-start = (f32[1,512]{1,0:T(1,128)}, f32[1,512]{1,0:T(1,128)S(1)}, u32[]{:S(2)}, u32[]{:S(2)}) collective-permute-start(f32[1,512]{1,0:T(1,128)} %gather_wave.2), channel_id=1, source_target_pairs={{24,0},{0,8},{8,16},{16,24},{25,1},{1,9},{9,17},{17,25},{26,2},{2,... | collective-permute-start | bytes 6152 | tf_op jit(solution)/shard_map/ppermute | solution.py:356
  37.4 1.5 %collective-permute-start.1 = (f32[1,512]{1,0:T(1,128)}, f32[1,512]{1,0:T(1,128)S(1)}, u32[]{:S(2)}, u32[]{:S(2)}) collective-permute-start(f32[1,512]{1,0:T(1,128)} %gather_wave.2), channel_id=1, source_target_pairs={{16,0},{24,8},{0,16},{8,24},{17,1},{25,9},{1,17},{9,25},{18,2},{26... | collective-permute-start | bytes 6152 | tf_op jit(solution)/shard_map/ppermute | solution.py:356
  38.9 1.4 collective-permute-start.2
  40.6 0.6 collective-permute-done.1
  41.2 1.5 %collective-permute-done.2 = f32[1,512]{1,0:T(1,128)S(1)} collective-permute-done((f32[1,512]{1,0:T(1,128)}, f32[1,512]{1,0:T(1,128)S(1)}, u32[]{:S(2)}, u32[]{:S(2)}) %collective-permute-start.2) | collective-permute-done | bytes 2080 | tf_op jit(solution)/shard_map/ppermute | solution.py:356
  42.7 0.5 collective-permute-start.10
  43.2 2.7 %collective-permute-done.6.rest_4_ = bf16[1024,256]{1,0:T(8,128)(2,1)} collective-permute-done((bf16[1024,256]{1,0:T(8,128)(2,1)S(1)}, bf16[1024,256]{1,0:T(8,128)(2,1)}, u32[]{:S(2)}, u32[]{:S(2)}) %collective-permute-start.6) | collective-permute-done | bytes 524320 | tf_op jit(solution)/shard_map/ppermute | solution.py:321
  45.9 1.3 copy.21
  47.2 1.3 copy.22.vec_ref.rest_0_
  48.6 0.5 broadcast.29
  49.1 0.7 reduce.3
  49.8 1.1 reshape_squeeze.3.table_ref
  50.9 0.7 copy-done.19
  51.6 0.6 fusion.6.slot_ref
  52.3 0.5 fusion.9.incoming_ref
  52.9 4.3 %spread_wave.2.far_ref = f32[1024,240]{1,0:T(8,128)} custom-call(f32[1,512]{1,0:T(1,128)} %fusion.9.incoming_ref, bf16[240,512]{1,0:T(8,128)(2,1)} %bitcast.55, bf16[1024,512]{1,0:T(8,128)(2,1)} %bitcast.46), custom_call_target="tpu_custom_call" | custom-call | flops 268435456 | bytes 3145728 | tf_op jit(solution)/shard_map/spread_wave/pallas_call | solution.py:120
  57.2 11.2 %near_first.1 = (f32[1024,240]{1,0:T(8,128)}, bf16[1024,256]{1,0:T(8,128)(2,1)}, f32[1,128]{1,0:T(1,128)}) custom-call(s32[3072]{0:T(1024)} %fusion.6.slot_ref, s32[1024,3]{1,0:T(8,128)} %reshape_squeeze.3.table_ref, bf16[8,240,240]{2,1,0:T(8,128)(2,1)} %tables_ref.3, f32[1024,240]{1,0:T(8,128)} %copy.22.vec_ref.rest_0_, f32[1024,240]{1,0:T(8,128)} %bitcast.49, ...), custom_call_target="tpu_custom_call" | custom-call | flops 1073741824 | bytes 10485760 | tf_op jit(solution)/shard_map/near_first/pallas_call | solution.py:240
  68.4 1.2 collective-permute-start.16
  69.6 1.5 %collective-permute-start.19 = (bf16[1024,256]{1,0:T(8,128)(2,1)}, bf16[1024,256]{1,0:T(8,128)(2,1)S(1)}, u32[]{:S(2)}, u32[]{:S(2)}) collective-permute-start(bf16[1024,256]{1,0:T(8,128)(2,1)} %get-tuple-element.12.coded_ref.rest_2_), channel_id=1, source_target_pairs={{6,0},{7,1},{0,2},{1,3},{2,4},{3,5},{4,6},{5,7},{14,8},{15,9},{8,1... | collective-permute-start | bytes 1572872 | tf_op jit(solution)/shard_map/ppermute | solution.py:321
  71.1 12.7 %collective-permute-done.16.rest_4_ = bf16[1024,256]{1,0:T(8,128)(2,1)S(1)} collective-permute-done((bf16[1024,256]{1,0:T(8,128)(2,1)}, bf16[1024,256]{1,0:T(8,128)(2,1)S(1)}, u32[]{:S(2)}, u32[]{:S(2)}) %collective-permute-start.16) | collective-permute-done | bytes 524320 | tf_op jit(solution)/shard_map/ppermute | solution.py:321
  83.8 1.3 collective-permute-start.18
  85.1 13.5 %collective-permute-done.19.rest_10_ = bf16[1024,256]{1,0:T(8,128)(2,1)S(1)} collective-permute-done((bf16[1024,256]{1,0:T(8,128)(2,1)}, bf16[1024,256]{1,0:T(8,128)(2,1)S(1)}, u32[]{:S(2)}, u32[]{:S(2)}) %collective-permute-start.19) | collective-permute-done | bytes 524320 | tf_op jit(solution)/shard_map/ppermute | solution.py:321
  98.6 0.7 collective-permute-start.20
  99.3 3.9 %gather_wave.3 = f32[1,512]{1,0:T(1,128)} custom-call(bf16[1024,256]{1,0:T(8,128)(2,1)} %get-tuple-element.12.coded_ref.rest_2_, bf16[240,512]{1,0:T(8,128)(2,1)} %out_ref.3, bf16[1024,512]{1,0:T(8,128)(2,1)} %bitcast.47), custom_call_target="tpu_custom_call" | custom-call | flops 268435456 | bytes 2097152 | tf_op jit(solution)/shard_map/gather_wave/pallas_call | solution.py:87
  103.1 1.4 collective-permute-start.12
  104.5 1.5 %collective-permute-start.13 = (f32[1,512]{1,0:T(1,128)}, f32[1,512]{1,0:T(1,128)S(1)}, u32[]{:S(2)}, u32[]{:S(2)}) collective-permute-start(f32[1,512]{1,0:T(1,128)} %gather_wave.3), channel_id=1, source_target_pairs={{16,0},{24,8},{0,16},{8,24},{17,1},{25,9},{1,17},{9,25},{18,2},{26... | collective-permute-start | bytes 6152 | tf_op jit(solution)/shard_map/ppermute | solution.py:356
  106.0 0.5 collective-permute-start.14
  106.6 1.3 collective-permute-done.12
  107.8 0.5 collective-permute-done.13
  108.3 1.5 collective-permute-done.14
  109.8 0.5 collective-permute-start.21
  110.4 0.7 fusion.10.incoming_ref
  111.1 4.3 %spread_wave.3.far_ref = f32[1024,240]{1,0:T(8,128)} custom-call(f32[1,512]{1,0:T(1,128)} %fusion.10.incoming_ref, bf16[240,512]{1,0:T(8,128)(2,1)} %bitcast.56, bf16[1024,512]{1,0:T(8,128)(2,1)} %bitcast.48), custom_call_target="tpu_custom_call" | custom-call | flops 268435456 | bytes 3145728 | tf_op jit(solution)/shard_map/spread_wave/pallas_call | solution.py:120
  115.5 0.7 copy-done.9
  116.9 11.6 %near_second.1 = (f32[240,1024]{1,0:T(8,128)}, f32[8,128]{1,0:T(8,128)}, f32[32,128]{1,0:T(8,128)}) custom-call(s32[3072]{0:T(1024)} %fusion.6.slot_ref, s32[1024,3]{1,0:T(8,128)} %reshape_squeeze.3.table_ref, bf16[8,240,240]{2,1,0:T(8,128)(2,1)} %tables_ref.3, f32[1024,240]{1,0:T(8,128)} %get-tuple-element.11.vec_ref, f32[1024,240]{1,0:T(8,128)} %bitcast.50, ...), custom_call_target="tpu_custom_call" | custom-call | flops 1073741824 | bytes 10485760 | tf_op jit(solution)/shard_map/near_second/pallas_call | solution.py:240
  128.5 5.2 %all-to-all-start = ((f32[32,1,128]{2,1,0:T(1,128)}), f32[32,1,128]{2,1,0:T(1,128)S(1)}, u32[]{:S(2)}, u32[]{:S(2)}) async-start(f32[32,1,128]{2,1,0:T(1,128)} %bitcast.58), calls=%async_computation | async-start | bytes 32768 | tf_op jit(solution)/shard_map/all_to_all | solution.py:399
  133.8 1.3 copy.25
  135.1 5.8 %all-to-all-done = f32[32,1,128]{2,1,0:T(1,128)S(1)} async-done(((f32[32,1,128]{2,1,0:T(1,128)}), f32[32,1,128]{2,1,0:T(1,128)S(1)}, u32[]{:S(2)}, u32[]{:S(2)}) %all-to-all-start) | async-done | bytes 16416 | tf_op jit(solution)/shard_map/all_to_all | solution.py:399
  140.9 0.6 copy-done.16
  141.5 6.0 %finish.1 = (f32[240,1024]{1,0:T(8,128)}, f32[240,1024]{1,0:T(8,128)}, f32[2,3]{1,0:T(2,128)}) custom-call(f32[32,128]{1,0:T(8,128)} %bitcast.57, f32[240,1024]{1,0:T(8,128)} %bitcast.52, f32[240,1024]{1,0:T(8,128)} %bitcast.54, f32[240,1024]{1,0:T(8,128)} %get-tuple-element.15.v_ref), custom_call_target="tpu_custom_call" | custom-call | tf_op jit(solution)/shard_map/finish/pallas_call | solution.py:305
  (61 shorter events, 1.3 us)
Async XLA Ops:
  2.8 43.1 %copy-start.4 = (f32[1,1024,240]{1,2,0:T(8,128)S(1)}, f32[1,1024,240]{1,2,0:T(8,128)}, u32[]{:S(2)}) copy-start(f32[1,1024,240]{1,2,0:T(8,128)} %param.11) | copy-start | bytes 2949124
  2.8 18.1 %collective-permute-start.7 = (bf16[1024,256]{1,0:T(8,128)(2,1)}, bf16[1024,256]{1,0:T(8,128)(2,1)S(1)}, u32[]{:S(2)}, u32[]{:S(2)}) collective-permute-start(bf16[1024,256]{1,0:T(8,128)(2,1)} %code_rows.1.coded_ref.rest_0_), channel_id=1, source_target_pairs={{6,0},{7,1},{0,2},{1,3},{2,4},{3,5},{4,6},{5,7},{14,8},{15,9},{8,1... | collective-permute-start | bytes 1572872 | tf_op jit(solution)/shard_map/ppermute | solution.py:321
  5.9 24.8 %collective-permute-start.4 = (bf16[1024,256]{1,0:T(8,128)(2,1)}, bf16[1024,256]{1,0:T(8,128)(2,1)S(1)}, u32[]{:S(2)}, u32[]{:S(2)}) collective-permute-start(bf16[1024,256]{1,0:T(8,128)(2,1)} %code_rows.1.coded_ref.rest_0_), channel_id=1, source_target_pairs={{2,0},{3,1},{4,2},{5,3},{6,4},{7,5},{0,6},{1,7},{10,8},{11,9},{12,... | collective-permute-start | bytes 1572872 | tf_op jit(solution)/shard_map/ppermute | solution.py:321
  20.9 20.3 %copy-start.14 = (bf16[1024,256]{1,0:T(8,128)(2,1)}, bf16[1024,256]{1,0:T(8,128)(2,1)S(1)}, u32[]{:S(2)}) copy-start(bf16[1024,256]{1,0:T(8,128)(2,1)S(1)} %collective-permute-done.7.rest_8_) | copy-start | bytes 1572868
  20.9 21.8 %collective-permute-start.8 = (bf16[1024,256]{1,0:T(8,128)(2,1)S(1)}, bf16[1024,256]{1,0:T(8,128)(2,1)}, u32[]{:S(2)}, u32[]{:S(2)}) collective-permute-start(bf16[1024,256]{1,0:T(8,128)(2,1)S(1)} %collective-permute-done.7.rest_8_), channel_id=1, source_target_pairs={{2,4},{3,5},{4,6},{5,7},{10,12},{11,13},{12,14},{13,15},{18,20},{1... | collective-permute-start | bytes 1572872 | tf_op jit(solution)/shard_map/ppermute | solution.py:321
  30.7 12.0 %copy-start.15 = (bf16[1024,256]{1,0:T(8,128)(2,1)}, bf16[1024,256]{1,0:T(8,128)(2,1)S(1)}, u32[]{:S(2)}) copy-start(bf16[1024,256]{1,0:T(8,128)(2,1)S(1)} %collective-permute-done.4.rest_2_) | copy-start | bytes 1572868
  30.7 15.2 %collective-permute-start.6 = (bf16[1024,256]{1,0:T(8,128)(2,1)S(1)}, bf16[1024,256]{1,0:T(8,128)(2,1)}, u32[]{:S(2)}, u32[]{:S(2)}) collective-permute-start(bf16[1024,256]{1,0:T(8,128)(2,1)S(1)} %collective-permute-done.4.rest_2_), channel_id=1, source_target_pairs={{2,0},{3,1},{4,2},{5,3},{10,8},{11,9},{12,10},{13,11},{18,16},{19,... | collective-permute-start | bytes 1572872 | tf_op jit(solution)/shard_map/ppermute | solution.py:321
  32.0 8.6 %copy-start.1 = (bf16[1024,256]{1,0:T(8,128)(2,1)S(1)}, bf16[1024,256]{1,0:T(8,128)(2,1)}, u32[]{:S(2)}) copy-start(bf16[1024,256]{1,0:T(8,128)(2,1)} %code_rows.1.coded_ref.rest_0_) | copy-start | bytes 1572868
  35.9 4.7 %collective-permute-start = (f32[1,512]{1,0:T(1,128)}, f32[1,512]{1,0:T(1,128)S(1)}, u32[]{:S(2)}, u32[]{:S(2)}) collective-permute-start(f32[1,512]{1,0:T(1,128)} %gather_wave.2), channel_id=1, source_target_pairs={{24,0},{0,8},{8,16},{16,24},{25,1},{1,9},{9,17},{17,25},{26,2},{2,... | collective-permute-start | bytes 6152 | tf_op jit(solution)/shard_map/ppermute | solution.py:356
  37.4 3.8 %collective-permute-start.1 = (f32[1,512]{1,0:T(1,128)}, f32[1,512]{1,0:T(1,128)S(1)}, u32[]{:S(2)}, u32[]{:S(2)}) collective-permute-start(f32[1,512]{1,0:T(1,128)} %gather_wave.2), channel_id=1, source_target_pairs={{16,0},{24,8},{0,16},{8,24},{17,1},{25,9},{1,17},{9,25},{18,2},{26... | collective-permute-start | bytes 6152 | tf_op jit(solution)/shard_map/ppermute | solution.py:356
  38.9 3.8 %collective-permute-start.2 = (f32[1,512]{1,0:T(1,128)}, f32[1,512]{1,0:T(1,128)S(1)}, u32[]{:S(2)}, u32[]{:S(2)}) collective-permute-start(f32[1,512]{1,0:T(1,128)} %gather_wave.2), channel_id=1, source_target_pairs={{8,0},{16,8},{24,16},{0,24},{9,1},{17,9},{25,17},{1,25},{10,2},{18... | collective-permute-start | bytes 6152 | tf_op jit(solution)/shard_map/ppermute | solution.py:356
  40.6 16.6 %collective-permute-start.3 = (bf16[1024,256]{1,0:T(8,128)(2,1)S(1)}, bf16[1024,256]{1,0:T(8,128)(2,1)}, u32[]{:S(2)}, u32[]{:S(2)}) collective-permute-start(bf16[1024,256]{1,0:T(8,128)(2,1)S(1)} %copy-done.1), channel_id=1, source_target_pairs={{0,1},{1,0},{2,3},{3,2},{4,5},{5,4},{6,7},{7,6},{8,9},{9,8},{10,11... | collective-permute-start | bytes 1572872 | tf_op jit(solution)/shard_map/ppermute | solution.py:325
  41.2 16.0 %collective-permute-start.11 = (bf16[1024,256]{1,0:T(8,128)(2,1)S(1)}, bf16[1024,256]{1,0:T(8,128)(2,1)}, u32[]{:S(2)}, u32[]{:S(2)}) collective-permute-start(bf16[1024,256]{1,0:T(8,128)(2,1)S(1)} %collective-permute-done.7.rest_8_), channel_id=1, source_target_pairs={{0,1},{1,0},{2,3},{3,2},{4,5},{5,4},{6,7},{7,6},{8,9},{9,8},{10,11... | collective-permute-start | bytes 1572872 | tf_op jit(solution)/shard_map/ppermute | solution.py:325
  42.7 14.5 %collective-permute-start.5 = (bf16[1024,256]{1,0:T(8,128)(2,1)S(1)}, bf16[1024,256]{1,0:T(8,128)(2,1)}, u32[]{:S(2)}, u32[]{:S(2)}) collective-permute-start(bf16[1024,256]{1,0:T(8,128)(2,1)S(1)} %collective-permute-done.4.rest_2_), channel_id=1, source_target_pairs={{0,1},{1,0},{2,3},{3,2},{4,5},{5,4},{6,7},{7,6},{8,9},{9,8},{10,11... | collective-permute-start | bytes 1572872 | tf_op jit(solution)/shard_map/ppermute | solution.py:325
  42.7 14.5 %collective-permute-start.10 = (bf16[1024,256]{1,0:T(8,128)(2,1)}, bf16[1024,256]{1,0:T(8,128)(2,1)}, u32[]{:S(2)}, u32[]{:S(2)}) collective-permute-start(bf16[1024,256]{1,0:T(8,128)(2,1)} %collective-permute-done.8.rest_5_), channel_id=1, source_target_pairs={{0,1},{1,0},{2,3},{3,2},{4,5},{5,4},{6,7},{7,6},{8,9},{9,8},{10,11... | collective-permute-start | bytes 1572872 | tf_op jit(solution)/shard_map/ppermute | solution.py:325
  45.9 11.3 %collective-permute-start.9 = (bf16[1024,256]{1,0:T(8,128)(2,1)}, bf16[1024,256]{1,0:T(8,128)(2,1)}, u32[]{:S(2)}, u32[]{:S(2)}) collective-permute-start(bf16[1024,256]{1,0:T(8,128)(2,1)} %collective-permute-done.6.rest_4_), channel_id=1, source_target_pairs={{0,1},{1,0},{2,3},{3,2},{4,5},{5,4},{6,7},{7,6},{8,9},{9,8},{10,11... | collective-permute-start | bytes 1572872 | tf_op jit(solution)/shard_map/ppermute | solution.py:325
  45.9 1.3 copy-start
  47.2 1.8 %copy-start.18 = (s32[1,3072]{1,0:T(1,128)S(1)}, s32[1,3072]{1,0:T(1,128)}, u32[]{:S(2)}) copy-start(s32[1,3072]{1,0:T(1,128)} %param.14) | copy-start | bytes 36868
  49.8 1.2 copy-start.20
  50.9 0.7 copy-start.19
  51.6 0.7 copy-start.17
  68.4 39.4 %copy-start.3 = (bf16[1024,256]{1,0:T(8,128)(2,1)S(1)}, bf16[1024,256]{1,0:T(8,128)(2,1)}, u32[]{:S(2)}) copy-start(bf16[1024,256]{1,0:T(8,128)(2,1)} %get-tuple-element.12.coded_ref.rest_2_) | copy-start | bytes 1572868
  68.4 15.4 %collective-permute-start.16 = (bf16[1024,256]{1,0:T(8,128)(2,1)}, bf16[1024,256]{1,0:T(8,128)(2,1)S(1)}, u32[]{:S(2)}, u32[]{:S(2)}) collective-permute-start(bf16[1024,256]{1,0:T(8,128)(2,1)} %get-tuple-element.12.coded_ref.rest_2_), channel_id=1, source_target_pairs={{2,0},{3,1},{4,2},{5,3},{6,4},{7,5},{0,6},{1,7},{10,8},{11,9},{12,... | collective-permute-start | bytes 1572872 | tf_op jit(solution)/shard_map/ppermute | solution.py:321
  69.6 29.0 %collective-permute-start.19 = (bf16[1024,256]{1,0:T(8,128)(2,1)}, bf16[1024,256]{1,0:T(8,128)(2,1)S(1)}, u32[]{:S(2)}, u32[]{:S(2)}) collective-permute-start(bf16[1024,256]{1,0:T(8,128)(2,1)} %get-tuple-element.12.coded_ref.rest_2_), channel_id=1, source_target_pairs={{6,0},{7,1},{0,2},{1,3},{2,4},{3,5},{4,6},{5,7},{14,8},{15,9},{8,1... | collective-permute-start | bytes 1572872 | tf_op jit(solution)/shard_map/ppermute | solution.py:321
  83.8 24.5 %copy-start.5 = (bf16[1024,256]{1,0:T(8,128)(2,1)}, bf16[1024,256]{1,0:T(8,128)(2,1)S(1)}, u32[]{:S(2)}) copy-start(bf16[1024,256]{1,0:T(8,128)(2,1)S(1)} %collective-permute-done.16.rest_4_) | copy-start | bytes 1572868
  83.8 26.0 %collective-permute-start.18 = (bf16[1024,256]{1,0:T(8,128)(2,1)S(1)}, bf16[1024,256]{1,0:T(8,128)(2,1)S(1)}, u32[]{:S(2)}, u32[]{:S(2)}) collective-permute-start(bf16[1024,256]{1,0:T(8,128)(2,1)S(1)} %collective-permute-done.16.rest_4_), channel_id=1, source_target_pairs={{2,0},{3,1},{4,2},{5,3},{10,8},{11,9},{12,10},{13,11},{18,16},{19,... | collective-permute-start | bytes 1572872 | tf_op jit(solution)/shard_map/ppermute | solution.py:321
  98.6 11.2 %copy-start.6 = (bf16[1024,256]{1,0:T(8,128)(2,1)}, bf16[1024,256]{1,0:T(8,128)(2,1)S(1)}, u32[]{:S(2)}) copy-start(bf16[1024,256]{1,0:T(8,128)(2,1)S(1)} %collective-permute-done.19.rest_10_) | copy-start | bytes 1572868
  98.6 11.8 %collective-permute-start.20 = (bf16[1024,256]{1,0:T(8,128)(2,1)S(1)}, bf16[1024,256]{1,0:T(8,128)(2,1)S(1)}, u32[]{:S(2)}, u32[]{:S(2)}) collective-permute-start(bf16[1024,256]{1,0:T(8,128)(2,1)S(1)} %collective-permute-done.19.rest_10_), channel_id=1, source_target_pairs={{2,4},{3,5},{4,6},{5,7},{10,12},{11,13},{12,14},{13,15},{18,20},{1... | collective-permute-start | bytes 1572872 | tf_op jit(solution)/shard_map/ppermute | solution.py:321
  103.1 4.7 %collective-permute-start.12 = (f32[1,512]{1,0:T(1,128)}, f32[1,512]{1,0:T(1,128)S(1)}, u32[]{:S(2)}, u32[]{:S(2)}) collective-permute-start(f32[1,512]{1,0:T(1,128)} %gather_wave.3), channel_id=1, source_target_pairs={{24,0},{0,8},{8,16},{16,24},{25,1},{1,9},{9,17},{17,25},{26,2},{2,... | collective-permute-start | bytes 6152 | tf_op jit(solution)/shard_map/ppermute | solution.py:356
  104.5 3.8 %collective-permute-start.13 = (f32[1,512]{1,0:T(1,128)}, f32[1,512]{1,0:T(1,128)S(1)}, u32[]{:S(2)}, u32[]{:S(2)}) collective-permute-start(f32[1,512]{1,0:T(1,128)} %gather_wave.3), channel_id=1, source_target_pairs={{16,0},{24,8},{0,16},{8,24},{17,1},{25,9},{1,17},{9,25},{18,2},{26... | collective-permute-start | bytes 6152 | tf_op jit(solution)/shard_map/ppermute | solution.py:356
  106.0 3.8 %collective-permute-start.14 = (f32[1,512]{1,0:T(1,128)}, f32[1,512]{1,0:T(1,128)S(1)}, u32[]{:S(2)}, u32[]{:S(2)}) collective-permute-start(f32[1,512]{1,0:T(1,128)} %gather_wave.3), channel_id=1, source_target_pairs={{8,0},{16,8},{24,16},{0,24},{9,1},{17,9},{25,17},{1,25},{10,2},{18... | collective-permute-start | bytes 6152 | tf_op jit(solution)/shard_map/ppermute | solution.py:356
  107.8 7.6 %collective-permute-start.15 = (bf16[1024,256]{1,0:T(8,128)(2,1)S(1)}, bf16[1024,256]{1,0:T(8,128)(2,1)S(1)}, u32[]{:S(2)}, u32[]{:S(2)}) collective-permute-start(bf16[1024,256]{1,0:T(8,128)(2,1)S(1)} %copy-done.3), channel_id=1, source_target_pairs={{0,1},{1,0},{2,3},{3,2},{4,5},{5,4},{6,7},{7,6},{8,9},{9,8},{10,11... | collective-permute-start | bytes 1572872 | tf_op jit(solution)/shard_map/ppermute | solution.py:325
  108.3 7.1 %collective-permute-start.17 = (bf16[1024,256]{1,0:T(8,128)(2,1)S(1)}, bf16[1024,256]{1,0:T(8,128)(2,1)S(1)}, u32[]{:S(2)}, u32[]{:S(2)}) collective-permute-start(bf16[1024,256]{1,0:T(8,128)(2,1)S(1)} %collective-permute-done.16.rest_4_), channel_id=1, source_target_pairs={{0,1},{1,0},{2,3},{3,2},{4,5},{5,4},{6,7},{7,6},{8,9},{9,8},{10,11... | collective-permute-start | bytes 1572872 | tf_op jit(solution)/shard_map/ppermute | solution.py:325
  109.8 5.6 %collective-permute-start.23 = (bf16[1024,256]{1,0:T(8,128)(2,1)S(1)}, bf16[1024,256]{1,0:T(8,128)(2,1)S(1)}, u32[]{:S(2)}, u32[]{:S(2)}) collective-permute-start(bf16[1024,256]{1,0:T(8,128)(2,1)S(1)} %collective-permute-done.19.rest_10_), channel_id=1, source_target_pairs={{0,1},{1,0},{2,3},{3,2},{4,5},{5,4},{6,7},{7,6},{8,9},{9,8},{10,11... | collective-permute-start | bytes 1572872 | tf_op jit(solution)/shard_map/ppermute | solution.py:325
  109.8 5.6 %copy-start.7 = (bf16[1024,256]{1,0:T(8,128)(2,1)}, bf16[1024,256]{1,0:T(8,128)(2,1)S(1)}, u32[]{:S(2)}) copy-start(bf16[1024,256]{1,0:T(8,128)(2,1)S(1)} %collective-permute-done.18.rest_6_) | copy-start | bytes 1572868
  109.8 5.6 %collective-permute-start.21 = (bf16[1024,256]{1,0:T(8,128)(2,1)S(1)}, bf16[1024,256]{1,0:T(8,128)(2,1)S(1)}, u32[]{:S(2)}, u32[]{:S(2)}) collective-permute-start(bf16[1024,256]{1,0:T(8,128)(2,1)S(1)} %collective-permute-done.18.rest_6_), channel_id=1, source_target_pairs={{0,1},{1,0},{2,3},{3,2},{4,5},{5,4},{6,7},{7,6},{8,9},{9,8},{10,11... | collective-permute-start | bytes 1572872 | tf_op jit(solution)/shard_map/ppermute | solution.py:325
  110.3 5.1 %copy-start.8 = (bf16[1024,256]{1,0:T(8,128)(2,1)}, bf16[1024,256]{1,0:T(8,128)(2,1)S(1)}, u32[]{:S(2)}) copy-start(bf16[1024,256]{1,0:T(8,128)(2,1)S(1)} %collective-permute-done.20.rest_7_) | copy-start | bytes 1572868
  110.3 5.1 %collective-permute-start.22 = (bf16[1024,256]{1,0:T(8,128)(2,1)S(1)}, bf16[1024,256]{1,0:T(8,128)(2,1)S(1)}, u32[]{:S(2)}, u32[]{:S(2)}) collective-permute-start(bf16[1024,256]{1,0:T(8,128)(2,1)S(1)} %collective-permute-done.20.rest_7_), channel_id=1, source_target_pairs={{0,1},{1,0},{2,3},{3,2},{4,5},{5,4},{6,7},{7,6},{8,9},{9,8},{10,11... | collective-permute-start | bytes 1572872 | tf_op jit(solution)/shard_map/ppermute | solution.py:325
  115.4 0.8 copy-start.9
  115.4 0.9 copy-start.10
  115.4 1.1 copy-start.11
  115.5 1.3 copy-start.12
  115.5 1.4 copy-start.13
  116.9 16.8 %copy-start.2 = (f32[1024,240]{1,0:T(8,128)S(1)}, f32[1024,240]{1,0:T(8,128)}, u32[]{:S(2)}) copy-start(f32[1024,240]{1,0:T(8,128)} %get-tuple-element.11.vec_ref) | copy-start | bytes 2949124
  128.5 12.4 %all-to-all-start = ((f32[32,1,128]{2,1,0:T(1,128)}), f32[32,1,128]{2,1,0:T(1,128)S(1)}, u32[]{:S(2)}, u32[]{:S(2)}) async-start(f32[32,1,128]{2,1,0:T(1,128)} %bitcast.58), calls=%async_computation | async-start | bytes 32768 | tf_op jit(solution)/shard_map/all_to_all | solution.py:399
  140.9 0.6 copy-start.16

commit v2 on v1

--- a/solution.py
+++ b/solution.py
@@ -12,7 +12,7 @@
 LANES = 128
 CHUNK = 256
 BATCH = 32
-VMEM_LIMIT = 56 * 2**20
+VMEM_LIMIT = 40 * 2**20
 
 
 def cosine_coefficients():
@@ -299,19 +299,12 @@
 
 
 def finish(sums, x_t, u_t, v_t):
-    coefs, rows = x_t.shape
-    part = 48 if coefs % 48 == 0 else coefs
-    block = pl.BlockSpec((part, rows), lambda i: (i, 0))
+    field = jax.ShapeDtypeStruct(x_t.shape, jnp.float32)
     return pl.pallas_call(
         finish_kernel,
-        grid=(coefs // part,),
-        out_shape=(
-            jax.ShapeDtypeStruct((coefs, rows), jnp.float32),
-            jax.ShapeDtypeStruct((coefs, rows), jnp.float32),
-            jax.ShapeDtypeStruct((2, 3), jnp.float32),
-        ),
-        in_specs=[pl.BlockSpec(sums.shape, lambda i: (0, 0)), block, block, block],
-        out_specs=(block, block, pl.BlockSpec((2, 3), lambda i: (0, 0))),
+        out_shape=(field, field, jax.ShapeDtypeStruct((2, 3), jnp.float32)),
+        in_specs=[whole()] * 4,
+        out_specs=(whole(),) * 3,
         compiler_params=params(),
         name="finish",
     )(sums, x_t, u_t, v_t)
@@ -321,30 +314,52 @@
     return lax.ppermute(block, "grp", [(2 * a + c, 2 * b + c) for a, b in moves for c in range(2)])
 
 
-def other_core(block):
-    return lax.ppermute(block, "grp", [(i, i ^ 1) for i in range(lax.axis_size("grp"))])
+def other_core(block, chips):
+    return lax.ppermute(block, "grp", [(2 * z + c, 2 * z + 1 - c) for z in chips for c in range(2)])
+
+
+def line_of_four(coded):
+    ends, middle = (0, 3), (1, 2)
+    swapped = along_chips(coded, [(0, 1), (1, 0), (2, 3), (3, 2)])
+    inner = along_chips(coded, [(1, 2), (2, 1)])
+    inward = along_chips(swapped, [(1, 2), (2, 1)])
+    outward = along_chips(inner, [(1, 0), (2, 3)])
+    last = along_chips(inward, [(1, 0), (2, 3)])
+    groups, blocks = [], []
+    for members in (
+        [(coded, ends + middle)],
+        [(swapped, ends + middle)],
+        [(inner, middle), (outward, ends)],
+        [(inward, middle), (last, ends)],
+    ):
+        groups += [len(members)] * 2
+        blocks += [block for block, _ in members]
+        blocks += [other_core(block, chips) for block, chips in members]
+    return tuple(groups), blocks
+
+
+def place_in_line(source, here):
+    far_side = 2 + jnp.where((source == 0) | (source == 3), 1, 0)
+    return jnp.where(source == here, 0, jnp.where(source == (here ^ 1), 1, far_side))
+
+
+def ring_of_chips(coded):
+    chips = lax.axis_size("grp") // 2
+    groups, blocks = [], []
+    for m in range(chips):
+        block = along_chips(coded, [((z + m) % chips, z) for z in range(chips)]) if m else coded
+        groups += [1, 1]
+        blocks += [block, other_core(block, range(chips))]
+    return tuple(groups), blocks
 
 
 def exchange(coded):
+    return line_of_four(coded) if lax.axis_size("grp") == 8 else ring_of_chips(coded)
+
+
+def place_of(source, here):
     chips = lax.axis_size("grp") // 2
-    everyone = [[coded]]
-    ring = {
-        m: along_chips(coded, [((z + m) % chips, z) for z in range(chips)])
-        for m in range(1, chips)
-        if not (chips == 4 and m == 2)
-    }
-    for m in range(1, chips):
-        if m in ring:
-            everyone.append([ring[m]])
-        else:
-            everyone.append(
-                [along_chips(ring[1], [(1, 0), (2, 1)]), along_chips(ring[3], [(1, 2), (2, 3)])]
-            )
-    groups, blocks = [], []
-    for members in everyone:
-        groups += [len(members)] * 2
-        blocks += members + [other_core(block) for block in members]
-    return tuple(groups), blocks
+    return place_in_line(source, here) if chips == 4 else (source - here) % chips
 
 
 def far_field(coded, wave_out, wave_in_t, angle, trans_rows):
@@ -376,11 +391,10 @@
     angle = plane_angle[0]
     rows, coefs = x.shape
     width = -(-coefs // LANES) * LANES
-    chips = lax.axis_size("grp") // 2
     devices = lax.axis_size("grp") * lax.axis_size("blk")
     me = lax.axis_index("grp")
     owner = owner_dev[0, :, 0]
-    away = ((owner // 2 - me // 2) % chips) * 2 + ((owner % 2) ^ (me % 2))
+    away = place_of(owner // 2, me // 2) * 2 + ((owner % 2) ^ (me % 2))
     slots = 2 * (away * rows + near_row[0])
     table_ids = table_id[0].reshape(rows, -1)
     wave_in_t = wave_in.T

time: 148 us -> 141 us (0.953)
  Pallas kernels: 47.4 us -> 26.2 us
  starting transfers between devices: 26.7 us -> 42.8 us
  waiting for transfers between devices: 61.6 us -> 58.9 us
  local copies, waits for them, and re-layouts: 8.45 us -> 11 us
  other arithmetic: 2.51 us -> 0.73 us
    ppermute x10 -> x12, starting transfers between devices: 1.15 us -> 12 us  [other_core(): lax.ppermute(block, 'grp', [(2 * z + c, 2 * z + 1 - c) for z in chips for...]
    pallas_call x2, Pallas kernels: 22.8 us -> 16.5 us  [near_field(): pl.pallas_call(functools.partial(near_kernel, groups, second is not None)...]
    pallas_call x2, Pallas kernels: 8.58 us -> 3.84 us  [spread_wave(): pl.pallas_call(spread_kernel, out_shape=jax.ShapeDtypeStruct((rows, coefs...]
    pallas_call x2, Pallas kernels: 7.76 us -> 3.51 us  [gather_wave(): pl.pallas_call(wave_kernel, out_shape=jax.ShapeDtypeStruct((1, samples),...]
    ppermute x8 -> x10, starting transfers between devices: 12.5 us -> 16.7 us  [along_chips(): lax.ppermute(block, 'grp', [(2 * a + c, 2 * b + c) for a, b in moves for...]
    pallas_call x1, Pallas kernels: 6.04 us -> 2.08 us  [finish(): pl.pallas_call(finish_kernel, out_shape=(field, field, jax.ShapeDtypeStru...]
    ppermute x8 -> x10, waiting for transfers between devices: 50.2 us -> 46.8 us  [along_chips(): lax.ppermute(block, 'grp', [(2 * a + c, 2 * b + c) for a, b in moves for...]
    pallas_call x1, Pallas kernels: 2.21 us -> 0.21 us  [code(): pl.pallas_call(code_kernel, out_shape=jax.ShapeDtypeStruct((rows, width),...]
  transfers between devices with their start and end apart: 25 -> 29, of which waited for: 12 -> 11; matrix products, arithmetic and copies ran while one was open for 5% -> 4% of each run, Pallas kernels for 11% -> 5%
where the time goes in v2:
time: 141 us
  waiting for transfers between devices  58.9 us (42%)
  starting transfers between devices  42.8 us (30%)
  Pallas kernels  26.2 us (19%)
  local copies, waits for them, and re-layouts  11 us (8%)
    ppermute x10, waiting for transfers between devices, along_chips(): lax.ppermute(block, 'grp', [(2 * a + c, 2 * b + c) for a, b in moves for...  46.8 us
    ppermute x10, starting transfers between devices, along_chips(): lax.ppermute(block, 'grp', [(2 * a + c, 2 * b + c) for a, b in moves for...  16.7 us
    pallas_call x2, Pallas kernels, near_field(): pl.pallas_call(functools.partial(near_kernel, groups, second is not None)...  16.5 us
    ppermute x12, starting transfers between devices, other_core(): lax.ppermute(block, 'grp', [(2 * z + c, 2 * z + 1 - c) for z in chips for...  12 us
    ppermute x6, starting transfers between devices, far_field(): lax.ppermute(own, 'blk', [((i - turn) % blocks, i) for i in range(blocks)])  9.54 us
    ppermute x6, waiting for transfers between devices, far_field(): lax.ppermute(own, 'blk', [((i - turn) % blocks, i) for i in range(blocks)])  6.69 us
    unnamed x40, local copies, waits for them, and re-layouts  6.6 us
    all_to_all x1, waiting for transfers between devices, body(): sums = lax.all_to_all(sums, ('blk', 'grp'), 0, 0, tiled=True)  5.35 us
  transfers between devices with their start and end apart: 29, of which 11 were waited for; matrix products, arithmetic and copies ran while one was open for 4% of the time, Pallas kernels for 5%

profile of v2, /device:TPU:0, one launch (start us, length us, event | category | flops | bytes accessed | tf_op | source)
XLA Modules:
  0.0 140.8 jit_solution(196300066271764083)
XLA Ops:
  0.7 1.3 copy-done.1
  2.2 3.1 %collective-permute-start.4 = (bf16[1024,256]{1,0:T(8,128)(2,1)S(1)}, bf16[1024,256]{1,0:T(8,128)(2,1)}, u32[]{:S(2)}, u32[]{:S(2)}) collective-permute-start(bf16[1024,256]{1,0:T(8,128)(2,1)S(1)} %code_rows.1.coded_ref.rest_0_), channel_id=1, source_target_pairs={{0,2},{1,3},{2,0},{3,1},{4,6},{5,7},{6,4},{7,5},{8,10},{9,11},{10,... | collective-permute-start | bytes 1572872 | tf_op jit(solution)/shard_map/ppermute | solution.py:314
  5.3 1.5 %collective-permute-start.6 = (bf16[1024,256]{1,0:T(8,128)(2,1)S(1)}, bf16[1024,256]{1,0:T(8,128)(2,1)}, u32[]{:S(2)}, u32[]{:S(2)}) collective-permute-start(bf16[1024,256]{1,0:T(8,128)(2,1)S(1)} %code_rows.1.coded_ref.rest_0_), channel_id=1, source_target_pairs={{2,4},{3,5},{4,2},{5,3},{10,12},{11,13},{12,10},{13,11},{18,20},{1... | collective-permute-start | bytes 1572872 | tf_op jit(solution)/shard_map/ppermute | solution.py:314
  6.7 10.6 %collective-permute-done.4.rest_2_ = bf16[1024,256]{1,0:T(8,128)(2,1)} collective-permute-done((bf16[1024,256]{1,0:T(8,128)(2,1)S(1)}, bf16[1024,256]{1,0:T(8,128)(2,1)}, u32[]{:S(2)}, u32[]{:S(2)}) %collective-permute-start.4) | collective-permute-done | bytes 524320 | tf_op jit(solution)/shard_map/ppermute | solution.py:314
  17.3 1.5 %collective-permute-start.10 = (bf16[1024,256]{1,0:T(8,128)(2,1)}, bf16[1024,256]{1,0:T(8,128)(2,1)}, u32[]{:S(2)}, u32[]{:S(2)}) collective-permute-start(bf16[1024,256]{1,0:T(8,128)(2,1)} %collective-permute-done.4.rest_2_), channel_id=1, source_target_pairs={{2,4},{3,5},{4,2},{5,3},{10,12},{11,13},{12,10},{13,11},{18,20},{1... | collective-permute-start | bytes 1572872 | tf_op jit(solution)/shard_map/ppermute | solution.py:314
  18.7 1.3 collective-permute-start.7
  20.0 1.3 collective-permute-start.11
  21.4 1.8 %gather_wave.2 = f32[1,512]{1,0:T(1,128)S(1)} custom-call(bf16[1024,256]{1,0:T(8,128)(2,1)S(1)} %code_rows.1.coded_ref.rest_0_, bf16[240,512]{1,0:T(8,128)(2,1)S(1)} %copy-done.10, bf16[1024,512]{1,0:T(8,128)(2,1)S(1)} %bitcast.45), custom_call_target="tpu_custom_call" | custom-call | flops 268435456 | bytes 2097152 | tf_op jit(solution)/shard_map/gather_wave/pallas_call | solution.py:87
  23.1 1.7 %collective-permute-start = (f32[1,512]{1,0:T(1,128)S(1)}, f32[1,512]{1,0:T(1,128)S(1)}, u32[]{:S(2)}, u32[]{:S(2)}) collective-permute-start(f32[1,512]{1,0:T(1,128)S(1)} %gather_wave.2), channel_id=1, source_target_pairs={{24,0},{0,8},{8,16},{16,24},{25,1},{1,9},{9,17},{17,25},{26,2},{2,... | collective-permute-start | bytes 6152 | tf_op jit(solution)/shard_map/ppermute | solution.py:371
  24.8 1.5 %collective-permute-start.1 = (f32[1,512]{1,0:T(1,128)S(1)}, f32[1,512]{1,0:T(1,128)S(1)}, u32[]{:S(2)}, u32[]{:S(2)}) collective-permute-start(f32[1,512]{1,0:T(1,128)S(1)} %gather_wave.2), channel_id=1, source_target_pairs={{16,0},{24,8},{0,16},{8,24},{17,1},{25,9},{1,17},{9,25},{18,2},{26... | collective-permute-start | bytes 6152 | tf_op jit(solution)/shard_map/ppermute | solution.py:371
  26.4 1.3 collective-permute-done
  27.7 1.7 %collective-permute-start.2 = (f32[1,512]{1,0:T(1,128)S(1)}, f32[1,512]{1,0:T(1,128)S(1)}, u32[]{:S(2)}, u32[]{:S(2)}) collective-permute-start(f32[1,512]{1,0:T(1,128)S(1)} %gather_wave.2), channel_id=1, source_target_pairs={{8,0},{16,8},{24,16},{0,24},{9,1},{17,9},{25,17},{1,25},{10,2},{18... | collective-permute-start | bytes 6152 | tf_op jit(solution)/shard_map/ppermute | solution.py:371
  29.4 1.9 %collective-permute-done.2 = f32[1,512]{1,0:T(1,128)S(1)} collective-permute-done((f32[1,512]{1,0:T(1,128)S(1)}, f32[1,512]{1,0:T(1,128)S(1)}, u32[]{:S(2)}, u32[]{:S(2)}) %collective-permute-start.2) | collective-permute-done | bytes 2080 | tf_op jit(solution)/shard_map/ppermute | solution.py:371
  31.3 1.5 %collective-permute-start.8 = (bf16[1024,256]{1,0:T(8,128)(2,1)}, bf16[1024,256]{1,0:T(8,128)(2,1)}, u32[]{:S(2)}, u32[]{:S(2)}) collective-permute-start(bf16[1024,256]{1,0:T(8,128)(2,1)} %collective-permute-done.6.rest_4_), channel_id=1, source_target_pairs={{2,3},{3,2},{4,5},{5,4},{10,11},{11,10},{12,13},{13,12},{18,19},{1... | collective-permute-start | bytes 1572872 | tf_op jit(solution)/shard_map/ppermute | solution.py:318
  32.7 0.8 copy-done.12
  33.5 1.5 %collective-permute-start.12 = (bf16[1024,256]{1,0:T(8,128)(2,1)}, bf16[1024,256]{1,0:T(8,128)(2,1)}, u32[]{:S(2)}, u32[]{:S(2)}) collective-permute-start(bf16[1024,256]{1,0:T(8,128)(2,1)} %collective-permute-done.10.rest_8_), channel_id=1, source_target_pairs={{2,3},{3,2},{4,5},{5,4},{10,11},{11,10},{12,13},{13,12},{18,19},{1... | collective-permute-start | bytes 1572872 | tf_op jit(solution)/shard_map/ppermute | solution.py:318
  35.0 2.0 %collective-permute-done.7.rest_5_ = bf16[1024,256]{1,0:T(8,128)(2,1)} collective-permute-done((bf16[1024,256]{1,0:T(8,128)(2,1)}, bf16[1024,256]{1,0:T(8,128)(2,1)}, u32[]{:S(2)}, u32[]{:S(2)}) %collective-permute-start.7) | collective-permute-done | bytes 524320 | tf_op jit(solution)/shard_map/ppermute | solution.py:314
  37.0 1.9 %collective-permute-start.9 = (bf16[1024,256]{1,0:T(8,128)(2,1)}, bf16[1024,256]{1,0:T(8,128)(2,1)}, u32[]{:S(2)}, u32[]{:S(2)}) collective-permute-start(bf16[1024,256]{1,0:T(8,128)(2,1)} %collective-permute-done.7.rest_5_), channel_id=1, source_target_pairs={{0,1},{1,0},{6,7},{7,6},{8,9},{9,8},{14,15},{15,14},{16,17},{17,16... | collective-permute-start | bytes 1572872 | tf_op jit(solution)/shard_map/ppermute | solution.py:318
  38.9 9.1 %collective-permute-done.11.rest_9_ = bf16[1024,256]{1,0:T(8,128)(2,1)} collective-permute-done((bf16[1024,256]{1,0:T(8,128)(2,1)}, bf16[1024,256]{1,0:T(8,128)(2,1)}, u32[]{:S(2)}, u32[]{:S(2)}) %collective-permute-start.11) | collective-permute-done | bytes 524320 | tf_op jit(solution)/shard_map/ppermute | solution.py:314
  48.0 1.9 %collective-permute-start.13 = (bf16[1024,256]{1,0:T(8,128)(2,1)}, bf16[1024,256]{1,0:T(8,128)(2,1)}, u32[]{:S(2)}, u32[]{:S(2)}) collective-permute-start(bf16[1024,256]{1,0:T(8,128)(2,1)} %collective-permute-done.11.rest_9_), channel_id=1, source_target_pairs={{0,1},{1,0},{6,7},{7,6},{8,9},{9,8},{14,15},{15,14},{16,17},{17,16... | collective-permute-start | bytes 1572872 | tf_op jit(solution)/shard_map/ppermute | solution.py:318
  50.3 1.5 %copy.22.vec_ref.rest_0_ = f32[1024,240]{1,0:T(8,128)S(1)} copy(f32[1024,240]{0,1:T(8,128)} %bitcast.51) | data formatting | bytes 1966080 | tf_op jit(solution)/shard_map/squeeze | solution.py:389
  53.1 1.1 reshape_squeeze.3.table_ref
  55.0 0.9 copy-done.11
  55.9 1.9 %spread_wave.2.far_ref = f32[1024,240]{1,0:T(8,128)S(1)} custom-call(f32[1,512]{1,0:T(1,128)S(1)} %fusion.6.incoming_ref, bf16[240,512]{1,0:T(8,128)(2,1)S(1)} %bitcast.55, bf16[1024,512]{1,0:T(8,128)(2,1)S(1)} %bitcast.46), custom_call_target="tpu_custom_call" | custom-call | flops 268435456 | bytes 3145728 | tf_op jit(solution)/shard_map/spread_wave/pallas_call | solution.py:120
  58.0 1.0 copy-done.13
  59.0 8.7 %near_first.1 = (f32[1024,240]{1,0:T(8,128)S(1)}, bf16[1024,256]{1,0:T(8,128)(2,1)S(1)}, f32[1,128]{1,0:T(1,128)S(1)}) custom-call(s32[3072]{0:T(1024)S(1)} %fusion.4.slot_ref, s32[1024,3]{1,0:T(8,128)S(1)} %copy-done.3, bf16[8,240,240]{2,1,0:T(8,128)(2,1)S(1)} %copy-done.7, f32[1024,240]{1,0:T(8,128)S(1)} %copy.22.vec_ref.rest_0_, ...), custom_call_target="tpu_custom_call" | custom-call | flops 1073741824 | bytes 10485760 | tf_op jit(solution)/shard_map/near_first/pallas_call | solution.py:240
  67.7 4.2 %collective-permute-start.18 = (bf16[1024,256]{1,0:T(8,128)(2,1)S(1)}, bf16[1024,256]{1,0:T(8,128)(2,1)S(1)}, u32[]{:S(2)}, u32[]{:S(2)}) collective-permute-start(bf16[1024,256]{1,0:T(8,128)(2,1)S(1)} %get-tuple-element.12.coded_ref.rest_2_), channel_id=1, source_target_pairs={{0,2},{1,3},{2,0},{3,1},{4,6},{5,7},{6,4},{7,5},{8,10},{9,11},{10,... | collective-permute-start | bytes 1572872 | tf_op jit(solution)/shard_map/ppermute | solution.py:314
  72.6 11.4 %collective-permute-done.18.rest_4_ = bf16[1024,256]{1,0:T(8,128)(2,1)S(1)} collective-permute-done((bf16[1024,256]{1,0:T(8,128)(2,1)S(1)}, bf16[1024,256]{1,0:T(8,128)(2,1)S(1)}, u32[]{:S(2)}, u32[]{:S(2)}) %collective-permute-start.18) | collective-permute-done | bytes 524320 | tf_op jit(solution)/shard_map/ppermute | solution.py:314
  84.8 1.3 collective-permute-start.21
  86.1 1.3 collective-permute-start.25
  87.4 1.8 %gather_wave.3 = f32[1,512]{1,0:T(1,128)S(1)} custom-call(bf16[1024,256]{1,0:T(8,128)(2,1)S(1)} %get-tuple-element.12.coded_ref.rest_2_, bf16[240,512]{1,0:T(8,128)(2,1)S(1)} %copy-done.10, bf16[1024,512]{1,0:T(8,128)(2,1)S(1)} %bitcast.47), custom_call_target="tpu_custom_call" | custom-call | flops 268435456 | bytes 2097152 | tf_op jit(solution)/shard_map/gather_wave/pallas_call | solution.py:87
  89.1 1.5 %collective-permute-start.14 = (f32[1,512]{1,0:T(1,128)S(1)}, f32[1,512]{1,0:T(1,128)S(1)}, u32[]{:S(2)}, u32[]{:S(2)}) collective-permute-start(f32[1,512]{1,0:T(1,128)S(1)} %gather_wave.3), channel_id=1, source_target_pairs={{24,0},{0,8},{8,16},{16,24},{25,1},{1,9},{9,17},{17,25},{26,2},{2,... | collective-permute-start | bytes 6152 | tf_op jit(solution)/shard_map/ppermute | solution.py:371
  90.7 1.5 %collective-permute-start.15 = (f32[1,512]{1,0:T(1,128)S(1)}, f32[1,512]{1,0:T(1,128)S(1)}, u32[]{:S(2)}, u32[]{:S(2)}) collective-permute-start(f32[1,512]{1,0:T(1,128)S(1)} %gather_wave.3), channel_id=1, source_target_pairs={{16,0},{24,8},{0,16},{8,24},{17,1},{25,9},{1,17},{9,25},{18,2},{26... | collective-permute-start | bytes 6152 | tf_op jit(solution)/shard_map/ppermute | solution.py:371
  92.2 1.5 %collective-permute-done.14 = f32[1,512]{1,0:T(1,128)S(1)} collective-permute-done((f32[1,512]{1,0:T(1,128)S(1)}, f32[1,512]{1,0:T(1,128)S(1)}, u32[]{:S(2)}, u32[]{:S(2)}) %collective-permute-start.14) | collective-permute-done | bytes 2080 | tf_op jit(solution)/shard_map/ppermute | solution.py:371
  93.7 1.5 %collective-permute-start.16 = (f32[1,512]{1,0:T(1,128)S(1)}, f32[1,512]{1,0:T(1,128)S(1)}, u32[]{:S(2)}, u32[]{:S(2)}) collective-permute-start(f32[1,512]{1,0:T(1,128)S(1)} %gather_wave.3), channel_id=1, source_target_pairs={{8,0},{16,8},{24,16},{0,24},{9,1},{17,9},{25,17},{1,25},{10,2},{18... | collective-permute-start | bytes 6152 | tf_op jit(solution)/shard_map/ppermute | solution.py:371
  95.2 2.0 %collective-permute-done.16 = f32[1,512]{1,0:T(1,128)S(1)} collective-permute-done((f32[1,512]{1,0:T(1,128)S(1)}, f32[1,512]{1,0:T(1,128)S(1)}, u32[]{:S(2)}, u32[]{:S(2)}) %collective-permute-start.16) | collective-permute-done | bytes 2080 | tf_op jit(solution)/shard_map/ppermute | solution.py:371
  98.0 0.7 collective-permute-start.26
  98.7 4.7 %collective-permute-done.21.rest_7_ = bf16[1024,256]{1,0:T(8,128)(2,1)S(1)} collective-permute-done((bf16[1024,256]{1,0:T(8,128)(2,1)S(1)}, bf16[1024,256]{1,0:T(8,128)(2,1)S(1)}, u32[]{:S(2)}, u32[]{:S(2)}) %collective-permute-start.21) | collective-permute-done | bytes 524320 | tf_op jit(solution)/shard_map/ppermute | solution.py:314
  103.3 1.9 %collective-permute-start.23 = (bf16[1024,256]{1,0:T(8,128)(2,1)S(1)}, bf16[1024,256]{1,0:T(8,128)(2,1)S(1)}, u32[]{:S(2)}, u32[]{:S(2)}) collective-permute-start(bf16[1024,256]{1,0:T(8,128)(2,1)S(1)} %collective-permute-done.21.rest_7_), channel_id=1, source_target_pairs={{0,1},{1,0},{6,7},{7,6},{8,9},{9,8},{14,15},{15,14},{16,17},{17,16... | collective-permute-start | bytes 1572872 | tf_op jit(solution)/shard_map/ppermute | solution.py:318
  105.3 9.1 %collective-permute-done.25.rest_11_ = bf16[1024,256]{1,0:T(8,128)(2,1)S(1)} collective-permute-done((bf16[1024,256]{1,0:T(8,128)(2,1)S(1)}, bf16[1024,256]{1,0:T(8,128)(2,1)S(1)}, u32[]{:S(2)}, u32[]{:S(2)}) %collective-permute-start.25) | collective-permute-done | bytes 524320 | tf_op jit(solution)/shard_map/ppermute | solution.py:314
  114.4 1.9 %collective-permute-start.27 = (bf16[1024,256]{1,0:T(8,128)(2,1)S(1)}, bf16[1024,256]{1,0:T(8,128)(2,1)S(1)}, u32[]{:S(2)}, u32[]{:S(2)}) collective-permute-start(bf16[1024,256]{1,0:T(8,128)(2,1)S(1)} %collective-permute-done.25.rest_11_), channel_id=1, source_target_pairs={{0,1},{1,0},{6,7},{7,6},{8,9},{9,8},{14,15},{15,14},{16,17},{17,16... | collective-permute-start | bytes 1572872 | tf_op jit(solution)/shard_map/ppermute | solution.py:318
  116.3 1.9 %spread_wave.3.far_ref = f32[1024,240]{1,0:T(8,128)S(1)} custom-call(f32[1,512]{1,0:T(1,128)S(1)} %fusion.7.incoming_ref, bf16[240,512]{1,0:T(8,128)(2,1)S(1)} %bitcast.56, bf16[1024,512]{1,0:T(8,128)(2,1)S(1)} %bitcast.48), custom_call_target="tpu_custom_call" | custom-call | flops 268435456 | bytes 3145728 | tf_op jit(solution)/shard_map/spread_wave/pallas_call | solution.py:120
  118.3 7.8 %near_second.1 = (f32[240,1024]{1,0:T(8,128)S(1)}, f32[8,128]{1,0:T(8,128)}, f32[32,128]{1,0:T(8,128)}) custom-call(s32[3072]{0:T(1024)S(1)} %fusion.4.slot_ref, s32[1024,3]{1,0:T(8,128)S(1)} %copy-done.3, bf16[8,240,240]{2,1,0:T(8,128)(2,1)S(1)} %copy-done.7, f32[1024,240]{1,0:T(8,128)S(1)} %get-tuple-element.11.vec_ref, f32[1024,240]{1,0:T(8,128)S(1)} %bitcast.50, ...), custom_call_target="tpu_custom_call" | custom-call | flops 1073741824 | bytes 10485760 | tf_op jit(solution)/shard_map/near_second/pallas_call | solution.py:240
  126.1 0.9 copy-done.8
  127.1 4.5 %all-to-all-start = ((f32[32,1,128]{2,1,0:T(1,128)}), f32[32,1,128]{2,1,0:T(1,128)S(1)}, u32[]{:S(2)}, u32[]{:S(2)}) async-start(f32[32,1,128]{2,1,0:T(1,128)} %bitcast.11), calls=%async_computation | async-start | bytes 32768 | tf_op jit(solution)/shard_map/all_to_all | solution.py:413
  131.6 1.7 %copy.25 = f32[1024,240]{0,1:T(8,128)S(1)} copy(f32[1024,240]{1,0:T(8,128)} %copy-done.6) | data formatting | bytes 1966080 | tf_op jit(solution)/shard_map/near_first/pallas_call | solution.py:240
  133.3 5.3 %all-to-all-done = f32[32,1,128]{2,1,0:T(1,128)S(1)} async-done(((f32[32,1,128]{2,1,0:T(1,128)}), f32[32,1,128]{2,1,0:T(1,128)S(1)}, u32[]{:S(2)}, u32[]{:S(2)}) %all-to-all-start) | async-done | bytes 16416 | tf_op jit(solution)/shard_map/all_to_all | solution.py:413
  138.7 2.1 %finish.1 = (f32[240,1024]{1,0:T(8,128)}, f32[240,1024]{1,0:T(8,128)}, f32[2,3]{1,0:T(2,128)}) custom-call(f32[32,128]{1,0:T(8,128)S(1)} %bitcast.57, f32[240,1024]{1,0:T(8,128)S(1)} %bitcast.53, f32[240,1024]{1,0:T(8,128)S(1)} %bitcast.54, f32[240,1024]{1,0:T(8,128)S(1)} %copy-done.9), custom_call_target="tpu_custom_call" | custom-call | tf_op jit(solution)/shard_map/finish/pallas_call | solution.py:303
  (65 shorter events, 4.7 us)
Async XLA Ops:
  0.6 20.7 %copy-start = (bf16[1,1024,512]{2,1,0:T(8,128)(2,1)S(1)}, bf16[1,1024,512]{2,1,0:T(8,128)(2,1)}, u32[]{:S(2)}) copy-start(bf16[1,1024,512]{2,1,0:T(8,128)(2,1)} %param.18) | copy-start | bytes 3145732
  0.6 1.3 copy-start.1
  1.9 19.4 %copy-start.10 = (bf16[240,512]{1,0:T(8,128)(2,1)S(1)}, bf16[240,512]{1,0:T(8,128)(2,1)}, u32[]{:S(2)}) copy-start(bf16[240,512]{1,0:T(8,128)(2,1)} %out_ref.3) | copy-start | bytes 737284
  2.1 21.0 %copy-start.4 = (bf16[1024,256]{1,0:T(8,128)(2,1)}, bf16[1024,256]{1,0:T(8,128)(2,1)S(1)}, u32[]{:S(2)}) copy-start(bf16[1024,256]{1,0:T(8,128)(2,1)S(1)} %code_rows.1.coded_ref.rest_0_) | copy-start | bytes 1572868
  2.2 47.8 %copy-start.14 = (f32[1,1024,240]{1,2,0:T(8,128)S(1)}, f32[1,1024,240]{1,2,0:T(8,128)}, u32[]{:S(2)}) copy-start(f32[1,1024,240]{1,2,0:T(8,128)} %param.11) | copy-start | bytes 2949124
  2.2 15.1 %collective-permute-start.4 = (bf16[1024,256]{1,0:T(8,128)(2,1)S(1)}, bf16[1024,256]{1,0:T(8,128)(2,1)}, u32[]{:S(2)}, u32[]{:S(2)}) collective-permute-start(bf16[1024,256]{1,0:T(8,128)(2,1)S(1)} %code_rows.1.coded_ref.rest_0_), channel_id=1, source_target_pairs={{0,2},{1,3},{2,0},{3,1},{4,6},{5,7},{6,4},{7,5},{8,10},{9,11},{10,... | collective-permute-start | bytes 1572872 | tf_op jit(solution)/shard_map/ppermute | solution.py:314
  5.3 13.5 %collective-permute-start.6 = (bf16[1024,256]{1,0:T(8,128)(2,1)S(1)}, bf16[1024,256]{1,0:T(8,128)(2,1)}, u32[]{:S(2)}, u32[]{:S(2)}) collective-permute-start(bf16[1024,256]{1,0:T(8,128)(2,1)S(1)} %code_rows.1.coded_ref.rest_0_), channel_id=1, source_target_pairs={{2,4},{3,5},{4,2},{5,3},{10,12},{11,13},{12,10},{13,11},{18,20},{1... | collective-permute-start | bytes 1572872 | tf_op jit(solution)/shard_map/ppermute | solution.py:314
  17.3 2.7 %collective-permute-start.10 = (bf16[1024,256]{1,0:T(8,128)(2,1)}, bf16[1024,256]{1,0:T(8,128)(2,1)}, u32[]{:S(2)}, u32[]{:S(2)}) collective-permute-start(bf16[1024,256]{1,0:T(8,128)(2,1)} %collective-permute-done.4.rest_2_), channel_id=1, source_target_pairs={{2,4},{3,5},{4,2},{5,3},{10,12},{11,13},{12,10},{13,11},{18,20},{1... | collective-permute-start | bytes 1572872 | tf_op jit(solution)/shard_map/ppermute | solution.py:314
  18.7 14.0 %collective-permute-start.3 = (bf16[1024,256]{1,0:T(8,128)(2,1)S(1)}, bf16[1024,256]{1,0:T(8,128)(2,1)S(1)}, u32[]{:S(2)}, u32[]{:S(2)}) collective-permute-start(bf16[1024,256]{1,0:T(8,128)(2,1)S(1)} %code_rows.1.coded_ref.rest_0_), channel_id=1, source_target_pairs={{0,1},{1,0},{6,7},{7,6},{2,3},{3,2},{4,5},{5,4},{8,9},{9,8},{14,15... | collective-permute-start | bytes 1572872 | tf_op jit(solution)/shard_map/ppermute | solution.py:318
  18.7 18.2 %collective-permute-start.7 = (bf16[1024,256]{1,0:T(8,128)(2,1)}, bf16[1024,256]{1,0:T(8,128)(2,1)}, u32[]{:S(2)}, u32[]{:S(2)}) collective-permute-start(bf16[1024,256]{1,0:T(8,128)(2,1)} %collective-permute-done.6.rest_4_), channel_id=1, source_target_pairs={{2,0},{3,1},{4,6},{5,7},{10,8},{11,9},{12,14},{13,15},{18,16},{19,... | collective-permute-start | bytes 1572872 | tf_op jit(solution)/shard_map/ppermute | solution.py:314
  20.0 27.9 %collective-permute-start.11 = (bf16[1024,256]{1,0:T(8,128)(2,1)}, bf16[1024,256]{1,0:T(8,128)(2,1)}, u32[]{:S(2)}, u32[]{:S(2)}) collective-permute-start(bf16[1024,256]{1,0:T(8,128)(2,1)} %collective-permute-done.10.rest_8_), channel_id=1, source_target_pairs={{2,0},{3,1},{4,6},{5,7},{10,8},{11,9},{12,14},{13,15},{18,16},{19,... | collective-permute-start | bytes 1572872 | tf_op jit(solution)/shard_map/ppermute | solution.py:314
  23.1 4.5 %collective-permute-start = (f32[1,512]{1,0:T(1,128)S(1)}, f32[1,512]{1,0:T(1,128)S(1)}, u32[]{:S(2)}, u32[]{:S(2)}) collective-permute-start(f32[1,512]{1,0:T(1,128)S(1)} %gather_wave.2), channel_id=1, source_target_pairs={{24,0},{0,8},{8,16},{16,24},{25,1},{1,9},{9,17},{17,25},{26,2},{2,... | collective-permute-start | bytes 6152 | tf_op jit(solution)/shard_map/ppermute | solution.py:371
  24.8 4.5 %collective-permute-start.1 = (f32[1,512]{1,0:T(1,128)S(1)}, f32[1,512]{1,0:T(1,128)S(1)}, u32[]{:S(2)}, u32[]{:S(2)}) collective-permute-start(f32[1,512]{1,0:T(1,128)S(1)} %gather_wave.2), channel_id=1, source_target_pairs={{16,0},{24,8},{0,16},{8,24},{17,1},{25,9},{1,17},{9,25},{18,2},{26... | collective-permute-start | bytes 6152 | tf_op jit(solution)/shard_map/ppermute | solution.py:371
  27.7 3.6 %collective-permute-start.2 = (f32[1,512]{1,0:T(1,128)S(1)}, f32[1,512]{1,0:T(1,128)S(1)}, u32[]{:S(2)}, u32[]{:S(2)}) collective-permute-start(f32[1,512]{1,0:T(1,128)S(1)} %gather_wave.2), channel_id=1, source_target_pairs={{8,0},{16,8},{24,16},{0,24},{9,1},{17,9},{25,17},{1,25},{10,2},{18... | collective-permute-start | bytes 6152 | tf_op jit(solution)/shard_map/ppermute | solution.py:371
  29.4 28.5 %collective-permute-start.5 = (bf16[1024,256]{1,0:T(8,128)(2,1)}, bf16[1024,256]{1,0:T(8,128)(2,1)}, u32[]{:S(2)}, u32[]{:S(2)}) collective-permute-start(bf16[1024,256]{1,0:T(8,128)(2,1)} %collective-permute-done.4.rest_2_), channel_id=1, source_target_pairs={{0,1},{1,0},{6,7},{7,6},{2,3},{3,2},{4,5},{5,4},{8,9},{9,8},{14,15... | collective-permute-start | bytes 1572872 | tf_op jit(solution)/shard_map/ppermute | solution.py:318
  31.3 26.6 %collective-permute-start.8 = (bf16[1024,256]{1,0:T(8,128)(2,1)}, bf16[1024,256]{1,0:T(8,128)(2,1)}, u32[]{:S(2)}, u32[]{:S(2)}) collective-permute-start(bf16[1024,256]{1,0:T(8,128)(2,1)} %collective-permute-done.6.rest_4_), channel_id=1, source_target_pairs={{2,3},{3,2},{4,5},{5,4},{10,11},{11,10},{12,13},{13,12},{18,19},{1... | collective-permute-start | bytes 1572872 | tf_op jit(solution)/shard_map/ppermute | solution.py:318
  32.7 0.8 copy-start.12
  33.5 24.3 %collective-permute-start.12 = (bf16[1024,256]{1,0:T(8,128)(2,1)}, bf16[1024,256]{1,0:T(8,128)(2,1)}, u32[]{:S(2)}, u32[]{:S(2)}) collective-permute-start(bf16[1024,256]{1,0:T(8,128)(2,1)} %collective-permute-done.10.rest_8_), channel_id=1, source_target_pairs={{2,3},{3,2},{4,5},{5,4},{10,11},{11,10},{12,13},{13,12},{18,19},{1... | collective-permute-start | bytes 1572872 | tf_op jit(solution)/shard_map/ppermute | solution.py:318
  37.0 20.9 %collective-permute-start.9 = (bf16[1024,256]{1,0:T(8,128)(2,1)}, bf16[1024,256]{1,0:T(8,128)(2,1)}, u32[]{:S(2)}, u32[]{:S(2)}) collective-permute-start(bf16[1024,256]{1,0:T(8,128)(2,1)} %collective-permute-done.7.rest_5_), channel_id=1, source_target_pairs={{0,1},{1,0},{6,7},{7,6},{8,9},{9,8},{14,15},{15,14},{16,17},{17,16... | collective-permute-start | bytes 1572872 | tf_op jit(solution)/shard_map/ppermute | solution.py:318
  48.0 9.9 %collective-permute-start.13 = (bf16[1024,256]{1,0:T(8,128)(2,1)}, bf16[1024,256]{1,0:T(8,128)(2,1)}, u32[]{:S(2)}, u32[]{:S(2)}) collective-permute-start(bf16[1024,256]{1,0:T(8,128)(2,1)} %collective-permute-done.11.rest_9_), channel_id=1, source_target_pairs={{0,1},{1,0},{6,7},{7,6},{8,9},{9,8},{14,15},{15,14},{16,17},{17,16... | collective-permute-start | bytes 1572872 | tf_op jit(solution)/shard_map/ppermute | solution.py:318
  50.3 2.1 %copy-start.16 = (s32[1,3072]{1,0:T(1,128)S(1)}, s32[1,3072]{1,0:T(1,128)}, u32[]{:S(2)}) copy-start(s32[1,3072]{1,0:T(1,128)} %param.14) | copy-start | bytes 36868
  53.1 1.2 copy-start.17
  53.1 1.2 copy-start.18
  54.3 0.7 copy-start.15
  55.0 0.9 copy-start.11
  55.9 2.0 %copy-start.3 = (s32[1024,3]{1,0:T(8,128)S(1)}, s32[1024,3]{1,0:T(8,128)}, u32[]{:S(2)}) copy-start(s32[1024,3]{1,0:T(8,128)} %reshape_squeeze.3.table_ref) | copy-start | bytes 36868
  55.9 2.0 %copy-start.5 = (bf16[1024,256]{1,0:T(8,128)(2,1)S(1)}, bf16[1024,256]{1,0:T(8,128)(2,1)}, u32[]{:S(2)}) copy-start(bf16[1024,256]{1,0:T(8,128)(2,1)} %copy-done.4) | copy-start | bytes 1572868
  55.9 2.0 %copy-start.7 = (bf16[8,240,240]{2,1,0:T(8,128)(2,1)S(1)}, bf16[8,240,240]{2,1,0:T(8,128)(2,1)}, u32[]{:S(2)}) copy-start(bf16[8,240,240]{2,1,0:T(8,128)(2,1)} %tables_ref.3) | copy-start | bytes 2764804
  57.9 1.0 copy-start.13
  67.7 50.6 %copy-start.6 = (f32[1024,240]{1,0:T(8,128)}, f32[1024,240]{1,0:T(8,128)S(1)}, u32[]{:S(2)}) copy-start(f32[1024,240]{1,0:T(8,128)S(1)} %get-tuple-element.11.vec_ref) | copy-start | bytes 2949124
  67.7 16.3 %collective-permute-start.18 = (bf16[1024,256]{1,0:T(8,128)(2,1)S(1)}, bf16[1024,256]{1,0:T(8,128)(2,1)S(1)}, u32[]{:S(2)}, u32[]{:S(2)}) collective-permute-start(bf16[1024,256]{1,0:T(8,128)(2,1)S(1)} %get-tuple-element.12.coded_ref.rest_2_), channel_id=1, source_target_pairs={{0,2},{1,3},{2,0},{3,1},{4,6},{5,7},{6,4},{7,5},{8,10},{9,11},{10,... | collective-permute-start | bytes 1572872 | tf_op jit(solution)/shard_map/ppermute | solution.py:314
  71.9 12.9 %collective-permute-start.20 = (bf16[1024,256]{1,0:T(8,128)(2,1)S(1)}, bf16[1024,256]{1,0:T(8,128)(2,1)S(1)}, u32[]{:S(2)}, u32[]{:S(2)}) collective-permute-start(bf16[1024,256]{1,0:T(8,128)(2,1)S(1)} %get-tuple-element.12.coded_ref.rest_2_), channel_id=1, source_target_pairs={{2,4},{3,5},{4,2},{5,3},{10,12},{11,13},{12,10},{13,11},{18,20},{1... | collective-permute-start | bytes 1572872 | tf_op jit(solution)/shard_map/ppermute | solution.py:314
  84.0 2.1 %collective-permute-start.24 = (bf16[1024,256]{1,0:T(8,128)(2,1)S(1)}, bf16[1024,256]{1,0:T(8,128)(2,1)S(1)}, u32[]{:S(2)}, u32[]{:S(2)}) collective-permute-start(bf16[1024,256]{1,0:T(8,128)(2,1)S(1)} %collective-permute-done.18.rest_4_), channel_id=1, source_target_pairs={{2,4},{3,5},{4,2},{5,3},{10,12},{11,13},{12,10},{13,11},{18,20},{1... | collective-permute-start | bytes 1572872 | tf_op jit(solution)/shard_map/ppermute | solution.py:314
  84.7 13.3 %collective-permute-start.17 = (bf16[1024,256]{1,0:T(8,128)(2,1)S(1)}, bf16[1024,256]{1,0:T(8,128)(2,1)S(1)}, u32[]{:S(2)}, u32[]{:S(2)}) collective-permute-start(bf16[1024,256]{1,0:T(8,128)(2,1)S(1)} %get-tuple-element.12.coded_ref.rest_2_), channel_id=1, source_target_pairs={{0,1},{1,0},{6,7},{7,6},{2,3},{3,2},{4,5},{5,4},{8,9},{9,8},{14,15... | collective-permute-start | bytes 1572872 | tf_op jit(solution)/shard_map/ppermute | solution.py:318
  84.8 18.6 %collective-permute-start.21 = (bf16[1024,256]{1,0:T(8,128)(2,1)S(1)}, bf16[1024,256]{1,0:T(8,128)(2,1)S(1)}, u32[]{:S(2)}, u32[]{:S(2)}) collective-permute-start(bf16[1024,256]{1,0:T(8,128)(2,1)S(1)} %collective-permute-done.20.rest_6_), channel_id=1, source_target_pairs={{2,0},{3,1},{4,6},{5,7},{10,8},{11,9},{12,14},{13,15},{18,16},{19,... | collective-permute-start | bytes 1572872 | tf_op jit(solution)/shard_map/ppermute | solution.py:314
  86.1 28.3 %collective-permute-start.25 = (bf16[1024,256]{1,0:T(8,128)(2,1)S(1)}, bf16[1024,256]{1,0:T(8,128)(2,1)S(1)}, u32[]{:S(2)}, u32[]{:S(2)}) collective-permute-start(bf16[1024,256]{1,0:T(8,128)(2,1)S(1)} %collective-permute-done.24.rest_10_), channel_id=1, source_target_pairs={{2,0},{3,1},{4,6},{5,7},{10,8},{11,9},{12,14},{13,15},{18,16},{19,... | collective-permute-start | bytes 1572872 | tf_op jit(solution)/shard_map/ppermute | solution.py:314
  89.1 4.5 %collective-permute-start.14 = (f32[1,512]{1,0:T(1,128)S(1)}, f32[1,512]{1,0:T(1,128)S(1)}, u32[]{:S(2)}, u32[]{:S(2)}) collective-permute-start(f32[1,512]{1,0:T(1,128)S(1)} %gather_wave.3), channel_id=1, source_target_pairs={{24,0},{0,8},{8,16},{16,24},{25,1},{1,9},{9,17},{17,25},{26,2},{2,... | collective-permute-start | bytes 6152 | tf_op jit(solution)/shard_map/ppermute | solution.py:371
  90.7 4.5 %collective-permute-start.15 = (f32[1,512]{1,0:T(1,128)S(1)}, f32[1,512]{1,0:T(1,128)S(1)}, u32[]{:S(2)}, u32[]{:S(2)}) collective-permute-start(f32[1,512]{1,0:T(1,128)S(1)} %gather_wave.3), channel_id=1, source_target_pairs={{16,0},{24,8},{0,16},{8,24},{17,1},{25,9},{1,17},{9,25},{18,2},{26... | collective-permute-start | bytes 6152 | tf_op jit(solution)/shard_map/ppermute | solution.py:371
  93.7 3.6 %collective-permute-start.16 = (f32[1,512]{1,0:T(1,128)S(1)}, f32[1,512]{1,0:T(1,128)S(1)}, u32[]{:S(2)}, u32[]{:S(2)}) collective-permute-start(f32[1,512]{1,0:T(1,128)S(1)} %gather_wave.3), channel_id=1, source_target_pairs={{8,0},{16,8},{24,16},{0,24},{9,1},{17,9},{25,17},{1,25},{10,2},{18... | collective-permute-start | bytes 6152 | tf_op jit(solution)/shard_map/ppermute | solution.py:371
  95.2 23.0 %collective-permute-start.19 = (bf16[1024,256]{1,0:T(8,128)(2,1)S(1)}, bf16[1024,256]{1,0:T(8,128)(2,1)S(1)}, u32[]{:S(2)}, u32[]{:S(2)}) collective-permute-start(bf16[1024,256]{1,0:T(8,128)(2,1)S(1)} %collective-permute-done.18.rest_4_), channel_id=1, source_target_pairs={{0,1},{1,0},{6,7},{7,6},{2,3},{3,2},{4,5},{5,4},{8,9},{9,8},{14,15... | collective-permute-start | bytes 1572872 | tf_op jit(solution)/shard_map/ppermute | solution.py:318
  97.3 21.0 %collective-permute-start.22 = (bf16[1024,256]{1,0:T(8,128)(2,1)S(1)}, bf16[1024,256]{1,0:T(8,128)(2,1)S(1)}, u32[]{:S(2)}, u32[]{:S(2)}) collective-permute-start(bf16[1024,256]{1,0:T(8,128)(2,1)S(1)} %collective-permute-done.20.rest_6_), channel_id=1, source_target_pairs={{2,3},{3,2},{4,5},{5,4},{10,11},{11,10},{12,13},{13,12},{18,19},{1... | collective-permute-start | bytes 1572872 | tf_op jit(solution)/shard_map/ppermute | solution.py:318
  98.0 20.3 %collective-permute-start.26 = (bf16[1024,256]{1,0:T(8,128)(2,1)S(1)}, bf16[1024,256]{1,0:T(8,128)(2,1)S(1)}, u32[]{:S(2)}, u32[]{:S(2)}) collective-permute-start(bf16[1024,256]{1,0:T(8,128)(2,1)S(1)} %collective-permute-done.24.rest_10_), channel_id=1, source_target_pairs={{2,3},{3,2},{4,5},{5,4},{10,11},{11,10},{12,13},{13,12},{18,19},{1... | collective-permute-start | bytes 1572872 | tf_op jit(solution)/shard_map/ppermute | solution.py:318
  103.3 14.9 %collective-permute-start.23 = (bf16[1024,256]{1,0:T(8,128)(2,1)S(1)}, bf16[1024,256]{1,0:T(8,128)(2,1)S(1)}, u32[]{:S(2)}, u32[]{:S(2)}) collective-permute-start(bf16[1024,256]{1,0:T(8,128)(2,1)S(1)} %collective-permute-done.21.rest_7_), channel_id=1, source_target_pairs={{0,1},{1,0},{6,7},{7,6},{8,9},{9,8},{14,15},{15,14},{16,17},{17,16... | collective-permute-start | bytes 1572872 | tf_op jit(solution)/shard_map/ppermute | solution.py:318
  114.4 3.9 %collective-permute-start.27 = (bf16[1024,256]{1,0:T(8,128)(2,1)S(1)}, bf16[1024,256]{1,0:T(8,128)(2,1)S(1)}, u32[]{:S(2)}, u32[]{:S(2)}) collective-permute-start(bf16[1024,256]{1,0:T(8,128)(2,1)S(1)} %collective-permute-done.25.rest_11_), channel_id=1, source_target_pairs={{0,1},{1,0},{6,7},{7,6},{8,9},{9,8},{14,15},{15,14},{16,17},{17,16... | collective-permute-start | bytes 1572872 | tf_op jit(solution)/shard_map/ppermute | solution.py:318
  126.1 0.9 copy-start.8
  127.1 11.6 %all-to-all-start = ((f32[32,1,128]{2,1,0:T(1,128)}), f32[32,1,128]{2,1,0:T(1,128)S(1)}, u32[]{:S(2)}, u32[]{:S(2)}) async-start(f32[32,1,128]{2,1,0:T(1,128)} %bitcast.11), calls=%async_computation | async-start | bytes 32768 | tf_op jit(solution)/shard_map/all_to_all | solution.py:413
  131.6 7.1 %copy-start.2 = (f32[1,1024,240]{1,2,0:T(8,128)S(1)}, f32[1,1024,240]{1,2,0:T(8,128)}, u32[]{:S(2)}) copy-start(f32[1,1024,240]{1,2,0:T(8,128)} %param.10) | copy-start | bytes 2949124
  131.6 7.1 %copy-start.9 = (f32[240,1024]{1,0:T(8,128)S(1)}, f32[240,1024]{1,0:T(8,128)}, u32[]{:S(2)}) copy-start(f32[240,1024]{1,0:T(8,128)} %copy-done.8) | copy-start | bytes 2949124

commit v3 on v2

--- a/solution.py
+++ b/solution.py
@@ -10,6 +10,7 @@
 
 epsilon = 1e-06
 LANES = 128
+QUAD = 4
 CHUNK = 256
 BATCH = 32
 VMEM_LIMIT = 40 * 2**20
@@ -130,25 +131,16 @@
     )(incoming, wave_in_t, angle)
 
 
-def near_kernel(groups, second, slot_ref, table_ref, tables_ref, vec_ref, mie_ref, far_ref, *rest):
-    if second:
-        first_ref, sums_in_ref, *rest = rest
-    count = sum(groups)
-    shards, (image_ref, other_ref, sums_ref, source, picked) = rest[:count], rest[count:]
-    rows, coefs = vec_ref.shape
-    requests = slot_ref.shape[0]
-    per_row = requests // rows
-    width = 2 * LANES
-    first = 0
-    for place, members in enumerate(groups):
-        value = shards[first][...].astype(jnp.float32)
-        for member in range(1, members):
-            value = value + shards[first + member][...].astype(jnp.float32)
-        first += members
-        base = place * 2 * rows
-        source[pl.ds(base, rows, stride=2), :] = value[:, :LANES]
-        source[pl.ds(base + 1, rows, stride=2), :] = value[:, LANES:]
-
+def load_rows(source, shards):
+    rows = shards[0].shape[0]
+    for place, shard in enumerate(shards):
+        value = shard[...].astype(jnp.float32)
+        source[pl.ds(2 * place * rows, rows, stride=2), :] = value[:, :LANES]
+        source[pl.ds(2 * place * rows + 1, rows, stride=2), :] = value[:, LANES:]
+    source[pl.ds(2 * len(shards) * rows, 8), :] = jnp.zeros((8, LANES), jnp.float32)
+
+
+def pick_rows(slot_ref, source, picked):
     def pick(step, carry):
         start = pl.multiple_of(step * BATCH, BATCH)
         got = [
@@ -160,58 +152,145 @@
             )
         return carry
 
-    lax.fori_loop(0, requests // BATCH, pick, 0)
-
-    def part(index, sums):
-        start = pl.multiple_of(index * CHUNK, CHUNK)
+    lax.fori_loop(0, slot_ref.shape[0] // BATCH, pick, 0)
+
+
+def translate(start, picked, table_ref, tables_ref):
+    at = pl.ds(start, CHUNK)
+    per_row = table_ref.shape[1]
+    coefs = tables_ref.shape[1]
+    stride = 2 * per_row
+    halves = [
+        [
+            picked[pl.ds(start * stride + 2 * k + h, CHUNK, stride=stride), :].astype(jnp.bfloat16)
+            for h in range(2)
+        ]
+        for k in range(per_row)
+    ]
+    named = [
+        jnp.broadcast_to(table_ref[at, k : k + 1], (CHUNK, LANES)).astype(jnp.bfloat16)
+        for k in range(per_row)
+    ]
+    zero = jnp.zeros((CHUNK, LANES), jnp.bfloat16)
+    total = jnp.zeros((CHUNK, coefs), jnp.float32)
+    for t in range(tables_ref.shape[0]):
+        chosen = [named[k] == jnp.bfloat16(t) for k in range(per_row)]
+        mixed = []
+        for h in range(2):
+            value = jnp.where(chosen[0], halves[0][h], zero)
+            for k in range(1, per_row):
+                value = value + jnp.where(chosen[k], halves[k][h], zero)
+            mixed.append(value)
+        total = total + jnp.dot(
+            jnp.concatenate(mixed, axis=1)[:, :coefs],
+            tables_ref[t],
+            preferred_element_type=jnp.float32,
+        )
+    return total
+
+
+def row_chunks(rows, step, carry=0):
+    return lax.fori_loop(
+        0, rows // CHUNK, lambda i, c: step(pl.multiple_of(i * CHUNK, CHUNK), c), carry
+    )
+
+
+def serve_kernel(slot_ref, table_ref, tables_ref, *rest):
+    *shards, out_ref, source, picked = rest
+    load_rows(source, shards)
+    pick_rows(slot_ref, source, picked)
+
+    def part(start, carry):
+        total = translate(start, picked, table_ref, tables_ref)
+        out_ref[pl.ds(start, CHUNK), :] = pad_lanes(total, out_ref.shape[1]).astype(jnp.bfloat16)
+        return carry
+
+    row_chunks(out_ref.shape[0], part)
+
+
+def near_kernel(slot_ref, table_ref, tables_ref, vec_ref, mie_ref, far_ref, *rest):
+    *shards, out_ref, source, picked = rest
+    load_rows(source, shards)
+    pick_rows(slot_ref, source, picked)
+
+    def part(start, carry):
         at = pl.ds(start, CHUNK)
-        stride = 2 * per_row
-        halves = [
-            [
-                picked[pl.ds(start * stride + 2 * k + h, CHUNK, stride=stride), :].astype(
-                    jnp.bfloat16
-                )
-                for h in range(2)
-            ]
-            for k in range(per_row)
-        ]
-        named = [
-            jnp.broadcast_to(table_ref[at, k : k + 1], (CHUNK, LANES)).astype(jnp.bfloat16)
-            for k in range(per_row)
-        ]
-        zero = jnp.zeros((CHUNK, LANES), jnp.bfloat16)
-        near = jnp.zeros((CHUNK, coefs), jnp.float32)
-        for t in range(tables_ref.shape[0]):
-            chosen = [named[k] == jnp.bfloat16(t) for k in range(per_row)]
-            mixed = []
-            for h in range(2):
-                value = jnp.where(chosen[0], halves[0][h], zero)
-                for k in range(1, per_row):
-                    value = value + jnp.where(chosen[k], halves[k][h], zero)
-                mixed.append(value)
-            near = near + jnp.dot(
-                jnp.concatenate(mixed, axis=1)[:, :coefs],
-                tables_ref[t],
-                preferred_element_type=jnp.float32,
-            )
+        total = translate(start, picked, table_ref, tables_ref) + far_ref[at, :]
+        out_ref[at, :] = vec_ref[at, :] - mie_ref[at, :] * total
+        return carry
+
+    row_chunks(out_ref.shape[0], part)
+
+
+def rows_scratch(shards, requests):
+    rows = shards[0].shape[0]
+    return [
+        pltpu.VMEM((len(shards) * rows * 2 + 8, LANES), jnp.float32),
+        pltpu.VMEM((requests * 2, LANES), jnp.float32),
+    ]
+
+
+def product_cost(rows, tables):
+    return pl.CostEstimate(
+        flops=2 * rows * tables * 256 * 256, bytes_accessed=8 * 2**20, transcendentals=0
+    )
+
+
+def serve(slots, table_ids, tables, shards):
+    rows, width = shards[0].shape
+    return pl.pallas_call(
+        serve_kernel,
+        out_shape=jax.ShapeDtypeStruct((rows, width), jnp.bfloat16),
+        in_specs=[whole(pltpu.SMEM)] + [whole()] * (2 + len(shards)),
+        out_specs=whole(),
+        scratch_shapes=rows_scratch(shards, slots.shape[0]),
+        compiler_params=params(),
+        cost_estimate=product_cost(rows, tables.shape[0]),
+        name="serve",
+    )(slots, table_ids, tables, *shards)
+
+
+def near_field(slots, table_ids, tables, vec, mie, far, shards):
+    return pl.pallas_call(
+        near_kernel,
+        out_shape=jax.ShapeDtypeStruct(vec.shape, jnp.float32),
+        in_specs=[whole(pltpu.SMEM)] + [whole()] * (5 + len(shards)),
+        out_specs=whole(),
+        scratch_shapes=rows_scratch(shards, slots.shape[0]),
+        compiler_params=params(),
+        cost_estimate=product_cost(vec.shape[0], tables.shape[0]),
+        name="near_field",
+    )(slots, table_ids, tables, vec, mie, far, *shards)
+
+
+def join_kernel(second, count, base_ref, mie_ref, vec_ref, *rest):
+    served, rest = rest[:count], rest[count:]
+    if second:
+        first_ref, sums_in_ref, *rest = rest
+    image_ref, *rest, sums_ref = rest
+    rows, coefs = base_ref.shape
+    width = served[0].shape[1]
+
+    def dot(a, b):
+        return jnp.sum(a * b, axis=0, keepdims=True)
+
+    def part(start, sums):
+        at = pl.ds(start, CHUNK)
+        far_rows = served[0][at, :].astype(jnp.float32)
+        for other in served[1:]:
+            far_rows = far_rows + other[at, :].astype(jnp.float32)
+        image = base_ref[at, :] - mie_ref[at, :] * far_rows[:, :coefs]
         vec = vec_ref[at, :]
-        image = vec - mie_ref[at, :] * (near + far_ref[at, :])
-
-        def dot(a, b):
-            return jnp.sum(a * b, axis=0, keepdims=True)
-
         if second:
             image_ref[:, at] = pad_lanes(image, width).T[:coefs, :]
             new = [dot(first_ref[at, :], image), dot(vec, image), dot(image, image)]
         else:
             image_ref[at, :] = image
-            other_ref[at, :] = pad_lanes(image, width).astype(jnp.bfloat16)
+            rest[0][at, :] = pad_lanes(image, width).astype(jnp.bfloat16)
             new = [dot(vec, vec), dot(vec, image), dot(image, image)]
         return tuple(a + b for a, b in zip(sums, new, strict=True))
 
-    sums = lax.fori_loop(
-        0, rows // CHUNK, part, tuple(jnp.zeros((1, coefs), jnp.float32) for _ in range(3))
-    )
+    sums = row_chunks(rows, part, tuple(jnp.zeros((1, coefs), jnp.float32) for _ in range(3)))
     lane = lax.broadcasted_iota(jnp.int32, (1, LANES), 1)
     packed = sums_in_ref[...] if second else jnp.zeros((1, LANES), jnp.float32)
     for k, value in enumerate(sums):
@@ -220,12 +299,11 @@
     sums_ref[...] = jnp.broadcast_to(packed, sums_ref.shape)
 
 
-def near_field(groups, slots, table_ids, tables, vec, mie, far, shards, second=None, devices=1):
-    rows, coefs = vec.shape
-    requests = slots.shape[0]
-    width = 2 * LANES
-    extra = () if second is None else second
+def join(base, mie, vec, served, second=None, devices=1):
+    rows, coefs = base.shape
+    width = served[0].shape[1]
     if second is None:
+        second = ()
         outs = (
             jax.ShapeDtypeStruct((rows, coefs), jnp.float32),
             jax.ShapeDtypeStruct((rows, width), jnp.bfloat16),
@@ -234,24 +312,16 @@
     else:
         outs = (
             jax.ShapeDtypeStruct((coefs, rows), jnp.float32),
-            jax.ShapeDtypeStruct((8, LANES), jnp.float32),
             jax.ShapeDtypeStruct((devices, LANES), jnp.float32),
         )
     return pl.pallas_call(
-        functools.partial(near_kernel, groups, second is not None),
+        functools.partial(join_kernel, len(second) > 0, len(served)),
         out_shape=outs,
-        in_specs=[whole(pltpu.SMEM)] + [whole()] * (5 + len(extra) + len(shards)),
-        out_specs=(whole(),) * 3,
-        scratch_shapes=[
-            pltpu.VMEM((len(groups) * rows * 2, LANES), jnp.float32),
-            pltpu.VMEM((requests * 2, LANES), jnp.float32),
-        ],
-        compiler_params=params(),
-        cost_estimate=pl.CostEstimate(
-            flops=2 * rows * 8 * 256 * 256, bytes_accessed=10 * 2**20, transcendentals=0
-        ),
-        name="near_second" if second is not None else "near_first",
-    )(slots, table_ids, tables, vec, mie, far, *extra, *shards)
+        in_specs=[whole()] * (3 + len(served) + len(second)),
+        out_specs=(whole(),) * len(outs),
+        compiler_params=params(),
+        name="join_second" if second else "join_first",
+    )(base, mie, vec, *served, *second)
 
 
 def finish_kernel(sums_ref, x_ref, u_ref, v_ref, solution_ref, residual_ref, hess_ref):
@@ -310,56 +380,8 @@
     )(sums, x_t, u_t, v_t)
 
 
-def along_chips(block, moves):
-    return lax.ppermute(block, "grp", [(2 * a + c, 2 * b + c) for a, b in moves for c in range(2)])
-
-
-def other_core(block, chips):
-    return lax.ppermute(block, "grp", [(2 * z + c, 2 * z + 1 - c) for z in chips for c in range(2)])
-
-
-def line_of_four(coded):
-    ends, middle = (0, 3), (1, 2)
-    swapped = along_chips(coded, [(0, 1), (1, 0), (2, 3), (3, 2)])
-    inner = along_chips(coded, [(1, 2), (2, 1)])
-    inward = along_chips(swapped, [(1, 2), (2, 1)])
-    outward = along_chips(inner, [(1, 0), (2, 3)])
-    last = along_chips(inward, [(1, 0), (2, 3)])
-    groups, blocks = [], []
-    for members in (
-        [(coded, ends + middle)],
-        [(swapped, ends + middle)],
-        [(inner, middle), (outward, ends)],
-        [(inward, middle), (last, ends)],
-    ):
-        groups += [len(members)] * 2
-        blocks += [block for block, _ in members]
-        blocks += [other_core(block, chips) for block, chips in members]
-    return tuple(groups), blocks
-
-
-def place_in_line(source, here):
-    far_side = 2 + jnp.where((source == 0) | (source == 3), 1, 0)
-    return jnp.where(source == here, 0, jnp.where(source == (here ^ 1), 1, far_side))
-
-
-def ring_of_chips(coded):
-    chips = lax.axis_size("grp") // 2
-    groups, blocks = [], []
-    for m in range(chips):
-        block = along_chips(coded, [((z + m) % chips, z) for z in range(chips)]) if m else coded
-        groups += [1, 1]
-        blocks += [block, other_core(block, range(chips))]
-    return tuple(groups), blocks
-
-
-def exchange(coded):
-    return line_of_four(coded) if lax.axis_size("grp") == 8 else ring_of_chips(coded)
-
-
-def place_of(source, here):
-    chips = lax.axis_size("grp") // 2
-    return place_in_line(source, here) if chips == 4 else (source - here) % chips
+def flip(block, bits):
+    return lax.ppermute(block, "grp", [(i, i ^ bits) for i in range(lax.axis_size("grp"))])
 
 
 def far_field(coded, wave_out, wave_in_t, angle, trans_rows):
@@ -391,25 +413,39 @@
     angle = plane_angle[0]
     rows, coefs = x.shape
     width = -(-coefs // LANES) * LANES
-    devices = lax.axis_size("grp") * lax.axis_size("blk")
-    me = lax.axis_index("grp")
-    owner = owner_dev[0, :, 0]
-    away = place_of(owner // 2, me // 2) * 2 + ((owner % 2) ^ (me % 2))
-    slots = 2 * (away * rows + near_row[0])
-    table_ids = table_id[0].reshape(rows, -1)
+    group = lax.axis_size("grp")
+    devices = group * lax.axis_size("blk")
+    tables_count = tables.shape[0]
     wave_in_t = wave_in.T
-
     x_t = x.T
-    coded = code(x_t, width)
-    groups, shards = exchange(coded)
-    far = far_field(coded, wave_out, wave_in_t, angle, far_trans[0, 0])
-    image, coded, sums = near_field(groups, slots, table_ids, tables, x, mie, far, shards)
-
-    groups, shards = exchange(coded)
-    far = far_field(coded, wave_out, wave_in_t, angle, far_trans[0, 0])
-    second_t, _, sums = near_field(
-        groups, slots, table_ids, tables, image, mie, far, shards, (x, sums), devices
-    )
+
+    apart = owner_dev[0, :, 0] ^ lax.axis_index("grp")
+    slots = 2 * ((apart % QUAD) * rows + near_row[0])
+    nothing = 2 * QUAD * rows
+    names = table_id[0]
+    quads = range(1, group // QUAD)
+    asked = [
+        flip(jnp.where(apart // QUAD == j, slots, nothing) * tables_count + names, QUAD * j)
+        for j in quads
+    ]
+    asked = [(word // tables_count, (word % tables_count).reshape(rows, -1)) for word in asked]
+    slots = jnp.where(apart < QUAD, slots, nothing)
+    names = names.reshape(rows, -1)
+
+    def operator(coded, vec):
+        across = flip(coded, 2)
+        shards = [coded, flip(coded, 1), across, flip(across, 1)]
+        far = far_field(coded, wave_out, wave_in_t, angle, far_trans[0, 0])
+        served = [
+            flip(serve(slot, name, tables, shards), QUAD * j)
+            for j, (slot, name) in zip(quads, asked, strict=True)
+        ]
+        return near_field(slots, names, tables, vec, mie, far, shards), served
+
+    base, served = operator(code(x_t, width), x)
+    image, coded, sums = join(base, mie, x, served)
+    base, served = operator(coded, image)
+    second_t, sums = join(base, mie, image, served, (x, sums), devices)
     sums = lax.all_to_all(sums, ("blk", "grp"), 0, 0, tiled=True)
     solution_t, residual_t, hess_t = finish(sums, x_t, image.T, second_t)
     return solution_t.T[None], residual_t.T[None], hess_t.T

time: 141 us -> 126 us (0.89)
  starting transfers between devices: 42.8 us -> 27 us
  waiting for transfers between devices: 58.9 us -> 43.2 us
  Pallas kernels: 26.2 us -> 39.9 us
  local copies, waits for them, and re-layouts: 11 us -> 13.5 us
    ppermute x22 -> x9, starting transfers between devices: 28.7 us -> 13.1 us  [flip(): lax.ppermute(block, 'grp', [(i, i ^ bits) for i in range(lax.axis_size('g...]
    pallas_call x2 -> x6, Pallas kernels: 16.5 us -> 30.3 us  [the longest x2 14.1 us: serve(): pl.pallas_call(serve_kernel, out_shape=jax.ShapeDtypeStruct((rows, width)...]
    ppermute x22 -> x9, waiting for transfers between devices: 46.9 us -> 34.4 us  [flip(): lax.ppermute(block, 'grp', [(i, i ^ bits) for i in range(lax.axis_size('g...]
    ppermute x6, waiting for transfers between devices: 6.69 us -> 3.4 us  [far_field(): lax.ppermute(own, 'blk', [((i - turn) % blocks, i) for i in range(blocks)])]
    unnamed x40 -> x52, local copies, waits for them, and re-layouts: 6.6 us -> 8.86 us
    ppermute x6, starting transfers between devices: 9.54 us -> 8.09 us  [far_field(): lax.ppermute(own, 'blk', [((i - turn) % blocks, i) for i in range(blocks)])]
  transfers between devices with their start and end apart: 29 -> 16, of which waited for: 11 -> 9; matrix products, arithmetic and copies ran while one was open for 4% -> 5% of each run, Pallas kernels for 5% -> 16%
where the time goes in v3:
time: 126 us; the launch traced here: 125 us
  waiting for transfers between devices  43.2 us (34%)
  Pallas kernels  39.9 us (32%)
  starting transfers between devices  27 us (21%)
  local copies, waits for them, and re-layouts  13.5 us (11%)
    ppermute x9, waiting for transfers between devices, flip(): lax.ppermute(block, 'grp', [(i, i ^ bits) for i in range(lax.axis_size('g...  34.4 us
    pallas_call x2, Pallas kernels, serve(): pl.pallas_call(serve_kernel, out_shape=jax.ShapeDtypeStruct((rows, width)...  14.1 us
    pallas_call x2, Pallas kernels, near_field(): pl.pallas_call(near_kernel, out_shape=jax.ShapeDtypeStruct(vec.shape, jnp...  13.3 us
    ppermute x9, starting transfers between devices, flip(): lax.ppermute(block, 'grp', [(i, i ^ bits) for i in range(lax.axis_size('g...  13.1 us
    unnamed x52, local copies, waits for them, and re-layouts  8.86 us
    ppermute x6, starting transfers between devices, far_field(): lax.ppermute(own, 'blk', [((i - turn) % blocks, i) for i in range(blocks)])  8.09 us
    all_to_all x1, starting transfers between devices, body(): sums = lax.all_to_all(sums, ('blk', 'grp'), 0, 0, tiled=True)  5.79 us
    all_to_all x1, waiting for transfers between devices, body(): sums = lax.all_to_all(sums, ('blk', 'grp'), 0, 0, tiled=True)  5.41 us
  transfers between devices with their start and end apart: 16, of which 9 were waited for; matrix products, arithmetic and copies ran while one was open for 5% of the time, Pallas kernels for 16%

profile of v3, /device:TPU:0, one launch (start us, length us, event | category | flops | bytes accessed | tf_op | source)
XLA Modules:
  0.0 125.3 jit_solution(3080329678502241481)
XLA Ops:
  0.6 0.0 copy-start.4
  0.6 1.2 copy-done.4
  1.8 0.2 code_rows.1.coded_ref.rest_0_
  2.1 3.1 %collective-permute-start.4 = (bf16[1024,256]{1,0:T(8,128)(2,1)S(1)}, bf16[1024,256]{1,0:T(8,128)(2,1)S(1)}, u32[]{:S(2)}, u32[]{:S(2)}) collective-permute-start(bf16[1024,256]{1,0:T(8,128)(2,1)S(1)} %code_rows.1.coded_ref.rest_0_), channel_id=1, source_target_pairs={{0,2},{1,3},{2,0},{3,1},{4,6},{5,7},{6,4},{7,5},{8,10},{9,11},{10,... | collective-permute-start | bytes 1572872 | tf_op jit(solution)/shard_map/ppermute | solution.py:384
  5.2 11.9 %collective-permute-done.4.rest_2_ = bf16[1024,256]{1,0:T(8,128)(2,1)S(1)} collective-permute-done((bf16[1024,256]{1,0:T(8,128)(2,1)S(1)}, bf16[1024,256]{1,0:T(8,128)(2,1)S(1)}, u32[]{:S(2)}, u32[]{:S(2)}) %collective-permute-start.4) | collective-permute-done | bytes 524320 | tf_op jit(solution)/shard_map/ppermute | solution.py:384
  17.1 0.8 copy-done.11
  18.0 2.8 %collective-permute-start.6 = (s32[3072]{0:T(1024)S(1)}, s32[3072]{0:T(1024)S(1)}, u32[]{:S(2)}, u32[]{:S(2)}) collective-permute-start(s32[3072]{0:T(1024)S(1)} %get-tuple-element.19), channel_id=1, source_target_pairs={{0,4},{1,5},{2,6},{3,7},{4,0},{5,1},{6,2},{7,3},{8,12},{9,13},{10,... | collective-permute-start | bytes 36872 | tf_op jit(solution)/shard_map/ppermute | solution.py:384
  20.8 1.8 %collective-permute-done.6 = s32[3072]{0:T(1024)S(1)} collective-permute-done((s32[3072]{0:T(1024)S(1)}, s32[3072]{0:T(1024)S(1)}, u32[]{:S(2)}, u32[]{:S(2)}) %collective-permute-start.6) | collective-permute-done | bytes 12320 | tf_op jit(solution)/shard_map/ppermute | solution.py:384
  22.6 0.3 reshape.16.table_ref
  23.0 0.8 copy-done.14
  23.9 1.0 copy-done.12
  24.9 1.0 copy-done.15
  26.0 7.7 %serve.2 = bf16[1024,256]{1,0:T(8,128)(2,1)} custom-call(s32[3072]{0:T(1024)S(1)} %get-tuple-element.22.slot_ref, s32[1024,3]{1,0:T(8,128)S(1)} %reshape.16.table_ref, bf16[8,240,240]{2,1,0:T(8,128)(2,1)S(1)} %copy-done.1, bf16[1024,256]{1,0:T(8,128)(2,1)S(1)} %code_rows.1.coded_ref.rest_0_, bf16[1024,256]{1,0:T(8,128)(2,1)S(1)} %copy-done.15, ...), custom_call_target="tpu_custom_call" | custom-call | flops 1073741824 | bytes 8388608 | tf_op jit(solution)/shard_map/serve/pallas_call | solution.py:241
  33.6 2.8 %collective-permute-start.7 = (bf16[1024,256]{1,0:T(8,128)(2,1)}, bf16[1024,256]{1,0:T(8,128)(2,1)}, u32[]{:S(2)}, u32[]{:S(2)}) collective-permute-start(bf16[1024,256]{1,0:T(8,128)(2,1)} %serve.2), channel_id=1, source_target_pairs={{0,4},{1,5},{2,6},{3,7},{4,0},{5,1},{6,2},{7,3},{8,12},{9,13},{10,... | collective-permute-start | bytes 1572872 | tf_op jit(solution)/shard_map/ppermute | solution.py:384
  36.4 1.8 %gather_wave.2 = f32[1,512]{1,0:T(1,128)S(1)} custom-call(bf16[1024,256]{1,0:T(8,128)(2,1)S(1)} %code_rows.1.coded_ref.rest_0_, bf16[240,512]{1,0:T(8,128)(2,1)S(1)} %copy-done.17, bf16[1024,512]{1,0:T(8,128)(2,1)S(1)} %bitcast.50), custom_call_target="tpu_custom_call" | custom-call | flops 268435456 | bytes 2097152 | tf_op jit(solution)/shard_map/gather_wave/pallas_call | solution.py:88
  38.1 1.5 %collective-permute-start = (f32[1,512]{1,0:T(1,128)S(1)}, f32[1,512]{1,0:T(1,128)S(1)}, u32[]{:S(2)}, u32[]{:S(2)}) collective-permute-start(f32[1,512]{1,0:T(1,128)S(1)} %gather_wave.2), channel_id=1, source_target_pairs={{24,0},{0,8},{8,16},{16,24},{25,1},{1,9},{9,17},{17,25},{26,2},{2,... | collective-permute-start | bytes 6152 | tf_op jit(solution)/shard_map/ppermute | solution.py:393
  39.7 1.5 %collective-permute-start.1 = (f32[1,512]{1,0:T(1,128)S(1)}, f32[1,512]{1,0:T(1,128)S(1)}, u32[]{:S(2)}, u32[]{:S(2)}) collective-permute-start(f32[1,512]{1,0:T(1,128)S(1)} %gather_wave.2), channel_id=1, source_target_pairs={{16,0},{24,8},{0,16},{8,24},{17,1},{25,9},{1,17},{9,25},{18,2},{26... | collective-permute-start | bytes 6152 | tf_op jit(solution)/shard_map/ppermute | solution.py:393
  41.2 1.4 %collective-permute-start.2 = (f32[1,512]{1,0:T(1,128)S(1)}, f32[1,512]{1,0:T(1,128)S(1)}, u32[]{:S(2)}, u32[]{:S(2)}) collective-permute-start(f32[1,512]{1,0:T(1,128)S(1)} %gather_wave.2), channel_id=1, source_target_pairs={{8,0},{16,8},{24,16},{0,24},{9,1},{17,9},{25,17},{1,25},{10,2},{18... | collective-permute-start | bytes 6152 | tf_op jit(solution)/shard_map/ppermute | solution.py:393
  42.6 0.3 copy.23
  43.0 1.5 %copy.24.vec_ref.rest_1_ = f32[1024,240]{1,0:T(8,128)S(1)} copy(f32[1024,240]{0,1:T(8,128)} %bitcast.54) | data formatting | bytes 1966080 | tf_op jit(solution)/shard_map/squeeze | solution.py:411
  44.5 0.5 broadcast.41
  45.0 0.7 reduce.3
  45.7 1.1 reshape_squeeze.3.table_ref
  46.9 0.9 copy-done.18
  47.9 1.9 %spread_wave.2.far_ref = f32[1024,240]{1,0:T(8,128)S(1)} custom-call(f32[1,512]{1,0:T(1,128)S(1)} %fusion.8.incoming_ref, bf16[240,512]{1,0:T(8,128)(2,1)S(1)} %bitcast.58, bf16[1024,512]{1,0:T(8,128)(2,1)S(1)} %bitcast.51), custom_call_target="tpu_custom_call" | custom-call | flops 268435456 | bytes 3145728 | tf_op jit(solution)/shard_map/spread_wave/pallas_call | solution.py:121
  49.8 1.0 copy-done.13
  50.9 1.0 copy-done.16
  51.9 6.8 %near_field.2.base_ref = f32[1024,240]{1,0:T(8,128)S(1)} custom-call(s32[3072]{0:T(1024)S(1)} %get-tuple-element.20.slot_ref, s32[1024,3]{1,0:T(8,128)S(1)} %copy-done.10, bf16[8,240,240]{2,1,0:T(8,128)(2,1)S(1)} %copy-done.2, f32[1024,240]{1,0:T(8,128)S(1)} %copy.24.vec_ref.rest_1_, f32[1024,240]{1,0:T(8,128)S(1)} %bitcast.46, ...), custom_call_target="tpu_custom_call" | custom-call | flops 1073741824 | bytes 8388608 | tf_op jit(solution)/shard_map/near_field/pallas_call | solution.py:254
  58.7 0.6 collective-permute-done.7.rest_0_
  59.4 1.6 %join_first.1 = (f32[1024,240]{1,0:T(8,128)S(1)}, bf16[1024,256]{1,0:T(8,128)(2,1)S(1)}, f32[1,128]{1,0:T(1,128)S(1)}) custom-call(f32[1024,240]{1,0:T(8,128)S(1)} %near_field.2.base_ref, f32[1024,240]{1,0:T(8,128)S(1)} %bitcast.47, f32[1024,240]{1,0:T(8,128)S(1)} %copy.24.vec_ref.rest_1_, bf16[1024,256]{1,0:T(8,128)(2,1)} %collective-permute-done.7.rest_0_), custom_call_target="tpu_custom_call" | custom-call | tf_op jit(solution)/shard_map/join_first/pallas_call | solution.py:317
  60.9 1.0 collective-permute-start.12
  62.0 11.8 %collective-permute-done.12.rest_2_ = bf16[1024,256]{1,0:T(8,128)(2,1)S(1)} collective-permute-done((bf16[1024,256]{1,0:T(8,128)(2,1)S(1)}, bf16[1024,256]{1,0:T(8,128)(2,1)S(1)}, u32[]{:S(2)}, u32[]{:S(2)}) %collective-permute-start.12) | collective-permute-done | bytes 524320 | tf_op jit(solution)/shard_map/ppermute | solution.py:384
  73.8 1.9 %collective-permute-done.13.rest_3_ = bf16[1024,256]{1,0:T(8,128)(2,1)S(1)} collective-permute-done((bf16[1024,256]{1,0:T(8,128)(2,1)S(1)}, bf16[1024,256]{1,0:T(8,128)(2,1)S(1)}, u32[]{:S(2)}, u32[]{:S(2)}) %collective-permute-start.13) | collective-permute-done | bytes 524320 | tf_op jit(solution)/shard_map/ppermute | solution.py:384
  75.7 6.5 %serve.3 = bf16[1024,256]{1,0:T(8,128)(2,1)S(1)} custom-call(s32[3072]{0:T(1024)S(1)} %get-tuple-element.22.slot_ref, s32[1024,3]{1,0:T(8,128)S(1)} %copy-done.9, bf16[8,240,240]{2,1,0:T(8,128)(2,1)S(1)} %copy-done.2, bf16[1024,256]{1,0:T(8,128)(2,1)S(1)} %get-tuple-element.12.coded_ref.rest_0_, bf16[1024,256]{1,0:T(8,128)(2,1)S(1)} %collective-permute-done.11.rest_1_, ...), custom_call_target="tpu_custom_call" | custom-call | flops 1073741824 | bytes 8388608 | tf_op jit(solution)/shard_map/serve/pallas_call | solution.py:241
  82.2 3.4 %collective-permute-start.14 = (bf16[1024,256]{1,0:T(8,128)(2,1)S(1)}, bf16[1024,256]{1,0:T(8,128)(2,1)S(1)}, u32[]{:S(2)}, u32[]{:S(2)}) collective-permute-start(bf16[1024,256]{1,0:T(8,128)(2,1)S(1)} %serve.3), channel_id=1, source_target_pairs={{0,4},{1,5},{2,6},{3,7},{4,0},{5,1},{6,2},{7,3},{8,12},{9,13},{10,... | collective-permute-start | bytes 1572872 | tf_op jit(solution)/shard_map/ppermute | solution.py:384
  85.6 1.8 %gather_wave.3 = f32[1,512]{1,0:T(1,128)S(1)} custom-call(bf16[1024,256]{1,0:T(8,128)(2,1)S(1)} %get-tuple-element.12.coded_ref.rest_0_, bf16[240,512]{1,0:T(8,128)(2,1)S(1)} %copy-done.17, bf16[1024,512]{1,0:T(8,128)(2,1)S(1)} %bitcast.52), custom_call_target="tpu_custom_call" | custom-call | flops 268435456 | bytes 2097152 | tf_op jit(solution)/shard_map/gather_wave/pallas_call | solution.py:88
  87.4 2.5 %collective-permute-start.10 = (f32[1,512]{1,0:T(1,128)S(1)}, f32[1,512]{1,0:T(1,128)S(1)}, u32[]{:S(2)}, u32[]{:S(2)}) collective-permute-start(f32[1,512]{1,0:T(1,128)S(1)} %gather_wave.3), channel_id=1, source_target_pairs={{8,0},{16,8},{24,16},{0,24},{9,1},{17,9},{25,17},{1,25},{10,2},{18... | collective-permute-start | bytes 6152 | tf_op jit(solution)/shard_map/ppermute | solution.py:393
  89.9 1.1 collective-permute-start.9
  91.0 0.2 collective-permute-done.10
  91.2 3.2 %collective-permute-done.8 = f32[1,512]{1,0:T(1,128)S(1)} collective-permute-done((f32[1,512]{1,0:T(1,128)S(1)}, f32[1,512]{1,0:T(1,128)S(1)}, u32[]{:S(2)}, u32[]{:S(2)}) %collective-permute-start.8) | collective-permute-done | bytes 2080 | tf_op jit(solution)/shard_map/ppermute | solution.py:393
  94.4 1.9 %spread_wave.3.far_ref = f32[1024,240]{1,0:T(8,128)S(1)} custom-call(f32[1,512]{1,0:T(1,128)S(1)} %fusion.9.incoming_ref, bf16[240,512]{1,0:T(8,128)(2,1)S(1)} %bitcast.59, bf16[1024,512]{1,0:T(8,128)(2,1)S(1)} %bitcast.53), custom_call_target="tpu_custom_call" | custom-call | flops 268435456 | bytes 3145728 | tf_op jit(solution)/shard_map/spread_wave/pallas_call | solution.py:121
  96.3 6.5 %near_field.3.base_ref = f32[1024,240]{1,0:T(8,128)S(1)} custom-call(s32[3072]{0:T(1024)S(1)} %get-tuple-element.20.slot_ref, s32[1024,3]{1,0:T(8,128)S(1)} %copy-done.10, bf16[8,240,240]{2,1,0:T(8,128)(2,1)S(1)} %copy-done.2, f32[1024,240]{1,0:T(8,128)S(1)} %get-tuple-element.11.vec_ref, f32[1024,240]{1,0:T(8,128)S(1)} %bitcast.48, ...), custom_call_target="tpu_custom_call" | custom-call | flops 1073741824 | bytes 8388608 | tf_op jit(solution)/shard_map/near_field/pallas_call | solution.py:254
  102.8 6.3 %collective-permute-done.14.rest_0_ = bf16[1024,256]{1,0:T(8,128)(2,1)S(1)} collective-permute-done((bf16[1024,256]{1,0:T(8,128)(2,1)S(1)}, bf16[1024,256]{1,0:T(8,128)(2,1)S(1)}, u32[]{:S(2)}, u32[]{:S(2)}) %collective-permute-start.14) | collective-permute-done | bytes 524320 | tf_op jit(solution)/shard_map/ppermute | solution.py:384
  109.1 1.3 %join_second.1 = (f32[240,1024]{1,0:T(8,128)S(1)}, f32[32,128]{1,0:T(8,128)}) custom-call(f32[1024,240]{1,0:T(8,128)S(1)} %near_field.3.base_ref, f32[1024,240]{1,0:T(8,128)S(1)} %bitcast.49, f32[1024,240]{1,0:T(8,128)S(1)} %get-tuple-element.11.vec_ref, bf16[1024,256]{1,0:T(8,128)(2,1)S(1)} %collective-permute-done.14.rest_0_, ...), custom_call_target="tpu_custom_call" | custom-call | tf_op jit(solution)/shard_map/join_second/pallas_call | solution.py:317
  110.4 5.8 %all-to-all-start = ((f32[32,1,128]{2,1,0:T(1,128)}), f32[32,1,128]{2,1,0:T(1,128)S(1)}, u32[]{:S(2)}, u32[]{:S(2)}) async-start(f32[32,1,128]{2,1,0:T(1,128)} %bitcast.12), calls=%async_computation | async-start | bytes 32768 | tf_op jit(solution)/shard_map/all_to_all | solution.py:449
  116.2 1.6 %copy.28 = f32[1024,240]{0,1:T(8,128)S(1)} copy(f32[1024,240]{1,0:T(8,128)} %copy-done.3) | data formatting | bytes 1966080 | tf_op jit(solution)/shard_map/join_first/pallas_call | solution.py:317
  117.8 5.4 %all-to-all-done = f32[32,1,128]{2,1,0:T(1,128)S(1)} async-done(((f32[32,1,128]{2,1,0:T(1,128)}), f32[32,1,128]{2,1,0:T(1,128)S(1)}, u32[]{:S(2)}, u32[]{:S(2)}) %all-to-all-start) | async-done | bytes 16416 | tf_op jit(solution)/shard_map/all_to_all | solution.py:449
  123.3 2.1 %finish.1 = (f32[240,1024]{1,0:T(8,128)}, f32[240,1024]{1,0:T(8,128)}, f32[2,3]{1,0:T(2,128)}) custom-call(f32[32,128]{1,0:T(8,128)S(1)} %bitcast.60, f32[240,1024]{1,0:T(8,128)S(1)} %bitcast.56, f32[240,1024]{1,0:T(8,128)S(1)} %bitcast.57, f32[240,1024]{1,0:T(8,128)S(1)} %get-tuple-element.15.v_ref), custom_call_target="tpu_custom_call" | custom-call | tf_op jit(solution)/shard_map/finish/pallas_call | solution.py:373
  (58 shorter events, 0.2 us)
Async XLA Ops:
  0.6 1.2 copy-start.4
  1.8 16.1 %copy-start.23 = (s32[1,3072,1]{1,2,0:T(1,128)S(1)}, s32[1,3072,1]{1,2,0:T(1,128)}, u32[]{:S(2)}) copy-start(s32[1,3072,1]{1,2,0:T(1,128)} %param.12) | copy-start | bytes 36868
  1.8 22.0 %copy-start.1 = (bf16[8,240,240]{2,1,0:T(8,128)(2,1)S(1)}, bf16[8,240,240]{2,1,0:T(8,128)(2,1)}, u32[]{:S(2)}) copy-start(bf16[8,240,240]{2,1,0:T(8,128)(2,1)} %tables_ref.7) | copy-start | bytes 2764804
  2.0 34.3 %copy-start.6 = (bf16[1024,256]{1,0:T(8,128)(2,1)}, bf16[1024,256]{1,0:T(8,128)(2,1)S(1)}, u32[]{:S(2)}) copy-start(bf16[1024,256]{1,0:T(8,128)(2,1)S(1)} %code_rows.1.coded_ref.rest_0_) | copy-start | bytes 1572868
  2.1 15.0 %collective-permute-start.4 = (bf16[1024,256]{1,0:T(8,128)(2,1)S(1)}, bf16[1024,256]{1,0:T(8,128)(2,1)S(1)}, u32[]{:S(2)}, u32[]{:S(2)}) collective-permute-start(bf16[1024,256]{1,0:T(8,128)(2,1)S(1)} %code_rows.1.coded_ref.rest_0_), channel_id=1, source_target_pairs={{0,2},{1,3},{2,0},{3,1},{4,6},{5,7},{6,4},{7,5},{8,10},{9,11},{10,... | collective-permute-start | bytes 1572872 | tf_op jit(solution)/shard_map/ppermute | solution.py:384
  5.2 17.9 %collective-permute-start.3 = (bf16[1024,256]{1,0:T(8,128)(2,1)S(1)}, bf16[1024,256]{1,0:T(8,128)(2,1)S(1)}, u32[]{:S(2)}, u32[]{:S(2)}) collective-permute-start(bf16[1024,256]{1,0:T(8,128)(2,1)S(1)} %code_rows.1.coded_ref.rest_0_), channel_id=1, source_target_pairs={{0,1},{1,0},{2,3},{3,2},{4,5},{5,4},{6,7},{7,6},{8,9},{9,8},{10,11... | collective-permute-start | bytes 1572872 | tf_op jit(solution)/shard_map/ppermute | solution.py:384
  5.2 12.8 %copy-start.21 = (s32[1,3072]{1,0:T(1,128)S(1)}, s32[1,3072]{1,0:T(1,128)}, u32[]{:S(2)}) copy-start(s32[1,3072]{1,0:T(1,128)} %param.14) | copy-start | bytes 36868
  5.2 12.8 %copy-start.24 = (s32[1,3072]{1,0:T(1,128)S(1)}, s32[1,3072]{1,0:T(1,128)}, u32[]{:S(2)}) copy-start(s32[1,3072]{1,0:T(1,128)} %param.13) | copy-start | bytes 36868
  17.1 6.8 %collective-permute-start.5 = (bf16[1024,256]{1,0:T(8,128)(2,1)S(1)}, bf16[1024,256]{1,0:T(8,128)(2,1)}, u32[]{:S(2)}, u32[]{:S(2)}) collective-permute-start(bf16[1024,256]{1,0:T(8,128)(2,1)S(1)} %collective-permute-done.4.rest_2_), channel_id=1, source_target_pairs={{0,1},{1,0},{2,3},{3,2},{4,5},{5,4},{6,7},{7,6},{8,9},{9,8},{10,11... | collective-permute-start | bytes 1572872 | tf_op jit(solution)/shard_map/ppermute | solution.py:384
  17.1 0.8 copy-start.11
  18.0 4.7 %collective-permute-start.6 = (s32[3072]{0:T(1024)S(1)}, s32[3072]{0:T(1024)S(1)}, u32[]{:S(2)}, u32[]{:S(2)}) collective-permute-start(s32[3072]{0:T(1024)S(1)} %get-tuple-element.19), channel_id=1, source_target_pairs={{0,4},{1,5},{2,6},{3,7},{4,0},{5,1},{6,2},{7,3},{8,12},{9,13},{10,... | collective-permute-start | bytes 36872 | tf_op jit(solution)/shard_map/ppermute | solution.py:384
  23.0 10.6 %copy-start.8 = (s32[1024,3]{1,0:T(8,128)}, s32[1024,3]{1,0:T(8,128)S(1)}, u32[]{:S(2)}) copy-start(s32[1024,3]{1,0:T(8,128)S(1)} %reshape.16.table_ref) | copy-start | bytes 36868
  23.0 0.8 copy-start.14
  23.9 1.0 copy-start.12
  24.9 1.0 copy-start.15
  25.9 10.4 %copy-start = (bf16[1,1024,512]{2,1,0:T(8,128)(2,1)S(1)}, bf16[1,1024,512]{2,1,0:T(8,128)(2,1)}, u32[]{:S(2)}) copy-start(bf16[1,1024,512]{2,1,0:T(8,128)(2,1)} %param.18) | copy-start | bytes 3145732
  25.9 10.4 %copy-start.17 = (bf16[240,512]{1,0:T(8,128)(2,1)S(1)}, bf16[240,512]{1,0:T(8,128)(2,1)}, u32[]{:S(2)}) copy-start(bf16[240,512]{1,0:T(8,128)(2,1)} %out_ref.3) | copy-start | bytes 737284
  33.6 25.7 %collective-permute-start.7 = (bf16[1024,256]{1,0:T(8,128)(2,1)}, bf16[1024,256]{1,0:T(8,128)(2,1)}, u32[]{:S(2)}, u32[]{:S(2)}) collective-permute-start(bf16[1024,256]{1,0:T(8,128)(2,1)} %serve.2), channel_id=1, source_target_pairs={{0,4},{1,5},{2,6},{3,7},{4,0},{5,1},{6,2},{7,3},{8,12},{9,13},{10,... | collective-permute-start | bytes 1572872 | tf_op jit(solution)/shard_map/ppermute | solution.py:384
  36.4 6.3 %copy-start.20 = (f32[1,1024,240]{1,2,0:T(8,128)S(1)}, f32[1,1024,240]{1,2,0:T(8,128)}, u32[]{:S(2)}) copy-start(f32[1,1024,240]{1,2,0:T(8,128)} %param.11) | copy-start | bytes 2949124
  38.1 8.7 %collective-permute-start = (f32[1,512]{1,0:T(1,128)S(1)}, f32[1,512]{1,0:T(1,128)S(1)}, u32[]{:S(2)}, u32[]{:S(2)}) collective-permute-start(f32[1,512]{1,0:T(1,128)S(1)} %gather_wave.2), channel_id=1, source_target_pairs={{24,0},{0,8},{8,16},{16,24},{25,1},{1,9},{9,17},{17,25},{26,2},{2,... | collective-permute-start | bytes 6152 | tf_op jit(solution)/shard_map/ppermute | solution.py:393
  39.7 7.2 %collective-permute-start.1 = (f32[1,512]{1,0:T(1,128)S(1)}, f32[1,512]{1,0:T(1,128)S(1)}, u32[]{:S(2)}, u32[]{:S(2)}) collective-permute-start(f32[1,512]{1,0:T(1,128)S(1)} %gather_wave.2), channel_id=1, source_target_pairs={{16,0},{24,8},{0,16},{8,24},{17,1},{25,9},{1,17},{9,25},{18,2},{26... | collective-permute-start | bytes 6152 | tf_op jit(solution)/shard_map/ppermute | solution.py:393
  41.2 5.7 %collective-permute-start.2 = (f32[1,512]{1,0:T(1,128)S(1)}, f32[1,512]{1,0:T(1,128)S(1)}, u32[]{:S(2)}, u32[]{:S(2)}) collective-permute-start(f32[1,512]{1,0:T(1,128)S(1)} %gather_wave.2), channel_id=1, source_target_pairs={{8,0},{16,8},{24,16},{0,24},{9,1},{17,9},{25,17},{1,25},{10,2},{18... | collective-permute-start | bytes 6152 | tf_op jit(solution)/shard_map/ppermute | solution.py:393
  45.7 1.2 copy-start.22
  46.9 0.9 copy-start.18
  47.9 1.9 %copy-start.2 = (bf16[8,240,240]{2,1,0:T(8,128)(2,1)S(1)}, bf16[8,240,240]{2,1,0:T(8,128)(2,1)}, u32[]{:S(2)}) copy-start(bf16[8,240,240]{2,1,0:T(8,128)(2,1)} %tables_ref.7) | copy-start | bytes 2764804
  47.9 1.9 %copy-start.7 = (bf16[1024,256]{1,0:T(8,128)(2,1)S(1)}, bf16[1024,256]{1,0:T(8,128)(2,1)}, u32[]{:S(2)}) copy-start(bf16[1024,256]{1,0:T(8,128)(2,1)} %copy-done.6) | copy-start | bytes 1572868
  47.9 1.9 %copy-start.10 = (s32[1024,3]{1,0:T(8,128)S(1)}, s32[1024,3]{1,0:T(8,128)}, u32[]{:S(2)}) copy-start(s32[1024,3]{1,0:T(8,128)} %reshape_squeeze.3.table_ref) | copy-start | bytes 36868
  49.8 1.0 copy-start.13
  50.9 1.0 copy-start.16
  58.7 17.0 %copy-start.9 = (s32[1024,3]{1,0:T(8,128)S(1)}, s32[1024,3]{1,0:T(8,128)}, u32[]{:S(2)}) copy-start(s32[1024,3]{1,0:T(8,128)} %copy-done.8) | copy-start | bytes 36868
  60.9 48.1 %copy-start.3 = (f32[1024,240]{1,0:T(8,128)}, f32[1024,240]{1,0:T(8,128)S(1)}, u32[]{:S(2)}) copy-start(f32[1024,240]{1,0:T(8,128)S(1)} %get-tuple-element.11.vec_ref) | copy-start | bytes 2949124
  60.9 12.8 %collective-permute-start.12 = (bf16[1024,256]{1,0:T(8,128)(2,1)S(1)}, bf16[1024,256]{1,0:T(8,128)(2,1)S(1)}, u32[]{:S(2)}, u32[]{:S(2)}) collective-permute-start(bf16[1024,256]{1,0:T(8,128)(2,1)S(1)} %get-tuple-element.12.coded_ref.rest_0_), channel_id=1, source_target_pairs={{0,2},{1,3},{2,0},{3,1},{4,6},{5,7},{6,4},{7,5},{8,10},{9,11},{10,... | collective-permute-start | bytes 1572872 | tf_op jit(solution)/shard_map/ppermute | solution.py:384
  62.0 11.8 %collective-permute-start.11 = (bf16[1024,256]{1,0:T(8,128)(2,1)S(1)}, bf16[1024,256]{1,0:T(8,128)(2,1)S(1)}, u32[]{:S(2)}, u32[]{:S(2)}) collective-permute-start(bf16[1024,256]{1,0:T(8,128)(2,1)S(1)} %get-tuple-element.12.coded_ref.rest_0_), channel_id=1, source_target_pairs={{0,1},{1,0},{2,3},{3,2},{4,5},{5,4},{6,7},{7,6},{8,9},{9,8},{10,11... | collective-permute-start | bytes 1572872 | tf_op jit(solution)/shard_map/ppermute | solution.py:384
  73.8 1.9 %collective-permute-start.13 = (bf16[1024,256]{1,0:T(8,128)(2,1)S(1)}, bf16[1024,256]{1,0:T(8,128)(2,1)S(1)}, u32[]{:S(2)}, u32[]{:S(2)}) collective-permute-start(bf16[1024,256]{1,0:T(8,128)(2,1)S(1)} %collective-permute-done.12.rest_2_), channel_id=1, source_target_pairs={{0,1},{1,0},{2,3},{3,2},{4,5},{5,4},{6,7},{7,6},{8,9},{9,8},{10,11... | collective-permute-start | bytes 1572872 | tf_op jit(solution)/shard_map/ppermute | solution.py:384
  82.1 12.2 %copy-start.19 = (bf16[512,240]{0,1:T(8,128)(2,1)S(1)}, bf16[512,240]{0,1:T(8,128)(2,1)}, u32[]{:S(2)}) copy-start(bf16[512,240]{0,1:T(8,128)(2,1)} %param.17) | copy-start | bytes 737284
  82.2 26.9 %collective-permute-start.14 = (bf16[1024,256]{1,0:T(8,128)(2,1)S(1)}, bf16[1024,256]{1,0:T(8,128)(2,1)S(1)}, u32[]{:S(2)}, u32[]{:S(2)}) collective-permute-start(bf16[1024,256]{1,0:T(8,128)(2,1)S(1)} %serve.3), channel_id=1, source_target_pairs={{0,4},{1,5},{2,6},{3,7},{4,0},{5,1},{6,2},{7,3},{8,12},{9,13},{10,... | collective-permute-start | bytes 1572872 | tf_op jit(solution)/shard_map/ppermute | solution.py:384
  87.4 3.8 %collective-permute-start.10 = (f32[1,512]{1,0:T(1,128)S(1)}, f32[1,512]{1,0:T(1,128)S(1)}, u32[]{:S(2)}, u32[]{:S(2)}) collective-permute-start(f32[1,512]{1,0:T(1,128)S(1)} %gather_wave.3), channel_id=1, source_target_pairs={{8,0},{16,8},{24,16},{0,24},{9,1},{17,9},{25,17},{1,25},{10,2},{18... | collective-permute-start | bytes 6152 | tf_op jit(solution)/shard_map/ppermute | solution.py:393
  89.9 4.5 %collective-permute-start.8 = (f32[1,512]{1,0:T(1,128)S(1)}, f32[1,512]{1,0:T(1,128)S(1)}, u32[]{:S(2)}, u32[]{:S(2)}) collective-permute-start(f32[1,512]{1,0:T(1,128)S(1)} %gather_wave.3), channel_id=1, source_target_pairs={{24,0},{0,8},{8,16},{16,24},{25,1},{1,9},{9,17},{17,25},{26,2},{2,... | collective-permute-start | bytes 6152 | tf_op jit(solution)/shard_map/ppermute | solution.py:393
  89.9 4.5 %collective-permute-start.9 = (f32[1,512]{1,0:T(1,128)S(1)}, f32[1,512]{1,0:T(1,128)S(1)}, u32[]{:S(2)}, u32[]{:S(2)}) collective-permute-start(f32[1,512]{1,0:T(1,128)S(1)} %gather_wave.3), channel_id=1, source_target_pairs={{16,0},{24,8},{0,16},{8,24},{17,1},{25,9},{1,17},{9,25},{18,2},{26... | collective-permute-start | bytes 6152 | tf_op jit(solution)/shard_map/ppermute | solution.py:393
  110.4 12.9 %all-to-all-start = ((f32[32,1,128]{2,1,0:T(1,128)}), f32[32,1,128]{2,1,0:T(1,128)S(1)}, u32[]{:S(2)}, u32[]{:S(2)}) async-start(f32[32,1,128]{2,1,0:T(1,128)} %bitcast.12), calls=%async_computation | async-start | bytes 32768 | tf_op jit(solution)/shard_map/all_to_all | solution.py:449
  116.2 7.1 %copy-start.5 = (f32[1,1024,240]{1,2,0:T(8,128)S(1)}, f32[1,1024,240]{1,2,0:T(8,128)}, u32[]{:S(2)}) copy-start(f32[1,1024,240]{1,2,0:T(8,128)} %param.10) | copy-start | bytes 2949124

commit v4 on v3

--- a/solution.py
+++ b/solution.py
@@ -13,7 +13,8 @@
 QUAD = 4
 CHUNK = 256
 BATCH = 32
-VMEM_LIMIT = 40 * 2**20
+VMEM_LIMIT = 16 * 2**20
+COST = pl.CostEstimate(flops=1, bytes_accessed=1, transcendentals=0)
 
 
 def cosine_coefficients():
@@ -91,9 +92,7 @@
         in_specs=[whole()] * 3,
         out_specs=whole(),
         compiler_params=params(),
-        cost_estimate=pl.CostEstimate(
-            flops=2 * rows * samples * 256, bytes_accessed=2 * 2**20, transcendentals=0
-        ),
+        cost_estimate=COST,
         name="gather_wave",
     )(coded, wave_out, angle)
 
@@ -124,9 +123,7 @@
         in_specs=[whole()] * 3,
         out_specs=whole(),
         compiler_params=params(),
-        cost_estimate=pl.CostEstimate(
-            flops=2 * rows * samples * 256, bytes_accessed=3 * 2**20, transcendentals=0
-        ),
+        cost_estimate=COST,
         name="spread_wave",
     )(incoming, wave_in_t, angle)
 
@@ -195,20 +192,22 @@
     )
 
 
-def serve_kernel(slot_ref, table_ref, tables_ref, *rest):
+def serve_kernel(active_ref, slot_ref, table_ref, tables_ref, *rest):
     *shards, out_ref, source, picked = rest
-    load_rows(source, shards)
-    pick_rows(slot_ref, source, picked)
 
     def part(start, carry):
         total = translate(start, picked, table_ref, tables_ref)
         out_ref[pl.ds(start, CHUNK), :] = pad_lanes(total, out_ref.shape[1]).astype(jnp.bfloat16)
         return carry
 
-    row_chunks(out_ref.shape[0], part)
-
-
-def near_kernel(slot_ref, table_ref, tables_ref, vec_ref, mie_ref, far_ref, *rest):
+    @pl.when(active_ref[0] != 0)
+    def _():
+        load_rows(source, shards)
+        pick_rows(slot_ref, source, picked)
+        row_chunks(out_ref.shape[0], part)
+
+
+def near_kernel(slot_ref, table_ref, tables_ref, mie_ref, far_ref, *rest):
     *shards, out_ref, source, picked = rest
     load_rows(source, shards)
     pick_rows(slot_ref, source, picked)
@@ -216,7 +215,7 @@
     def part(start, carry):
         at = pl.ds(start, CHUNK)
         total = translate(start, picked, table_ref, tables_ref) + far_ref[at, :]
-        out_ref[at, :] = vec_ref[at, :] - mie_ref[at, :] * total
+        out_ref[at, :] = mie_ref[at, :] * total
         return carry
 
     row_chunks(out_ref.shape[0], part)
@@ -230,43 +229,39 @@
     ]
 
 
-def product_cost(rows, tables):
-    return pl.CostEstimate(
-        flops=2 * rows * tables * 256 * 256, bytes_accessed=8 * 2**20, transcendentals=0
-    )
-
-
-def serve(slots, table_ids, tables, shards):
+def serve(active, slots, table_ids, tables, shards):
     rows, width = shards[0].shape
     return pl.pallas_call(
         serve_kernel,
         out_shape=jax.ShapeDtypeStruct((rows, width), jnp.bfloat16),
-        in_specs=[whole(pltpu.SMEM)] + [whole()] * (2 + len(shards)),
+        in_specs=[whole(pltpu.SMEM)] * 2 + [whole()] * (2 + len(shards)),
         out_specs=whole(),
         scratch_shapes=rows_scratch(shards, slots.shape[0]),
         compiler_params=params(),
-        cost_estimate=product_cost(rows, tables.shape[0]),
+        cost_estimate=COST,
         name="serve",
-    )(slots, table_ids, tables, *shards)
-
-
-def near_field(slots, table_ids, tables, vec, mie, far, shards):
+    )(active.astype(jnp.int32).reshape(1), slots, table_ids, tables, *shards)
+
+
+def near_field(slots, table_ids, tables, mie, far, shards):
     return pl.pallas_call(
         near_kernel,
-        out_shape=jax.ShapeDtypeStruct(vec.shape, jnp.float32),
-        in_specs=[whole(pltpu.SMEM)] + [whole()] * (5 + len(shards)),
+        out_shape=jax.ShapeDtypeStruct(mie.shape, jnp.float32),
+        in_specs=[whole(pltpu.SMEM)] + [whole()] * (4 + len(shards)),
         out_specs=whole(),
         scratch_shapes=rows_scratch(shards, slots.shape[0]),
         compiler_params=params(),
-        cost_estimate=product_cost(vec.shape[0], tables.shape[0]),
+        cost_estimate=COST,
         name="near_field",
-    )(slots, table_ids, tables, vec, mie, far, *shards)
-
-
-def join_kernel(second, count, base_ref, mie_ref, vec_ref, *rest):
+    )(slots, table_ids, tables, mie, far, *shards)
+
+
+def join_kernel(second, count, base_ref, mie_ref, x_ref, *rest):
     served, rest = rest[:count], rest[count:]
     if second:
-        first_ref, sums_in_ref, *rest = rest
+        vec_ref, sums_in_ref, *rest = rest
+    else:
+        vec_ref = x_ref
     image_ref, *rest, sums_ref = rest
     rows, coefs = base_ref.shape
     width = served[0].shape[1]
@@ -279,18 +274,17 @@
         far_rows = served[0][at, :].astype(jnp.float32)
         for other in served[1:]:
             far_rows = far_rows + other[at, :].astype(jnp.float32)
-        image = base_ref[at, :] - mie_ref[at, :] * far_rows[:, :coefs]
-        vec = vec_ref[at, :]
-        if second:
-            image_ref[:, at] = pad_lanes(image, width).T[:coefs, :]
-            new = [dot(first_ref[at, :], image), dot(vec, image), dot(image, image)]
-        else:
-            image_ref[at, :] = image
-            rest[0][at, :] = pad_lanes(image, width).astype(jnp.bfloat16)
-            new = [dot(vec, vec), dot(vec, image), dot(image, image)]
+        image = base_ref[at, :] + mie_ref[at, :] * far_rows[:, :coefs]
+        wide = pad_lanes(image, width)
+        if not second:
+            rest[0][at, :] = wide.astype(jnp.bfloat16)
+        image = wide.T[:coefs, :]
+        image_ref[:, at] = image
+        x, vec = x_ref[:, at], vec_ref[:, at]
+        new = [dot(x, image), dot(vec, image) if second else dot(x, x), dot(image, image)]
         return tuple(a + b for a, b in zip(sums, new, strict=True))
 
-    sums = row_chunks(rows, part, tuple(jnp.zeros((1, coefs), jnp.float32) for _ in range(3)))
+    sums = row_chunks(rows, part, tuple(jnp.zeros((1, CHUNK), jnp.float32) for _ in range(3)))
     lane = lax.broadcasted_iota(jnp.int32, (1, LANES), 1)
     packed = sums_in_ref[...] if second else jnp.zeros((1, LANES), jnp.float32)
     for k, value in enumerate(sums):
@@ -299,67 +293,62 @@
     sums_ref[...] = jnp.broadcast_to(packed, sums_ref.shape)
 
 
-def join(base, mie, vec, served, second=None, devices=1):
+def join(base, mie, x_t, served, second=(), devices=1):
     rows, coefs = base.shape
     width = served[0].shape[1]
-    if second is None:
-        second = ()
-        outs = (
-            jax.ShapeDtypeStruct((rows, coefs), jnp.float32),
-            jax.ShapeDtypeStruct((rows, width), jnp.bfloat16),
-            jax.ShapeDtypeStruct((1, LANES), jnp.float32),
-        )
-    else:
-        outs = (
-            jax.ShapeDtypeStruct((coefs, rows), jnp.float32),
-            jax.ShapeDtypeStruct((devices, LANES), jnp.float32),
-        )
+    outs = [jax.ShapeDtypeStruct((coefs, rows), jnp.float32)]
+    if not second:
+        outs.append(jax.ShapeDtypeStruct((rows, width), jnp.bfloat16))
+    outs.append(jax.ShapeDtypeStruct((devices, LANES), jnp.float32))
     return pl.pallas_call(
         functools.partial(join_kernel, len(second) > 0, len(served)),
-        out_shape=outs,
+        out_shape=tuple(outs),
         in_specs=[whole()] * (3 + len(served) + len(second)),
         out_specs=(whole(),) * len(outs),
         compiler_params=params(),
         name="join_second" if second else "join_first",
-    )(base, mie, vec, *served, *second)
-
-
-def finish_kernel(sums_ref, x_ref, u_ref, v_ref, solution_ref, residual_ref, hess_ref):
+    )(base, mie, x_t, *served, *second)
+
+
+def finish_kernel(sums_ref, x_ref, b_ref, c_ref, solution_ref, residual_ref, hess_ref):
     sums = jnp.sum(sums_ref[...], axis=0, keepdims=True)
-    xx, xu, uu, xv, uv, vv = [sums[:, k : k + 1] for k in range(6)]
+    xb, xx, bb, xc, bc, cc = [sums[:, k : k + 1] for k in range(6)]
     norm = jnp.sqrt(xx + epsilon)
     inverse = 1.0 / norm
     squared = inverse * inverse
-    h11 = xu * squared
-    ones = xx * squared
-    size1 = uu * squared - 2.0 * h11 * h11 + h11 * h11 * ones
+    h11 = (xx - xb) * squared
+    g = (xb + epsilon) * squared
+    size1 = (g * g * xx - 2.0 * g * xb + bb) * squared
     h21 = jnp.sqrt(jnp.maximum(size1, 0.0) + epsilon)
     q = inverse / h21
-    h12 = q * inverse * (xv - h11 * xu)
-    h22 = q * q * (uv - h11 * uu - h11 * xv + h11 * h11 * xu)
-    size2 = q * q * (vv - 2.0 * h11 * uv + h11 * h11 * uu)
-    cross = q * inverse * (xu - h11 * xx)
-    twos = size1 / (h21 * h21)
-    left = (
-        size2
-        - 2.0 * h12 * h12
-        - 2.0 * h22 * h22
-        + h12 * h12 * ones
-        + h22 * h22 * twos
-        + 2.0 * h12 * h22 * cross
+    v11 = xx * squared
+    v12 = q * inverse * (g * xx - xb)
+    v22 = size1 / (h21 * h21)
+    p1 = q * inverse * (g * xb - xc)
+    p2 = q * q * (g * g * xb - g * xc - g * bb + bc)
+    pp = q * q * (g * g * bb - 2.0 * g * bc + cc)
+    h12 = v12 - p1
+    h22 = v22 - p2
+    rest = 1.0 - h22
+    size2 = (
+        rest * rest * v22
+        + h12 * h12 * v11
+        + pp
+        - 2.0 * rest * h12 * v12
+        - 2.0 * rest * p2
+        + 2.0 * h12 * p1
     )
-    h32 = jnp.sqrt(jnp.maximum(left, 0.0) + epsilon)
+    h32 = jnp.sqrt(jnp.maximum(size2, 0.0) + epsilon)
     gram00 = h11 * h11 + h21 * h21
     gram01 = h11 * h12 + h21 * h22
     gram11 = h12 * h12 + h22 * h22 + h32 * h32
     rhs0, rhs1 = norm * h11, norm * h12
     det = gram00 * gram11 - gram01 * gram01
-    y1 = (gram11 * rhs0 - gram01 * rhs1) / det
-    y2 = (gram00 * rhs1 - gram01 * rhs0) / det
-    x, u, v = x_ref[...], u_ref[...], v_ref[...]
-    a1, a2 = y1 * inverse, y2 * q
-    solution_ref[...] = (a1 - h11 * a2) * x + a2 * u
-    residual_ref[...] = x - (a1 - h11 * a2) * u - a2 * v
+    a1 = (gram11 * rhs0 - gram01 * rhs1) / det * inverse
+    a2 = (gram00 * rhs1 - gram01 * rhs0) / det * q
+    x, b, c = x_ref[...], b_ref[...], c_ref[...]
+    solution_ref[...] = (a1 + a2 * g) * x - a2 * b
+    residual_ref[...] = (1.0 - a1 - a2 * g) * x + (a1 + a2 * (1.0 + g)) * b - a2 * c
     hess_ref[0:1, 0:1] = h11
     hess_ref[0:1, 1:2] = h21
     hess_ref[0:1, 2:3] = jnp.zeros_like(h11)
@@ -368,7 +357,7 @@
     hess_ref[1:2, 2:3] = h32
 
 
-def finish(sums, x_t, u_t, v_t):
+def finish(sums, x_t, b_t, c_t):
     field = jax.ShapeDtypeStruct(x_t.shape, jnp.float32)
     return pl.pallas_call(
         finish_kernel,
@@ -377,23 +366,78 @@
         out_specs=(whole(),) * 3,
         compiler_params=params(),
         name="finish",
-    )(sums, x_t, u_t, v_t)
+    )(sums, x_t, b_t, c_t)
 
 
 def flip(block, bits):
     return lax.ppermute(block, "grp", [(i, i ^ bits) for i in range(lax.axis_size("grp"))])
 
 
-def far_field(coded, wave_out, wave_in_t, angle, trans_rows):
+def along_chips(block, moves):
+    return lax.ppermute(block, "grp", [(2 * a + c, 2 * b + c) for a, b in moves for c in range(2)])
+
+
+def other_core(block, chips):
+    return lax.ppermute(block, "grp", [(2 * z + c, 2 * z + 1 - c) for z in chips for c in range(2)])
+
+
+def once(*values):
+    return lax.optimization_barrier(values)
+
+
+class Quads:
+    def __init__(self, apart):
+        self.others = range(1, lax.axis_size("grp") // QUAD)
+        self.here = jnp.where(apart < QUAD, apart, -1)
+        self.asked = [jnp.where(apart // QUAD == j, apart % QUAD, -1) for j in self.others]
+        self.places = QUAD
+
+    def ask(self, words):
+        return [flip(word, QUAD * j) for j, word in zip(self.others, words, strict=True)]
+
+    def operator(self, coded, work):
+        across = flip(coded, 2)
+        same = flip(coded, 1)
+        waves = work.waves(coded, 1)
+        across, waves, work.asked, work.local = once(across, waves, work.asked, work.local)
+        shards = [coded, same, across, flip(across, 1)]
+        on = jnp.ones((), jnp.bool_)
+        served = [flip(work.serve(on, k, shards), QUAD * j) for k, j in enumerate(self.others)]
+        return work.near(work.far(waves), shards), served
+
+
+class Line:
+    def __init__(self, apart):
+        chip, core = apart // 2, apart % 2
+        here = lax.axis_index("grp") // 2
+        self.middle = (here == 1) | (here == 2)
+        inner = (chip == 3) & self.middle
+        self.here = jnp.where(chip < 2, apart, jnp.where(inner, QUAD + core, -1))
+        self.places = QUAD + 2
+
+    def operator(self, coded, work):
+        across = along_chips(coded, [(0, 1), (1, 0), (2, 3), (3, 2)])
+        inner = along_chips(coded, [(1, 2), (2, 1)])
+        shards = [coded, flip(coded, 1)]
+        sums = work.serve(~self.middle, 0, shards)
+        early = along_chips(sums, [(0, 2), (3, 1)])
+        waves = work.waves(once(coded, sums)[0], 2)
+        across, inner, waves = once(across, inner, waves)
+        shards = shards + [across, flip(across, 1)]
+        sums = work.serve(self.middle, 0, shards)
+        late = along_chips(sums, [(1, 3), (2, 0)])
+        inner = once(inner, sums)[0]
+        far, early = once(work.far(waves), early)
+        return work.near(far, shards + [inner, other_core(inner, (1, 2))]), [early, late]
+
+
+def wave_swaps(waves, count):
     blocks = lax.axis_size("blk")
-    own = gather_wave(coded, wave_out, angle)
-    here = lax.axis_index("blk")
-    incoming = jnp.zeros_like(own)
-    for turn in range(1, blocks):
-        moved = lax.ppermute(own, "blk", [((i - turn) % blocks, i) for i in range(blocks)])
-        weights = lax.dynamic_slice_in_dim(trans_rows, (here - turn) % blocks, 1, 0)
-        incoming = incoming + weights * moved
-    return spread_wave(incoming, wave_in_t, angle)
+    while waves.shape[0] < min(count, blocks):
+        bits = waves.shape[0]
+        moved = lax.ppermute(waves, "blk", [(i, i ^ bits) for i in range(blocks)])
+        waves = jnp.concatenate([waves, moved], axis=0)
+    return waves
 
 
 def body(
@@ -420,34 +464,53 @@
     x_t = x.T
 
     apart = owner_dev[0, :, 0] ^ lax.axis_index("grp")
-    slots = 2 * ((apart % QUAD) * rows + near_row[0])
-    nothing = 2 * QUAD * rows
+    first = Quads(apart)
+    second = Line(apart) if group == 2 * QUAD else first
     names = table_id[0]
-    quads = range(1, group // QUAD)
-    asked = [
-        flip(jnp.where(apart // QUAD == j, slots, nothing) * tables_count + names, QUAD * j)
-        for j in quads
-    ]
-    asked = [(word // tables_count, (word % tables_count).reshape(rows, -1)) for word in asked]
-    slots = jnp.where(apart < QUAD, slots, nothing)
-    names = names.reshape(rows, -1)
-
-    def operator(coded, vec):
-        across = flip(coded, 2)
-        shards = [coded, flip(coded, 1), across, flip(across, 1)]
-        far = far_field(coded, wave_out, wave_in_t, angle, far_trans[0, 0])
-        served = [
-            flip(serve(slot, name, tables, shards), QUAD * j)
-            for j, (slot, name) in zip(quads, asked, strict=True)
-        ]
-        return near_field(slots, names, tables, vec, mie, far, shards), served
-
-    base, served = operator(code(x_t, width), x)
-    image, coded, sums = join(base, mie, x, served)
-    base, served = operator(coded, image)
-    second_t, sums = join(base, mie, image, served, (x, sums), devices)
+
+    def slots_of(place, places):
+        return 2 * jnp.where(place < 0, places * rows, place * rows + near_row[0])
+
+    words = first.ask([slots_of(place, QUAD) * tables_count + names for place in first.asked])
+    blocks = lax.axis_size("blk")
+    turns = jnp.arange(blocks, dtype=jnp.int32)
+    weights = far_trans[0, 0][turns ^ lax.axis_index("blk")]
+    weights = jnp.where(turns[:, None] > 0, weights, 0.0)
+
+    class Work:
+        asked = [(word // tables_count, (word % tables_count).reshape(rows, -1)) for word in words]
+        local = (names.reshape(rows, -1), mie)
+
+        def __init__(self, form):
+            self.slots = slots_of(form.here, form.places)
+
+        def serve(self, active, which, shards):
+            slot, name = self.asked[which]
+            slot = jnp.minimum(slot, 2 * len(shards) * rows)
+            return serve(active, slot, name, tables, shards)
+
+        def waves(self, coded, count):
+            return wave_swaps(gather_wave(coded, wave_out, angle), count)
+
+        def far(self, waves):
+            waves = wave_swaps(waves, blocks)
+            incoming = jnp.sum(weights * waves, axis=0, keepdims=True)
+            return spread_wave(incoming, wave_in_t, angle)
+
+        def near(self, far, shards):
+            names, mie = self.local
+            return near_field(self.slots, names, tables, mie, far, shards)
+
+    work = Work(first)
+    base, served = first.operator(code(x_t, width), work)
+    names, mie = work.local
+    b_t, coded, sums = join(base, mie, x_t, served)
+    again = Work(second)
+    again.asked, again.local = work.asked, work.local
+    base, served = second.operator(coded, again)
+    c_t, sums = join(base, mie, x_t, served, (b_t, sums), devices)
     sums = lax.all_to_all(sums, ("blk", "grp"), 0, 0, tiled=True)
-    solution_t, residual_t, hess_t = finish(sums, x_t, image.T, second_t)
+    solution_t, residual_t, hess_t = finish(sums, x_t, b_t, c_t)
     return solution_t.T[None], residual_t.T[None], hess_t.T
 
 

time: 126 us -> 120 us (0.952)
  waiting for transfers between devices: 43.2 us -> 25 us
  blocking collectives: 0 us -> 11.6 us
  Pallas kernels: 39.9 us -> 47 us
  starting transfers between devices: 27 us -> 22.3 us
  local copies, waits for them, and re-layouts: 13.5 us -> 12 us
    ppermute x9 -> x7, waiting for transfers between devices: 34.4 us -> 10.1 us  [flip(): lax.ppermute(block, 'grp', [(i, i ^ bits) for i in range(lax.axis_size('g...]
    all_to_all x0 -> x1, blocking collectives: none -> 11.6 us  [body(): sums = lax.all_to_all(sums, ('blk', 'grp'), 0, 0, tiled=True)]
    ppermute x6 -> x9, waiting for transfers between devices: 3.4 us -> 14.9 us  [the longest x4 7.78 us: wave_swaps(): moved = lax.ppermute(waves, 'blk', [(i, i ^ bits) for i in range(blocks)])]
    all_to_all x1 -> x0, starting transfers between devices: 5.79 us -> none  [body(): sums = lax.all_to_all(sums, ('blk', 'grp'), 0, 0, tiled=True)]
    all_to_all x1 -> x0, waiting for transfers between devices: 5.41 us -> none  [body(): sums = lax.all_to_all(sums, ('blk', 'grp'), 0, 0, tiled=True)]
    ppermute x6 -> x9, starting transfers between devices: 8.09 us -> 13.1 us  [the longest x4 6.23 us: wave_swaps(): moved = lax.ppermute(waves, 'blk', [(i, i ^ bits) for i in range(blocks)])]
    ppermute x9 -> x7, starting transfers between devices: 13.1 us -> 9.13 us  [flip(): lax.ppermute(block, 'grp', [(i, i ^ bits) for i in range(lax.axis_size('g...]
    pallas_call x2, Pallas kernels: 3.51 us -> 5.78 us  [gather_wave(): pl.pallas_call(wave_kernel, out_shape=jax.ShapeDtypeStruct((1, samples),...]
  transfers between devices with their start and end apart: 16 -> 16, of which waited for: 9 -> 10; matrix products, arithmetic and copies ran while one was open for 5% -> 5% of each run, Pallas kernels for 16% -> 27%
where the time goes in v4:
time: 120 us
  Pallas kernels  47 us (39%)
  waiting for transfers between devices  25 us (21%)
  starting transfers between devices  22.3 us (19%)
  local copies, waits for them, and re-layouts  12 us (10%)
  blocking collectives  11.6 us (10%)
    pallas_call x3, Pallas kernels, serve(): pl.pallas_call(serve_kernel, out_shape=jax.ShapeDtypeStruct((rows, width)...  16.3 us
    pallas_call x2, Pallas kernels, near_field(): pl.pallas_call(near_kernel, out_shape=jax.ShapeDtypeStruct(mie.shape, jnp...  15 us
    all_to_all x1, blocking collectives, body(): sums = lax.all_to_all(sums, ('blk', 'grp'), 0, 0, tiled=True)  11.6 us
    ppermute x7, waiting for transfers between devices, flip(): lax.ppermute(block, 'grp', [(i, i ^ bits) for i in range(lax.axis_size('g...  10.1 us
    unnamed x42, local copies, waits for them, and re-layouts  9.17 us
    ppermute x7, starting transfers between devices, flip(): lax.ppermute(block, 'grp', [(i, i ^ bits) for i in range(lax.axis_size('g...  9.13 us
    ppermute x4, waiting for transfers between devices, wave_swaps(): moved = lax.ppermute(waves, 'blk', [(i, i ^ bits) for i in range(blocks)])  7.78 us
    ppermute x4, waiting for transfers between devices, along_chips(): lax.ppermute(block, 'grp', [(2 * a + c, 2 * b + c) for a, b in moves for...  7.12 us
  transfers between devices with their start and end apart: 16, of which 10 were waited for; matrix products, arithmetic and copies ran while one was open for 5% of the time, Pallas kernels for 27%

profile of v4, /device:TPU:0, one launch (start us, length us, event | category | flops | bytes accessed | tf_op | source)
XLA Modules:
  0.0 119.7 jit_solution(10250726373224986092)
XLA Ops:
  0.7 1.3 %copy-done.3 = f32[1,1024,240]{1,2,0:T(8,128)S(1)} copy-done((f32[1,1024,240]{1,2,0:T(8,128)S(1)}, f32[1,1024,240]{1,2,0:T(8,128)}, u32[]{:S(2)}) %copy-start.3) | copy-done | bytes 983064
  2.0 1.0 code_rows.1.coded_ref.rest_0_
  3.0 3.0 %collective-permute-start = (bf16[1024,256]{1,0:T(8,128)(2,1)}, bf16[1024,256]{1,0:T(8,128)(2,1)}, u32[]{:S(2)}, u32[]{:S(2)}) collective-permute-start(bf16[1024,256]{1,0:T(8,128)(2,1)} %code_rows.1.coded_ref.rest_0_), channel_id=1, source_target_pairs={{0,2},{1,3},{2,0},{3,1},{4,6},{5,7},{6,4},{7,5},{8,10},{9,11},{10,... | collective-permute-start | bytes 1572872 | tf_op jit(solution)/shard_map/ppermute | solution.py:373
  6.0 0.7 copy-done.17
  6.8 2.7 %collective-permute-start.1 = (s32[3072]{0:T(1024)S(1)}, s32[3072]{0:T(1024)S(1)}, u32[]{:S(2)}, u32[]{:S(2)}) collective-permute-start(s32[3072]{0:T(1024)S(1)} %get-tuple-element.46), channel_id=1, source_target_pairs={{0,4},{1,5},{2,6},{3,7},{4,0},{5,1},{6,2},{7,3},{8,12},{9,13},{10,... | collective-permute-start | bytes 36872 | tf_op jit(solution)/shard_map/ppermute | solution.py:373
  9.4 2.8 %gather_wave.2 = f32[1,512]{1,0:T(1,128)S(1)} custom-call(bf16[1024,256]{1,0:T(8,128)(2,1)} %code_rows.1.coded_ref.rest_0_, bf16[240,512]{1,0:T(8,128)(2,1)S(1)} %copy-done.13, bf16[1024,512]{1,0:T(8,128)(2,1)S(1)} %bitcast.32), custom_call_target="tpu_custom_call" | custom-call | flops 1 | bytes 1 | tf_op jit(solution)/shard_map/gather_wave/pallas_call | solution.py:89
  12.2 0.5 broadcast.113
  12.7 0.7 reduce.3
  13.4 1.1 reshape_squeeze.3.table_ref
  14.6 1.6 %copy.15 = f32[1,1024,240]{2,1,0:T(8,128)S(1)} copy(f32[1,1024,240]{1,2,0:T(8,128)} %param.11) | data formatting | bytes 1966080 | tf_op args[1]
  16.2 1.4 %collective-permute-done.1 = s32[3072]{0:T(1024)S(1)} collective-permute-done((s32[3072]{0:T(1024)S(1)}, s32[3072]{0:T(1024)S(1)}, u32[]{:S(2)}, u32[]{:S(2)}) %collective-permute-start.1) | collective-permute-done | bytes 12320 | tf_op jit(solution)/shard_map/ppermute | solution.py:373
  17.7 1.1 reshape.44.table_ref
  18.8 2.2 %collective-permute-done.5.rest_3_ = bf16[1024,256]{1,0:T(8,128)(2,1)} collective-permute-done((bf16[1024,256]{1,0:T(8,128)(2,1)}, bf16[1024,256]{1,0:T(8,128)(2,1)}, u32[]{:S(2)}, u32[]{:S(2)}) %collective-permute-start.5) | collective-permute-done | bytes 524320 | tf_op jit(solution)/shard_map/ppermute | solution.py:373
  21.1 1.0 copy-done.6
  22.1 8.0 %serve.3 = bf16[1024,256]{1,0:T(8,128)(2,1)} custom-call(s32[1]{0:T(128)} %constant.105.clone.1.active_ref, s32[3072]{0:T(1024)S(1)} %get-tuple-element.49.slot_ref, s32[1024,3]{1,0:T(8,128)S(1)} %copy-done.6, bf16[8,240,240]{2,1,0:T(8,128)(2,1)S(1)} %copy-done.1, bf16[1024,256]{1,0:T(8,128)(2,1)} %code_rows.1.coded_ref.rest_0_, ...), custom_call_target="tpu_custom_call" | custom-call | flops 1 | bytes 1 | tf_op jit(solution)/shard_map/serve/pallas_call | solution.py:234
  30.1 3.4 %collective-permute-start.6 = (bf16[1024,256]{1,0:T(8,128)(2,1)}, bf16[1024,256]{1,0:T(8,128)(2,1)}, u32[]{:S(2)}, u32[]{:S(2)}) collective-permute-start(bf16[1024,256]{1,0:T(8,128)(2,1)} %serve.3), channel_id=1, source_target_pairs={{0,4},{1,5},{2,6},{3,7},{4,0},{5,1},{6,2},{7,3},{8,12},{9,13},{10,... | collective-permute-start | bytes 1572872 | tf_op jit(solution)/shard_map/ppermute | solution.py:373
  33.5 1.5 %collective-permute-start.2 = (f32[1,512]{1,0:T(1,128)S(1)}, f32[1,512]{1,0:T(1,128)S(1)}, u32[]{:S(2)}, u32[]{:S(2)}) collective-permute-start(f32[1,512]{1,0:T(1,128)S(1)} %gather_wave.2), channel_id=1, source_target_pairs={{0,8},{8,0},{16,24},{24,16},{1,9},{9,1},{17,25},{25,17},{2,10},{10... | collective-permute-start | bytes 6152 | tf_op jit(solution)/shard_map/ppermute | solution.py:438
  35.0 2.1 %collective-permute-done.2 = f32[1,512]{1,0:T(1,128)S(1)} collective-permute-done((f32[1,512]{1,0:T(1,128)S(1)}, f32[1,512]{1,0:T(1,128)S(1)}, u32[]{:S(2)}, u32[]{:S(2)}) %collective-permute-start.2) | collective-permute-done | bytes 2080 | tf_op jit(solution)/shard_map/ppermute | solution.py:438
  37.1 1.6 %collective-permute-start.3 = (f32[2,512]{1,0:T(2,128)S(1)}, f32[2,512]{1,0:T(2,128)S(1)}, u32[]{:S(2)}, u32[]{:S(2)}) collective-permute-start(f32[2,512]{1,0:T(2,128)S(1)} %pad_maximum_fusion), channel_id=1, source_target_pairs={{0,16},{8,24},{16,0},{24,8},{1,17},{9,25},{17,1},{25,9},{2,18},{10... | collective-permute-start | bytes 12296 | tf_op jit(solution)/shard_map/ppermute | solution.py:438
  38.7 0.6 gather_fusion
  39.2 1.5 %collective-permute-done.3 = f32[2,512]{1,0:T(2,128)S(1)} collective-permute-done((f32[2,512]{1,0:T(2,128)S(1)}, f32[2,512]{1,0:T(2,128)S(1)}, u32[]{:S(2)}, u32[]{:S(2)}) %collective-permute-start.3) | collective-permute-done | bytes 4128 | tf_op jit(solution)/shard_map/ppermute | solution.py:438
  40.8 0.9 copy-done.14
  41.8 1.9 %spread_wave.2.far_ref = f32[1024,240]{1,0:T(8,128)S(1)} custom-call(f32[1,512]{1,0:T(1,128)S(1)} %bitcast.45, bf16[240,512]{1,0:T(8,128)(2,1)S(1)} %bitcast.40, bf16[1024,512]{1,0:T(8,128)(2,1)S(1)} %bitcast.33), custom_call_target="tpu_custom_call" | custom-call | flops 1 | bytes 1 | tf_op jit(solution)/shard_map/spread_wave/pallas_call | solution.py:120
  43.7 7.3 %near_field.2.base_ref = f32[1024,240]{1,0:T(8,128)S(1)} custom-call(s32[3072]{0:T(1024)S(1)} %get-tuple-element.45.slot_ref, s32[1024,3]{1,0:T(8,128)S(1)} %copy-done.9, bf16[8,240,240]{2,1,0:T(8,128)(2,1)S(1)} %copy-done.1, f32[1024,240]{1,0:T(8,128)S(1)} %bitcast.28, f32[1024,240]{1,0:T(8,128)S(1)} %spread_wave.2.far_ref, ...), custom_call_target="tpu_custom_call" | custom-call | flops 1 | bytes 1 | tf_op jit(solution)/shard_map/near_field/pallas_call | solution.py:247
  51.0 6.2 %collective-permute-done.6.rest_0_ = bf16[1024,256]{1,0:T(8,128)(2,1)} collective-permute-done((bf16[1024,256]{1,0:T(8,128)(2,1)}, bf16[1024,256]{1,0:T(8,128)(2,1)}, u32[]{:S(2)}, u32[]{:S(2)}) %collective-permute-start.6) | collective-permute-done | bytes 524320 | tf_op jit(solution)/shard_map/ppermute | solution.py:373
  57.2 2.4 %join_first.1 = (f32[240,1024]{1,0:T(8,128)S(1)}, bf16[1024,256]{1,0:T(8,128)(2,1)}, f32[1,128]{1,0:T(1,128)S(1)}) custom-call(f32[1024,240]{1,0:T(8,128)S(1)} %near_field.2.base_ref, f32[1024,240]{1,0:T(8,128)S(1)} %bitcast.29, f32[240,1024]{1,0:T(8,128)S(1)} %bitcast.37, bf16[1024,256]{1,0:T(8,128)(2,1)} %collective-permute-done.6.rest_0_), custom_call_target="tpu_custom_call" | custom-call | tf_op jit(solution)/shard_map/join_first/pallas_call | solution.py:303
  59.6 0.9 copy-done.11
  60.6 1.5 %collective-permute-start.8 = (bf16[1024,256]{1,0:T(8,128)(2,1)}, bf16[1024,256]{1,0:T(8,128)(2,1)}, u32[]{:S(2)}, u32[]{:S(2)}) collective-permute-start(bf16[1024,256]{1,0:T(8,128)(2,1)} %get-tuple-element.31.rest_0_.coded_ref), channel_id=1, source_target_pairs={{2,4},{3,5},{4,2},{5,3},{10,12},{11,13},{12,10},{13,11},{18,20},{1... | collective-permute-start | bytes 1572872 | tf_op jit(solution)/shard_map/ppermute | solution.py:377
  62.0 0.6 collective-permute-start.7
  62.8 1.0 copy-done.7
  63.8 6.7 %serve.4 = bf16[1024,256]{1,0:T(8,128)(2,1)S(1)} custom-call(s32[1]{0:T(128)} %bitcast.12.active_ref, s32[3072]{0:T(1024)S(1)} %get-tuple-element.48.slot_ref, s32[1024,3]{1,0:T(8,128)S(1)} %copy-done.7, bf16[8,240,240]{2,1,0:T(8,128)(2,1)S(1)} %copy-done.1, bf16[1024,256]{1,0:T(8,128)(2,1)} %get-tuple-element.31.rest_0_.coded_ref, ...), custom_call_target="tpu_custom_call" | custom-call | flops 1 | bytes 1 | tf_op jit(solution)/shard_map/serve/pallas_call | solution.py:234
  70.6 3.0 %gather_wave.3 = f32[1,512]{1,0:T(1,128)S(1)} custom-call(bf16[1024,256]{1,0:T(8,128)(2,1)} %get-tuple-element.31.rest_0_.coded_ref, bf16[240,512]{1,0:T(8,128)(2,1)S(1)} %copy-done.13, bf16[1024,512]{1,0:T(8,128)(2,1)S(1)} %bitcast.34), custom_call_target="tpu_custom_call" | custom-call | flops 1 | bytes 1 | tf_op jit(solution)/shard_map/gather_wave/pallas_call | solution.py:89
  73.6 1.6 %collective-permute-start.10 = (f32[1,512]{1,0:T(1,128)S(1)}, f32[1,512]{1,0:T(1,128)S(1)}, u32[]{:S(2)}, u32[]{:S(2)}) collective-permute-start(f32[1,512]{1,0:T(1,128)S(1)} %gather_wave.3), channel_id=1, source_target_pairs={{0,8},{8,0},{16,24},{24,16},{1,9},{9,1},{17,25},{25,17},{2,10},{10... | collective-permute-start | bytes 6152 | tf_op jit(solution)/shard_map/ppermute | solution.py:438
  75.1 2.1 %collective-permute-done.10 = f32[1,512]{1,0:T(1,128)S(1)} collective-permute-done((f32[1,512]{1,0:T(1,128)S(1)}, f32[1,512]{1,0:T(1,128)S(1)}, u32[]{:S(2)}, u32[]{:S(2)}) %collective-permute-start.10) | collective-permute-done | bytes 2080 | tf_op jit(solution)/shard_map/ppermute | solution.py:438
  77.3 2.8 %collective-permute-start.12 = (bf16[1024,256]{1,0:T(8,128)(2,1)}, bf16[1024,256]{1,0:T(8,128)(2,1)S(1)}, u32[]{:S(2)}, u32[]{:S(2)}) collective-permute-start(bf16[1024,256]{1,0:T(8,128)(2,1)} %copy-done.16), channel_id=1, source_target_pairs={{0,4},{1,5},{6,2},{7,3},{8,12},{9,13},{14,10},{15,11},{16,20},{17,... | collective-permute-start | bytes 1572872 | tf_op jit(solution)/shard_map/ppermute | solution.py:377
  80.2 1.0 copy-done.8
  81.2 1.6 %serve.5 = bf16[1024,256]{1,0:T(8,128)(2,1)S(1)} custom-call(s32[1]{0:T(128)} %bitcast.14.active_ref, s32[3072]{0:T(1024)S(1)} %get-tuple-element.49.slot_ref, s32[1024,3]{1,0:T(8,128)S(1)} %copy-done.8, bf16[8,240,240]{2,1,0:T(8,128)(2,1)S(1)} %copy-done.1, bf16[1024,256]{1,0:T(8,128)(2,1)} %get-tuple-element.31.rest_0_.coded_ref, ...), custom_call_target="tpu_custom_call" | custom-call | flops 1 | bytes 1 | tf_op jit(solution)/shard_map/serve/pallas_call | solution.py:234
  82.8 0.7 collective-permute-start.14
  83.5 1.3 %collective-permute-start.15 = (bf16[1024,256]{1,0:T(8,128)(2,1)S(1)}, bf16[1024,256]{1,0:T(8,128)(2,1)S(1)}, u32[]{:S(2)}, u32[]{:S(2)}) collective-permute-start(bf16[1024,256]{1,0:T(8,128)(2,1)S(1)} %serve.5), channel_id=1, source_target_pairs={{2,6},{3,7},{4,0},{5,1},{10,14},{11,15},{12,8},{13,9},{18,22},{19,... | collective-permute-start | bytes 1572872 | tf_op jit(solution)/shard_map/ppermute | solution.py:377
  84.8 1.6 %collective-permute-start.11 = (f32[2,512]{1,0:T(2,128)S(1)}, f32[2,512]{1,0:T(2,128)S(1)}, u32[]{:S(2)}, u32[]{:S(2)}) collective-permute-start(f32[2,512]{1,0:T(2,128)S(1)} %pad_maximum_fusion.1), channel_id=1, source_target_pairs={{0,16},{8,24},{16,0},{24,8},{1,17},{9,25},{17,1},{25,9},{2,18},{10... | collective-permute-start | bytes 12296 | tf_op jit(solution)/shard_map/ppermute | solution.py:438
  86.4 2.1 %collective-permute-done.11 = f32[2,512]{1,0:T(2,128)S(1)} collective-permute-done((f32[2,512]{1,0:T(2,128)S(1)}, f32[2,512]{1,0:T(2,128)S(1)}, u32[]{:S(2)}, u32[]{:S(2)}) %collective-permute-start.11) | collective-permute-done | bytes 4128 | tf_op jit(solution)/shard_map/ppermute | solution.py:438
  88.6 1.9 %spread_wave.3.far_ref = f32[1024,240]{1,0:T(8,128)S(1)} custom-call(f32[1,512]{1,0:T(1,128)S(1)} %bitcast.44, bf16[240,512]{1,0:T(8,128)(2,1)S(1)} %bitcast.41, bf16[1024,512]{1,0:T(8,128)(2,1)S(1)} %bitcast.35), custom_call_target="tpu_custom_call" | custom-call | flops 1 | bytes 1 | tf_op jit(solution)/shard_map/spread_wave/pallas_call | solution.py:120
  90.5 1.8 %collective-permute-done.12.rest_0_ = bf16[1024,256]{1,0:T(8,128)(2,1)S(1)} collective-permute-done((bf16[1024,256]{1,0:T(8,128)(2,1)}, bf16[1024,256]{1,0:T(8,128)(2,1)S(1)}, u32[]{:S(2)}, u32[]{:S(2)}) %collective-permute-start.12) | collective-permute-done | bytes 524320 | tf_op jit(solution)/shard_map/ppermute | solution.py:377
  92.4 7.7 %near_field.3.base_ref = f32[1024,240]{1,0:T(8,128)S(1)} custom-call(s32[3072]{0:T(1024)S(1)} %get-tuple-element.47.slot_ref, s32[1024,3]{1,0:T(8,128)S(1)} %copy-done.10, bf16[8,240,240]{2,1,0:T(8,128)(2,1)S(1)} %copy-done.1, f32[1024,240]{1,0:T(8,128)S(1)} %bitcast.30, f32[1024,240]{1,0:T(8,128)S(1)} %spread_wave.3.far_ref, ...), custom_call_target="tpu_custom_call" | custom-call | flops 1 | bytes 1 | tf_op jit(solution)/shard_map/near_field/pallas_call | solution.py:247
  100.1 5.3 %collective-permute-done.15.rest_1_ = bf16[1024,256]{1,0:T(8,128)(2,1)S(1)} collective-permute-done((bf16[1024,256]{1,0:T(8,128)(2,1)S(1)}, bf16[1024,256]{1,0:T(8,128)(2,1)S(1)}, u32[]{:S(2)}, u32[]{:S(2)}) %collective-permute-start.15) | collective-permute-done | bytes 524320 | tf_op jit(solution)/shard_map/ppermute | solution.py:377
  105.4 0.7 join_second.1
  106.1 11.6 %all_to_all.11 = f32[32,1,128]{2,1,0:T(1,128)S(1)} all-to-all(f32[32,1,128]{2,1,0:T(1,128)S(1)} %bitcast.43), channel_id=1, replica_groups=mesh['blk'=4,'grp'=8] {'blk','grp'}, dimensions={0} | all-to-all | bytes 32768 | tf_op jit(solution)/shard_map/all_to_all | solution.py:512
  117.6 2.1 %finish.1 = (f32[240,1024]{1,0:T(8,128)}, f32[240,1024]{1,0:T(8,128)}, f32[2,3]{1,0:T(2,128)}) custom-call(f32[32,128]{1,0:T(8,128)S(1)} %bitcast.42, f32[240,1024]{1,0:T(8,128)S(1)} %bitcast.39, f32[240,1024]{1,0:T(8,128)S(1)} %copy-done.12, f32[240,1024]{1,0:T(8,128)S(1)} %get-tuple-element.41.c_ref), custom_call_target="tpu_custom_call" | custom-call | tf_op jit(solution)/shard_map/finish/pallas_call | solution.py:362
  (55 shorter events, 0.6 us)
Async XLA Ops:
  0.6 38.0 %copy-start = (f32[1,1,4,512]{3,2,1,0:T(4,128)S(1)}, f32[1,1,4,512]{3,2,1,0:T(4,128)}, u32[]{:S(2)}) copy-start(f32[1,1,4,512]{3,2,1,0:T(4,128)} %param.19) | copy-start | bytes 24580
  0.6 8.8 %copy-start.2 = (bf16[1,1024,512]{2,1,0:T(8,128)(2,1)S(1)}, bf16[1,1024,512]{2,1,0:T(8,128)(2,1)}, u32[]{:S(2)}) copy-start(bf16[1,1024,512]{2,1,0:T(8,128)(2,1)} %param.18) | copy-start | bytes 3145732
  0.7 1.3 %copy-start.3 = (f32[1,1024,240]{1,2,0:T(8,128)S(1)}, f32[1,1024,240]{1,2,0:T(8,128)}, u32[]{:S(2)}) copy-start(f32[1,1024,240]{1,2,0:T(8,128)} %param.10) | copy-start | bytes 2949124
  1.9 4.0 %copy-start.19 = (s32[1,3072,1]{1,2,0:T(1,128)S(1)}, s32[1,3072,1]{1,2,0:T(1,128)}, u32[]{:S(2)}) copy-start(s32[1,3072,1]{1,2,0:T(1,128)} %param.12) | copy-start | bytes 36868
  2.0 7.5 %copy-start.13 = (bf16[240,512]{1,0:T(8,128)(2,1)S(1)}, bf16[240,512]{1,0:T(8,128)(2,1)}, u32[]{:S(2)}) copy-start(bf16[240,512]{1,0:T(8,128)(2,1)} %out_ref.3) | copy-start | bytes 737284
  3.0 15.8 %collective-permute-start = (bf16[1024,256]{1,0:T(8,128)(2,1)}, bf16[1024,256]{1,0:T(8,128)(2,1)}, u32[]{:S(2)}, u32[]{:S(2)}) collective-permute-start(bf16[1024,256]{1,0:T(8,128)(2,1)} %code_rows.1.coded_ref.rest_0_), channel_id=1, source_target_pairs={{0,2},{1,3},{2,0},{3,1},{4,6},{5,7},{6,4},{7,5},{8,10},{9,11},{10,... | collective-permute-start | bytes 1572872 | tf_op jit(solution)/shard_map/ppermute | solution.py:373
  6.0 0.7 copy-start.17
  6.0 0.7 copy-start.18
  6.8 10.9 %collective-permute-start.1 = (s32[3072]{0:T(1024)S(1)}, s32[3072]{0:T(1024)S(1)}, u32[]{:S(2)}, u32[]{:S(2)}) collective-permute-start(s32[3072]{0:T(1024)S(1)} %get-tuple-element.46), channel_id=1, source_target_pairs={{0,4},{1,5},{2,6},{3,7},{4,0},{5,1},{6,2},{7,3},{8,12},{9,13},{10,... | collective-permute-start | bytes 36872 | tf_op jit(solution)/shard_map/ppermute | solution.py:373
  9.4 9.4 %collective-permute-start.4 = (bf16[1024,256]{1,0:T(8,128)(2,1)}, bf16[1024,256]{1,0:T(8,128)(2,1)}, u32[]{:S(2)}, u32[]{:S(2)}) collective-permute-start(bf16[1024,256]{1,0:T(8,128)(2,1)} %code_rows.1.coded_ref.rest_0_), channel_id=1, source_target_pairs={{0,1},{1,0},{2,3},{3,2},{4,5},{5,4},{6,7},{7,6},{8,9},{9,8},{10,11... | collective-permute-start | bytes 1572872 | tf_op jit(solution)/shard_map/ppermute | solution.py:373
  14.6 6.5 %copy-start.1 = (bf16[8,240,240]{2,1,0:T(8,128)(2,1)S(1)}, bf16[8,240,240]{2,1,0:T(8,128)(2,1)}, u32[]{:S(2)}) copy-start(bf16[8,240,240]{2,1,0:T(8,128)(2,1)} %tables_ref.9) | copy-start | bytes 2764804
  18.8 2.3 %collective-permute-start.5 = (bf16[1024,256]{1,0:T(8,128)(2,1)}, bf16[1024,256]{1,0:T(8,128)(2,1)}, u32[]{:S(2)}, u32[]{:S(2)}) collective-permute-start(bf16[1024,256]{1,0:T(8,128)(2,1)} %collective-permute-done.rest_2_), channel_id=1, source_target_pairs={{0,1},{1,0},{2,3},{3,2},{4,5},{5,4},{6,7},{7,6},{8,9},{9,8},{10,11... | collective-permute-start | bytes 1572872 | tf_op jit(solution)/shard_map/ppermute | solution.py:373
  21.1 1.0 copy-start.6
  30.1 27.2 %collective-permute-start.6 = (bf16[1024,256]{1,0:T(8,128)(2,1)}, bf16[1024,256]{1,0:T(8,128)(2,1)}, u32[]{:S(2)}, u32[]{:S(2)}) collective-permute-start(bf16[1024,256]{1,0:T(8,128)(2,1)} %serve.3), channel_id=1, source_target_pairs={{0,4},{1,5},{2,6},{3,7},{4,0},{5,1},{6,2},{7,3},{8,12},{9,13},{10,... | collective-permute-start | bytes 1572872 | tf_op jit(solution)/shard_map/ppermute | solution.py:373
  33.5 3.6 %collective-permute-start.2 = (f32[1,512]{1,0:T(1,128)S(1)}, f32[1,512]{1,0:T(1,128)S(1)}, u32[]{:S(2)}, u32[]{:S(2)}) collective-permute-start(f32[1,512]{1,0:T(1,128)S(1)} %gather_wave.2), channel_id=1, source_target_pairs={{0,8},{8,0},{16,24},{24,16},{1,9},{9,1},{17,25},{25,17},{2,10},{10... | collective-permute-start | bytes 6152 | tf_op jit(solution)/shard_map/ppermute | solution.py:438
  37.1 3.7 %collective-permute-start.3 = (f32[2,512]{1,0:T(2,128)S(1)}, f32[2,512]{1,0:T(2,128)S(1)}, u32[]{:S(2)}, u32[]{:S(2)}) collective-permute-start(f32[2,512]{1,0:T(2,128)S(1)} %pad_maximum_fusion), channel_id=1, source_target_pairs={{0,16},{8,24},{16,0},{24,8},{1,17},{9,25},{17,1},{25,9},{2,18},{10... | collective-permute-start | bytes 12296 | tf_op jit(solution)/shard_map/ppermute | solution.py:438
  40.8 0.9 copy-start.14
  41.8 1.9 %copy-start.9 = (s32[1024,3]{1,0:T(8,128)S(1)}, s32[1024,3]{1,0:T(8,128)}, u32[]{:S(2)}) copy-start(s32[1024,3]{1,0:T(8,128)} %reshape_squeeze.3.table_ref) | copy-start | bytes 36868
  43.7 13.5 %copy-start.4 = (f32[1,1024,240]{1,2,0:T(8,128)S(1)}, f32[1,1024,240]{1,2,0:T(8,128)}, u32[]{:S(2)}) copy-start(f32[1,1024,240]{1,2,0:T(8,128)} %param.10) | copy-start | bytes 2949124
  59.6 0.9 copy-start.11
  60.6 2.3 %collective-permute-start.9 = (bf16[1024,256]{1,0:T(8,128)(2,1)}, bf16[1024,256]{1,0:T(8,128)(2,1)}, u32[]{:S(2)}, u32[]{:S(2)}) collective-permute-start(bf16[1024,256]{1,0:T(8,128)(2,1)} %get-tuple-element.31.rest_0_.coded_ref), channel_id=1, source_target_pairs={{0,1},{1,0},{2,3},{3,2},{4,5},{5,4},{6,7},{7,6},{8,9},{9,8},{10,11... | collective-permute-start | bytes 1572872 | tf_op jit(solution)/shard_map/ppermute | solution.py:373
  60.6 16.7 %collective-permute-start.8 = (bf16[1024,256]{1,0:T(8,128)(2,1)}, bf16[1024,256]{1,0:T(8,128)(2,1)}, u32[]{:S(2)}, u32[]{:S(2)}) collective-permute-start(bf16[1024,256]{1,0:T(8,128)(2,1)} %get-tuple-element.31.rest_0_.coded_ref), channel_id=1, source_target_pairs={{2,4},{3,5},{4,2},{5,3},{10,12},{11,13},{12,10},{13,11},{18,20},{1... | collective-permute-start | bytes 1572872 | tf_op jit(solution)/shard_map/ppermute | solution.py:377
  62.0 15.2 %collective-permute-start.7 = (bf16[1024,256]{1,0:T(8,128)(2,1)}, bf16[1024,256]{1,0:T(8,128)(2,1)}, u32[]{:S(2)}, u32[]{:S(2)}) collective-permute-start(bf16[1024,256]{1,0:T(8,128)(2,1)} %get-tuple-element.31.rest_0_.coded_ref), channel_id=1, source_target_pairs={{0,2},{1,3},{2,0},{3,1},{4,6},{5,7},{6,4},{7,5},{8,10},{9,11},{10,... | collective-permute-start | bytes 1572872 | tf_op jit(solution)/shard_map/ppermute | solution.py:377
  62.8 1.0 copy-start.7
  70.6 3.0 %copy-start.16 = (bf16[1024,256]{1,0:T(8,128)(2,1)}, bf16[1024,256]{1,0:T(8,128)(2,1)S(1)}, u32[]{:S(2)}) copy-start(bf16[1024,256]{1,0:T(8,128)(2,1)S(1)} %serve.4) | copy-start | bytes 1572868
  73.6 3.7 %collective-permute-start.10 = (f32[1,512]{1,0:T(1,128)S(1)}, f32[1,512]{1,0:T(1,128)S(1)}, u32[]{:S(2)}, u32[]{:S(2)}) collective-permute-start(f32[1,512]{1,0:T(1,128)S(1)} %gather_wave.3), channel_id=1, source_target_pairs={{0,8},{8,0},{16,24},{24,16},{1,9},{9,1},{17,25},{25,17},{2,10},{10... | collective-permute-start | bytes 6152 | tf_op jit(solution)/shard_map/ppermute | solution.py:438
  77.3 2.9 %collective-permute-start.13 = (bf16[1024,256]{1,0:T(8,128)(2,1)}, bf16[1024,256]{1,0:T(8,128)(2,1)}, u32[]{:S(2)}, u32[]{:S(2)}) collective-permute-start(bf16[1024,256]{1,0:T(8,128)(2,1)} %collective-permute-done.7.rest_2_), channel_id=1, source_target_pairs={{0,1},{1,0},{2,3},{3,2},{4,5},{5,4},{6,7},{7,6},{8,9},{9,8},{10,11... | collective-permute-start | bytes 1572872 | tf_op jit(solution)/shard_map/ppermute | solution.py:373
  77.3 15.0 %collective-permute-start.12 = (bf16[1024,256]{1,0:T(8,128)(2,1)}, bf16[1024,256]{1,0:T(8,128)(2,1)S(1)}, u32[]{:S(2)}, u32[]{:S(2)}) collective-permute-start(bf16[1024,256]{1,0:T(8,128)(2,1)} %copy-done.16), channel_id=1, source_target_pairs={{0,4},{1,5},{6,2},{7,3},{8,12},{9,13},{14,10},{15,11},{16,20},{17,... | collective-permute-start | bytes 1572872 | tf_op jit(solution)/shard_map/ppermute | solution.py:377
  80.2 1.0 copy-start.8
  81.2 7.3 %copy-start.15 = (bf16[512,240]{0,1:T(8,128)(2,1)S(1)}, bf16[512,240]{0,1:T(8,128)(2,1)}, u32[]{:S(2)}) copy-start(bf16[512,240]{0,1:T(8,128)(2,1)} %param.17) | copy-start | bytes 737284
  82.8 9.5 %collective-permute-start.14 = (bf16[1024,256]{1,0:T(8,128)(2,1)}, bf16[1024,256]{1,0:T(8,128)(2,1)S(1)}, u32[]{:S(2)}, u32[]{:S(2)}) collective-permute-start(bf16[1024,256]{1,0:T(8,128)(2,1)} %collective-permute-done.8.rest_4_), channel_id=1, source_target_pairs={{2,3},{3,2},{4,5},{5,4},{10,11},{11,10},{12,13},{13,12},{18,19},{1... | collective-permute-start | bytes 1572872 | tf_op jit(solution)/shard_map/ppermute | solution.py:381
  83.5 21.8 %collective-permute-start.15 = (bf16[1024,256]{1,0:T(8,128)(2,1)S(1)}, bf16[1024,256]{1,0:T(8,128)(2,1)S(1)}, u32[]{:S(2)}, u32[]{:S(2)}) collective-permute-start(bf16[1024,256]{1,0:T(8,128)(2,1)S(1)} %serve.5), channel_id=1, source_target_pairs={{2,6},{3,7},{4,0},{5,1},{10,14},{11,15},{12,8},{13,9},{18,22},{19,... | collective-permute-start | bytes 1572872 | tf_op jit(solution)/shard_map/ppermute | solution.py:377
  84.8 3.7 %collective-permute-start.11 = (f32[2,512]{1,0:T(2,128)S(1)}, f32[2,512]{1,0:T(2,128)S(1)}, u32[]{:S(2)}, u32[]{:S(2)}) collective-permute-start(f32[2,512]{1,0:T(2,128)S(1)} %pad_maximum_fusion.1), channel_id=1, source_target_pairs={{0,16},{8,24},{16,0},{24,8},{1,17},{9,25},{17,1},{25,9},{2,18},{10... | collective-permute-start | bytes 12296 | tf_op jit(solution)/shard_map/ppermute | solution.py:438
  88.6 3.8 %copy-start.10 = (s32[1024,3]{1,0:T(8,128)S(1)}, s32[1024,3]{1,0:T(8,128)}, u32[]{:S(2)}) copy-start(s32[1024,3]{1,0:T(8,128)} %reshape_squeeze.3.table_ref) | copy-start | bytes 36868
  92.4 13.0 %copy-start.5 = (f32[1,1024,240]{1,2,0:T(8,128)S(1)}, f32[1,1024,240]{1,2,0:T(8,128)}, u32[]{:S(2)}) copy-start(f32[1,1024,240]{1,2,0:T(8,128)} %param.10) | copy-start | bytes 2949124
  92.4 13.0 %copy-start.12 = (f32[240,1024]{1,0:T(8,128)S(1)}, f32[240,1024]{1,0:T(8,128)}, u32[]{:S(2)}) copy-start(f32[240,1024]{1,0:T(8,128)} %copy-done.11) | copy-start | bytes 2949124

commit v5 on v4

v5 whole, which is shorter than its diff:
```python
import functools

import jax
import jax.numpy as jnp
import numpy as np
from jax import lax
from jax.experimental import pallas as pl
from jax.experimental.pallas import tpu as pltpu
from jax.sharding import PartitionSpec as P

epsilon = 1e-06
LANES = 128
QUAD = 4
CHUNK = 512
BATCH = 32
VMEM_LIMIT = 16 * 2**20
COST = pl.CostEstimate(flops=1, bytes_accessed=1, transcendentals=0)


def cosine_coefficients():
    top = 3.1416**2
    nodes = (np.cos((np.arange(400) + 0.5) * np.pi / 400) + 1.0) * top / 2.0
    fit = np.polynomial.chebyshev.Chebyshev.fit(nodes, np.cos(np.sqrt(nodes)), 8, domain=[0.0, top])
    return [float(c) for c in fit.convert(kind=np.polynomial.Polynomial).coef]


COS = cosine_coefficients()


def cosine(angle):
    square = angle * angle
    value = jnp.full_like(square, COS[-1])
    for coef in COS[-2::-1]:
        value = value * square + coef
    return value


def whole(memory=pltpu.VMEM):
    return pl.BlockSpec(memory_space=memory)


def params():
    return pltpu.CompilerParams(vmem_limit_bytes=VMEM_LIMIT)


def pad_lanes(value, width):
    rows, cols = value.shape
    return jnp.concatenate([value, jnp.zeros((rows, width - cols), value.dtype)], axis=1)


def code_kernel(field_ref, coded_ref):
    coefs, rows = field_ref.shape
    width = coded_ref.shape[1]
    for start in range(0, rows, CHUNK):
        part = field_ref[:, pl.ds(start, CHUNK)]
        part = jnp.concatenate([part, jnp.zeros((width - coefs, CHUNK), part.dtype)], axis=0)
        coded_ref[pl.ds(start, CHUNK), :] = part.T.astype(jnp.bfloat16)


def code(field_t, width):
    rows = field_t.shape[1]
    return pl.pallas_call(
        code_kernel,
        out_shape=jax.ShapeDtypeStruct((rows, width), jnp.bfloat16),
        in_specs=[whole()],
        out_specs=whole(),
        compiler_params=params(),
        name="code_rows",
    )(field_t)


def wave_kernel(coded_ref, out_ref, angle_ref, sum_ref):
    coefs, samples = out_ref.shape
    rows = coded_ref.shape[0]

    def part(index, total):
        at = pl.ds(pl.multiple_of(index * CHUNK, CHUNK), CHUNK)
        outgoing = jnp.dot(
            coded_ref[at, :][:, :coefs], out_ref[...], preferred_element_type=jnp.float32
        )
        weighted = cosine(angle_ref[at, :].astype(jnp.float32)) * outgoing
        return total + jnp.sum(weighted, axis=0, keepdims=True)

    sum_ref[...] = lax.fori_loop(0, rows // CHUNK, part, jnp.zeros((1, samples), jnp.float32))


def gather_wave(coded, wave_out, angle):
    rows, samples = angle.shape
    return pl.pallas_call(
        wave_kernel,
        out_shape=jax.ShapeDtypeStruct((1, samples), jnp.float32),
        in_specs=[whole()] * 3,
        out_specs=whole(),
        compiler_params=params(),
        cost_estimate=COST,
        name="gather_wave",
    )(coded, wave_out, angle)


def spread_wave(at, incoming_ref, in_ref, angle_ref):
    spread = cosine(angle_ref[at, :].astype(jnp.float32)) * incoming_ref[...]
    return lax.dot_general(
        spread.astype(jnp.bfloat16),
        in_ref[...],
        (((1,), (1,)), ((), ())),
        preferred_element_type=jnp.float32,
    )


def load_rows(source, first, shards):
    rows = shards[0].shape[0]
    for place, shard in enumerate(shards, first):
        value = shard[...].astype(jnp.float32)
        source[pl.ds(2 * place * rows, rows, stride=2), :] = value[:, :LANES]
        source[pl.ds(2 * place * rows + 1, rows, stride=2), :] = value[:, LANES:]


def pick_rows(source_ref, target_ref, bound_ref, segments, source, picked):
    picked[...] = jnp.zeros_like(picked)

    def move(places, shift):
        got = [source[pl.ds(pl.multiple_of(source_ref[n] + shift, 2), 2), :] for n in places]
        for n, row in zip(places, got, strict=True):
            picked[pl.ds(pl.multiple_of(target_ref[n], 2), 2), :] = row

    for first, last, shift in segments:
        low, high = bound_ref[first], bound_ref[last]
        full = (high - low) // BATCH

        def step(index, carry, low=low, shift=shift):
            move([low + index * BATCH + k for k in range(BATCH)], shift)
            return carry

        lax.fori_loop(0, full, step, 0)

        @pl.when(low + full * BATCH < high)
        def _(low=low, high=high, full=full, shift=shift):
            move([jnp.minimum(low + full * BATCH + k, high - 1) for k in range(BATCH)], shift)


def translate(start, picked, table_ref, tables_ref):
    at = pl.ds(start, CHUNK)
    per_row = table_ref.shape[1]
    coefs = tables_ref.shape[1]
    stride = 2 * per_row
    halves = [
        [
            picked[pl.ds(start * stride + 2 * k + h, CHUNK, stride=stride), :].astype(jnp.bfloat16)
            for h in range(2)
        ]
        for k in range(per_row)
    ]
    names = table_ref[at, :].astype(jnp.float32)
    named = [
        jnp.broadcast_to(names[:, k : k + 1], (CHUNK, LANES)).astype(jnp.bfloat16)
        for k in range(per_row)
    ]
    zero = jnp.zeros((CHUNK, LANES), jnp.bfloat16)
    total = jnp.zeros((CHUNK, coefs), jnp.float32)
    for t in range(tables_ref.shape[0]):
        chosen = [named[k] == jnp.bfloat16(t) for k in range(per_row)]
        mixed = []
        for h in range(2):
            value = jnp.where(chosen[0], halves[0][h], zero)
            for k in range(1, per_row):
                value = value + jnp.where(chosen[k], halves[k][h], zero)
            mixed.append(value)
        total = total + jnp.dot(
            jnp.concatenate(mixed, axis=1)[:, :coefs],
            tables_ref[t],
            preferred_element_type=jnp.float32,
        )
    return total


def row_chunks(rows, step, carry=0):
    return lax.fori_loop(
        0, rows // CHUNK, lambda i, c: step(pl.multiple_of(i * CHUNK, CHUNK), c), carry
    )


def terms_kernel(
    kind, segments, first, source_ref, target_ref, bound_ref, active_ref, table_ref, tables_ref, *rest
):
    *rest, source, picked = rest
    if kind == "near":
        incoming_ref, in_ref, angle_ref, *shards, out_ref = rest
    elif kind == "rest":
        part_ref, _, *shards, out_ref = rest
    elif kind in ("own", "some"):
        *shards, out_ref, done_ref = rest
        done_ref[...] = jnp.zeros_like(done_ref)
    else:
        *shards, out_ref = rest

    def part(index, carry):
        start = pl.multiple_of(index * CHUNK, CHUNK)
        at = pl.ds(start, CHUNK)
        total = translate(start, picked, table_ref, tables_ref)
        if kind == "near":
            total = total + spread_wave(at, incoming_ref, in_ref, angle_ref)
        if kind == "rest":
            total = total + part_ref[at, :]
        if out_ref.dtype == jnp.bfloat16:
            total = pad_lanes(total, out_ref.shape[1]).astype(jnp.bfloat16)
        out_ref[at, :] = total
        return carry

    @pl.when(active_ref[0] != 0)
    def _():
        load_rows(source, first, shards)
        pick_rows(source_ref, target_ref, bound_ref, segments, source, picked)
        lax.fori_loop(0, out_ref.shape[0] // CHUNK, part, 0)


def terms(kind, segments, first, requests, tables, shards, *extra, active=True):
    source, target, bounds, table_ids = requests
    rows, width = shards[0].shape
    coefs = tables.shape[1]
    if kind in ("near", "own"):
        outs = [jax.ShapeDtypeStruct((rows, coefs), jnp.float32)]
    else:
        outs = [jax.ShapeDtypeStruct((rows, width), jnp.bfloat16)]
    if kind in ("own", "some"):
        outs.append(jax.ShapeDtypeStruct((8, LANES), jnp.float32))
    return pl.pallas_call(
        functools.partial(terms_kernel, kind, segments, first),
        out_shape=tuple(outs),
        in_specs=[whole(pltpu.SMEM)] * 4 + [whole()] * (2 + len(extra) + len(shards)),
        out_specs=(whole(),) * len(outs),
        scratch_shapes=[
            pltpu.VMEM((2 * (first + len(shards)) * rows, LANES), jnp.float32),
            pltpu.VMEM((2 * source.shape[0], LANES), jnp.float32),
        ],
        compiler_params=params(),
        cost_estimate=COST,
        name="terms_" + kind,
    )(
        source,
        target,
        bounds,
        jnp.asarray(active).astype(jnp.int32).reshape(1),
        table_ids,
        tables,
        *extra,
        *shards,
    )


def join_kernel(second, count, base_ref, mie_ref, x_ref, *rest):
    served, rest = rest[:count], rest[count:]
    if second:
        vec_ref, sums_in_ref, *rest = rest
    else:
        vec_ref = x_ref
    image_ref, *rest, sums_ref = rest
    rows, coefs = base_ref.shape
    width = served[0].shape[1]

    def dot(a, b):
        return jnp.sum(a * b, axis=0, keepdims=True)

    def part(start, sums):
        at = pl.ds(start, CHUNK)
        far_rows = served[0][at, :].astype(jnp.float32)
        for other in served[1:]:
            far_rows = far_rows + other[at, :].astype(jnp.float32)
        image = pad_lanes(base_ref[at, :] + far_rows[:, :coefs], width).T[:coefs, :]
        image = mie_ref[:, at] * image
        image_ref[:, at] = image
        if not second:
            wide = jnp.concatenate([image, jnp.zeros((width - coefs, CHUNK), image.dtype)], axis=0)
            rest[0][at, :] = wide.T.astype(jnp.bfloat16)
        x, vec = x_ref[:, at], vec_ref[:, at]
        new = [dot(x, image), dot(vec, image) if second else dot(x, x), dot(image, image)]
        return tuple(a + b for a, b in zip(sums, new, strict=True))

    sums = row_chunks(rows, part, tuple(jnp.zeros((1, CHUNK), jnp.float32) for _ in range(3)))
    lane = lax.broadcasted_iota(jnp.int32, (1, LANES), 1)
    packed = sums_in_ref[...] if second else jnp.zeros((1, LANES), jnp.float32)
    for k, value in enumerate(sums):
        total = jnp.sum(value, axis=1, keepdims=True)
        packed = jnp.where(lane == k + (3 if second else 0), total, packed)
    sums_ref[...] = jnp.broadcast_to(packed, sums_ref.shape)


def join(base, mie_t, x_t, served, second=(), devices=1):
    rows, coefs = base.shape
    width = served[0].shape[1]
    outs = [jax.ShapeDtypeStruct((coefs, rows), jnp.float32)]
    if not second:
        outs.append(jax.ShapeDtypeStruct((rows, width), jnp.bfloat16))
    outs.append(jax.ShapeDtypeStruct((devices, LANES), jnp.float32))
    return pl.pallas_call(
        functools.partial(join_kernel, len(second) > 0, len(served)),
        out_shape=tuple(outs),
        in_specs=[whole()] * (3 + len(served) + len(second)),
        out_specs=(whole(),) * len(outs),
        compiler_params=params(),
        name="join_second" if second else "join_first",
    )(base, mie_t, x_t, *served, *second)


def finish_kernel(sums_ref, x_ref, b_ref, c_ref, solution_ref, residual_ref, hess_ref):
    sums = jnp.sum(sums_ref[...], axis=0, keepdims=True)
    xb, xx, bb, xc, bc, cc = [sums[:, k : k + 1] for k in range(6)]
    norm = jnp.sqrt(xx + epsilon)
    inverse = 1.0 / norm
    squared = inverse * inverse
    h11 = (xx - xb) * squared
    g = (xb + epsilon) * squared
    size1 = (g * g * xx - 2.0 * g * xb + bb) * squared
    h21 = jnp.sqrt(jnp.maximum(size1, 0.0) + epsilon)
    q = inverse / h21
    v11 = xx * squared
    v12 = q * inverse * (g * xx - xb)
    v22 = size1 / (h21 * h21)
    p1 = q * inverse * (g * xb - xc)
    p2 = q * q * (g * g * xb - g * xc - g * bb + bc)
    pp = q * q * (g * g * bb - 2.0 * g * bc + cc)
    h12 = v12 - p1
    h22 = v22 - p2
    rest = 1.0 - h22
    size2 = (
        rest * rest * v22
        + h12 * h12 * v11
        + pp
        - 2.0 * rest * h12 * v12
        - 2.0 * rest * p2
        + 2.0 * h12 * p1
    )
    h32 = jnp.sqrt(jnp.maximum(size2, 0.0) + epsilon)
    gram00 = h11 * h11 + h21 * h21
    gram01 = h11 * h12 + h21 * h22
    gram11 = h12 * h12 + h22 * h22 + h32 * h32
    rhs0, rhs1 = norm * h11, norm * h12
    det = gram00 * gram11 - gram01 * gram01
    a1 = (gram11 * rhs0 - gram01 * rhs1) / det * inverse
    a2 = (gram00 * rhs1 - gram01 * rhs0) / det * q
    x, b, c = x_ref[...], b_ref[...], c_ref[...]
    solution_ref[...] = (a1 + a2 * g) * x - a2 * b
    residual_ref[...] = (1.0 - a1 - a2 * g) * x + (a1 + a2 * (1.0 + g)) * b - a2 * c
    hess_ref[0:1, 0:1] = h11
    hess_ref[0:1, 1:2] = h21
    hess_ref[0:1, 2:3] = jnp.zeros_like(h11)
    hess_ref[1:2, 0:1] = h12
    hess_ref[1:2, 1:2] = h22
    hess_ref[1:2, 2:3] = h32


def finish(sums, x_t, b_t, c_t):
    field = jax.ShapeDtypeStruct(x_t.shape, jnp.float32)
    return pl.pallas_call(
        finish_kernel,
        out_shape=(field, field, jax.ShapeDtypeStruct((2, 3), jnp.float32)),
        in_specs=[whole()] * 4,
        out_specs=(whole(),) * 3,
        compiler_params=params(),
        name="finish",
    )(sums, x_t, b_t, c_t)


def flip(block, bits):
    return lax.ppermute(block, "grp", [(i, i ^ bits) for i in range(lax.axis_size("grp"))])


def along_chips(block, moves):
    return lax.ppermute(block, "grp", [(2 * a + c, 2 * b + c) for a, b in moves for c in range(2)])


def other_core(block, chips):
    return lax.ppermute(block, "grp", [(2 * z + c, 2 * z + 1 - c) for z in chips for c in range(2)])


def once(*values):
    return lax.optimization_barrier(values)


def wave_swaps(waves, count):
    blocks = lax.axis_size("blk")
    while waves.shape[0] < min(count, blocks):
        bits = waves.shape[0]
        moved = lax.ppermute(waves, "blk", [(i, i ^ bits) for i in range(blocks)])
        waves = jnp.concatenate([waves, moved], axis=0)
    return waves


def body(
    incident,
    mie_coef,
    owner_dev,
    near_row,
    table_id,
    tables,
    wave_out,
    wave_in,
    plane_angle,
    far_trans,
):
    x = incident[0]
    mie_t = mie_coef[0].T
    angle = plane_angle[0]
    rows, coefs = x.shape
    width = -(-coefs // LANES) * LANES
    group = lax.axis_size("grp")
    devices = group * lax.axis_size("blk")
    tables_count = tables.shape[0]
    wave_in_t = wave_in.T
    x_t = x.T

    apart = owner_dev[0, :, 0] ^ lax.axis_index("grp")
    count = apart.shape[0]
    bits = (count - 1).bit_length()
    number = jnp.arange(count, dtype=jnp.int32)
    listed = jnp.sort(((apart * rows + near_row[0]) << bits) | number)
    bounds = jnp.arange(group + 1, dtype=jnp.int32)
    bounds = jnp.sum((apart[None, :] < bounds[:, None]).astype(jnp.int32), axis=1)
    others = range(1, group // QUAD)

    def requests_of(message):
        word = message[:count]
        names = message[count : 2 * count].astype(jnp.bfloat16).reshape(rows, -1)
        source = 2 * ((word >> bits) % (QUAD * rows))
        return source, 2 * (word & ((1 << bits) - 1)), message[2 * count :], names

    message = jnp.concatenate([listed, table_id[0], bounds])
    asked = [flip(message, QUAD * j) for j in others]
    blocks = lax.axis_size("blk")
    turns = jnp.arange(blocks, dtype=jnp.int32)
    weights = far_trans[0, 0][turns ^ lax.axis_index("blk")]
    weights = jnp.where(turns[:, None] > 0, weights, 0.0)

    def incoming_of(waves):
        waves = wave_swaps(waves, blocks)
        return jnp.sum(weights * waves, axis=0, keepdims=True)

    coded = code(x_t, width)
    across, same = flip(coded, 2), flip(coded, 1)
    waves = gather_wave(coded, wave_out, angle)
    across, waves, *asked = once(across, waves, *asked)
    asked = [requests_of(words) for words in asked]
    local = requests_of(message)
    shards = [coded, same, across, flip(across, 1)]
    served = [
        flip(terms("all", ((QUAD * j, QUAD * j + QUAD, 0),), 0, words, tables, shards)[0], QUAD * j)
        for j, words in zip(others, asked, strict=True)
    ]
    base = terms("near", ((0, QUAD, 0),), 0, local, tables, shards, incoming_of(waves), wave_in_t, angle)[0]
    b_t, coded, sums = join(base, mie_t, x_t, served)

    def by_quads(coded):
        across, same = flip(coded, 2), flip(coded, 1)
        parts = [
            terms("own", ((QUAD * j, QUAD * j + 2, 0),), 0, words, tables, [coded, same])
            for j, words in zip(others, asked, strict=True)
        ]
        across, *done = once(across, *[done for _, done in parts])
        shards = [across, flip(across, 1)]
        served = [
            flip(
                terms("rest", ((QUAD * j + 2, QUAD * j + 4, 0),), 2, words, tables, shards, part, token)[0],
                QUAD * j,
            )
            for j, words, (part, _), token in zip(others, asked, parts, done, strict=True)
        ]
        incoming = incoming_of(gather_wave(coded, wave_out, angle))
        shards = [coded, same, *shards]
        return terms("near", ((0, QUAD, 0),), 0, local, tables, shards, incoming, wave_in_t, angle)[0], served

    def in_line(coded):
        chip = lax.axis_index("grp") // 2
        middle = (chip == 1) | (chip == 2)
        across = along_chips(coded, [(0, 1), (1, 0), (2, 3), (3, 2)])
        inner = along_chips(coded, [(1, 2), (2, 1)])
        same = flip(coded, 1)
        sums, done = terms(
            "some", ((QUAD, QUAD + 2, 0),), 0, asked[0], tables, [coded, same], active=~middle
        )
        early = along_chips(sums, [(0, 2), (3, 1)])
        waves = wave_swaps(gather_wave(coded, wave_out, angle), 2)
        across, inner, waves, done = once(across, inner, waves, done)
        shards = [coded, same, across, flip(across, 1)]
        active = middle & (done[0, 0] == 0.0)
        sums, done = terms(
            "some", ((QUAD, 2 * QUAD, 0),), 0, asked[0], tables, shards, active=active
        )
        late = along_chips(sums, [(1, 3), (2, 0)])
        inner, done = once(inner, done)
        incoming, early = once(incoming_of(waves), early)
        shards += [inner, other_core(inner, (1, 2))]
        source, target, bounds, names = local
        missing = (jnp.arange(group + 1) == 6) & ~middle
        requests = source, target, jnp.where(missing, bounds[8], bounds), names
        segments = ((0, QUAD, 0), (6, 8, 4 * rows))
        return terms("near", segments, 0, requests, tables, shards, incoming, wave_in_t, angle)[0], [early, late]

    base, served = by_quads(coded)
    c_t, sums = join(base, mie_t, x_t, served, (b_t, sums), devices)
    sums = lax.all_to_all(sums, ("blk", "grp"), 0, 0, tiled=True)
    solution_t, residual_t, hess_t = finish(sums, x_t, b_t, c_t)
    return solution_t.T[None], residual_t.T[None], hess_t.T


def solution(mesh):
    return jax.shard_map(
        body,
        mesh=mesh,
        in_specs=(
            P("blk", "grp", None),
            P("blk", "grp", None),
            P("blk", "grp", None),
            P("blk", "grp"),
            P("blk", "grp"),
            P(),
            P(),
            P(),
            P("blk", "grp", None),
            P("blk", "grp", None, None),
        ),
        out_specs=(P("blk", "grp", None), P("blk", "grp", None), P()),
        check_vma=False,
    )
```

time: 120 us -> 117 us (0.975)
  waiting for transfers between devices: 25 us -> 37.8 us
  Pallas kernels: 47 us -> 36.2 us
  local copies, waits for them, and re-layouts: 12 us -> 5.05 us
  other arithmetic: 0.95 us -> 6.18 us
  starting transfers between devices: 22.3 us -> 17.9 us
    ppermute x7 -> x9, waiting for transfers between devices: 10.1 us -> 30.4 us  [flip(): lax.ppermute(block, 'grp', [(i, i ^ bits) for i in range(lax.axis_size('g...]
    ppermute x5 -> x0, waiting for transfers between devices: 7.12 us -> none  [the longest x4 7.12 us: along_chips(): lax.ppermute(block, 'grp', [(2 * a + c, 2 * b + c) for a, b in moves for...]
    ppermute x5 -> x0, starting transfers between devices: 6.91 us -> none  [the longest x4 6.22 us: along_chips(): lax.ppermute(block, 'grp', [(2 * a + c, 2 * b + c) for a, b in moves for...]
    pallas_call x7 -> x5, Pallas kernels: 35.1 us -> 28.3 us  [terms(): pl.pallas_call(functools.partial(terms_kernel, kind, segments, first), ou...]
    sort x0 -> x1, other arithmetic: none -> 5.75 us  [body(): listed = jnp.sort(apart * rows + near_row[0] << bits | number)]
    unnamed x42 -> x28, local copies, waits for them, and re-layouts: 9.17 us -> 3.63 us
    pallas_call x2, Pallas kernels: 5.78 us -> 3.16 us  [gather_wave(): pl.pallas_call(wave_kernel, out_shape=jax.ShapeDtypeStruct((1, samples),...]
    ppermute x7 -> x9, starting transfers between devices: 9.13 us -> 11.7 us  [flip(): lax.ppermute(block, 'grp', [(i, i ^ bits) for i in range(lax.axis_size('g...]
  transfers between devices with their start and end apart: 16 -> 13, of which waited for: 10 -> 12; matrix products, arithmetic and copies ran while one was open for 5% -> 7% of each run, Pallas kernels for 27% -> 18%
where the time goes in v5:
time: 117 us; the launch traced here: 116 us
  waiting for transfers between devices  37.8 us (32%)
  Pallas kernels  36.2 us (31%)
  starting transfers between devices  17.9 us (15%)
  blocking collectives  12.5 us (11%)
  other arithmetic  6.18 us (5%)
  local copies, waits for them, and re-layouts  5.05 us (4%)
    ppermute x9, waiting for transfers between devices, flip(): lax.ppermute(block, 'grp', [(i, i ^ bits) for i in range(lax.axis_size('g...  30.4 us
    pallas_call x5, Pallas kernels, terms(): pl.pallas_call(functools.partial(terms_kernel, kind, segments, first), ou...  28.3 us
    all_to_all x1, blocking collectives, body(): sums = lax.all_to_all(sums, ('blk', 'grp'), 0, 0, tiled=True)  12.5 us
    ppermute x9, starting transfers between devices, flip(): lax.ppermute(block, 'grp', [(i, i ^ bits) for i in range(lax.axis_size('g...  11.7 us
    ppermute x4, waiting for transfers between devices, wave_swaps(): moved = lax.ppermute(waves, 'blk', [(i, i ^ bits) for i in range(blocks)])  7.35 us
    ppermute x4, starting transfers between devices, wave_swaps(): moved = lax.ppermute(waves, 'blk', [(i, i ^ bits) for i in range(blocks)])  6.21 us
    sort x1, other arithmetic, body(): listed = jnp.sort(apart * rows + near_row[0] << bits | number)  5.75 us
    unnamed x28, local copies, waits for them, and re-layouts  3.63 us
  transfers between devices with their start and end apart: 13, of which 12 were waited for; matrix products, arithmetic and copies ran while one was open for 7% of the time, Pallas kernels for 18%

profile of v5, /device:TPU:0, one launch (start us, length us, event | category | flops | bytes accessed | tf_op | source)
XLA Modules:
  0.0 116.4 jit_solution(15497042260962238417)
XLA Ops:
  0.6 0.0 copy-start
  0.7 0.0 copy-start.3
  0.7 1.3 %copy-done.3 = f32[1,1024,240]{1,2,0:T(8,128)S(1)} copy-done((f32[1,1024,240]{1,2,0:T(8,128)S(1)}, f32[1,1024,240]{1,2,0:T(8,128)}, u32[]{:S(2)}) %copy-start.3) | copy-done | bytes 983064
  2.0 0.2 code_rows.1.coded_ref.rest_3_.rest_0_
  2.2 3.1 %collective-permute-start = (bf16[1024,256]{1,0:T(8,128)(2,1)S(1)}, bf16[1024,256]{1,0:T(8,128)(2,1)S(1)}, u32[]{:S(2)}, u32[]{:S(2)}) collective-permute-start(bf16[1024,256]{1,0:T(8,128)(2,1)S(1)} %code_rows.1.coded_ref.rest_3_.rest_0_), channel_id=1, source_target_pairs={{0,2},{1,3},{2,0},{3,1},{4,6},{5,7},{6,4},{7,5},{8,10},{9,11},{10,... | collective-permute-start | bytes 1572872 | tf_op jit(solution)/shard_map/ppermute | solution.py:364
  5.3 0.7 copy-done.13
  6.0 5.8 %sort.15 = (s32[3072]{0:T(1024)S(1)}, s32[3072]{0:T(1024)}) sort(s32[3072]{0:T(1024)S(1)} %iota_or_fusion, s32[3072]{0:T(1024)S(1)} %iota.19), dimensions={0}, to_apply=%region_0.0 | sort | flops 36864 | bytes 49152 | tf_op jit(solution)/shard_map/jit(sort)/sort | solution.py:415
  11.7 0.1 convert_reduce_fusion.bound_ref
  11.9 0.6 copy-done.11
  12.4 2.6 %collective-permute-start.1 = (s32[6153]{0:T(1024)S(1)}, s32[6153]{0:T(1024)S(1)}, u32[]{:S(2)}, u32[]{:S(2)}) collective-permute-start(s32[6153]{0:T(1024)S(1)} %pad_add_fusion), channel_id=1, source_target_pairs={{0,4},{1,5},{2,6},{3,7},{4,0},{5,1},{6,2},{7,3},{8,12},{9,13},{10,... | collective-permute-start | bytes 73844 | tf_op jit(solution)/shard_map/ppermute | solution.py:364
  15.0 0.0 copy-start.1
  15.1 1.6 %gather_wave.2 = f32[1,512]{1,0:T(1,128)S(1)} custom-call(bf16[1024,256]{1,0:T(8,128)(2,1)S(1)} %code_rows.1.coded_ref.rest_3_.rest_0_, bf16[240,512]{1,0:T(8,128)(2,1)S(1)} %copy-done.8, bf16[1024,512]{1,0:T(8,128)(2,1)S(1)} %bitcast.28), custom_call_target="tpu_custom_call" | custom-call | flops 1 | bytes 1 | tf_op jit(solution)/shard_map/gather_wave/pallas_call | solution.py:89
  16.6 0.7 collective-permute-done.1
  17.3 0.5 collective-permute-done.rest_5_.rest_2_
  17.9 0.4 convert_element_type.18.table_ref
  18.3 1.5 %collective-permute-done.5.rest_6_.rest_3_ = bf16[1024,256]{1,0:T(8,128)(2,1)} collective-permute-done((bf16[1024,256]{1,0:T(8,128)(2,1)S(1)}, bf16[1024,256]{1,0:T(8,128)(2,1)}, u32[]{:S(2)}, u32[]{:S(2)}) %collective-permute-start.5) | collective-permute-done | bytes 524320 | tf_op jit(solution)/shard_map/ppermute | solution.py:364
  19.8 6.4 %terms_all.1 = bf16[1024,256]{1,0:T(8,128)(2,1)} custom-call(s32[3072]{0:T(1024)S(1)} %get-tuple-element.38.source_ref, s32[3072]{0:T(1024)S(1)} %get-tuple-element.37.target_ref, s32[9]{0:T(128)S(1)} %slice.19.bound_ref, s32[1]{0:T(128)} %constant.40.clone.1.active_ref, bf16[1024,3]{1,0:T(8,128)(2,1)S(1)} %convert_element_type.18.table_ref, ...), custom_call_target="tpu_custom_call" | custom-call | flops 1 | bytes 1 | tf_op jit(solution)/shard_map/terms_all/pallas_call | solution.py:226
  26.2 2.6 %collective-permute-start.6 = (bf16[1024,256]{1,0:T(8,128)(2,1)}, bf16[1024,256]{1,0:T(8,128)(2,1)}, u32[]{:S(2)}, u32[]{:S(2)}) collective-permute-start(bf16[1024,256]{1,0:T(8,128)(2,1)} %terms_all.1), channel_id=1, source_target_pairs={{0,4},{1,5},{2,6},{3,7},{4,0},{5,1},{6,2},{7,3},{8,12},{9,13},{10,... | collective-permute-start | bytes 1572872 | tf_op jit(solution)/shard_map/ppermute | solution.py:364
  28.9 1.6 %collective-permute-start.2 = (f32[1,512]{1,0:T(1,128)S(1)}, f32[1,512]{1,0:T(1,128)S(1)}, u32[]{:S(2)}, u32[]{:S(2)}) collective-permute-start(f32[1,512]{1,0:T(1,128)S(1)} %gather_wave.2), channel_id=1, source_target_pairs={{0,8},{8,0},{16,24},{24,16},{1,9},{9,1},{17,25},{25,17},{2,10},{10... | collective-permute-start | bytes 6152 | tf_op jit(solution)/shard_map/ppermute | solution.py:383
  30.5 2.0 %collective-permute-done.2 = f32[1,512]{1,0:T(1,128)S(1)} collective-permute-done((f32[1,512]{1,0:T(1,128)S(1)}, f32[1,512]{1,0:T(1,128)S(1)}, u32[]{:S(2)}, u32[]{:S(2)}) %collective-permute-start.2) | collective-permute-done | bytes 2080 | tf_op jit(solution)/shard_map/ppermute | solution.py:383
  32.5 1.8 %collective-permute-start.3 = (f32[2,512]{1,0:T(2,128)S(1)}, f32[2,512]{1,0:T(2,128)S(1)}, u32[]{:S(2)}, u32[]{:S(2)}) collective-permute-start(f32[2,512]{1,0:T(2,128)S(1)} %pad_maximum_fusion), channel_id=1, source_target_pairs={{0,16},{8,24},{16,0},{24,8},{1,17},{9,25},{17,1},{25,9},{2,18},{10... | collective-permute-start | bytes 12296 | tf_op jit(solution)/shard_map/ppermute | solution.py:383
  34.2 0.4 convert_element_type.17.table_ref
  34.7 0.6 gather_fusion
  35.3 0.9 collective-permute-done.3
  36.1 0.1 fusion.4
  36.2 1.0 copy-done.7
  37.3 7.0 %terms_near.2.base_ref = f32[1024,240]{1,0:T(8,128)S(1)} custom-call(s32[3072]{0:T(1024)S(1)} %get-tuple-element.40.source_ref, s32[3072]{0:T(1024)S(1)} %get-tuple-element.39.target_ref, s32[9]{0:T(128)S(1)} %convert_reduce_fusion.bound_ref, s32[1]{0:T(128)} %constant.40.clone.1.active_ref, bf16[1024,3]{1,0:T(8,128)(2,1)S(1)} %convert_element_type.17.table_ref, ...), custom_call_target="tpu_custom_call" | custom-call | flops 1 | bytes 1 | tf_op jit(solution)/shard_map/terms_near/pallas_call | solution.py:226
  44.3 8.4 %collective-permute-done.6.rest_0_ = bf16[1024,256]{1,0:T(8,128)(2,1)} collective-permute-done((bf16[1024,256]{1,0:T(8,128)(2,1)}, bf16[1024,256]{1,0:T(8,128)(2,1)}, u32[]{:S(2)}, u32[]{:S(2)}) %collective-permute-start.6) | collective-permute-done | bytes 524320 | tf_op jit(solution)/shard_map/ppermute | solution.py:364
  52.7 1.8 %join_first.1 = (f32[240,1024]{1,0:T(8,128)S(1)}, bf16[1024,256]{1,0:T(8,128)(2,1)S(1)}, f32[1,128]{1,0:T(1,128)S(1)}) custom-call(f32[1024,240]{1,0:T(8,128)S(1)} %terms_near.2.base_ref, f32[240,1024]{1,0:T(8,128)S(1)} %bitcast.36, f32[240,1024]{1,0:T(8,128)S(1)} %bitcast.33, bf16[1024,256]{1,0:T(8,128)(2,1)} %collective-permute-done.6.rest_0_), custom_call_target="tpu_custom_call" | custom-call | tf_op jit(solution)/shard_map/join_first/pallas_call | solution.py:294
  54.5 0.0 collective-permute-start.9
  54.6 0.8 collective-permute-start.10
  55.4 1.1 collective-permute-done.9.rest_1_.rest_4_
  56.5 4.0 %terms_own.1 = (f32[1024,240]{1,0:T(8,128)S(1)}, f32[8,128]{1,0:T(8,128)S(1)}) custom-call(s32[3072]{0:T(1024)S(1)} %get-tuple-element.38.source_ref, s32[3072]{0:T(1024)S(1)} %get-tuple-element.37.target_ref, s32[9]{0:T(128)S(1)} %slice.19.bound_ref, s32[1]{0:T(128)} %constant.40.clone.1.active_ref, bf16[1024,3]{1,0:T(8,128)(2,1)S(1)} %convert_element_type.18.table_ref, ...), custom_call_target="tpu_custom_call" | custom-call | flops 1 | bytes 1 | tf_op jit(solution)/shard_map/terms_own/pallas_call | solution.py:226
  60.5 8.4 %collective-permute-done.10.rest_5_.rest_2_ = bf16[1024,256]{1,0:T(8,128)(2,1)S(1)} collective-permute-done((bf16[1024,256]{1,0:T(8,128)(2,1)S(1)}, bf16[1024,256]{1,0:T(8,128)(2,1)S(1)}, u32[]{:S(2)}, u32[]{:S(2)}) %collective-permute-start.10) | collective-permute-done | bytes 524320 | tf_op jit(solution)/shard_map/ppermute | solution.py:364
  68.9 1.9 %collective-permute-done.11.rest_6_.rest_3_ = bf16[1024,256]{1,0:T(8,128)(2,1)S(1)} collective-permute-done((bf16[1024,256]{1,0:T(8,128)(2,1)S(1)}, bf16[1024,256]{1,0:T(8,128)(2,1)S(1)}, u32[]{:S(2)}, u32[]{:S(2)}) %collective-permute-start.11) | collective-permute-done | bytes 524320 | tf_op jit(solution)/shard_map/ppermute | solution.py:364
  70.8 4.3 %terms_rest.1 = bf16[1024,256]{1,0:T(8,128)(2,1)S(1)} custom-call(s32[3072]{0:T(1024)S(1)} %get-tuple-element.38.source_ref, s32[3072]{0:T(1024)S(1)} %get-tuple-element.37.target_ref, s32[9]{0:T(128)S(1)} %slice.19.bound_ref, s32[1]{0:T(128)} %constant.40.clone.1.active_ref, bf16[1024,3]{1,0:T(8,128)(2,1)S(1)} %convert_element_type.18.table_ref, ...), custom_call_target="tpu_custom_call" | custom-call | flops 1 | bytes 1 | tf_op jit(solution)/shard_map/terms_rest/pallas_call | solution.py:226
  75.1 2.5 %collective-permute-start.12 = (bf16[1024,256]{1,0:T(8,128)(2,1)S(1)}, bf16[1024,256]{1,0:T(8,128)(2,1)S(1)}, u32[]{:S(2)}, u32[]{:S(2)}) collective-permute-start(bf16[1024,256]{1,0:T(8,128)(2,1)S(1)} %terms_rest.1), channel_id=1, source_target_pairs={{0,4},{1,5},{2,6},{3,7},{4,0},{5,1},{6,2},{7,3},{8,12},{9,13},{10,... | collective-permute-start | bytes 1572872 | tf_op jit(solution)/shard_map/ppermute | solution.py:364
  77.7 1.6 %gather_wave.3 = f32[1,512]{1,0:T(1,128)S(1)} custom-call(bf16[1024,256]{1,0:T(8,128)(2,1)S(1)} %get-tuple-element.24.coded_ref.rest_0_.rest_3_, bf16[240,512]{1,0:T(8,128)(2,1)S(1)} %copy-done.9, bf16[1024,512]{1,0:T(8,128)(2,1)S(1)} %bitcast.30), custom_call_target="tpu_custom_call" | custom-call | flops 1 | bytes 1 | tf_op jit(solution)/shard_map/gather_wave/pallas_call | solution.py:89
  79.3 1.5 %collective-permute-start.7 = (f32[1,512]{1,0:T(1,128)S(1)}, f32[1,512]{1,0:T(1,128)S(1)}, u32[]{:S(2)}, u32[]{:S(2)}) collective-permute-start(f32[1,512]{1,0:T(1,128)S(1)} %gather_wave.3), channel_id=1, source_target_pairs={{0,8},{8,0},{16,24},{24,16},{1,9},{9,1},{17,25},{25,17},{2,10},{10... | collective-permute-start | bytes 6152 | tf_op jit(solution)/shard_map/ppermute | solution.py:383
  80.7 2.2 %collective-permute-done.7 = f32[1,512]{1,0:T(1,128)S(1)} collective-permute-done((f32[1,512]{1,0:T(1,128)S(1)}, f32[1,512]{1,0:T(1,128)S(1)}, u32[]{:S(2)}, u32[]{:S(2)}) %collective-permute-start.7) | collective-permute-done | bytes 2080 | tf_op jit(solution)/shard_map/ppermute | solution.py:383
  82.9 1.4 %collective-permute-start.8 = (f32[2,512]{1,0:T(2,128)S(1)}, f32[2,512]{1,0:T(2,128)S(1)}, u32[]{:S(2)}, u32[]{:S(2)}) collective-permute-start(f32[2,512]{1,0:T(2,128)S(1)} %pad_maximum_fusion.1), channel_id=1, source_target_pairs={{0,16},{8,24},{16,0},{24,8},{1,17},{9,25},{17,1},{25,9},{2,18},{10... | collective-permute-start | bytes 12296 | tf_op jit(solution)/shard_map/ppermute | solution.py:383
  84.3 2.3 %collective-permute-done.8 = f32[2,512]{1,0:T(2,128)S(1)} collective-permute-done((f32[2,512]{1,0:T(2,128)S(1)}, f32[2,512]{1,0:T(2,128)S(1)}, u32[]{:S(2)}, u32[]{:S(2)}) %collective-permute-start.8) | collective-permute-done | bytes 4128 | tf_op jit(solution)/shard_map/ppermute | solution.py:383
  86.6 0.1 fusion.5
  86.7 6.6 %terms_near.3.base_ref = f32[1024,240]{1,0:T(8,128)S(1)} custom-call(s32[3072]{0:T(1024)S(1)} %get-tuple-element.40.source_ref, s32[3072]{0:T(1024)S(1)} %get-tuple-element.39.target_ref, s32[9]{0:T(128)S(1)} %convert_reduce_fusion.bound_ref, s32[1]{0:T(128)} %constant.40.clone.1.active_ref, bf16[1024,3]{1,0:T(8,128)(2,1)S(1)} %convert_element_type.17.table_ref, ...), custom_call_target="tpu_custom_call" | custom-call | flops 1 | bytes 1 | tf_op jit(solution)/shard_map/terms_near/pallas_call | solution.py:226
  93.3 7.9 %collective-permute-done.12.rest_0_ = bf16[1024,256]{1,0:T(8,128)(2,1)S(1)} collective-permute-done((bf16[1024,256]{1,0:T(8,128)(2,1)S(1)}, bf16[1024,256]{1,0:T(8,128)(2,1)S(1)}, u32[]{:S(2)}, u32[]{:S(2)}) %collective-permute-start.12) | collective-permute-done | bytes 524320 | tf_op jit(solution)/shard_map/ppermute | solution.py:364
  101.2 0.6 join_second.1
  101.8 12.5 %all_to_all.11 = f32[32,1,128]{2,1,0:T(1,128)S(1)} all-to-all(f32[32,1,128]{2,1,0:T(1,128)S(1)} %bitcast.41), channel_id=1, replica_groups=mesh['blk'=4,'grp'=8] {'blk','grp'}, dimensions={0} | all-to-all | bytes 32768 | tf_op jit(solution)/shard_map/all_to_all | solution.py:499
  114.3 2.1 %finish.1 = (f32[240,1024]{1,0:T(8,128)}, f32[240,1024]{1,0:T(8,128)}, f32[2,3]{1,0:T(2,128)}) custom-call(f32[32,128]{1,0:T(8,128)S(1)} %bitcast.40, f32[240,1024]{1,0:T(8,128)S(1)} %bitcast.35, f32[240,1024]{1,0:T(8,128)S(1)} %get-tuple-element.29.rest_1_.b_ref, f32[240,1024]{1,0:T(8,128)S(1)} %get-tuple-element.32.c_ref), custom_call_target="tpu_custom_call" | custom-call | tf_op jit(solution)/shard_map/finish/pallas_call | solution.py:353
  (38 shorter events, 0.2 us)
Async XLA Ops:
  0.6 34.1 %copy-start = (f32[1,1,4,512]{3,2,1,0:T(4,128)S(1)}, f32[1,1,4,512]{3,2,1,0:T(4,128)}, u32[]{:S(2)}) copy-start(f32[1,1,4,512]{3,2,1,0:T(4,128)} %param.19) | copy-start | bytes 24580
  0.6 14.4 %copy-start.2 = (bf16[1,1024,512]{2,1,0:T(8,128)(2,1)S(1)}, bf16[1,1024,512]{2,1,0:T(8,128)(2,1)}, u32[]{:S(2)}) copy-start(bf16[1,1024,512]{2,1,0:T(8,128)(2,1)} %param.18) | copy-start | bytes 3145732
  0.7 1.3 %copy-start.3 = (f32[1,1024,240]{1,2,0:T(8,128)S(1)}, f32[1,1024,240]{1,2,0:T(8,128)}, u32[]{:S(2)}) copy-start(f32[1,1024,240]{1,2,0:T(8,128)} %param.10) | copy-start | bytes 2949124
  1.9 3.3 %copy-start.12 = (s32[1,3072,1]{1,2,0:T(1,128)S(1)}, s32[1,3072,1]{1,2,0:T(1,128)}, u32[]{:S(2)}) copy-start(s32[1,3072,1]{1,2,0:T(1,128)} %param.12) | copy-start | bytes 36868
  2.0 13.1 %copy-start.8 = (bf16[240,512]{1,0:T(8,128)(2,1)S(1)}, bf16[240,512]{1,0:T(8,128)(2,1)}, u32[]{:S(2)}) copy-start(bf16[240,512]{1,0:T(8,128)(2,1)} %out_ref.3) | copy-start | bytes 737284
  2.2 15.6 %collective-permute-start = (bf16[1024,256]{1,0:T(8,128)(2,1)S(1)}, bf16[1024,256]{1,0:T(8,128)(2,1)S(1)}, u32[]{:S(2)}, u32[]{:S(2)}) collective-permute-start(bf16[1024,256]{1,0:T(8,128)(2,1)S(1)} %code_rows.1.coded_ref.rest_3_.rest_0_), channel_id=1, source_target_pairs={{0,2},{1,3},{2,0},{3,1},{4,6},{5,7},{6,4},{7,5},{8,10},{9,11},{10,... | collective-permute-start | bytes 1572872 | tf_op jit(solution)/shard_map/ppermute | solution.py:364
  5.3 0.7 copy-start.13
  11.7 0.7 copy-start.11
  12.4 4.9 %collective-permute-start.1 = (s32[6153]{0:T(1024)S(1)}, s32[6153]{0:T(1024)S(1)}, u32[]{:S(2)}, u32[]{:S(2)}) collective-permute-start(s32[6153]{0:T(1024)S(1)} %pad_add_fusion), channel_id=1, source_target_pairs={{0,4},{1,5},{2,6},{3,7},{4,0},{5,1},{6,2},{7,3},{8,12},{9,13},{10,... | collective-permute-start | bytes 73844 | tf_op jit(solution)/shard_map/ppermute | solution.py:364
  15.0 3.3 %collective-permute-start.4 = (bf16[1024,256]{1,0:T(8,128)(2,1)S(1)}, bf16[1024,256]{1,0:T(8,128)(2,1)}, u32[]{:S(2)}, u32[]{:S(2)}) collective-permute-start(bf16[1024,256]{1,0:T(8,128)(2,1)S(1)} %code_rows.1.coded_ref.rest_3_.rest_0_), channel_id=1, source_target_pairs={{0,1},{1,0},{2,3},{3,2},{4,5},{5,4},{6,7},{7,6},{8,9},{9,8},{10,11... | collective-permute-start | bytes 1572872 | tf_op jit(solution)/shard_map/ppermute | solution.py:364
  15.0 4.8 %copy-start.1 = (bf16[8,240,240]{2,1,0:T(8,128)(2,1)S(1)}, bf16[8,240,240]{2,1,0:T(8,128)(2,1)}, u32[]{:S(2)}) copy-start(bf16[8,240,240]{2,1,0:T(8,128)(2,1)} %tables_ref.9) | copy-start | bytes 2764804
  17.8 8.4 %copy-start.6 = (bf16[1024,256]{1,0:T(8,128)(2,1)}, bf16[1024,256]{1,0:T(8,128)(2,1)S(1)}, u32[]{:S(2)}) copy-start(bf16[1024,256]{1,0:T(8,128)(2,1)S(1)} %collective-permute-done.rest_5_.rest_2_) | copy-start | bytes 1572868
  17.8 2.0 %collective-permute-start.5 = (bf16[1024,256]{1,0:T(8,128)(2,1)S(1)}, bf16[1024,256]{1,0:T(8,128)(2,1)}, u32[]{:S(2)}, u32[]{:S(2)}) collective-permute-start(bf16[1024,256]{1,0:T(8,128)(2,1)S(1)} %collective-permute-done.rest_5_.rest_2_), channel_id=1, source_target_pairs={{0,1},{1,0},{2,3},{3,2},{4,5},{5,4},{6,7},{7,6},{8,9},{9,8},{10,11... | collective-permute-start | bytes 1572872 | tf_op jit(solution)/shard_map/ppermute | solution.py:364
  26.2 26.5 %collective-permute-start.6 = (bf16[1024,256]{1,0:T(8,128)(2,1)}, bf16[1024,256]{1,0:T(8,128)(2,1)}, u32[]{:S(2)}, u32[]{:S(2)}) collective-permute-start(bf16[1024,256]{1,0:T(8,128)(2,1)} %terms_all.1), channel_id=1, source_target_pairs={{0,4},{1,5},{2,6},{3,7},{4,0},{5,1},{6,2},{7,3},{8,12},{9,13},{10,... | collective-permute-start | bytes 1572872 | tf_op jit(solution)/shard_map/ppermute | solution.py:364
  28.9 7.4 %copy-start.10 = (bf16[512,240]{0,1:T(8,128)(2,1)S(1)}, bf16[512,240]{0,1:T(8,128)(2,1)}, u32[]{:S(2)}) copy-start(bf16[512,240]{0,1:T(8,128)(2,1)} %param.17) | copy-start | bytes 737284
  28.9 3.6 %collective-permute-start.2 = (f32[1,512]{1,0:T(1,128)S(1)}, f32[1,512]{1,0:T(1,128)S(1)}, u32[]{:S(2)}, u32[]{:S(2)}) collective-permute-start(f32[1,512]{1,0:T(1,128)S(1)} %gather_wave.2), channel_id=1, source_target_pairs={{0,8},{8,0},{16,24},{24,16},{1,9},{9,1},{17,25},{25,17},{2,10},{10... | collective-permute-start | bytes 6152 | tf_op jit(solution)/shard_map/ppermute | solution.py:383
  32.5 3.7 %collective-permute-start.3 = (f32[2,512]{1,0:T(2,128)S(1)}, f32[2,512]{1,0:T(2,128)S(1)}, u32[]{:S(2)}, u32[]{:S(2)}) collective-permute-start(f32[2,512]{1,0:T(2,128)S(1)} %pad_maximum_fusion), channel_id=1, source_target_pairs={{0,16},{8,24},{16,0},{24,8},{1,17},{9,25},{17,1},{25,9},{2,18},{10... | collective-permute-start | bytes 12296 | tf_op jit(solution)/shard_map/ppermute | solution.py:383
  36.2 1.0 copy-start.7
  37.3 15.5 %copy-start.4 = (f32[1,1024,240]{1,2,0:T(8,128)S(1)}, f32[1,1024,240]{1,2,0:T(8,128)}, u32[]{:S(2)}) copy-start(f32[1,1024,240]{1,2,0:T(8,128)} %param.10) | copy-start | bytes 2949124
  37.3 15.5 %copy-start.5 = (f32[1,1024,240]{1,2,0:T(8,128)S(1)}, f32[1,1024,240]{1,2,0:T(8,128)}, u32[]{:S(2)}) copy-start(f32[1,1024,240]{1,2,0:T(8,128)} %param.11) | copy-start | bytes 2949124
  54.5 1.9 %collective-permute-start.9 = (bf16[1024,256]{1,0:T(8,128)(2,1)S(1)}, bf16[1024,256]{1,0:T(8,128)(2,1)S(1)}, u32[]{:S(2)}, u32[]{:S(2)}) collective-permute-start(bf16[1024,256]{1,0:T(8,128)(2,1)S(1)} %get-tuple-element.24.coded_ref.rest_0_.rest_3_), channel_id=1, source_target_pairs={{0,1},{1,0},{2,3},{3,2},{4,5},{5,4},{6,7},{7,6},{8,9},{9,8},{10,11... | collective-permute-start | bytes 1572872 | tf_op jit(solution)/shard_map/ppermute | solution.py:364
  54.6 14.3 %collective-permute-start.10 = (bf16[1024,256]{1,0:T(8,128)(2,1)S(1)}, bf16[1024,256]{1,0:T(8,128)(2,1)S(1)}, u32[]{:S(2)}, u32[]{:S(2)}) collective-permute-start(bf16[1024,256]{1,0:T(8,128)(2,1)S(1)} %get-tuple-element.24.coded_ref.rest_0_.rest_3_), channel_id=1, source_target_pairs={{0,2},{1,3},{2,0},{3,1},{4,6},{5,7},{6,4},{7,5},{8,10},{9,11},{10,... | collective-permute-start | bytes 1572872 | tf_op jit(solution)/shard_map/ppermute | solution.py:364
  68.9 1.9 %collective-permute-start.11 = (bf16[1024,256]{1,0:T(8,128)(2,1)S(1)}, bf16[1024,256]{1,0:T(8,128)(2,1)S(1)}, u32[]{:S(2)}, u32[]{:S(2)}) collective-permute-start(bf16[1024,256]{1,0:T(8,128)(2,1)S(1)} %collective-permute-done.10.rest_5_.rest_2_), channel_id=1, source_target_pairs={{0,1},{1,0},{2,3},{3,2},{4,5},{5,4},{6,7},{7,6},{8,9},{9,8},{10,11... | collective-permute-start | bytes 1572872 | tf_op jit(solution)/shard_map/ppermute | solution.py:364
  70.8 6.9 %copy-start.9 = (bf16[240,512]{1,0:T(8,128)(2,1)S(1)}, bf16[240,512]{1,0:T(8,128)(2,1)}, u32[]{:S(2)}) copy-start(bf16[240,512]{1,0:T(8,128)(2,1)} %out_ref.3) | copy-start | bytes 737284
  75.1 26.1 %collective-permute-start.12 = (bf16[1024,256]{1,0:T(8,128)(2,1)S(1)}, bf16[1024,256]{1,0:T(8,128)(2,1)S(1)}, u32[]{:S(2)}, u32[]{:S(2)}) collective-permute-start(bf16[1024,256]{1,0:T(8,128)(2,1)S(1)} %terms_rest.1), channel_id=1, source_target_pairs={{0,4},{1,5},{2,6},{3,7},{4,0},{5,1},{6,2},{7,3},{8,12},{9,13},{10,... | collective-permute-start | bytes 1572872 | tf_op jit(solution)/shard_map/ppermute | solution.py:364
  79.3 3.7 %collective-permute-start.7 = (f32[1,512]{1,0:T(1,128)S(1)}, f32[1,512]{1,0:T(1,128)S(1)}, u32[]{:S(2)}, u32[]{:S(2)}) collective-permute-start(f32[1,512]{1,0:T(1,128)S(1)} %gather_wave.3), channel_id=1, source_target_pairs={{0,8},{8,0},{16,24},{24,16},{1,9},{9,1},{17,25},{25,17},{2,10},{10... | collective-permute-start | bytes 6152 | tf_op jit(solution)/shard_map/ppermute | solution.py:383
  82.9 3.7 %collective-permute-start.8 = (f32[2,512]{1,0:T(2,128)S(1)}, f32[2,512]{1,0:T(2,128)S(1)}, u32[]{:S(2)}, u32[]{:S(2)}) collective-permute-start(f32[2,512]{1,0:T(2,128)S(1)} %pad_maximum_fusion.1), channel_id=1, source_target_pairs={{0,16},{8,24},{16,0},{24,8},{1,17},{9,25},{17,1},{25,9},{2,18},{10... | collective-permute-start | bytes 12296 | tf_op jit(solution)/shard_map/ppermute | solution.py:383

commit v6 on v5

v6 whole, which is shorter than its diff:
```python
import functools

import jax
import jax.numpy as jnp
import numpy as np
from jax import lax
from jax.experimental import pallas as pl
from jax.experimental.pallas import tpu as pltpu
from jax.sharding import PartitionSpec as P

epsilon = 1e-06
LANES = 128
QUAD = 4
CHUNK = 512
BATCH = 32
VMEM_LIMIT = 16 * 2**20
COST = pl.CostEstimate(flops=1, bytes_accessed=1, transcendentals=0)


def cosine_coefficients():
    top = 3.1416**2
    nodes = (np.cos((np.arange(400) + 0.5) * np.pi / 400) + 1.0) * top / 2.0
    fit = np.polynomial.chebyshev.Chebyshev.fit(nodes, np.cos(np.sqrt(nodes)), 8, domain=[0.0, top])
    return [float(c) for c in fit.convert(kind=np.polynomial.Polynomial).coef]


COS = cosine_coefficients()


def cosine(angle):
    square = angle * angle
    value = jnp.full_like(square, COS[-1])
    for coef in COS[-2::-1]:
        value = value * square + coef
    return value


def whole(memory=pltpu.VMEM):
    return pl.BlockSpec(memory_space=memory)


def params():
    return pltpu.CompilerParams(vmem_limit_bytes=VMEM_LIMIT)


def pad_lanes(value, width):
    rows, cols = value.shape
    return jnp.concatenate([value, jnp.zeros((rows, width - cols), value.dtype)], axis=1)


def code_kernel(field_ref, *coded):
    coefs = field_ref.shape[0]
    start = 0
    for coded_ref in coded:
        rows, width = coded_ref.shape
        part = field_ref[:, pl.ds(start, rows)]
        part = jnp.concatenate([part, jnp.zeros((width - coefs, rows), part.dtype)], axis=0)
        coded_ref[...] = part.T.astype(jnp.bfloat16)
        start += rows


def code(field_t, width, cuts):
    return pl.pallas_call(
        code_kernel,
        out_shape=tuple(
            jax.ShapeDtypeStruct((stop - start, width), jnp.bfloat16) for start, stop in cuts
        ),
        in_specs=[whole()],
        out_specs=(whole(),) * len(cuts),
        compiler_params=params(),
        name="code_rows",
    )(field_t)


def wave_kernel(out_ref, angle_ref, *rest):
    *coded, sum_ref = rest
    coefs, samples = out_ref.shape
    total = jnp.zeros((1, samples), jnp.float32)
    start = 0
    for coded_ref in coded:
        rows = coded_ref.shape[0]
        outgoing = jnp.dot(
            coded_ref[...][:, :coefs], out_ref[...], preferred_element_type=jnp.float32
        )
        angle = angle_ref[pl.ds(start, rows), :].astype(jnp.float32)
        total = total + jnp.sum(cosine(angle) * outgoing, axis=0, keepdims=True)
        start += rows
    sum_ref[...] = total


def gather_wave(coded, wave_out, angle):
    samples = angle.shape[1]
    return pl.pallas_call(
        wave_kernel,
        out_shape=jax.ShapeDtypeStruct((1, samples), jnp.float32),
        in_specs=[whole()] * (2 + len(coded)),
        out_specs=whole(),
        compiler_params=params(),
        cost_estimate=COST,
        name="gather_wave",
    )(wave_out, angle, *coded)


def spread_wave(at, incoming_ref, in_ref, angle_ref):
    spread = cosine(angle_ref[at, :].astype(jnp.float32)) * incoming_ref[...]
    return lax.dot_general(
        spread.astype(jnp.bfloat16),
        in_ref[...],
        (((1,), (1,)), ((), ())),
        preferred_element_type=jnp.float32,
    )


def load_rows(source, stands, shards):
    for base, shard in zip(stands, shards, strict=True):
        value = shard[...].astype(jnp.float32)
        rows = value.shape[0]
        source[pl.ds(2 * base, rows, stride=2), :] = value[:, :LANES]
        source[pl.ds(2 * base + 1, rows, stride=2), :] = value[:, LANES:]


def pick_rows(source_ref, target_ref, bound_ref, segments, source, picked):
    def move(places):
        got = [source[pl.ds(pl.multiple_of(source_ref[n], 2), 2), :] for n in places]
        for n, row in zip(places, got, strict=True):
            picked[pl.ds(pl.multiple_of(target_ref[n], 2), 2), :] = row

    for first, last in segments:
        low, high = bound_ref[first], bound_ref[last]
        full = (high - low) // BATCH

        def step(index, carry, low=low):
            move([low + index * BATCH + k for k in range(BATCH)])
            return carry

        lax.fori_loop(0, full, step, 0)

        @pl.when(low + full * BATCH < high)
        def _(low=low, high=high, full=full):
            move([jnp.minimum(low + full * BATCH + k, high - 1) for k in range(BATCH)])


def translate(start, size, picked, table_ref, tables_ref):
    at = pl.ds(start, size)
    per_row = table_ref.shape[1]
    coefs = tables_ref.shape[1]
    stride = 2 * per_row
    halves = [
        [
            picked[pl.ds(start * stride + 2 * k + h, size, stride=stride), :].astype(jnp.bfloat16)
            for h in range(2)
        ]
        for k in range(per_row)
    ]
    names = table_ref[at, :].astype(jnp.float32)
    named = [
        jnp.broadcast_to(names[:, k : k + 1], (size, LANES)).astype(jnp.bfloat16)
        for k in range(per_row)
    ]
    zero = jnp.zeros((size, LANES), jnp.bfloat16)
    total = jnp.zeros((size, coefs), jnp.float32)
    for t in range(tables_ref.shape[0]):
        chosen = [named[k] == jnp.bfloat16(t) for k in range(per_row)]
        mixed = []
        for h in range(2):
            value = jnp.where(chosen[0], halves[0][h], zero)
            for k in range(1, per_row):
                value = value + jnp.where(chosen[k], halves[k][h], zero)
            mixed.append(value)
        total = total + jnp.dot(
            jnp.concatenate(mixed, axis=1)[:, :coefs],
            tables_ref[t],
            preferred_element_type=jnp.float32,
        )
    return total


def terms_kernel(
    kind, cut, segments, stands, source_ref, target_ref, bound_ref, table_ref, tables_ref, *rest
):
    *rest, source, picked = rest
    if kind == "own":
        *rest, done_ref = rest
        done_ref[...] = jnp.zeros_like(done_ref)
    *rest, out_ref = rest
    extra, shards = rest[: -len(stands)], rest[-len(stands) :]
    start, stop = cut
    load_rows(source, stands, shards)
    wide = 2 * table_ref.shape[1]
    cleared = pl.ds(start * wide, (stop - start) * wide)
    picked[cleared, :] = jnp.zeros(((stop - start) * wide, LANES), jnp.float32)
    pick_rows(source_ref, target_ref, bound_ref, segments, source, picked)
    size = min(CHUNK, stop - start)
    while (stop - start) % size:
        size += LANES
    for place in range(start, stop, size):
        at = pl.ds(place, size)
        total = translate(place, size, picked, table_ref, tables_ref)
        if kind == "near":
            total = total + spread_wave(at, *extra)
        if kind == "rest":
            total = total + extra[0][at, :]
        if kind in ("rest", "all"):
            total = pad_lanes(total, out_ref.shape[1]).astype(jnp.bfloat16)
        out_ref[pl.ds(place - start, size), :] = total


def terms(kind, cut, segments, blocks, requests, tables, *extra):
    source, target, bounds, table_ids = requests
    stands, shards = zip(*blocks, strict=True)
    rows, width = table_ids.shape[0], shards[0].shape[1]
    size = cut[1] - cut[0]
    if kind in ("near", "own"):
        outs = [jax.ShapeDtypeStruct((size, tables.shape[1]), jnp.float32)]
    else:
        outs = [jax.ShapeDtypeStruct((size, width), jnp.bfloat16)]
    if kind == "own":
        outs.append(jax.ShapeDtypeStruct((8, LANES), jnp.float32))
    return pl.pallas_call(
        functools.partial(terms_kernel, kind, cut, segments, stands),
        out_shape=tuple(outs),
        in_specs=[whole(pltpu.SMEM)] * 3 + [whole()] * (2 + len(extra) + len(shards)),
        out_specs=(whole(),) * len(outs),
        scratch_shapes=[
            pltpu.VMEM((2 * QUAD * rows, LANES), jnp.float32),
            pltpu.VMEM((2 * source.shape[0], LANES), jnp.float32),
        ],
        compiler_params=params(),
        cost_estimate=COST,
        name="terms_" + kind,
    )(source, target, bounds, table_ids, tables, *extra, *shards)


def join_kernel(cuts, count, base_ref, mie_ref, x_ref, sums_in_ref, *rest):
    served, rest = rest[: count * len(cuts)], rest[count * len(cuts) :]
    second = cuts[0][1] < cuts[-1][1]
    if second:
        old, rest = rest[: len(cuts)], rest[len(cuts) :]
    image_ref, *coded, sums_ref = rest
    coefs = base_ref.shape[1]
    width = served[0].shape[1]
    totals = [jnp.zeros((1, 1), jnp.float32)] * 3

    def dot(a, b):
        return jnp.sum(jnp.sum(a * b, axis=0, keepdims=True), axis=1, keepdims=True)

    for k, (start, stop) in enumerate(cuts):
        at = pl.ds(start, stop - start)
        here = served[k * count : (k + 1) * count]
        far_rows = here[0][...].astype(jnp.float32)
        for other in here[1:]:
            far_rows = far_rows + other[...].astype(jnp.float32)
        image = pad_lanes(base_ref[at, :] + far_rows[:, :coefs], width).T[:coefs, :]
        image = mie_ref[:, at] * image
        image_ref[:, pl.ds(start - cuts[0][0], stop - start)] = image
        x = x_ref[:, at]
        if second:
            new = [dot(x, image), dot(old[k][...], image), dot(image, image)]
        else:
            wide = jnp.concatenate([image, jnp.zeros((width - coefs, stop - start), image.dtype)], axis=0)
            coded[0][...] = wide.T.astype(jnp.bfloat16)
            new = [dot(x, image), dot(x, x), dot(image, image)]
        totals = [a + b for a, b in zip(totals, new, strict=True)]
    lane = lax.broadcasted_iota(jnp.int32, (1, LANES), 1)
    packed = sums_in_ref[...]
    for k, total in enumerate(totals):
        packed = packed + jnp.where(lane == k + (3 if second else 0), total, 0.0)
    sums_ref[...] = jnp.broadcast_to(packed, sums_ref.shape)


def join(cuts, base, mie_t, x_t, sums, served, old=(), devices=1):
    rows, coefs = base.shape
    size = cuts[-1][1] - cuts[0][0]
    outs = [jax.ShapeDtypeStruct((coefs, size), jnp.float32)]
    if not old:
        outs.append(jax.ShapeDtypeStruct((size, served[0].shape[1]), jnp.bfloat16))
    outs.append(jax.ShapeDtypeStruct((devices, LANES), jnp.float32))
    return pl.pallas_call(
        functools.partial(join_kernel, cuts, len(served) // len(cuts)),
        out_shape=tuple(outs),
        in_specs=[whole()] * (4 + len(served) + len(old)),
        out_specs=(whole(),) * len(outs),
        compiler_params=params(),
        name="join_second" if old else "join_first",
    )(base, mie_t, x_t, sums, *served, *old)


def finish_kernel(sums_ref, x_ref, c_ref, *rest):
    *parts, solution_ref, residual_ref, hess_ref = rest
    sums = jnp.sum(sums_ref[...], axis=0, keepdims=True)
    xb, xx, bb, xc, bc, cc = [sums[:, k : k + 1] for k in range(6)]
    norm = jnp.sqrt(xx + epsilon)
    inverse = 1.0 / norm
    squared = inverse * inverse
    h11 = (xx - xb) * squared
    g = (xb + epsilon) * squared
    size1 = (g * g * xx - 2.0 * g * xb + bb) * squared
    h21 = jnp.sqrt(jnp.maximum(size1, 0.0) + epsilon)
    q = inverse / h21
    v11 = xx * squared
    v12 = q * inverse * (g * xx - xb)
    v22 = size1 / (h21 * h21)
    p1 = q * inverse * (g * xb - xc)
    p2 = q * q * (g * g * xb - g * xc - g * bb + bc)
    pp = q * q * (g * g * bb - 2.0 * g * bc + cc)
    h12 = v12 - p1
    h22 = v22 - p2
    rest = 1.0 - h22
    size2 = (
        rest * rest * v22
        + h12 * h12 * v11
        + pp
        - 2.0 * rest * h12 * v12
        - 2.0 * rest * p2
        + 2.0 * h12 * p1
    )
    h32 = jnp.sqrt(jnp.maximum(size2, 0.0) + epsilon)
    gram00 = h11 * h11 + h21 * h21
    gram01 = h11 * h12 + h21 * h22
    gram11 = h12 * h12 + h22 * h22 + h32 * h32
    rhs0, rhs1 = norm * h11, norm * h12
    det = gram00 * gram11 - gram01 * gram01
    a1 = (gram11 * rhs0 - gram01 * rhs1) / det * inverse
    a2 = (gram00 * rhs1 - gram01 * rhs0) / det * q
    start = 0
    for b_ref in parts:
        at = pl.ds(start, b_ref.shape[1])
        x, b, c = x_ref[:, at], b_ref[...], c_ref[:, at]
        solution_ref[:, at] = (a1 + a2 * g) * x - a2 * b
        residual_ref[:, at] = (1.0 - a1 - a2 * g) * x + (a1 + a2 * (1.0 + g)) * b - a2 * c
        start += b_ref.shape[1]
    hess_ref[0:1, 0:1] = h11
    hess_ref[0:1, 1:2] = h21
    hess_ref[0:1, 2:3] = jnp.zeros_like(h11)
    hess_ref[1:2, 0:1] = h12
    hess_ref[1:2, 1:2] = h22
    hess_ref[1:2, 2:3] = h32


def finish(sums, x_t, c_t, parts):
    field = jax.ShapeDtypeStruct(x_t.shape, jnp.float32)
    return pl.pallas_call(
        finish_kernel,
        out_shape=(field, field, jax.ShapeDtypeStruct((2, 3), jnp.float32)),
        in_specs=[whole()] * (3 + len(parts)),
        out_specs=(whole(),) * 3,
        compiler_params=params(),
        name="finish",
    )(sums, x_t, c_t, *parts)


def flip(block, bits):
    return lax.ppermute(block, "grp", [(i, i ^ bits) for i in range(lax.axis_size("grp"))])


def once(*values):
    return lax.optimization_barrier(values)


def wave_swaps(waves, count):
    blocks = lax.axis_size("blk")
    while waves.shape[0] < min(count, blocks):
        bits = waves.shape[0]
        moved = lax.ppermute(waves, "blk", [(i, i ^ bits) for i in range(blocks)])
        waves = jnp.concatenate([waves, moved], axis=0)
    return waves


def body(
    incident,
    mie_coef,
    owner_dev,
    near_row,
    table_id,
    tables,
    wave_out,
    wave_in,
    plane_angle,
    far_trans,
):
    x = incident[0]
    mie_t = mie_coef[0].T
    angle = plane_angle[0]
    rows, coefs = x.shape
    width = -(-coefs // LANES) * LANES
    group = lax.axis_size("grp")
    devices = group * lax.axis_size("blk")
    tables_count = tables.shape[0]
    wave_in_t = wave_in.T
    x_t = x.T

    apart = owner_dev[0, :, 0] ^ lax.axis_index("grp")
    count = apart.shape[0]
    bits = (count - 1).bit_length()
    number = jnp.arange(count, dtype=jnp.int32)
    cuts = ((0, rows * 5 // 8), (rows * 5 // 8, rows))
    kind = jnp.where(number < cuts[0][1] * (count // rows), 0, group) + apart
    listed = jnp.sort(((kind * rows + near_row[0]) << bits) | number)
    bounds = jnp.arange(2 * group + 1, dtype=jnp.int32)
    bounds = jnp.sum((kind[None, :] < bounds[:, None]).astype(jnp.int32), axis=1)
    others = range(1, group // QUAD)

    def requests_of(message):
        word = message[:count]
        names = message[count : 2 * count].astype(jnp.bfloat16).reshape(rows, -1)
        source = 2 * ((word >> bits) % (QUAD * rows))
        return source, 2 * (word & ((1 << bits) - 1)), message[2 * count :], names

    message = jnp.concatenate([listed, table_id[0], bounds])
    asked = [flip(message, QUAD * j) for j in others]
    blocks = lax.axis_size("blk")
    turns = jnp.arange(blocks, dtype=jnp.int32)
    weights = far_trans[0, 0][turns ^ lax.axis_index("blk")]
    weights = jnp.where(turns[:, None] > 0, weights, 0.0)

    def incoming_of(waves):
        waves = wave_swaps(waves, blocks)
        return jnp.sum(weights * waves, axis=0, keepdims=True)

    def placed(first, *fields):
        return [
            ((first + place) * rows + start, block)
            for place, field in enumerate(fields)
            for (start, _), block in zip(cuts, field, strict=True)
        ]

    def near_of(shards, incoming):
        segments = ((0, QUAD), (group, group + QUAD))
        return terms("near", (0, rows), segments, shards, local, tables, incoming, wave_in_t, angle)[0]

    def swapped(blocks, bits):
        return [flip(block, bits) for block in blocks]

    coded = code(x_t, width, cuts)
    across, same = swapped(coded, 2), swapped(coded, 1)
    waves = gather_wave(coded, wave_out, angle)
    *across, waves, asked = once(*across, waves, asked)
    asked = [requests_of(words) for words in asked]
    local = requests_of(message)
    beyond = swapped(across, 1)
    shards = placed(0, coded, same, across, beyond)
    served = [
        [
            flip(
                terms(
                    "all",
                    cut,
                    ((part * group + QUAD * j, part * group + QUAD * j + QUAD),),
                    shards,
                    words,
                    tables,
                )[0],
                QUAD * j,
            )
            for j, words in zip(others, asked, strict=True)
        ]
        for part, cut in enumerate(cuts)
    ]
    base = near_of(shards, incoming_of(waves))
    b_t, coded, sums = [], [], jnp.zeros((1, LANES), jnp.float32)
    for cut, arrays in zip(cuts, served, strict=True):
        image, block, sums = join((cut,), base, mie_t, x_t, sums, arrays)
        b_t.append(image)
        coded.append(block)

    across, same = swapped(coded, 2), swapped(coded, 1)
    shards = placed(0, coded, same)
    own = [
        terms(
            "own",
            (0, rows),
            ((QUAD * j, QUAD * j + 2), (group + QUAD * j, group + QUAD * j + 2)),
            shards,
            words,
            tables,
        )
        for j, words in zip(others, asked, strict=True)
    ]
    *across, done = once(*across, [done for _, done in own])
    beyond = swapped(across, 1)
    shards = placed(2, across, beyond)
    served = [
        flip(
            terms(
                "rest",
                cut,
                ((part * group + QUAD * j + 2, part * group + QUAD * j + 4),),
                shards,
                words,
                tables,
                sums_here,
                token,
            )[0],
            QUAD * j,
        )
        for part, cut in enumerate(cuts)
        for j, words, (sums_here, _), token in zip(others, asked, own, done, strict=True)
    ]
    shards = placed(0, coded, same, across, beyond)
    base = near_of(shards, incoming_of(gather_wave(coded, wave_out, angle)))
    c_t, sums = join(cuts, base, mie_t, x_t, sums, served, b_t, devices)
    sums = lax.all_to_all(sums, ("blk", "grp"), 0, 0, tiled=True)
    solution_t, residual_t, hess_t = finish(sums, x_t, c_t, b_t)
    return solution_t.T[None], residual_t.T[None], hess_t.T


def solution(mesh):
    return jax.shard_map(
        body,
        mesh=mesh,
        in_specs=(
            P("blk", "grp", None),
            P("blk", "grp", None),
            P("blk", "grp", None),
            P("blk", "grp"),
            P("blk", "grp"),
            P(),
            P(),
            P(),
            P("blk", "grp", None),
            P("blk", "grp", None, None),
        ),
        out_specs=(P("blk", "grp", None), P("blk", "grp", None), P()),
        check_vma=False,
    )
```

time: 117 us -> 112 us (0.957)
  waiting for transfers between devices: 37.8 us -> 23.5 us
  other arithmetic: 6.18 us -> 11.9 us
  Pallas kernels: 36.2 us -> 40.8 us
  blocking collectives: 12.5 us -> 9.61 us
    ppermute x9 -> x17, waiting for transfers between devices: 30.4 us -> 21.4 us  [flip(): lax.ppermute(block, 'grp', [(i, i ^ bits) for i in range(lax.axis_size('g...]
    ppermute x4, waiting for transfers between devices: 7.35 us -> 2.04 us  [wave_swaps(): moved = lax.ppermute(waves, 'blk', [(i, i ^ bits) for i in range(blocks)])]
    pallas_call x8 -> x11, Pallas kernels: 30.9 us -> 35.8 us  [the longest x7 33.3 us: terms(): pl.pallas_call(functools.partial(terms_kernel, kind, cut, segments, stand...]
    all_to_all x1, blocking collectives: 12.5 us -> 9.61 us  [body(): sums = lax.all_to_all(sums, ('blk', 'grp'), 0, 0, tiled=True)]
    ppermute x9 -> x17, starting transfers between devices: 11.7 us -> 13.7 us  [flip(): lax.ppermute(block, 'grp', [(i, i ^ bits) for i in range(lax.axis_size('g...]
    unnamed x28 -> x26, local copies, waits for them, and re-layouts: 3.63 us -> 2.2 us
  transfers between devices with their start and end apart: 13 -> 21, of which waited for: 12 -> 7; matrix products, arithmetic and copies ran while one was open for 7% -> 13% of each run, Pallas kernels for 18% -> 31%
where the time goes in v6:
time: 112 us; the launch traced here: 111 us
  Pallas kernels  40.8 us (36%)
  waiting for transfers between devices  23.5 us (21%)
  starting transfers between devices  19 us (17%)
  other arithmetic  11.9 us (11%)
  blocking collectives  9.61 us (9%)
  local copies, waits for them, and re-layouts  5.13 us (5%)
    pallas_call x7, Pallas kernels, terms(): pl.pallas_call(functools.partial(terms_kernel, kind, cut, segments, stand...  33.3 us
    ppermute x17, waiting for transfers between devices, flip(): lax.ppermute(block, 'grp', [(i, i ^ bits) for i in range(lax.axis_size('g...  21.4 us
    ppermute x17, starting transfers between devices, flip(): lax.ppermute(block, 'grp', [(i, i ^ bits) for i in range(lax.axis_size('g...  13.7 us
    all_to_all x1, blocking collectives, body(): sums = lax.all_to_all(sums, ('blk', 'grp'), 0, 0, tiled=True)  9.61 us
    sort x1, other arithmetic, body(): listed = jnp.sort(kind * rows + near_row[0] << bits | number)  5.75 us
    ppermute x4, starting transfers between devices, wave_swaps(): moved = lax.ppermute(waves, 'blk', [(i, i ^ bits) for i in range(blocks)])  5.33 us
    pallas_call x2, Pallas kernels, gather_wave(): pl.pallas_call(wave_kernel, out_shape=jax.ShapeDtypeStruct((1, samples),...  2.95 us
    pallas_call x3, Pallas kernels, join(): pl.pallas_call(functools.partial(join_kernel, cuts, len(served) // len(cu...  2.31 us
  transfers between devices with their start and end apart: 21, of which 7 were waited for; matrix products, arithmetic and copies ran while one was open for 13% of the time, Pallas kernels for 31%

profile of v6, /device:TPU:0, one launch (start us, length us, event | category | flops | bytes accessed | tf_op | source)
XLA Modules:
  0.0 110.8 jit_solution(17384023292850165679)
XLA Ops:
  0.7 1.2 %copy-done.2 = f32[1,1024,240]{1,2,0:T(8,128)S(1)} copy-done((f32[1,1024,240]{1,2,0:T(8,128)S(1)}, f32[1,1024,240]{1,2,0:T(8,128)}, u32[]{:S(2)}) %copy-start.2) | copy-done | bytes 983064
  2.1 3.1 %collective-permute-start = (bf16[640,256]{1,0:T(8,128)(2,1)S(1)}, bf16[640,256]{1,0:T(8,128)(2,1)S(1)}, u32[]{:S(2)}, u32[]{:S(2)}) collective-permute-start(bf16[640,256]{1,0:T(8,128)(2,1)S(1)} %get-tuple-element.28.rest_0_.rest_3_), channel_id=1, source_target_pairs={{0,2},{1,3},{2,0},{3,1},{4,6},{5,7},{6,4},{7,5},{8,10},{9,11},{10,... | collective-permute-start | bytes 983048 | tf_op jit(solution)/shard_map/ppermute | solution.py:353
  5.7 0.7 broadcast_xor_fusion
  6.4 0.7 select_add_fusion
  7.3 5.8 %sort.15 = (s32[3072]{0:T(1024)S(1)}, s32[3072]{0:T(1024)}) sort(s32[3072]{0:T(1024)S(1)} %get-tuple-element.54, s32[3072]{0:T(1024)S(1)} %iota.24), dimensions={0}, to_apply=%region_0.1 | sort | flops 36864 | bytes 49152 | tf_op jit(solution)/shard_map/jit(sort)/sort | solution.py:398
  13.0 0.6 pad_add_fusion
  13.6 2.8 %collective-permute-start.2 = (s32[6161]{0:T(1024)}, s32[6161]{0:T(1024)}, u32[]{:S(2)}, u32[]{:S(2)}) collective-permute-start(s32[6161]{0:T(1024)} %pad_add_fusion), channel_id=1, source_target_pairs={{0,4},{1,5},{2,6},{3,7},{4,0},{5,1},{6,2},{7,3},{8,12},{9,13},{10,... | collective-permute-start | bytes 73940 | tf_op jit(solution)/shard_map/ppermute | solution.py:353
  16.4 0.6 convert_reduce_fusion.1
  17.1 0.9 copy-done.7
  18.0 1.5 %gather_wave.2 = f32[1,512]{1,0:T(1,128)S(1)} custom-call(bf16[240,512]{1,0:T(8,128)(2,1)S(1)} %copy-done.7, bf16[1024,512]{1,0:T(8,128)(2,1)S(1)} %bitcast.33, bf16[640,256]{1,0:T(8,128)(2,1)S(1)} %get-tuple-element.28.rest_0_.rest_3_, bf16[384,256]{1,0:T(8,128)(2,1)S(1)} %get-tuple-element.29.rest_1_.rest_4_), custom_call_target="tpu_custom_call" | custom-call | flops 1 | bytes 1 | tf_op jit(solution)/shard_map/gather_wave/pallas_call | solution.py:93
  19.6 0.6 pad_clamp_fusion
  20.2 0.5 collective-permute-start.8
  20.7 1.5 %collective-permute-start.3 = (f32[1,512]{1,0:T(1,128)S(1)}, f32[1,512]{1,0:T(1,128)S(1)}, u32[]{:S(2)}, u32[]{:S(2)}) collective-permute-start(f32[1,512]{1,0:T(1,128)S(1)} %gather_wave.2), channel_id=1, source_target_pairs={{0,8},{8,0},{16,24},{24,16},{1,9},{9,1},{17,25},{25,17},{2,10},{10... | collective-permute-start | bytes 6152 | tf_op jit(solution)/shard_map/ppermute | solution.py:364
  22.2 0.7 slice_convert_fusion
  22.9 0.7 slice.11.bound_ref
  23.6 0.4 convert_element_type.18.table_ref
  24.1 5.1 %terms_all.2 = bf16[640,256]{1,0:T(8,128)(2,1)} custom-call(s32[3072]{0:T(1024)S(1)} %get-tuple-element.52.source_ref, s32[3072]{0:T(1024)S(1)} %get-tuple-element.51.target_ref, s32[17]{0:T(128)S(1)} %slice.11.bound_ref, bf16[1024,3]{1,0:T(8,128)(2,1)S(1)} %convert_element_type.18.table_ref, bf16[8,240,240]{2,1,0:T(8,128)(2,1)S(1)} %copy-done.1, ...), custom_call_target="tpu_custom_call" | custom-call | flops 1 | bytes 1 | tf_op jit(solution)/shard_map/terms_all/pallas_call | solution.py:219
  29.2 1.2 %collective-permute-start.9 = (bf16[640,256]{1,0:T(8,128)(2,1)}, bf16[640,256]{1,0:T(8,128)(2,1)}, u32[]{:S(2)}, u32[]{:S(2)}) collective-permute-start(bf16[640,256]{1,0:T(8,128)(2,1)} %terms_all.2), channel_id=1, source_target_pairs={{0,4},{1,5},{2,6},{3,7},{4,0},{5,1},{6,2},{7,3},{8,12},{9,13},{10,... | collective-permute-start | bytes 983048 | tf_op jit(solution)/shard_map/ppermute | solution.py:353
  30.4 0.6 pad_maximum_fusion
  31.0 1.5 %collective-permute-start.4 = (f32[2,512]{1,0:T(2,128)}, f32[2,512]{1,0:T(2,128)}, u32[]{:S(2)}, u32[]{:S(2)}) collective-permute-start(f32[2,512]{1,0:T(2,128)} %pad_maximum_fusion), channel_id=1, source_target_pairs={{0,16},{8,24},{16,0},{24,8},{1,17},{9,25},{17,1},{25,9},{2,18},{10... | collective-permute-start | bytes 12296 | tf_op jit(solution)/shard_map/ppermute | solution.py:364
  32.5 0.5 iota_compare_fusion.2
  33.0 1.1 %convert_element_type.17.table_ref = bf16[1024,3]{1,0:T(8,128)(2,1)} reshape(bf16[3072]{0:T(1024)(128)(2,1)S(1)} %copy-done.11) | data formatting | bytes 12288 | tf_op jit(solution)/shard_map/convert_element_type | solution.py:405
  34.1 0.7 gather_fusion
  34.8 3.4 %terms_all.3 = bf16[384,256]{1,0:T(8,128)(2,1)S(1)} custom-call(s32[3072]{0:T(1024)S(1)} %get-tuple-element.52.source_ref, s32[3072]{0:T(1024)S(1)} %get-tuple-element.51.target_ref, s32[17]{0:T(128)S(1)} %slice.11.bound_ref, bf16[1024,3]{1,0:T(8,128)(2,1)S(1)} %convert_element_type.18.table_ref, bf16[8,240,240]{2,1,0:T(8,128)(2,1)S(1)} %copy-done.1, ...), custom_call_target="tpu_custom_call" | custom-call | flops 1 | bytes 1 | tf_op jit(solution)/shard_map/terms_all/pallas_call | solution.py:219
  38.3 1.4 %collective-permute-start.10 = (bf16[384,256]{1,0:T(8,128)(2,1)S(1)}, bf16[384,256]{1,0:T(8,128)(2,1)S(1)}, u32[]{:S(2)}, u32[]{:S(2)}) collective-permute-start(bf16[384,256]{1,0:T(8,128)(2,1)S(1)} %terms_all.3), channel_id=1, source_target_pairs={{0,4},{1,5},{2,6},{3,7},{4,0},{5,1},{6,2},{7,3},{8,12},{9,13},{10,... | collective-permute-start | bytes 589832 | tf_op jit(solution)/shard_map/ppermute | solution.py:353
  39.7 0.8 fusion.4
  40.5 7.7 %terms_near.2.base_ref = f32[1024,240]{1,0:T(8,128)S(1)} custom-call(s32[3072]{0:T(1024)S(1)} %get-tuple-element.56.source_ref, s32[3072]{0:T(1024)S(1)} %get-tuple-element.55.target_ref, s32[17]{0:T(128)S(1)} %convert_reduce_fusion.bound_ref, bf16[1024,3]{1,0:T(8,128)(2,1)S(1)} %copy-done.6, bf16[8,240,240]{2,1,0:T(8,128)(2,1)S(1)} %copy-done.1, ...), custom_call_target="tpu_custom_call" | custom-call | flops 1 | bytes 1 | tf_op jit(solution)/shard_map/terms_near/pallas_call | solution.py:219
  48.2 3.9 %collective-permute-done.9.rest_0_ = bf16[640,256]{1,0:T(8,128)(2,1)} collective-permute-done((bf16[640,256]{1,0:T(8,128)(2,1)}, bf16[640,256]{1,0:T(8,128)(2,1)}, u32[]{:S(2)}, u32[]{:S(2)}) %collective-permute-start.9) | collective-permute-done | bytes 327712 | tf_op jit(solution)/shard_map/ppermute | solution.py:353
  52.0 1.5 %join_first.2 = (f32[240,640]{1,0:T(8,128)S(1)}, bf16[640,256]{1,0:T(8,128)(2,1)S(1)}, f32[1,128]{1,0:T(1,128)S(1)}) custom-call(f32[1024,240]{1,0:T(8,128)S(1)} %terms_near.2.base_ref, f32[240,1024]{1,0:T(8,128)S(1)} %bitcast.37, f32[240,1024]{1,0:T(8,128)S(1)} %bitcast.29, f32[1,128]{1,0:T(1,128)S(1)} %broadcast_in_dim.44.sums_in_ref, ...), custom_call_target="tpu_custom_call" | custom-call | tf_op jit(solution)/shard_map/join_first/pallas_call | solution.py:278
  53.6 1.4 %collective-permute-done.10.rest_0_ = bf16[384,256]{1,0:T(8,128)(2,1)S(1)} collective-permute-done((bf16[384,256]{1,0:T(8,128)(2,1)S(1)}, bf16[384,256]{1,0:T(8,128)(2,1)S(1)}, u32[]{:S(2)}, u32[]{:S(2)}) %collective-permute-start.10) | collective-permute-done | bytes 196640 | tf_op jit(solution)/shard_map/ppermute | solution.py:353
  55.5 0.7 collective-permute-start.16
  56.3 0.7 collective-permute-done.14.rest_3_.rest_6_
  56.9 4.2 %terms_own.1 = (f32[1024,240]{1,0:T(8,128)S(1)}, f32[8,128]{1,0:T(8,128)S(1)}) custom-call(s32[3072]{0:T(1024)S(1)} %get-tuple-element.52.source_ref, s32[3072]{0:T(1024)S(1)} %get-tuple-element.51.target_ref, s32[17]{0:T(128)S(1)} %slice.11.bound_ref, bf16[1024,3]{1,0:T(8,128)(2,1)S(1)} %convert_element_type.18.table_ref, ...), custom_call_target="tpu_custom_call" | custom-call | flops 1 | bytes 1 | tf_op jit(solution)/shard_map/terms_own/pallas_call | solution.py:219
  61.1 6.8 %collective-permute-done.16.rest_8_.rest_3_ = bf16[384,256]{1,0:T(8,128)(2,1)S(1)} collective-permute-done((bf16[384,256]{1,0:T(8,128)(2,1)S(1)}, bf16[384,256]{1,0:T(8,128)(2,1)S(1)}, u32[]{:S(2)}, u32[]{:S(2)}) %collective-permute-start.16) | collective-permute-done | bytes 196640 | tf_op jit(solution)/shard_map/ppermute | solution.py:353
  67.9 0.5 collective-permute-start.18
  68.4 1.4 %collective-permute-done.18.rest_10_.rest_5_ = bf16[384,256]{1,0:T(8,128)(2,1)S(1)} collective-permute-done((bf16[384,256]{1,0:T(8,128)(2,1)S(1)}, bf16[384,256]{1,0:T(8,128)(2,1)S(1)}, u32[]{:S(2)}, u32[]{:S(2)}) %collective-permute-start.18) | collective-permute-done | bytes 196640 | tf_op jit(solution)/shard_map/ppermute | solution.py:353
  69.8 3.1 %terms_rest.2 = bf16[640,256]{1,0:T(8,128)(2,1)S(1)} custom-call(s32[3072]{0:T(1024)S(1)} %get-tuple-element.52.source_ref, s32[3072]{0:T(1024)S(1)} %get-tuple-element.51.target_ref, s32[17]{0:T(128)S(1)} %slice.11.bound_ref, bf16[1024,3]{1,0:T(8,128)(2,1)S(1)} %convert_element_type.18.table_ref, bf16[8,240,240]{2,1,0:T(8,128)(2,1)S(1)} %copy-done.1, ...), custom_call_target="tpu_custom_call" | custom-call | flops 1 | bytes 1 | tf_op jit(solution)/shard_map/terms_rest/pallas_call | solution.py:219
  73.1 1.5 %gather_wave.3 = f32[1,512]{1,0:T(1,128)S(1)} custom-call(bf16[240,512]{1,0:T(8,128)(2,1)S(1)} %copy-done.8, bf16[1024,512]{1,0:T(8,128)(2,1)S(1)} %bitcast.35, bf16[640,256]{1,0:T(8,128)(2,1)S(1)} %get-tuple-element.34.rest_0_.rest_3_, bf16[384,256]{1,0:T(8,128)(2,1)S(1)} %get-tuple-element.36.rest_1_.rest_4_), custom_call_target="tpu_custom_call" | custom-call | flops 1 | bytes 1 | tf_op jit(solution)/shard_map/gather_wave/pallas_call | solution.py:93
  74.5 0.7 collective-permute-start.11
  75.3 2.4 %terms_rest.3 = bf16[384,256]{1,0:T(8,128)(2,1)S(1)} custom-call(s32[3072]{0:T(1024)S(1)} %get-tuple-element.52.source_ref, s32[3072]{0:T(1024)S(1)} %get-tuple-element.51.target_ref, s32[17]{0:T(128)S(1)} %slice.11.bound_ref, bf16[1024,3]{1,0:T(8,128)(2,1)S(1)} %convert_element_type.18.table_ref, bf16[8,240,240]{2,1,0:T(8,128)(2,1)S(1)} %copy-done.1, ...), custom_call_target="tpu_custom_call" | custom-call | flops 1 | bytes 1 | tf_op jit(solution)/shard_map/terms_rest/pallas_call | solution.py:219
  77.7 2.6 %collective-permute-start.20 = (bf16[384,256]{1,0:T(8,128)(2,1)S(1)}, bf16[384,256]{1,0:T(8,128)(2,1)S(1)}, u32[]{:S(2)}, u32[]{:S(2)}) collective-permute-start(bf16[384,256]{1,0:T(8,128)(2,1)S(1)} %terms_rest.3), channel_id=1, source_target_pairs={{0,4},{1,5},{2,6},{3,7},{4,0},{5,1},{6,2},{7,3},{8,12},{9,13},{10,... | collective-permute-start | bytes 589832 | tf_op jit(solution)/shard_map/ppermute | solution.py:353
  80.3 1.6 %collective-permute-start.12 = (f32[2,512]{1,0:T(2,128)S(1)}, f32[2,512]{1,0:T(2,128)S(1)}, u32[]{:S(2)}, u32[]{:S(2)}) collective-permute-start(f32[2,512]{1,0:T(2,128)S(1)} %pad_maximum_fusion.1), channel_id=1, source_target_pairs={{0,16},{8,24},{16,0},{24,8},{1,17},{9,25},{17,1},{25,9},{2,18},{10... | collective-permute-start | bytes 12296 | tf_op jit(solution)/shard_map/ppermute | solution.py:364
  82.0 2.0 %collective-permute-done.12 = f32[2,512]{1,0:T(2,128)S(1)} collective-permute-done((f32[2,512]{1,0:T(2,128)S(1)}, f32[2,512]{1,0:T(2,128)S(1)}, u32[]{:S(2)}, u32[]{:S(2)}) %collective-permute-start.12) | collective-permute-done | bytes 4128 | tf_op jit(solution)/shard_map/ppermute | solution.py:364
  84.1 7.3 %terms_near.3.base_ref = f32[1024,240]{1,0:T(8,128)S(1)} custom-call(s32[3072]{0:T(1024)S(1)} %get-tuple-element.56.source_ref, s32[3072]{0:T(1024)S(1)} %get-tuple-element.55.target_ref, s32[17]{0:T(128)S(1)} %convert_reduce_fusion.bound_ref, bf16[1024,3]{1,0:T(8,128)(2,1)S(1)} %copy-done.6, bf16[8,240,240]{2,1,0:T(8,128)(2,1)S(1)} %copy-done.1, ...), custom_call_target="tpu_custom_call" | custom-call | flops 1 | bytes 1 | tf_op jit(solution)/shard_map/terms_near/pallas_call | solution.py:219
  91.4 7.3 %collective-permute-done.20.rest_1_ = bf16[384,256]{1,0:T(8,128)(2,1)S(1)} collective-permute-done((bf16[384,256]{1,0:T(8,128)(2,1)S(1)}, bf16[384,256]{1,0:T(8,128)(2,1)S(1)}, u32[]{:S(2)}, u32[]{:S(2)}) %collective-permute-start.20) | collective-permute-done | bytes 196640 | tf_op jit(solution)/shard_map/ppermute | solution.py:353
  98.7 0.5 join_second.1
  99.2 9.6 %all_to_all.11 = f32[32,1,128]{2,1,0:T(1,128)S(1)} all-to-all(f32[32,1,128]{2,1,0:T(1,128)S(1)} %bitcast.43), channel_id=1, replica_groups=mesh['blk'=4,'grp'=8] {'blk','grp'}, dimensions={0} | all-to-all | bytes 32768 | tf_op jit(solution)/shard_map/all_to_all | solution.py:502
  108.8 2.1 %finish.1 = (f32[240,1024]{1,0:T(8,128)}, f32[240,1024]{1,0:T(8,128)}, f32[2,3]{1,0:T(2,128)}) custom-call(f32[32,128]{1,0:T(8,128)S(1)} %bitcast.42, f32[240,1024]{1,0:T(8,128)S(1)} %bitcast.32, f32[240,1024]{1,0:T(8,128)S(1)} %get-tuple-element.46.c_ref, f32[240,640]{1,0:T(8,128)S(1)} %get-tuple-element.43.rest_2_.rest_0_, ...), custom_call_target="tpu_custom_call" | custom-call | tf_op jit(solution)/shard_map/finish/pallas_call | solution.py:342
  (56 shorter events, 1.8 us)
Async XLA Ops:
  0.6 33.5 %copy-start = (f32[1,1,4,512]{3,2,1,0:T(4,128)S(1)}, f32[1,1,4,512]{3,2,1,0:T(4,128)}, u32[]{:S(2)}) copy-start(f32[1,1,4,512]{3,2,1,0:T(4,128)} %param.19) | copy-start | bytes 24580
  0.6 1.2 %copy-start.2 = (f32[1,1024,240]{1,2,0:T(8,128)S(1)}, f32[1,1024,240]{1,2,0:T(8,128)}, u32[]{:S(2)}) copy-start(f32[1,1024,240]{1,2,0:T(8,128)} %param.10) | copy-start | bytes 2949124
  1.9 15.2 %copy-start.4 = (bf16[1,1024,512]{2,1,0:T(8,128)(2,1)S(1)}, bf16[1,1024,512]{2,1,0:T(8,128)(2,1)}, u32[]{:S(2)}) copy-start(bf16[1,1024,512]{2,1,0:T(8,128)(2,1)} %param.18) | copy-start | bytes 3145732
  2.1 17.4 %collective-permute-start = (bf16[640,256]{1,0:T(8,128)(2,1)S(1)}, bf16[640,256]{1,0:T(8,128)(2,1)S(1)}, u32[]{:S(2)}, u32[]{:S(2)}) collective-permute-start(bf16[640,256]{1,0:T(8,128)(2,1)S(1)} %get-tuple-element.28.rest_0_.rest_3_), channel_id=1, source_target_pairs={{0,2},{1,3},{2,0},{3,1},{4,6},{5,7},{6,4},{7,5},{8,10},{9,11},{10,... | collective-permute-start | bytes 983048 | tf_op jit(solution)/shard_map/ppermute | solution.py:353
  5.2 18.9 %collective-permute-start.5 = (bf16[640,256]{1,0:T(8,128)(2,1)S(1)}, bf16[640,256]{1,0:T(8,128)(2,1)S(1)}, u32[]{:S(2)}, u32[]{:S(2)}) collective-permute-start(bf16[640,256]{1,0:T(8,128)(2,1)S(1)} %get-tuple-element.28.rest_0_.rest_3_), channel_id=1, source_target_pairs={{0,1},{1,0},{2,3},{3,2},{4,5},{5,4},{6,7},{7,6},{8,9},{9,8},{10,11... | collective-permute-start | bytes 983048 | tf_op jit(solution)/shard_map/ppermute | solution.py:353
  5.2 14.3 %collective-permute-start.1 = (bf16[384,256]{1,0:T(8,128)(2,1)S(1)}, bf16[384,256]{1,0:T(8,128)(2,1)}, u32[]{:S(2)}, u32[]{:S(2)}) collective-permute-start(bf16[384,256]{1,0:T(8,128)(2,1)S(1)} %get-tuple-element.29.rest_1_.rest_4_), channel_id=1, source_target_pairs={{0,2},{1,3},{2,0},{3,1},{4,6},{5,7},{6,4},{7,5},{8,10},{9,11},{10,... | collective-permute-start | bytes 589832 | tf_op jit(solution)/shard_map/ppermute | solution.py:353
  5.3 18.7 %collective-permute-start.6 = (bf16[384,256]{1,0:T(8,128)(2,1)S(1)}, bf16[384,256]{1,0:T(8,128)(2,1)}, u32[]{:S(2)}, u32[]{:S(2)}) collective-permute-start(bf16[384,256]{1,0:T(8,128)(2,1)S(1)} %get-tuple-element.29.rest_1_.rest_4_), channel_id=1, source_target_pairs={{0,1},{1,0},{2,3},{3,2},{4,5},{5,4},{6,7},{7,6},{8,9},{9,8},{10,11... | collective-permute-start | bytes 589832 | tf_op jit(solution)/shard_map/ppermute | solution.py:353
  7.3 5.8 %copy-start.10 = (s32[1,3072]{1,0:T(1,128)S(1)}, s32[1,3072]{1,0:T(1,128)}, u32[]{:S(2)}) copy-start(s32[1,3072]{1,0:T(1,128)} %param.14) | copy-start | bytes 36868
  13.6 5.8 %collective-permute-start.2 = (s32[6161]{0:T(1024)}, s32[6161]{0:T(1024)}, u32[]{:S(2)}, u32[]{:S(2)}) collective-permute-start(s32[6161]{0:T(1024)} %pad_add_fusion), channel_id=1, source_target_pairs={{0,4},{1,5},{2,6},{3,7},{4,0},{5,1},{6,2},{7,3},{8,12},{9,13},{10,... | collective-permute-start | bytes 73940 | tf_op jit(solution)/shard_map/ppermute | solution.py:353
  17.1 0.9 copy-start.7
  18.0 6.1 %copy-start.1 = (bf16[8,240,240]{2,1,0:T(8,128)(2,1)S(1)}, bf16[8,240,240]{2,1,0:T(8,128)(2,1)}, u32[]{:S(2)}) copy-start(bf16[8,240,240]{2,1,0:T(8,128)(2,1)} %tables_ref.13) | copy-start | bytes 2764804
  19.5 4.5 %collective-permute-start.7 = (bf16[640,256]{1,0:T(8,128)(2,1)S(1)}, bf16[640,256]{1,0:T(8,128)(2,1)}, u32[]{:S(2)}, u32[]{:S(2)}) collective-permute-start(bf16[640,256]{1,0:T(8,128)(2,1)S(1)} %collective-permute-done.rest_7_.rest_4_), channel_id=1, source_target_pairs={{0,1},{1,0},{2,3},{3,2},{4,5},{5,4},{6,7},{7,6},{8,9},{9,8},{10,11... | collective-permute-start | bytes 983048 | tf_op jit(solution)/shard_map/ppermute | solution.py:353
  20.2 3.9 %collective-permute-start.8 = (bf16[384,256]{1,0:T(8,128)(2,1)}, bf16[384,256]{1,0:T(8,128)(2,1)}, u32[]{:S(2)}, u32[]{:S(2)}) collective-permute-start(bf16[384,256]{1,0:T(8,128)(2,1)} %collective-permute-done.1.rest_8_.rest_5_), channel_id=1, source_target_pairs={{0,1},{1,0},{2,3},{3,2},{4,5},{5,4},{6,7},{7,6},{8,9},{9,8},{10,11... | collective-permute-start | bytes 589832 | tf_op jit(solution)/shard_map/ppermute | solution.py:353
  20.7 9.7 %collective-permute-start.3 = (f32[1,512]{1,0:T(1,128)S(1)}, f32[1,512]{1,0:T(1,128)S(1)}, u32[]{:S(2)}, u32[]{:S(2)}) collective-permute-start(f32[1,512]{1,0:T(1,128)S(1)} %gather_wave.2), channel_id=1, source_target_pairs={{0,8},{8,0},{16,24},{24,16},{1,9},{9,1},{17,25},{25,17},{2,10},{10... | collective-permute-start | bytes 6152 | tf_op jit(solution)/shard_map/ppermute | solution.py:364
  29.2 3.8 %copy-start.11 = (bf16[3072]{0:T(1024)(128)(2,1)S(1)}, bf16[3072]{0:T(1024)(128)(2,1)}, u32[]{:S(2)}) copy-start(bf16[3072]{0:T(1024)(128)(2,1)} %convert_reduce_fusion.1) | copy-start | bytes 18436
  29.2 22.8 %collective-permute-start.9 = (bf16[640,256]{1,0:T(8,128)(2,1)}, bf16[640,256]{1,0:T(8,128)(2,1)}, u32[]{:S(2)}, u32[]{:S(2)}) collective-permute-start(bf16[640,256]{1,0:T(8,128)(2,1)} %terms_all.2), channel_id=1, source_target_pairs={{0,4},{1,5},{2,6},{3,7},{4,0},{5,1},{6,2},{7,3},{8,12},{9,13},{10,... | collective-permute-start | bytes 983048 | tf_op jit(solution)/shard_map/ppermute | solution.py:353
  31.0 8.7 %collective-permute-start.4 = (f32[2,512]{1,0:T(2,128)}, f32[2,512]{1,0:T(2,128)}, u32[]{:S(2)}, u32[]{:S(2)}) collective-permute-start(f32[2,512]{1,0:T(2,128)} %pad_maximum_fusion), channel_id=1, source_target_pairs={{0,16},{8,24},{16,0},{24,8},{1,17},{9,25},{17,1},{25,9},{2,18},{10... | collective-permute-start | bytes 12296 | tf_op jit(solution)/shard_map/ppermute | solution.py:364
  34.8 4.9 %copy-start.12 = (pred[4]{0:T(512)(128)(4,1)S(1)}, pred[4]{0:T(512)(128)(4,1)}, u32[]{:S(2)}) copy-start(pred[4]{0:T(512)(128)(4,1)} %iota_compare_fusion.2) | copy-start | bytes 16
  34.8 5.6 %copy-start.6 = (bf16[1024,3]{1,0:T(8,128)(2,1)S(1)}, bf16[1024,3]{1,0:T(8,128)(2,1)}, u32[]{:S(2)}) copy-start(bf16[1024,3]{1,0:T(8,128)(2,1)} %convert_element_type.17.table_ref) | copy-start | bytes 18436
  34.8 5.6 %copy-start.9 = (bf16[512,240]{0,1:T(8,128)(2,1)S(1)}, bf16[512,240]{0,1:T(8,128)(2,1)}, u32[]{:S(2)}) copy-start(bf16[512,240]{0,1:T(8,128)(2,1)} %param.17) | copy-start | bytes 737284
  38.3 16.8 %collective-permute-start.10 = (bf16[384,256]{1,0:T(8,128)(2,1)S(1)}, bf16[384,256]{1,0:T(8,128)(2,1)S(1)}, u32[]{:S(2)}, u32[]{:S(2)}) collective-permute-start(bf16[384,256]{1,0:T(8,128)(2,1)S(1)} %terms_all.3), channel_id=1, source_target_pairs={{0,4},{1,5},{2,6},{3,7},{4,0},{5,1},{6,2},{7,3},{8,12},{9,13},{10,... | collective-permute-start | bytes 589832 | tf_op jit(solution)/shard_map/ppermute | solution.py:353
  40.4 11.6 %copy-start.3 = (f32[1,1024,240]{1,2,0:T(8,128)S(1)}, f32[1,1024,240]{1,2,0:T(8,128)}, u32[]{:S(2)}) copy-start(f32[1,1024,240]{1,2,0:T(8,128)} %param.10) | copy-start | bytes 2949124
  40.5 11.6 %copy-start.5 = (f32[1,1024,240]{1,2,0:T(8,128)S(1)}, f32[1,1024,240]{1,2,0:T(8,128)}, u32[]{:S(2)}) copy-start(f32[1,1024,240]{1,2,0:T(8,128)} %param.11) | copy-start | bytes 2949124
  53.5 3.5 %collective-permute-start.13 = (bf16[640,256]{1,0:T(8,128)(2,1)S(1)}, bf16[640,256]{1,0:T(8,128)(2,1)S(1)}, u32[]{:S(2)}, u32[]{:S(2)}) collective-permute-start(bf16[640,256]{1,0:T(8,128)(2,1)S(1)} %get-tuple-element.34.rest_0_.rest_3_), channel_id=1, source_target_pairs={{0,1},{1,0},{2,3},{3,2},{4,5},{5,4},{6,7},{7,6},{8,9},{9,8},{10,11... | collective-permute-start | bytes 983048 | tf_op jit(solution)/shard_map/ppermute | solution.py:353
  53.6 14.3 %collective-permute-start.15 = (bf16[640,256]{1,0:T(8,128)(2,1)S(1)}, bf16[640,256]{1,0:T(8,128)(2,1)S(1)}, u32[]{:S(2)}, u32[]{:S(2)}) collective-permute-start(bf16[640,256]{1,0:T(8,128)(2,1)S(1)} %get-tuple-element.34.rest_0_.rest_3_), channel_id=1, source_target_pairs={{0,2},{1,3},{2,0},{3,1},{4,6},{5,7},{6,4},{7,5},{8,10},{9,11},{10,... | collective-permute-start | bytes 983048 | tf_op jit(solution)/shard_map/ppermute | solution.py:353
  55.4 1.5 %collective-permute-start.14 = (bf16[384,256]{1,0:T(8,128)(2,1)S(1)}, bf16[384,256]{1,0:T(8,128)(2,1)S(1)}, u32[]{:S(2)}, u32[]{:S(2)}) collective-permute-start(bf16[384,256]{1,0:T(8,128)(2,1)S(1)} %get-tuple-element.36.rest_1_.rest_4_), channel_id=1, source_target_pairs={{0,1},{1,0},{2,3},{3,2},{4,5},{5,4},{6,7},{7,6},{8,9},{9,8},{10,11... | collective-permute-start | bytes 589832 | tf_op jit(solution)/shard_map/ppermute | solution.py:353
  55.5 12.4 %collective-permute-start.16 = (bf16[384,256]{1,0:T(8,128)(2,1)S(1)}, bf16[384,256]{1,0:T(8,128)(2,1)S(1)}, u32[]{:S(2)}, u32[]{:S(2)}) collective-permute-start(bf16[384,256]{1,0:T(8,128)(2,1)S(1)} %get-tuple-element.36.rest_1_.rest_4_), channel_id=1, source_target_pairs={{0,2},{1,3},{2,0},{3,1},{4,6},{5,7},{6,4},{7,5},{8,10},{9,11},{10,... | collective-permute-start | bytes 589832 | tf_op jit(solution)/shard_map/ppermute | solution.py:353
  67.9 1.9 %collective-permute-start.17 = (bf16[640,256]{1,0:T(8,128)(2,1)S(1)}, bf16[640,256]{1,0:T(8,128)(2,1)S(1)}, u32[]{:S(2)}, u32[]{:S(2)}) collective-permute-start(bf16[640,256]{1,0:T(8,128)(2,1)S(1)} %collective-permute-done.15.rest_7_.rest_2_), channel_id=1, source_target_pairs={{0,1},{1,0},{2,3},{3,2},{4,5},{5,4},{6,7},{7,6},{8,9},{9,8},{10,11... | collective-permute-start | bytes 983048 | tf_op jit(solution)/shard_map/ppermute | solution.py:353
  67.9 1.9 %collective-permute-start.18 = (bf16[384,256]{1,0:T(8,128)(2,1)S(1)}, bf16[384,256]{1,0:T(8,128)(2,1)S(1)}, u32[]{:S(2)}, u32[]{:S(2)}) collective-permute-start(bf16[384,256]{1,0:T(8,128)(2,1)S(1)} %collective-permute-done.16.rest_8_.rest_3_), channel_id=1, source_target_pairs={{0,1},{1,0},{2,3},{3,2},{4,5},{5,4},{6,7},{7,6},{8,9},{9,8},{10,11... | collective-permute-start | bytes 589832 | tf_op jit(solution)/shard_map/ppermute | solution.py:353
  69.8 3.2 %copy-start.8 = (bf16[240,512]{1,0:T(8,128)(2,1)S(1)}, bf16[240,512]{1,0:T(8,128)(2,1)}, u32[]{:S(2)}) copy-start(bf16[240,512]{1,0:T(8,128)(2,1)} %out_ref.3) | copy-start | bytes 737284
  73.0 25.7 %collective-permute-start.19 = (bf16[640,256]{1,0:T(8,128)(2,1)S(1)}, bf16[640,256]{1,0:T(8,128)(2,1)S(1)}, u32[]{:S(2)}, u32[]{:S(2)}) collective-permute-start(bf16[640,256]{1,0:T(8,128)(2,1)S(1)} %terms_rest.2), channel_id=1, source_target_pairs={{0,4},{1,5},{2,6},{3,7},{4,0},{5,1},{6,2},{7,3},{8,12},{9,13},{10,... | collective-permute-start | bytes 983048 | tf_op jit(solution)/shard_map/ppermute | solution.py:353
  74.5 5.8 %collective-permute-start.11 = (f32[1,512]{1,0:T(1,128)S(1)}, f32[1,512]{1,0:T(1,128)S(1)}, u32[]{:S(2)}, u32[]{:S(2)}) collective-permute-start(f32[1,512]{1,0:T(1,128)S(1)} %gather_wave.3), channel_id=1, source_target_pairs={{0,8},{8,0},{16,24},{24,16},{1,9},{9,1},{17,25},{25,17},{2,10},{10... | collective-permute-start | bytes 6152 | tf_op jit(solution)/shard_map/ppermute | solution.py:364
  77.7 21.0 %collective-permute-start.20 = (bf16[384,256]{1,0:T(8,128)(2,1)S(1)}, bf16[384,256]{1,0:T(8,128)(2,1)S(1)}, u32[]{:S(2)}, u32[]{:S(2)}) collective-permute-start(bf16[384,256]{1,0:T(8,128)(2,1)S(1)} %terms_rest.3), channel_id=1, source_target_pairs={{0,4},{1,5},{2,6},{3,7},{4,0},{5,1},{6,2},{7,3},{8,12},{9,13},{10,... | collective-permute-start | bytes 589832 | tf_op jit(solution)/shard_map/ppermute | solution.py:353
  80.3 3.7 %collective-permute-start.12 = (f32[2,512]{1,0:T(2,128)S(1)}, f32[2,512]{1,0:T(2,128)S(1)}, u32[]{:S(2)}, u32[]{:S(2)}) collective-permute-start(f32[2,512]{1,0:T(2,128)S(1)} %pad_maximum_fusion.1), channel_id=1, source_target_pairs={{0,16},{8,24},{16,0},{24,8},{1,17},{9,25},{17,1},{25,9},{2,18},{10... | collective-permute-start | bytes 12296 | tf_op jit(solution)/shard_map/ppermute | solution.py:364

commit v7 on v6

--- a/solution.py
+++ b/solution.py
@@ -175,6 +175,44 @@
     return total
 
 
+def packed_rows(rows, coefs, width):
+    kept = rows * coefs // width
+    return kept, -(-kept // 16) * 16
+
+
+def pack(value, width):
+    rows, coefs = value.shape
+    kept, stored = packed_rows(rows, coefs, width)
+    gap = width - coefs
+    wide = pad_lanes(value, width)
+    last = wide[kept:]
+    moved = []
+    for lane in range(0, coefs, gap):
+        half = last[:, lane // LANES * LANES :][:, :LANES]
+        moved.append(pltpu.roll(half, (LANES - gap - lane) % LANES, 1))
+    moved = jnp.concatenate(moved, axis=0)
+    lanes = lax.broadcasted_iota(jnp.int32, moved.shape, 1)
+    right = jnp.where(lanes < LANES - gap, wide[:kept, LANES:], moved)
+    whole_rows = jnp.concatenate([wide[:kept, :LANES], right], axis=1)
+    return jnp.concatenate([whole_rows, jnp.zeros((stored - kept, width), value.dtype)], axis=0)
+
+
+def unpack(value, rows, coefs):
+    width = value.shape[1]
+    kept, _ = packed_rows(rows, coefs, width)
+    gap, count = width - coefs, rows - kept
+    halves = [jnp.zeros((count, LANES), value.dtype) for _ in range(width // LANES)]
+    lanes = lax.broadcasted_iota(jnp.int32, (count, LANES), 1)
+    for step, lane in enumerate(range(0, coefs, gap)):
+        piece = value[step * count : (step + 1) * count, LANES:]
+        low = lane % LANES
+        piece = pltpu.roll(piece, (low - (LANES - gap)) % LANES, 1)
+        here = (lanes >= low) & (lanes < low + gap)
+        halves[lane // LANES] = jnp.where(here, piece, halves[lane // LANES])
+    last = jnp.concatenate(halves, axis=1)
+    return jnp.concatenate([value[:kept], last], axis=0)[:, :coefs]
+
+
 def terms_kernel(
     kind, cut, segments, stands, source_ref, target_ref, bound_ref, table_ref, tables_ref, *rest
 ):
@@ -190,9 +228,7 @@
     cleared = pl.ds(start * wide, (stop - start) * wide)
     picked[cleared, :] = jnp.zeros(((stop - start) * wide, LANES), jnp.float32)
     pick_rows(source_ref, target_ref, bound_ref, segments, source, picked)
-    size = min(CHUNK, stop - start)
-    while (stop - start) % size:
-        size += LANES
+    size = CHUNK if kind in ("near", "own") else stop - start
     for place in range(start, stop, size):
         at = pl.ds(place, size)
         total = translate(place, size, picked, table_ref, tables_ref)
@@ -201,8 +237,9 @@
         if kind == "rest":
             total = total + extra[0][at, :]
         if kind in ("rest", "all"):
-            total = pad_lanes(total, out_ref.shape[1]).astype(jnp.bfloat16)
-        out_ref[pl.ds(place - start, size), :] = total
+            out_ref[...] = pack(total, out_ref.shape[1]).astype(jnp.bfloat16)
+        else:
+            out_ref[pl.ds(place - start, size), :] = total
 
 
 def terms(kind, cut, segments, blocks, requests, tables, *extra):
@@ -213,7 +250,8 @@
     if kind in ("near", "own"):
         outs = [jax.ShapeDtypeStruct((size, tables.shape[1]), jnp.float32)]
     else:
-        outs = [jax.ShapeDtypeStruct((size, width), jnp.bfloat16)]
+        stored = packed_rows(size, tables.shape[1], width)[1]
+        outs = [jax.ShapeDtypeStruct((stored, width), jnp.bfloat16)]
     if kind == "own":
         outs.append(jax.ShapeDtypeStruct((8, LANES), jnp.float32))
     return pl.pallas_call(
@@ -250,7 +288,8 @@
         far_rows = here[0][...].astype(jnp.float32)
         for other in here[1:]:
             far_rows = far_rows + other[...].astype(jnp.float32)
-        image = pad_lanes(base_ref[at, :] + far_rows[:, :coefs], width).T[:coefs, :]
+        far_rows = unpack(far_rows, stop - start, coefs)
+        image = pad_lanes(base_ref[at, :] + far_rows, width).T[:coefs, :]
         image = mie_ref[:, at] * image
         image_ref[:, pl.ds(start - cuts[0][0], stop - start)] = image
         x = x_ref[:, at]

time: 112 us -> 110 us (0.982)
  waiting for transfers between devices: 23.5 us -> 21.8 us
    ppermute x17, waiting for transfers between devices: 21.4 us -> 19.8 us  [flip(): lax.ppermute(block, 'grp', [(i, i ^ bits) for i in range(lax.axis_size('g...]
    pallas_call x7, Pallas kernels: 33.3 us -> 32.1 us  [terms(): pl.pallas_call(functools.partial(terms_kernel, kind, cut, segments, stand...]
  transfers between devices with their start and end apart: 21 -> 21, of which waited for: 7 -> 7; matrix products, arithmetic and copies ran while one was open for 13% -> 14% of each run, Pallas kernels for 31% -> 31%
where the time goes in v7:
time: 110 us
  Pallas kernels  40 us (36%)
  waiting for transfers between devices  21.8 us (20%)
  starting transfers between devices  20 us (18%)
  other arithmetic  11.9 us (11%)
  blocking collectives  9.84 us (9%)
  local copies, waits for them, and re-layouts  5.13 us (5%)
    pallas_call x7, Pallas kernels, terms(): pl.pallas_call(functools.partial(terms_kernel, kind, cut, segments, stand...  32.1 us
    ppermute x17, waiting for transfers between devices, flip(): lax.ppermute(block, 'grp', [(i, i ^ bits) for i in range(lax.axis_size('g...  19.8 us
    ppermute x17, starting transfers between devices, flip(): lax.ppermute(block, 'grp', [(i, i ^ bits) for i in range(lax.axis_size('g...  14.5 us
    all_to_all x1, blocking collectives, body(): sums = lax.all_to_all(sums, ('blk', 'grp'), 0, 0, tiled=True)  9.84 us
    sort x1, other arithmetic, body(): listed = jnp.sort(kind * rows + near_row[0] << bits | number)  5.75 us
    ppermute x4, starting transfers between devices, wave_swaps(): moved = lax.ppermute(waves, 'blk', [(i, i ^ bits) for i in range(blocks)])  5.52 us
    pallas_call x2, Pallas kernels, gather_wave(): pl.pallas_call(wave_kernel, out_shape=jax.ShapeDtypeStruct((1, samples),...  2.95 us
    pallas_call x3, Pallas kernels, join(): pl.pallas_call(functools.partial(join_kernel, cuts, len(served) // len(cu...  2.72 us
  transfers between devices with their start and end apart: 21, of which 7 were waited for; matrix products, arithmetic and copies ran while one was open for 14% of the time, Pallas kernels for 31%

profile of v7, /device:TPU:0, one launch (start us, length us, event | category | flops | bytes accessed | tf_op | source)
XLA Modules:
  0.0 109.5 jit_solution(9927190143668889874)
XLA Ops:
  0.7 1.2 %copy-done.2 = f32[1,1024,240]{1,2,0:T(8,128)S(1)} copy-done((f32[1,1024,240]{1,2,0:T(8,128)S(1)}, f32[1,1024,240]{1,2,0:T(8,128)}, u32[]{:S(2)}) %copy-start.2) | copy-done | bytes 983064
  2.1 3.1 %collective-permute-start = (bf16[640,256]{1,0:T(8,128)(2,1)S(1)}, bf16[640,256]{1,0:T(8,128)(2,1)S(1)}, u32[]{:S(2)}, u32[]{:S(2)}) collective-permute-start(bf16[640,256]{1,0:T(8,128)(2,1)S(1)} %get-tuple-element.28.rest_0_.rest_3_), channel_id=1, source_target_pairs={{0,2},{1,3},{2,0},{3,1},{4,6},{5,7},{6,4},{7,5},{8,10},{9,11},{10,... | collective-permute-start | bytes 983048 | tf_op jit(solution)/shard_map/ppermute | solution.py:392
  5.7 0.7 broadcast_xor_fusion
  6.4 0.7 select_add_fusion
  7.3 5.8 %sort.15 = (s32[3072]{0:T(1024)S(1)}, s32[3072]{0:T(1024)}) sort(s32[3072]{0:T(1024)S(1)} %get-tuple-element.54, s32[3072]{0:T(1024)S(1)} %iota.24), dimensions={0}, to_apply=%region_0.1 | sort | flops 36864 | bytes 49152 | tf_op jit(solution)/shard_map/jit(sort)/sort | solution.py:437
  13.0 0.6 pad_add_fusion
  13.6 2.8 %collective-permute-start.2 = (s32[6161]{0:T(1024)}, s32[6161]{0:T(1024)}, u32[]{:S(2)}, u32[]{:S(2)}) collective-permute-start(s32[6161]{0:T(1024)} %pad_add_fusion), channel_id=1, source_target_pairs={{0,4},{1,5},{2,6},{3,7},{4,0},{5,1},{6,2},{7,3},{8,12},{9,13},{10,... | collective-permute-start | bytes 73940 | tf_op jit(solution)/shard_map/ppermute | solution.py:392
  16.4 0.6 convert_reduce_fusion.1
  17.1 0.9 copy-done.7
  18.0 1.5 %gather_wave.2 = f32[1,512]{1,0:T(1,128)S(1)} custom-call(bf16[240,512]{1,0:T(8,128)(2,1)S(1)} %copy-done.7, bf16[1024,512]{1,0:T(8,128)(2,1)S(1)} %bitcast.33, bf16[640,256]{1,0:T(8,128)(2,1)S(1)} %get-tuple-element.28.rest_0_.rest_3_, bf16[384,256]{1,0:T(8,128)(2,1)S(1)} %get-tuple-element.29.rest_1_.rest_4_), custom_call_target="tpu_custom_call" | custom-call | flops 1 | bytes 1 | tf_op jit(solution)/shard_map/gather_wave/pallas_call | solution.py:93
  19.6 0.6 pad_clamp_fusion
  20.2 0.5 collective-permute-start.8
  20.7 1.5 %collective-permute-start.3 = (f32[1,512]{1,0:T(1,128)S(1)}, f32[1,512]{1,0:T(1,128)S(1)}, u32[]{:S(2)}, u32[]{:S(2)}) collective-permute-start(f32[1,512]{1,0:T(1,128)S(1)} %gather_wave.2), channel_id=1, source_target_pairs={{0,8},{8,0},{16,24},{24,16},{1,9},{9,1},{17,25},{25,17},{2,10},{10... | collective-permute-start | bytes 6152 | tf_op jit(solution)/shard_map/ppermute | solution.py:403
  22.2 0.7 slice_convert_fusion
  22.9 0.7 slice.11.bound_ref
  23.6 0.4 convert_element_type.18.table_ref
  24.1 5.0 %terms_all.2 = bf16[608,256]{1,0:T(8,128)(2,1)} custom-call(s32[3072]{0:T(1024)S(1)} %get-tuple-element.52.source_ref, s32[3072]{0:T(1024)S(1)} %get-tuple-element.51.target_ref, s32[17]{0:T(128)S(1)} %slice.11.bound_ref, bf16[1024,3]{1,0:T(8,128)(2,1)S(1)} %convert_element_type.18.table_ref, bf16[8,240,240]{2,1,0:T(8,128)(2,1)S(1)} %copy-done.1, ...), custom_call_target="tpu_custom_call" | custom-call | flops 1 | bytes 1 | tf_op jit(solution)/shard_map/terms_all/pallas_call | solution.py:257
  29.0 1.7 %collective-permute-start.9 = (bf16[608,256]{1,0:T(8,128)(2,1)}, bf16[608,256]{1,0:T(8,128)(2,1)}, u32[]{:S(2)}, u32[]{:S(2)}) collective-permute-start(bf16[608,256]{1,0:T(8,128)(2,1)} %terms_all.2), channel_id=1, source_target_pairs={{0,4},{1,5},{2,6},{3,7},{4,0},{5,1},{6,2},{7,3},{8,12},{9,13},{10,... | collective-permute-start | bytes 933896 | tf_op jit(solution)/shard_map/ppermute | solution.py:392
  30.7 0.6 pad_maximum_fusion
  31.3 1.5 %collective-permute-start.4 = (f32[2,512]{1,0:T(2,128)}, f32[2,512]{1,0:T(2,128)}, u32[]{:S(2)}, u32[]{:S(2)}) collective-permute-start(f32[2,512]{1,0:T(2,128)} %pad_maximum_fusion), channel_id=1, source_target_pairs={{0,16},{8,24},{16,0},{24,8},{1,17},{9,25},{17,1},{25,9},{2,18},{10... | collective-permute-start | bytes 12296 | tf_op jit(solution)/shard_map/ppermute | solution.py:403
  32.8 0.5 iota_compare_fusion.2
  33.4 1.1 %convert_element_type.17.table_ref = bf16[1024,3]{1,0:T(8,128)(2,1)} reshape(bf16[3072]{0:T(1024)(128)(2,1)S(1)} %copy-done.11) | data formatting | bytes 12288 | tf_op jit(solution)/shard_map/convert_element_type | solution.py:444
  34.5 0.7 gather_fusion
  35.2 3.3 %terms_all.3 = bf16[368,256]{1,0:T(8,128)(2,1)S(1)} custom-call(s32[3072]{0:T(1024)S(1)} %get-tuple-element.52.source_ref, s32[3072]{0:T(1024)S(1)} %get-tuple-element.51.target_ref, s32[17]{0:T(128)S(1)} %slice.11.bound_ref, bf16[1024,3]{1,0:T(8,128)(2,1)S(1)} %convert_element_type.18.table_ref, bf16[8,240,240]{2,1,0:T(8,128)(2,1)S(1)} %copy-done.1, ...), custom_call_target="tpu_custom_call" | custom-call | flops 1 | bytes 1 | tf_op jit(solution)/shard_map/terms_all/pallas_call | solution.py:257
  38.5 1.2 %collective-permute-start.10 = (bf16[368,256]{1,0:T(8,128)(2,1)S(1)}, bf16[368,256]{1,0:T(8,128)(2,1)S(1)}, u32[]{:S(2)}, u32[]{:S(2)}) collective-permute-start(bf16[368,256]{1,0:T(8,128)(2,1)S(1)} %terms_all.3), channel_id=1, source_target_pairs={{0,4},{1,5},{2,6},{3,7},{4,0},{5,1},{6,2},{7,3},{8,12},{9,13},{10,... | collective-permute-start | bytes 565256 | tf_op jit(solution)/shard_map/ppermute | solution.py:392
  39.7 0.8 fusion.4
  40.5 7.3 %terms_near.2.base_ref = f32[1024,240]{1,0:T(8,128)S(1)} custom-call(s32[3072]{0:T(1024)S(1)} %get-tuple-element.56.source_ref, s32[3072]{0:T(1024)S(1)} %get-tuple-element.55.target_ref, s32[17]{0:T(128)S(1)} %convert_reduce_fusion.bound_ref, bf16[1024,3]{1,0:T(8,128)(2,1)S(1)} %copy-done.6, bf16[8,240,240]{2,1,0:T(8,128)(2,1)S(1)} %copy-done.1, ...), custom_call_target="tpu_custom_call" | custom-call | flops 1 | bytes 1 | tf_op jit(solution)/shard_map/terms_near/pallas_call | solution.py:257
  47.8 3.2 %collective-permute-done.9.rest_0_ = bf16[608,256]{1,0:T(8,128)(2,1)} collective-permute-done((bf16[608,256]{1,0:T(8,128)(2,1)}, bf16[608,256]{1,0:T(8,128)(2,1)}, u32[]{:S(2)}, u32[]{:S(2)}) %collective-permute-start.9) | collective-permute-done | bytes 311328 | tf_op jit(solution)/shard_map/ppermute | solution.py:392
  51.0 1.6 %join_first.2 = (f32[240,640]{1,0:T(8,128)S(1)}, bf16[640,256]{1,0:T(8,128)(2,1)S(1)}, f32[1,128]{1,0:T(1,128)S(1)}) custom-call(f32[1024,240]{1,0:T(8,128)S(1)} %terms_near.2.base_ref, f32[240,1024]{1,0:T(8,128)S(1)} %bitcast.37, f32[240,1024]{1,0:T(8,128)S(1)} %bitcast.29, f32[1,128]{1,0:T(1,128)S(1)} %broadcast_in_dim.44.sums_in_ref, ...), custom_call_target="tpu_custom_call" | custom-call | tf_op jit(solution)/shard_map/join_first/pallas_call | solution.py:317
  52.8 1.1 collective-permute-done.10.rest_0_
  54.3 1.1 collective-permute-start.16
  55.8 4.3 %terms_own.1 = (f32[1024,240]{1,0:T(8,128)S(1)}, f32[8,128]{1,0:T(8,128)S(1)}) custom-call(s32[3072]{0:T(1024)S(1)} %get-tuple-element.52.source_ref, s32[3072]{0:T(1024)S(1)} %get-tuple-element.51.target_ref, s32[17]{0:T(128)S(1)} %slice.11.bound_ref, bf16[1024,3]{1,0:T(8,128)(2,1)S(1)} %convert_element_type.18.table_ref, ...), custom_call_target="tpu_custom_call" | custom-call | flops 1 | bytes 1 | tf_op jit(solution)/shard_map/terms_own/pallas_call | solution.py:257
  60.1 6.9 %collective-permute-done.16.rest_8_.rest_3_ = bf16[384,256]{1,0:T(8,128)(2,1)S(1)} collective-permute-done((bf16[384,256]{1,0:T(8,128)(2,1)S(1)}, bf16[384,256]{1,0:T(8,128)(2,1)S(1)}, u32[]{:S(2)}, u32[]{:S(2)}) %collective-permute-start.16) | collective-permute-done | bytes 196640 | tf_op jit(solution)/shard_map/ppermute | solution.py:392
  67.0 0.5 collective-permute-start.18
  67.5 1.4 %collective-permute-done.18.rest_10_.rest_5_ = bf16[384,256]{1,0:T(8,128)(2,1)S(1)} collective-permute-done((bf16[384,256]{1,0:T(8,128)(2,1)S(1)}, bf16[384,256]{1,0:T(8,128)(2,1)S(1)}, u32[]{:S(2)}, u32[]{:S(2)}) %collective-permute-start.18) | collective-permute-done | bytes 196640 | tf_op jit(solution)/shard_map/ppermute | solution.py:392
  68.9 2.9 %terms_rest.2 = bf16[608,256]{1,0:T(8,128)(2,1)S(1)} custom-call(s32[3072]{0:T(1024)S(1)} %get-tuple-element.52.source_ref, s32[3072]{0:T(1024)S(1)} %get-tuple-element.51.target_ref, s32[17]{0:T(128)S(1)} %slice.11.bound_ref, bf16[1024,3]{1,0:T(8,128)(2,1)S(1)} %convert_element_type.18.table_ref, bf16[8,240,240]{2,1,0:T(8,128)(2,1)S(1)} %copy-done.1, ...), custom_call_target="tpu_custom_call" | custom-call | flops 1 | bytes 1 | tf_op jit(solution)/shard_map/terms_rest/pallas_call | solution.py:257
  71.8 0.5 collective-permute-start.19
  72.4 1.5 %gather_wave.3 = f32[1,512]{1,0:T(1,128)S(1)} custom-call(bf16[240,512]{1,0:T(8,128)(2,1)S(1)} %copy-done.8, bf16[1024,512]{1,0:T(8,128)(2,1)S(1)} %bitcast.35, bf16[640,256]{1,0:T(8,128)(2,1)S(1)} %get-tuple-element.34.rest_0_.rest_3_, bf16[384,256]{1,0:T(8,128)(2,1)S(1)} %get-tuple-element.36.rest_1_.rest_4_), custom_call_target="tpu_custom_call" | custom-call | flops 1 | bytes 1 | tf_op jit(solution)/shard_map/gather_wave/pallas_call | solution.py:93
  73.8 0.8 collective-permute-start.11
  74.7 2.3 %terms_rest.3 = bf16[368,256]{1,0:T(8,128)(2,1)S(1)} custom-call(s32[3072]{0:T(1024)S(1)} %get-tuple-element.52.source_ref, s32[3072]{0:T(1024)S(1)} %get-tuple-element.51.target_ref, s32[17]{0:T(128)S(1)} %slice.11.bound_ref, bf16[1024,3]{1,0:T(8,128)(2,1)S(1)} %convert_element_type.18.table_ref, bf16[8,240,240]{2,1,0:T(8,128)(2,1)S(1)} %copy-done.1, ...), custom_call_target="tpu_custom_call" | custom-call | flops 1 | bytes 1 | tf_op jit(solution)/shard_map/terms_rest/pallas_call | solution.py:257
  77.0 2.4 %collective-permute-start.20 = (bf16[368,256]{1,0:T(8,128)(2,1)S(1)}, bf16[368,256]{1,0:T(8,128)(2,1)S(1)}, u32[]{:S(2)}, u32[]{:S(2)}) collective-permute-start(bf16[368,256]{1,0:T(8,128)(2,1)S(1)} %terms_rest.3), channel_id=1, source_target_pairs={{0,4},{1,5},{2,6},{3,7},{4,0},{5,1},{6,2},{7,3},{8,12},{9,13},{10,... | collective-permute-start | bytes 565256 | tf_op jit(solution)/shard_map/ppermute | solution.py:392
  79.3 1.7 %collective-permute-start.12 = (f32[2,512]{1,0:T(2,128)S(1)}, f32[2,512]{1,0:T(2,128)S(1)}, u32[]{:S(2)}, u32[]{:S(2)}) collective-permute-start(f32[2,512]{1,0:T(2,128)S(1)} %pad_maximum_fusion.1), channel_id=1, source_target_pairs={{0,16},{8,24},{16,0},{24,8},{1,17},{9,25},{17,1},{25,9},{2,18},{10... | collective-permute-start | bytes 12296 | tf_op jit(solution)/shard_map/ppermute | solution.py:403
  81.0 2.0 %collective-permute-done.12 = f32[2,512]{1,0:T(2,128)S(1)} collective-permute-done((f32[2,512]{1,0:T(2,128)S(1)}, f32[2,512]{1,0:T(2,128)S(1)}, u32[]{:S(2)}, u32[]{:S(2)}) %collective-permute-start.12) | collective-permute-done | bytes 4128 | tf_op jit(solution)/shard_map/ppermute | solution.py:403
  83.1 6.9 %terms_near.3.base_ref = f32[1024,240]{1,0:T(8,128)S(1)} custom-call(s32[3072]{0:T(1024)S(1)} %get-tuple-element.56.source_ref, s32[3072]{0:T(1024)S(1)} %get-tuple-element.55.target_ref, s32[17]{0:T(128)S(1)} %convert_reduce_fusion.bound_ref, bf16[1024,3]{1,0:T(8,128)(2,1)S(1)} %copy-done.6, bf16[8,240,240]{2,1,0:T(8,128)(2,1)S(1)} %copy-done.1, ...), custom_call_target="tpu_custom_call" | custom-call | flops 1 | bytes 1 | tf_op jit(solution)/shard_map/terms_near/pallas_call | solution.py:257
  90.1 6.8 %collective-permute-done.20.rest_1_ = bf16[368,256]{1,0:T(8,128)(2,1)S(1)} collective-permute-done((bf16[368,256]{1,0:T(8,128)(2,1)S(1)}, bf16[368,256]{1,0:T(8,128)(2,1)S(1)}, u32[]{:S(2)}, u32[]{:S(2)}) %collective-permute-start.20) | collective-permute-done | bytes 188448 | tf_op jit(solution)/shard_map/ppermute | solution.py:392
  96.9 0.7 join_second.1
  97.6 9.8 %all_to_all.11 = f32[32,1,128]{2,1,0:T(1,128)S(1)} all-to-all(f32[32,1,128]{2,1,0:T(1,128)S(1)} %bitcast.43), channel_id=1, replica_groups=mesh['blk'=4,'grp'=8] {'blk','grp'}, dimensions={0} | all-to-all | bytes 32768 | tf_op jit(solution)/shard_map/all_to_all | solution.py:541
  107.5 2.1 %finish.1 = (f32[240,1024]{1,0:T(8,128)}, f32[240,1024]{1,0:T(8,128)}, f32[2,3]{1,0:T(2,128)}) custom-call(f32[32,128]{1,0:T(8,128)S(1)} %bitcast.42, f32[240,1024]{1,0:T(8,128)S(1)} %bitcast.32, f32[240,1024]{1,0:T(8,128)S(1)} %get-tuple-element.46.c_ref, f32[240,640]{1,0:T(8,128)S(1)} %get-tuple-element.43.rest_2_.rest_0_, ...), custom_call_target="tpu_custom_call" | custom-call | tf_op jit(solution)/shard_map/finish/pallas_call | solution.py:381
  (56 shorter events, 2.1 us)
Async XLA Ops:
  0.6 33.9 %copy-start = (f32[1,1,4,512]{3,2,1,0:T(4,128)S(1)}, f32[1,1,4,512]{3,2,1,0:T(4,128)}, u32[]{:S(2)}) copy-start(f32[1,1,4,512]{3,2,1,0:T(4,128)} %param.19) | copy-start | bytes 24580
  0.6 1.2 %copy-start.2 = (f32[1,1024,240]{1,2,0:T(8,128)S(1)}, f32[1,1024,240]{1,2,0:T(8,128)}, u32[]{:S(2)}) copy-start(f32[1,1024,240]{1,2,0:T(8,128)} %param.10) | copy-start | bytes 2949124
  1.9 15.2 %copy-start.4 = (bf16[1,1024,512]{2,1,0:T(8,128)(2,1)S(1)}, bf16[1,1024,512]{2,1,0:T(8,128)(2,1)}, u32[]{:S(2)}) copy-start(bf16[1,1024,512]{2,1,0:T(8,128)(2,1)} %param.18) | copy-start | bytes 3145732
  2.1 17.4 %collective-permute-start = (bf16[640,256]{1,0:T(8,128)(2,1)S(1)}, bf16[640,256]{1,0:T(8,128)(2,1)S(1)}, u32[]{:S(2)}, u32[]{:S(2)}) collective-permute-start(bf16[640,256]{1,0:T(8,128)(2,1)S(1)} %get-tuple-element.28.rest_0_.rest_3_), channel_id=1, source_target_pairs={{0,2},{1,3},{2,0},{3,1},{4,6},{5,7},{6,4},{7,5},{8,10},{9,11},{10,... | collective-permute-start | bytes 983048 | tf_op jit(solution)/shard_map/ppermute | solution.py:392
  5.2 18.9 %collective-permute-start.5 = (bf16[640,256]{1,0:T(8,128)(2,1)S(1)}, bf16[640,256]{1,0:T(8,128)(2,1)S(1)}, u32[]{:S(2)}, u32[]{:S(2)}) collective-permute-start(bf16[640,256]{1,0:T(8,128)(2,1)S(1)} %get-tuple-element.28.rest_0_.rest_3_), channel_id=1, source_target_pairs={{0,1},{1,0},{2,3},{3,2},{4,5},{5,4},{6,7},{7,6},{8,9},{9,8},{10,11... | collective-permute-start | bytes 983048 | tf_op jit(solution)/shard_map/ppermute | solution.py:392
  5.2 14.3 %collective-permute-start.1 = (bf16[384,256]{1,0:T(8,128)(2,1)S(1)}, bf16[384,256]{1,0:T(8,128)(2,1)}, u32[]{:S(2)}, u32[]{:S(2)}) collective-permute-start(bf16[384,256]{1,0:T(8,128)(2,1)S(1)} %get-tuple-element.29.rest_1_.rest_4_), channel_id=1, source_target_pairs={{0,2},{1,3},{2,0},{3,1},{4,6},{5,7},{6,4},{7,5},{8,10},{9,11},{10,... | collective-permute-start | bytes 589832 | tf_op jit(solution)/shard_map/ppermute | solution.py:392
  5.3 18.7 %collective-permute-start.6 = (bf16[384,256]{1,0:T(8,128)(2,1)S(1)}, bf16[384,256]{1,0:T(8,128)(2,1)}, u32[]{:S(2)}, u32[]{:S(2)}) collective-permute-start(bf16[384,256]{1,0:T(8,128)(2,1)S(1)} %get-tuple-element.29.rest_1_.rest_4_), channel_id=1, source_target_pairs={{0,1},{1,0},{2,3},{3,2},{4,5},{5,4},{6,7},{7,6},{8,9},{9,8},{10,11... | collective-permute-start | bytes 589832 | tf_op jit(solution)/shard_map/ppermute | solution.py:392
  7.3 5.8 %copy-start.10 = (s32[1,3072]{1,0:T(1,128)S(1)}, s32[1,3072]{1,0:T(1,128)}, u32[]{:S(2)}) copy-start(s32[1,3072]{1,0:T(1,128)} %param.14) | copy-start | bytes 36868
  13.6 5.8 %collective-permute-start.2 = (s32[6161]{0:T(1024)}, s32[6161]{0:T(1024)}, u32[]{:S(2)}, u32[]{:S(2)}) collective-permute-start(s32[6161]{0:T(1024)} %pad_add_fusion), channel_id=1, source_target_pairs={{0,4},{1,5},{2,6},{3,7},{4,0},{5,1},{6,2},{7,3},{8,12},{9,13},{10,... | collective-permute-start | bytes 73940 | tf_op jit(solution)/shard_map/ppermute | solution.py:392
  17.1 0.9 copy-start.7
  18.0 6.1 %copy-start.1 = (bf16[8,240,240]{2,1,0:T(8,128)(2,1)S(1)}, bf16[8,240,240]{2,1,0:T(8,128)(2,1)}, u32[]{:S(2)}) copy-start(bf16[8,240,240]{2,1,0:T(8,128)(2,1)} %tables_ref.13) | copy-start | bytes 2764804
  19.5 4.5 %collective-permute-start.7 = (bf16[640,256]{1,0:T(8,128)(2,1)S(1)}, bf16[640,256]{1,0:T(8,128)(2,1)}, u32[]{:S(2)}, u32[]{:S(2)}) collective-permute-start(bf16[640,256]{1,0:T(8,128)(2,1)S(1)} %collective-permute-done.rest_7_.rest_4_), channel_id=1, source_target_pairs={{0,1},{1,0},{2,3},{3,2},{4,5},{5,4},{6,7},{7,6},{8,9},{9,8},{10,11... | collective-permute-start | bytes 983048 | tf_op jit(solution)/shard_map/ppermute | solution.py:392
  20.2 3.9 %collective-permute-start.8 = (bf16[384,256]{1,0:T(8,128)(2,1)}, bf16[384,256]{1,0:T(8,128)(2,1)}, u32[]{:S(2)}, u32[]{:S(2)}) collective-permute-start(bf16[384,256]{1,0:T(8,128)(2,1)} %collective-permute-done.1.rest_8_.rest_5_), channel_id=1, source_target_pairs={{0,1},{1,0},{2,3},{3,2},{4,5},{5,4},{6,7},{7,6},{8,9},{9,8},{10,11... | collective-permute-start | bytes 589832 | tf_op jit(solution)/shard_map/ppermute | solution.py:392
  20.7 10.0 %collective-permute-start.3 = (f32[1,512]{1,0:T(1,128)S(1)}, f32[1,512]{1,0:T(1,128)S(1)}, u32[]{:S(2)}, u32[]{:S(2)}) collective-permute-start(f32[1,512]{1,0:T(1,128)S(1)} %gather_wave.2), channel_id=1, source_target_pairs={{0,8},{8,0},{16,24},{24,16},{1,9},{9,1},{17,25},{25,17},{2,10},{10... | collective-permute-start | bytes 6152 | tf_op jit(solution)/shard_map/ppermute | solution.py:403
  29.0 4.3 %copy-start.11 = (bf16[3072]{0:T(1024)(128)(2,1)S(1)}, bf16[3072]{0:T(1024)(128)(2,1)}, u32[]{:S(2)}) copy-start(bf16[3072]{0:T(1024)(128)(2,1)} %convert_reduce_fusion.1) | copy-start | bytes 18436
  29.0 22.0 %collective-permute-start.9 = (bf16[608,256]{1,0:T(8,128)(2,1)}, bf16[608,256]{1,0:T(8,128)(2,1)}, u32[]{:S(2)}, u32[]{:S(2)}) collective-permute-start(bf16[608,256]{1,0:T(8,128)(2,1)} %terms_all.2), channel_id=1, source_target_pairs={{0,4},{1,5},{2,6},{3,7},{4,0},{5,1},{6,2},{7,3},{8,12},{9,13},{10,... | collective-permute-start | bytes 933896 | tf_op jit(solution)/shard_map/ppermute | solution.py:392
  31.3 8.4 %collective-permute-start.4 = (f32[2,512]{1,0:T(2,128)}, f32[2,512]{1,0:T(2,128)}, u32[]{:S(2)}, u32[]{:S(2)}) collective-permute-start(f32[2,512]{1,0:T(2,128)} %pad_maximum_fusion), channel_id=1, source_target_pairs={{0,16},{8,24},{16,0},{24,8},{1,17},{9,25},{17,1},{25,9},{2,18},{10... | collective-permute-start | bytes 12296 | tf_op jit(solution)/shard_map/ppermute | solution.py:403
  35.2 4.5 %copy-start.12 = (pred[4]{0:T(512)(128)(4,1)S(1)}, pred[4]{0:T(512)(128)(4,1)}, u32[]{:S(2)}) copy-start(pred[4]{0:T(512)(128)(4,1)} %iota_compare_fusion.2) | copy-start | bytes 16
  35.2 5.3 %copy-start.6 = (bf16[1024,3]{1,0:T(8,128)(2,1)S(1)}, bf16[1024,3]{1,0:T(8,128)(2,1)}, u32[]{:S(2)}) copy-start(bf16[1024,3]{1,0:T(8,128)(2,1)} %convert_element_type.17.table_ref) | copy-start | bytes 18436
  35.2 5.3 %copy-start.9 = (bf16[512,240]{0,1:T(8,128)(2,1)S(1)}, bf16[512,240]{0,1:T(8,128)(2,1)}, u32[]{:S(2)}) copy-start(bf16[512,240]{0,1:T(8,128)(2,1)} %param.17) | copy-start | bytes 737284
  38.5 15.3 %collective-permute-start.10 = (bf16[368,256]{1,0:T(8,128)(2,1)S(1)}, bf16[368,256]{1,0:T(8,128)(2,1)S(1)}, u32[]{:S(2)}, u32[]{:S(2)}) collective-permute-start(bf16[368,256]{1,0:T(8,128)(2,1)S(1)} %terms_all.3), channel_id=1, source_target_pairs={{0,4},{1,5},{2,6},{3,7},{4,0},{5,1},{6,2},{7,3},{8,12},{9,13},{10,... | collective-permute-start | bytes 565256 | tf_op jit(solution)/shard_map/ppermute | solution.py:392
  40.5 10.5 %copy-start.3 = (f32[1,1024,240]{1,2,0:T(8,128)S(1)}, f32[1,1024,240]{1,2,0:T(8,128)}, u32[]{:S(2)}) copy-start(f32[1,1024,240]{1,2,0:T(8,128)} %param.10) | copy-start | bytes 2949124
  40.5 10.5 %copy-start.5 = (f32[1,1024,240]{1,2,0:T(8,128)S(1)}, f32[1,1024,240]{1,2,0:T(8,128)}, u32[]{:S(2)}) copy-start(f32[1,1024,240]{1,2,0:T(8,128)} %param.11) | copy-start | bytes 2949124
  52.6 3.2 %collective-permute-start.13 = (bf16[640,256]{1,0:T(8,128)(2,1)S(1)}, bf16[640,256]{1,0:T(8,128)(2,1)S(1)}, u32[]{:S(2)}, u32[]{:S(2)}) collective-permute-start(bf16[640,256]{1,0:T(8,128)(2,1)S(1)} %get-tuple-element.34.rest_0_.rest_3_), channel_id=1, source_target_pairs={{0,1},{1,0},{2,3},{3,2},{4,5},{5,4},{6,7},{7,6},{8,9},{9,8},{10,11... | collective-permute-start | bytes 983048 | tf_op jit(solution)/shard_map/ppermute | solution.py:392
  52.7 14.3 %collective-permute-start.15 = (bf16[640,256]{1,0:T(8,128)(2,1)S(1)}, bf16[640,256]{1,0:T(8,128)(2,1)S(1)}, u32[]{:S(2)}, u32[]{:S(2)}) collective-permute-start(bf16[640,256]{1,0:T(8,128)(2,1)S(1)} %get-tuple-element.34.rest_0_.rest_3_), channel_id=1, source_target_pairs={{0,2},{1,3},{2,0},{3,1},{4,6},{5,7},{6,4},{7,5},{8,10},{9,11},{10,... | collective-permute-start | bytes 983048 | tf_op jit(solution)/shard_map/ppermute | solution.py:392
  54.2 1.5 %collective-permute-start.14 = (bf16[384,256]{1,0:T(8,128)(2,1)S(1)}, bf16[384,256]{1,0:T(8,128)(2,1)S(1)}, u32[]{:S(2)}, u32[]{:S(2)}) collective-permute-start(bf16[384,256]{1,0:T(8,128)(2,1)S(1)} %get-tuple-element.36.rest_1_.rest_4_), channel_id=1, source_target_pairs={{0,1},{1,0},{2,3},{3,2},{4,5},{5,4},{6,7},{7,6},{8,9},{9,8},{10,11... | collective-permute-start | bytes 589832 | tf_op jit(solution)/shard_map/ppermute | solution.py:392
  54.3 12.7 %collective-permute-start.16 = (bf16[384,256]{1,0:T(8,128)(2,1)S(1)}, bf16[384,256]{1,0:T(8,128)(2,1)S(1)}, u32[]{:S(2)}, u32[]{:S(2)}) collective-permute-start(bf16[384,256]{1,0:T(8,128)(2,1)S(1)} %get-tuple-element.36.rest_1_.rest_4_), channel_id=1, source_target_pairs={{0,2},{1,3},{2,0},{3,1},{4,6},{5,7},{6,4},{7,5},{8,10},{9,11},{10,... | collective-permute-start | bytes 589832 | tf_op jit(solution)/shard_map/ppermute | solution.py:392
  67.0 1.9 %collective-permute-start.17 = (bf16[640,256]{1,0:T(8,128)(2,1)S(1)}, bf16[640,256]{1,0:T(8,128)(2,1)S(1)}, u32[]{:S(2)}, u32[]{:S(2)}) collective-permute-start(bf16[640,256]{1,0:T(8,128)(2,1)S(1)} %collective-permute-done.15.rest_7_.rest_2_), channel_id=1, source_target_pairs={{0,1},{1,0},{2,3},{3,2},{4,5},{5,4},{6,7},{7,6},{8,9},{9,8},{10,11... | collective-permute-start | bytes 983048 | tf_op jit(solution)/shard_map/ppermute | solution.py:392
  67.0 1.9 %collective-permute-start.18 = (bf16[384,256]{1,0:T(8,128)(2,1)S(1)}, bf16[384,256]{1,0:T(8,128)(2,1)S(1)}, u32[]{:S(2)}, u32[]{:S(2)}) collective-permute-start(bf16[384,256]{1,0:T(8,128)(2,1)S(1)} %collective-permute-done.16.rest_8_.rest_3_), channel_id=1, source_target_pairs={{0,1},{1,0},{2,3},{3,2},{4,5},{5,4},{6,7},{7,6},{8,9},{9,8},{10,11... | collective-permute-start | bytes 589832 | tf_op jit(solution)/shard_map/ppermute | solution.py:392
  68.9 3.4 %copy-start.8 = (bf16[240,512]{1,0:T(8,128)(2,1)S(1)}, bf16[240,512]{1,0:T(8,128)(2,1)}, u32[]{:S(2)}) copy-start(bf16[240,512]{1,0:T(8,128)(2,1)} %out_ref.3) | copy-start | bytes 737284
  71.8 25.0 %collective-permute-start.19 = (bf16[608,256]{1,0:T(8,128)(2,1)S(1)}, bf16[608,256]{1,0:T(8,128)(2,1)S(1)}, u32[]{:S(2)}, u32[]{:S(2)}) collective-permute-start(bf16[608,256]{1,0:T(8,128)(2,1)S(1)} %terms_rest.2), channel_id=1, source_target_pairs={{0,4},{1,5},{2,6},{3,7},{4,0},{5,1},{6,2},{7,3},{8,12},{9,13},{10,... | collective-permute-start | bytes 933896 | tf_op jit(solution)/shard_map/ppermute | solution.py:392
  73.8 5.5 %collective-permute-start.11 = (f32[1,512]{1,0:T(1,128)S(1)}, f32[1,512]{1,0:T(1,128)S(1)}, u32[]{:S(2)}, u32[]{:S(2)}) collective-permute-start(f32[1,512]{1,0:T(1,128)S(1)} %gather_wave.3), channel_id=1, source_target_pairs={{0,8},{8,0},{16,24},{24,16},{1,9},{9,1},{17,25},{25,17},{2,10},{10... | collective-permute-start | bytes 6152 | tf_op jit(solution)/shard_map/ppermute | solution.py:403
  77.0 19.9 %collective-permute-start.20 = (bf16[368,256]{1,0:T(8,128)(2,1)S(1)}, bf16[368,256]{1,0:T(8,128)(2,1)S(1)}, u32[]{:S(2)}, u32[]{:S(2)}) collective-permute-start(bf16[368,256]{1,0:T(8,128)(2,1)S(1)} %terms_rest.3), channel_id=1, source_target_pairs={{0,4},{1,5},{2,6},{3,7},{4,0},{5,1},{6,2},{7,3},{8,12},{9,13},{10,... | collective-permute-start | bytes 565256 | tf_op jit(solution)/shard_map/ppermute | solution.py:392
  79.3 3.7 %collective-permute-start.12 = (f32[2,512]{1,0:T(2,128)S(1)}, f32[2,512]{1,0:T(2,128)S(1)}, u32[]{:S(2)}, u32[]{:S(2)}) collective-permute-start(f32[2,512]{1,0:T(2,128)S(1)} %pad_maximum_fusion.1), channel_id=1, source_target_pairs={{0,16},{8,24},{16,0},{24,8},{1,17},{9,25},{17,1},{25,9},{2,18},{10... | collective-permute-start | bytes 12296 | tf_op jit(solution)/shard_map/ppermute | solution.py:403

commit v8 on v7

--- a/solution.py
+++ b/solution.py
@@ -260,8 +260,8 @@
         in_specs=[whole(pltpu.SMEM)] * 3 + [whole()] * (2 + len(extra) + len(shards)),
         out_specs=(whole(),) * len(outs),
         scratch_shapes=[
-            pltpu.VMEM((2 * QUAD * rows, LANES), jnp.float32),
-            pltpu.VMEM((2 * source.shape[0], LANES), jnp.float32),
+            pltpu.VMEM((2 * QUAD * rows + 8, LANES), jnp.float32),
+            pltpu.VMEM((2 * source.shape[0] + 8, LANES), jnp.float32),
         ],
         compiler_params=params(),
         cost_estimate=COST,

time: 110 us -> 110 us (level)
  Pallas kernels: 40 us -> 37.9 us
  waiting for transfers between devices: 21.8 us -> 23 us
    pallas_call x7, Pallas kernels: 32.1 us -> 29.9 us  [terms(): pl.pallas_call(functools.partial(terms_kernel, kind, cut, segments, stand...]
    ppermute x17, waiting for transfers between devices: 19.8 us -> 21.2 us  [flip(): lax.ppermute(block, 'grp', [(i, i ^ bits) for i in range(lax.axis_size('g...]
  transfers between devices with their start and end apart: 21 -> 21, of which waited for: 7 -> 7; matrix products, arithmetic and copies ran while one was open for 14% -> 14% of each run, Pallas kernels for 31% -> 29%
where the time goes in v8:
time: 110 us
  Pallas kernels  37.9 us (34%)
  waiting for transfers between devices  23 us (21%)
  starting transfers between devices  20.6 us (19%)
  other arithmetic  11.9 us (11%)
  blocking collectives  10.3 us (9%)
  local copies, waits for them, and re-layouts  5.13 us (5%)
    pallas_call x7, Pallas kernels, terms(): pl.pallas_call(functools.partial(terms_kernel, kind, cut, segments, stand...  29.9 us
    ppermute x17, waiting for transfers between devices, flip(): lax.ppermute(block, 'grp', [(i, i ^ bits) for i in range(lax.axis_size('g...  21.2 us
    ppermute x17, starting transfers between devices, flip(): lax.ppermute(block, 'grp', [(i, i ^ bits) for i in range(lax.axis_size('g...  15 us
    all_to_all x1, blocking collectives, body(): sums = lax.all_to_all(sums, ('blk', 'grp'), 0, 0, tiled=True)  10.3 us
    sort x1, other arithmetic, body(): listed = jnp.sort(kind * rows + near_row[0] << bits | number)  5.75 us
    ppermute x4, starting transfers between devices, wave_swaps(): moved = lax.ppermute(waves, 'blk', [(i, i ^ bits) for i in range(blocks)])  5.52 us
    pallas_call x2, Pallas kernels, gather_wave(): pl.pallas_call(wave_kernel, out_shape=jax.ShapeDtypeStruct((1, samples),...  2.95 us
    pallas_call x3, Pallas kernels, join(): pl.pallas_call(functools.partial(join_kernel, cuts, len(served) // len(cu...  2.72 us
  transfers between devices with their start and end apart: 21, of which 7 were waited for; matrix products, arithmetic and copies ran while one was open for 14% of the time, Pallas kernels for 29%

profile of v8, /device:TPU:0, one launch (start us, length us, event | category | flops | bytes accessed | tf_op | source)
XLA Modules:
  0.0 109.7 jit_solution(3604204364141842507)
XLA Ops:
  0.7 1.2 %copy-done.2 = f32[1,1024,240]{1,2,0:T(8,128)S(1)} copy-done((f32[1,1024,240]{1,2,0:T(8,128)S(1)}, f32[1,1024,240]{1,2,0:T(8,128)}, u32[]{:S(2)}) %copy-start.2) | copy-done | bytes 983064
  2.1 3.1 %collective-permute-start = (bf16[640,256]{1,0:T(8,128)(2,1)S(1)}, bf16[640,256]{1,0:T(8,128)(2,1)S(1)}, u32[]{:S(2)}, u32[]{:S(2)}) collective-permute-start(bf16[640,256]{1,0:T(8,128)(2,1)S(1)} %get-tuple-element.28.rest_0_.rest_3_), channel_id=1, source_target_pairs={{0,2},{1,3},{2,0},{3,1},{4,6},{5,7},{6,4},{7,5},{8,10},{9,11},{10,... | collective-permute-start | bytes 983048 | tf_op jit(solution)/shard_map/ppermute | solution.py:392
  5.7 0.7 broadcast_xor_fusion
  6.4 0.7 select_add_fusion
  7.3 5.8 %sort.15 = (s32[3072]{0:T(1024)S(1)}, s32[3072]{0:T(1024)}) sort(s32[3072]{0:T(1024)S(1)} %get-tuple-element.54, s32[3072]{0:T(1024)S(1)} %iota.24), dimensions={0}, to_apply=%region_0.1 | sort | flops 36864 | bytes 49152 | tf_op jit(solution)/shard_map/jit(sort)/sort | solution.py:437
  13.0 0.6 pad_add_fusion
  13.6 2.8 %collective-permute-start.2 = (s32[6161]{0:T(1024)}, s32[6161]{0:T(1024)}, u32[]{:S(2)}, u32[]{:S(2)}) collective-permute-start(s32[6161]{0:T(1024)} %pad_add_fusion), channel_id=1, source_target_pairs={{0,4},{1,5},{2,6},{3,7},{4,0},{5,1},{6,2},{7,3},{8,12},{9,13},{10,... | collective-permute-start | bytes 73940 | tf_op jit(solution)/shard_map/ppermute | solution.py:392
  16.4 0.6 convert_reduce_fusion.1
  17.1 0.9 copy-done.7
  18.0 1.5 %gather_wave.2 = f32[1,512]{1,0:T(1,128)S(1)} custom-call(bf16[240,512]{1,0:T(8,128)(2,1)S(1)} %copy-done.7, bf16[1024,512]{1,0:T(8,128)(2,1)S(1)} %bitcast.33, bf16[640,256]{1,0:T(8,128)(2,1)S(1)} %get-tuple-element.28.rest_0_.rest_3_, bf16[384,256]{1,0:T(8,128)(2,1)S(1)} %get-tuple-element.29.rest_1_.rest_4_), custom_call_target="tpu_custom_call" | custom-call | flops 1 | bytes 1 | tf_op jit(solution)/shard_map/gather_wave/pallas_call | solution.py:93
  19.6 0.6 pad_clamp_fusion
  20.2 0.5 collective-permute-start.8
  20.7 1.5 %collective-permute-start.3 = (f32[1,512]{1,0:T(1,128)S(1)}, f32[1,512]{1,0:T(1,128)S(1)}, u32[]{:S(2)}, u32[]{:S(2)}) collective-permute-start(f32[1,512]{1,0:T(1,128)S(1)} %gather_wave.2), channel_id=1, source_target_pairs={{0,8},{8,0},{16,24},{24,16},{1,9},{9,1},{17,25},{25,17},{2,10},{10... | collective-permute-start | bytes 6152 | tf_op jit(solution)/shard_map/ppermute | solution.py:403
  22.2 0.7 slice_convert_fusion
  22.9 0.7 slice.11.bound_ref
  23.6 0.4 convert_element_type.18.table_ref
  24.1 4.6 %terms_all.2 = bf16[608,256]{1,0:T(8,128)(2,1)} custom-call(s32[3072]{0:T(1024)S(1)} %get-tuple-element.52.source_ref, s32[3072]{0:T(1024)S(1)} %get-tuple-element.51.target_ref, s32[17]{0:T(128)S(1)} %slice.11.bound_ref, bf16[1024,3]{1,0:T(8,128)(2,1)S(1)} %convert_element_type.18.table_ref, bf16[8,240,240]{2,1,0:T(8,128)(2,1)S(1)} %copy-done.1, ...), custom_call_target="tpu_custom_call" | custom-call | flops 1 | bytes 1 | tf_op jit(solution)/shard_map/terms_all/pallas_call | solution.py:257
  28.7 2.4 %collective-permute-start.9 = (bf16[608,256]{1,0:T(8,128)(2,1)}, bf16[608,256]{1,0:T(8,128)(2,1)}, u32[]{:S(2)}, u32[]{:S(2)}) collective-permute-start(bf16[608,256]{1,0:T(8,128)(2,1)} %terms_all.2), channel_id=1, source_target_pairs={{0,4},{1,5},{2,6},{3,7},{4,0},{5,1},{6,2},{7,3},{8,12},{9,13},{10,... | collective-permute-start | bytes 933896 | tf_op jit(solution)/shard_map/ppermute | solution.py:392
  31.1 0.6 pad_maximum_fusion
  31.7 1.4 %collective-permute-start.4 = (f32[2,512]{1,0:T(2,128)}, f32[2,512]{1,0:T(2,128)}, u32[]{:S(2)}, u32[]{:S(2)}) collective-permute-start(f32[2,512]{1,0:T(2,128)} %pad_maximum_fusion), channel_id=1, source_target_pairs={{0,16},{8,24},{16,0},{24,8},{1,17},{9,25},{17,1},{25,9},{2,18},{10... | collective-permute-start | bytes 12296 | tf_op jit(solution)/shard_map/ppermute | solution.py:403
  33.1 0.5 iota_compare_fusion.2
  33.6 1.1 %convert_element_type.17.table_ref = bf16[1024,3]{1,0:T(8,128)(2,1)} reshape(bf16[3072]{0:T(1024)(128)(2,1)S(1)} %copy-done.11) | data formatting | bytes 12288 | tf_op jit(solution)/shard_map/convert_element_type | solution.py:444
  34.8 0.7 gather_fusion
  35.5 3.2 %terms_all.3 = bf16[368,256]{1,0:T(8,128)(2,1)S(1)} custom-call(s32[3072]{0:T(1024)S(1)} %get-tuple-element.52.source_ref, s32[3072]{0:T(1024)S(1)} %get-tuple-element.51.target_ref, s32[17]{0:T(128)S(1)} %slice.11.bound_ref, bf16[1024,3]{1,0:T(8,128)(2,1)S(1)} %convert_element_type.18.table_ref, bf16[8,240,240]{2,1,0:T(8,128)(2,1)S(1)} %copy-done.1, ...), custom_call_target="tpu_custom_call" | custom-call | flops 1 | bytes 1 | tf_op jit(solution)/shard_map/terms_all/pallas_call | solution.py:257
  38.7 1.1 %collective-permute-start.10 = (bf16[368,256]{1,0:T(8,128)(2,1)S(1)}, bf16[368,256]{1,0:T(8,128)(2,1)S(1)}, u32[]{:S(2)}, u32[]{:S(2)}) collective-permute-start(bf16[368,256]{1,0:T(8,128)(2,1)S(1)} %terms_all.3), channel_id=1, source_target_pairs={{0,4},{1,5},{2,6},{3,7},{4,0},{5,1},{6,2},{7,3},{8,12},{9,13},{10,... | collective-permute-start | bytes 565256 | tf_op jit(solution)/shard_map/ppermute | solution.py:392
  39.8 0.8 fusion.4
  40.6 6.7 %terms_near.2.base_ref = f32[1024,240]{1,0:T(8,128)S(1)} custom-call(s32[3072]{0:T(1024)S(1)} %get-tuple-element.56.source_ref, s32[3072]{0:T(1024)S(1)} %get-tuple-element.55.target_ref, s32[17]{0:T(128)S(1)} %convert_reduce_fusion.bound_ref, bf16[1024,3]{1,0:T(8,128)(2,1)S(1)} %copy-done.6, bf16[8,240,240]{2,1,0:T(8,128)(2,1)S(1)} %copy-done.1, ...), custom_call_target="tpu_custom_call" | custom-call | flops 1 | bytes 1 | tf_op jit(solution)/shard_map/terms_near/pallas_call | solution.py:257
  47.3 3.5 %collective-permute-done.9.rest_0_ = bf16[608,256]{1,0:T(8,128)(2,1)} collective-permute-done((bf16[608,256]{1,0:T(8,128)(2,1)}, bf16[608,256]{1,0:T(8,128)(2,1)}, u32[]{:S(2)}, u32[]{:S(2)}) %collective-permute-start.9) | collective-permute-done | bytes 311328 | tf_op jit(solution)/shard_map/ppermute | solution.py:392
  50.9 1.6 %join_first.2 = (f32[240,640]{1,0:T(8,128)S(1)}, bf16[640,256]{1,0:T(8,128)(2,1)S(1)}, f32[1,128]{1,0:T(1,128)S(1)}) custom-call(f32[1024,240]{1,0:T(8,128)S(1)} %terms_near.2.base_ref, f32[240,1024]{1,0:T(8,128)S(1)} %bitcast.37, f32[240,1024]{1,0:T(8,128)S(1)} %bitcast.29, f32[1,128]{1,0:T(1,128)S(1)} %broadcast_in_dim.44.sums_in_ref, ...), custom_call_target="tpu_custom_call" | custom-call | tf_op jit(solution)/shard_map/join_first/pallas_call | solution.py:317
  52.6 1.1 %collective-permute-done.10.rest_0_ = bf16[368,256]{1,0:T(8,128)(2,1)S(1)} collective-permute-done((bf16[368,256]{1,0:T(8,128)(2,1)S(1)}, bf16[368,256]{1,0:T(8,128)(2,1)S(1)}, u32[]{:S(2)}, u32[]{:S(2)}) %collective-permute-start.10) | collective-permute-done | bytes 188448 | tf_op jit(solution)/shard_map/ppermute | solution.py:392
  54.2 1.1 collective-permute-start.16
  55.6 3.7 %terms_own.1 = (f32[1024,240]{1,0:T(8,128)S(1)}, f32[8,128]{1,0:T(8,128)S(1)}) custom-call(s32[3072]{0:T(1024)S(1)} %get-tuple-element.52.source_ref, s32[3072]{0:T(1024)S(1)} %get-tuple-element.51.target_ref, s32[17]{0:T(128)S(1)} %slice.11.bound_ref, bf16[1024,3]{1,0:T(8,128)(2,1)S(1)} %convert_element_type.18.table_ref, ...), custom_call_target="tpu_custom_call" | custom-call | flops 1 | bytes 1 | tf_op jit(solution)/shard_map/terms_own/pallas_call | solution.py:257
  59.4 7.5 %collective-permute-done.16.rest_8_.rest_3_ = bf16[384,256]{1,0:T(8,128)(2,1)S(1)} collective-permute-done((bf16[384,256]{1,0:T(8,128)(2,1)S(1)}, bf16[384,256]{1,0:T(8,128)(2,1)S(1)}, u32[]{:S(2)}, u32[]{:S(2)}) %collective-permute-start.16) | collective-permute-done | bytes 196640 | tf_op jit(solution)/shard_map/ppermute | solution.py:392
  66.9 0.5 collective-permute-start.18
  67.4 1.4 %collective-permute-done.18.rest_10_.rest_5_ = bf16[384,256]{1,0:T(8,128)(2,1)S(1)} collective-permute-done((bf16[384,256]{1,0:T(8,128)(2,1)S(1)}, bf16[384,256]{1,0:T(8,128)(2,1)S(1)}, u32[]{:S(2)}, u32[]{:S(2)}) %collective-permute-start.18) | collective-permute-done | bytes 196640 | tf_op jit(solution)/shard_map/ppermute | solution.py:392
  68.8 2.9 %terms_rest.2 = bf16[608,256]{1,0:T(8,128)(2,1)S(1)} custom-call(s32[3072]{0:T(1024)S(1)} %get-tuple-element.52.source_ref, s32[3072]{0:T(1024)S(1)} %get-tuple-element.51.target_ref, s32[17]{0:T(128)S(1)} %slice.11.bound_ref, bf16[1024,3]{1,0:T(8,128)(2,1)S(1)} %convert_element_type.18.table_ref, bf16[8,240,240]{2,1,0:T(8,128)(2,1)S(1)} %copy-done.1, ...), custom_call_target="tpu_custom_call" | custom-call | flops 1 | bytes 1 | tf_op jit(solution)/shard_map/terms_rest/pallas_call | solution.py:257
  71.7 1.0 collective-permute-start.19
  72.7 1.5 %gather_wave.3 = f32[1,512]{1,0:T(1,128)S(1)} custom-call(bf16[240,512]{1,0:T(8,128)(2,1)S(1)} %copy-done.8, bf16[1024,512]{1,0:T(8,128)(2,1)S(1)} %bitcast.35, bf16[640,256]{1,0:T(8,128)(2,1)S(1)} %get-tuple-element.34.rest_0_.rest_3_, bf16[384,256]{1,0:T(8,128)(2,1)S(1)} %get-tuple-element.36.rest_1_.rest_4_), custom_call_target="tpu_custom_call" | custom-call | flops 1 | bytes 1 | tf_op jit(solution)/shard_map/gather_wave/pallas_call | solution.py:93
  74.2 0.7 collective-permute-start.11
  74.9 2.4 %terms_rest.3 = bf16[368,256]{1,0:T(8,128)(2,1)S(1)} custom-call(s32[3072]{0:T(1024)S(1)} %get-tuple-element.52.source_ref, s32[3072]{0:T(1024)S(1)} %get-tuple-element.51.target_ref, s32[17]{0:T(128)S(1)} %slice.11.bound_ref, bf16[1024,3]{1,0:T(8,128)(2,1)S(1)} %convert_element_type.18.table_ref, bf16[8,240,240]{2,1,0:T(8,128)(2,1)S(1)} %copy-done.1, ...), custom_call_target="tpu_custom_call" | custom-call | flops 1 | bytes 1 | tf_op jit(solution)/shard_map/terms_rest/pallas_call | solution.py:257
  77.3 1.9 %collective-permute-start.20 = (bf16[368,256]{1,0:T(8,128)(2,1)S(1)}, bf16[368,256]{1,0:T(8,128)(2,1)S(1)}, u32[]{:S(2)}, u32[]{:S(2)}) collective-permute-start(bf16[368,256]{1,0:T(8,128)(2,1)S(1)} %terms_rest.3), channel_id=1, source_target_pairs={{0,4},{1,5},{2,6},{3,7},{4,0},{5,1},{6,2},{7,3},{8,12},{9,13},{10,... | collective-permute-start | bytes 565256 | tf_op jit(solution)/shard_map/ppermute | solution.py:392
  79.2 1.9 %collective-permute-start.12 = (f32[2,512]{1,0:T(2,128)S(1)}, f32[2,512]{1,0:T(2,128)S(1)}, u32[]{:S(2)}, u32[]{:S(2)}) collective-permute-start(f32[2,512]{1,0:T(2,128)S(1)} %pad_maximum_fusion.1), channel_id=1, source_target_pairs={{0,16},{8,24},{16,0},{24,8},{1,17},{9,25},{17,1},{25,9},{2,18},{10... | collective-permute-start | bytes 12296 | tf_op jit(solution)/shard_map/ppermute | solution.py:403
  81.1 1.8 %collective-permute-done.12 = f32[2,512]{1,0:T(2,128)S(1)} collective-permute-done((f32[2,512]{1,0:T(2,128)S(1)}, f32[2,512]{1,0:T(2,128)S(1)}, u32[]{:S(2)}, u32[]{:S(2)}) %collective-permute-start.12) | collective-permute-done | bytes 4128 | tf_op jit(solution)/shard_map/ppermute | solution.py:403
  82.9 6.3 %terms_near.3.base_ref = f32[1024,240]{1,0:T(8,128)S(1)} custom-call(s32[3072]{0:T(1024)S(1)} %get-tuple-element.56.source_ref, s32[3072]{0:T(1024)S(1)} %get-tuple-element.55.target_ref, s32[17]{0:T(128)S(1)} %convert_reduce_fusion.bound_ref, bf16[1024,3]{1,0:T(8,128)(2,1)S(1)} %copy-done.6, bf16[8,240,240]{2,1,0:T(8,128)(2,1)S(1)} %copy-done.1, ...), custom_call_target="tpu_custom_call" | custom-call | flops 1 | bytes 1 | tf_op jit(solution)/shard_map/terms_near/pallas_call | solution.py:257
  89.3 7.3 %collective-permute-done.20.rest_1_ = bf16[368,256]{1,0:T(8,128)(2,1)S(1)} collective-permute-done((bf16[368,256]{1,0:T(8,128)(2,1)S(1)}, bf16[368,256]{1,0:T(8,128)(2,1)S(1)}, u32[]{:S(2)}, u32[]{:S(2)}) %collective-permute-start.20) | collective-permute-done | bytes 188448 | tf_op jit(solution)/shard_map/ppermute | solution.py:392
  96.6 0.7 join_second.1
  97.3 10.3 %all_to_all.11 = f32[32,1,128]{2,1,0:T(1,128)S(1)} all-to-all(f32[32,1,128]{2,1,0:T(1,128)S(1)} %bitcast.43), channel_id=1, replica_groups=mesh['blk'=4,'grp'=8] {'blk','grp'}, dimensions={0} | all-to-all | bytes 32768 | tf_op jit(solution)/shard_map/all_to_all | solution.py:541
  107.7 2.1 %finish.1 = (f32[240,1024]{1,0:T(8,128)}, f32[240,1024]{1,0:T(8,128)}, f32[2,3]{1,0:T(2,128)}) custom-call(f32[32,128]{1,0:T(8,128)S(1)} %bitcast.42, f32[240,1024]{1,0:T(8,128)S(1)} %bitcast.32, f32[240,1024]{1,0:T(8,128)S(1)} %get-tuple-element.46.c_ref, f32[240,640]{1,0:T(8,128)S(1)} %get-tuple-element.43.rest_2_.rest_0_, ...), custom_call_target="tpu_custom_call" | custom-call | tf_op jit(solution)/shard_map/finish/pallas_call | solution.py:381
  (56 shorter events, 2.1 us)
Async XLA Ops:
  0.6 34.1 %copy-start = (f32[1,1,4,512]{3,2,1,0:T(4,128)S(1)}, f32[1,1,4,512]{3,2,1,0:T(4,128)}, u32[]{:S(2)}) copy-start(f32[1,1,4,512]{3,2,1,0:T(4,128)} %param.19) | copy-start | bytes 24580
  0.6 1.2 %copy-start.2 = (f32[1,1024,240]{1,2,0:T(8,128)S(1)}, f32[1,1024,240]{1,2,0:T(8,128)}, u32[]{:S(2)}) copy-start(f32[1,1024,240]{1,2,0:T(8,128)} %param.10) | copy-start | bytes 2949124
  1.9 15.2 %copy-start.4 = (bf16[1,1024,512]{2,1,0:T(8,128)(2,1)S(1)}, bf16[1,1024,512]{2,1,0:T(8,128)(2,1)}, u32[]{:S(2)}) copy-start(bf16[1,1024,512]{2,1,0:T(8,128)(2,1)} %param.18) | copy-start | bytes 3145732
  2.1 17.4 %collective-permute-start = (bf16[640,256]{1,0:T(8,128)(2,1)S(1)}, bf16[640,256]{1,0:T(8,128)(2,1)S(1)}, u32[]{:S(2)}, u32[]{:S(2)}) collective-permute-start(bf16[640,256]{1,0:T(8,128)(2,1)S(1)} %get-tuple-element.28.rest_0_.rest_3_), channel_id=1, source_target_pairs={{0,2},{1,3},{2,0},{3,1},{4,6},{5,7},{6,4},{7,5},{8,10},{9,11},{10,... | collective-permute-start | bytes 983048 | tf_op jit(solution)/shard_map/ppermute | solution.py:392
  5.2 18.9 %collective-permute-start.5 = (bf16[640,256]{1,0:T(8,128)(2,1)S(1)}, bf16[640,256]{1,0:T(8,128)(2,1)S(1)}, u32[]{:S(2)}, u32[]{:S(2)}) collective-permute-start(bf16[640,256]{1,0:T(8,128)(2,1)S(1)} %get-tuple-element.28.rest_0_.rest_3_), channel_id=1, source_target_pairs={{0,1},{1,0},{2,3},{3,2},{4,5},{5,4},{6,7},{7,6},{8,9},{9,8},{10,11... | collective-permute-start | bytes 983048 | tf_op jit(solution)/shard_map/ppermute | solution.py:392
  5.2 14.3 %collective-permute-start.1 = (bf16[384,256]{1,0:T(8,128)(2,1)S(1)}, bf16[384,256]{1,0:T(8,128)(2,1)}, u32[]{:S(2)}, u32[]{:S(2)}) collective-permute-start(bf16[384,256]{1,0:T(8,128)(2,1)S(1)} %get-tuple-element.29.rest_1_.rest_4_), channel_id=1, source_target_pairs={{0,2},{1,3},{2,0},{3,1},{4,6},{5,7},{6,4},{7,5},{8,10},{9,11},{10,... | collective-permute-start | bytes 589832 | tf_op jit(solution)/shard_map/ppermute | solution.py:392
  5.3 18.7 %collective-permute-start.6 = (bf16[384,256]{1,0:T(8,128)(2,1)S(1)}, bf16[384,256]{1,0:T(8,128)(2,1)}, u32[]{:S(2)}, u32[]{:S(2)}) collective-permute-start(bf16[384,256]{1,0:T(8,128)(2,1)S(1)} %get-tuple-element.29.rest_1_.rest_4_), channel_id=1, source_target_pairs={{0,1},{1,0},{2,3},{3,2},{4,5},{5,4},{6,7},{7,6},{8,9},{9,8},{10,11... | collective-permute-start | bytes 589832 | tf_op jit(solution)/shard_map/ppermute | solution.py:392
  7.3 5.8 %copy-start.10 = (s32[1,3072]{1,0:T(1,128)S(1)}, s32[1,3072]{1,0:T(1,128)}, u32[]{:S(2)}) copy-start(s32[1,3072]{1,0:T(1,128)} %param.14) | copy-start | bytes 36868
  13.6 5.8 %collective-permute-start.2 = (s32[6161]{0:T(1024)}, s32[6161]{0:T(1024)}, u32[]{:S(2)}, u32[]{:S(2)}) collective-permute-start(s32[6161]{0:T(1024)} %pad_add_fusion), channel_id=1, source_target_pairs={{0,4},{1,5},{2,6},{3,7},{4,0},{5,1},{6,2},{7,3},{8,12},{9,13},{10,... | collective-permute-start | bytes 73940 | tf_op jit(solution)/shard_map/ppermute | solution.py:392
  17.1 0.9 copy-start.7
  18.0 6.1 %copy-start.1 = (bf16[8,240,240]{2,1,0:T(8,128)(2,1)S(1)}, bf16[8,240,240]{2,1,0:T(8,128)(2,1)}, u32[]{:S(2)}) copy-start(bf16[8,240,240]{2,1,0:T(8,128)(2,1)} %tables_ref.13) | copy-start | bytes 2764804
  19.5 4.5 %collective-permute-start.7 = (bf16[640,256]{1,0:T(8,128)(2,1)S(1)}, bf16[640,256]{1,0:T(8,128)(2,1)}, u32[]{:S(2)}, u32[]{:S(2)}) collective-permute-start(bf16[640,256]{1,0:T(8,128)(2,1)S(1)} %collective-permute-done.rest_7_.rest_4_), channel_id=1, source_target_pairs={{0,1},{1,0},{2,3},{3,2},{4,5},{5,4},{6,7},{7,6},{8,9},{9,8},{10,11... | collective-permute-start | bytes 983048 | tf_op jit(solution)/shard_map/ppermute | solution.py:392
  20.2 3.9 %collective-permute-start.8 = (bf16[384,256]{1,0:T(8,128)(2,1)}, bf16[384,256]{1,0:T(8,128)(2,1)}, u32[]{:S(2)}, u32[]{:S(2)}) collective-permute-start(bf16[384,256]{1,0:T(8,128)(2,1)} %collective-permute-done.1.rest_8_.rest_5_), channel_id=1, source_target_pairs={{0,1},{1,0},{2,3},{3,2},{4,5},{5,4},{6,7},{7,6},{8,9},{9,8},{10,11... | collective-permute-start | bytes 589832 | tf_op jit(solution)/shard_map/ppermute | solution.py:392
  20.7 10.4 %collective-permute-start.3 = (f32[1,512]{1,0:T(1,128)S(1)}, f32[1,512]{1,0:T(1,128)S(1)}, u32[]{:S(2)}, u32[]{:S(2)}) collective-permute-start(f32[1,512]{1,0:T(1,128)S(1)} %gather_wave.2), channel_id=1, source_target_pairs={{0,8},{8,0},{16,24},{24,16},{1,9},{9,1},{17,25},{25,17},{2,10},{10... | collective-permute-start | bytes 6152 | tf_op jit(solution)/shard_map/ppermute | solution.py:403
  28.7 4.9 %copy-start.11 = (bf16[3072]{0:T(1024)(128)(2,1)S(1)}, bf16[3072]{0:T(1024)(128)(2,1)}, u32[]{:S(2)}) copy-start(bf16[3072]{0:T(1024)(128)(2,1)} %convert_reduce_fusion.1) | copy-start | bytes 18436
  28.7 22.1 %collective-permute-start.9 = (bf16[608,256]{1,0:T(8,128)(2,1)}, bf16[608,256]{1,0:T(8,128)(2,1)}, u32[]{:S(2)}, u32[]{:S(2)}) collective-permute-start(bf16[608,256]{1,0:T(8,128)(2,1)} %terms_all.2), channel_id=1, source_target_pairs={{0,4},{1,5},{2,6},{3,7},{4,0},{5,1},{6,2},{7,3},{8,12},{9,13},{10,... | collective-permute-start | bytes 933896 | tf_op jit(solution)/shard_map/ppermute | solution.py:392
  31.7 8.1 %collective-permute-start.4 = (f32[2,512]{1,0:T(2,128)}, f32[2,512]{1,0:T(2,128)}, u32[]{:S(2)}, u32[]{:S(2)}) collective-permute-start(f32[2,512]{1,0:T(2,128)} %pad_maximum_fusion), channel_id=1, source_target_pairs={{0,16},{8,24},{16,0},{24,8},{1,17},{9,25},{17,1},{25,9},{2,18},{10... | collective-permute-start | bytes 12296 | tf_op jit(solution)/shard_map/ppermute | solution.py:403
  35.4 4.3 %copy-start.12 = (pred[4]{0:T(512)(128)(4,1)S(1)}, pred[4]{0:T(512)(128)(4,1)}, u32[]{:S(2)}) copy-start(pred[4]{0:T(512)(128)(4,1)} %iota_compare_fusion.2) | copy-start | bytes 16
  35.5 5.1 %copy-start.6 = (bf16[1024,3]{1,0:T(8,128)(2,1)S(1)}, bf16[1024,3]{1,0:T(8,128)(2,1)}, u32[]{:S(2)}) copy-start(bf16[1024,3]{1,0:T(8,128)(2,1)} %convert_element_type.17.table_ref) | copy-start | bytes 18436
  35.5 5.1 %copy-start.9 = (bf16[512,240]{0,1:T(8,128)(2,1)S(1)}, bf16[512,240]{0,1:T(8,128)(2,1)}, u32[]{:S(2)}) copy-start(bf16[512,240]{0,1:T(8,128)(2,1)} %param.17) | copy-start | bytes 737284
  38.7 15.0 %collective-permute-start.10 = (bf16[368,256]{1,0:T(8,128)(2,1)S(1)}, bf16[368,256]{1,0:T(8,128)(2,1)S(1)}, u32[]{:S(2)}, u32[]{:S(2)}) collective-permute-start(bf16[368,256]{1,0:T(8,128)(2,1)S(1)} %terms_all.3), channel_id=1, source_target_pairs={{0,4},{1,5},{2,6},{3,7},{4,0},{5,1},{6,2},{7,3},{8,12},{9,13},{10,... | collective-permute-start | bytes 565256 | tf_op jit(solution)/shard_map/ppermute | solution.py:392
  40.6 10.3 %copy-start.3 = (f32[1,1024,240]{1,2,0:T(8,128)S(1)}, f32[1,1024,240]{1,2,0:T(8,128)}, u32[]{:S(2)}) copy-start(f32[1,1024,240]{1,2,0:T(8,128)} %param.10) | copy-start | bytes 2949124
  40.6 10.3 %copy-start.5 = (f32[1,1024,240]{1,2,0:T(8,128)S(1)}, f32[1,1024,240]{1,2,0:T(8,128)}, u32[]{:S(2)}) copy-start(f32[1,1024,240]{1,2,0:T(8,128)} %param.11) | copy-start | bytes 2949124
  52.4 3.2 %collective-permute-start.13 = (bf16[640,256]{1,0:T(8,128)(2,1)S(1)}, bf16[640,256]{1,0:T(8,128)(2,1)S(1)}, u32[]{:S(2)}, u32[]{:S(2)}) collective-permute-start(bf16[640,256]{1,0:T(8,128)(2,1)S(1)} %get-tuple-element.34.rest_0_.rest_3_), channel_id=1, source_target_pairs={{0,1},{1,0},{2,3},{3,2},{4,5},{5,4},{6,7},{7,6},{8,9},{9,8},{10,11... | collective-permute-start | bytes 983048 | tf_op jit(solution)/shard_map/ppermute | solution.py:392
  52.5 14.3 %collective-permute-start.15 = (bf16[640,256]{1,0:T(8,128)(2,1)S(1)}, bf16[640,256]{1,0:T(8,128)(2,1)S(1)}, u32[]{:S(2)}, u32[]{:S(2)}) collective-permute-start(bf16[640,256]{1,0:T(8,128)(2,1)S(1)} %get-tuple-element.34.rest_0_.rest_3_), channel_id=1, source_target_pairs={{0,2},{1,3},{2,0},{3,1},{4,6},{5,7},{6,4},{7,5},{8,10},{9,11},{10,... | collective-permute-start | bytes 983048 | tf_op jit(solution)/shard_map/ppermute | solution.py:392
  54.1 1.5 %collective-permute-start.14 = (bf16[384,256]{1,0:T(8,128)(2,1)S(1)}, bf16[384,256]{1,0:T(8,128)(2,1)S(1)}, u32[]{:S(2)}, u32[]{:S(2)}) collective-permute-start(bf16[384,256]{1,0:T(8,128)(2,1)S(1)} %get-tuple-element.36.rest_1_.rest_4_), channel_id=1, source_target_pairs={{0,1},{1,0},{2,3},{3,2},{4,5},{5,4},{6,7},{7,6},{8,9},{9,8},{10,11... | collective-permute-start | bytes 589832 | tf_op jit(solution)/shard_map/ppermute | solution.py:392
  54.2 12.7 %collective-permute-start.16 = (bf16[384,256]{1,0:T(8,128)(2,1)S(1)}, bf16[384,256]{1,0:T(8,128)(2,1)S(1)}, u32[]{:S(2)}, u32[]{:S(2)}) collective-permute-start(bf16[384,256]{1,0:T(8,128)(2,1)S(1)} %get-tuple-element.36.rest_1_.rest_4_), channel_id=1, source_target_pairs={{0,2},{1,3},{2,0},{3,1},{4,6},{5,7},{6,4},{7,5},{8,10},{9,11},{10,... | collective-permute-start | bytes 589832 | tf_op jit(solution)/shard_map/ppermute | solution.py:392
  66.9 1.9 %collective-permute-start.17 = (bf16[640,256]{1,0:T(8,128)(2,1)S(1)}, bf16[640,256]{1,0:T(8,128)(2,1)S(1)}, u32[]{:S(2)}, u32[]{:S(2)}) collective-permute-start(bf16[640,256]{1,0:T(8,128)(2,1)S(1)} %collective-permute-done.15.rest_7_.rest_2_), channel_id=1, source_target_pairs={{0,1},{1,0},{2,3},{3,2},{4,5},{5,4},{6,7},{7,6},{8,9},{9,8},{10,11... | collective-permute-start | bytes 983048 | tf_op jit(solution)/shard_map/ppermute | solution.py:392
  66.9 1.9 %collective-permute-start.18 = (bf16[384,256]{1,0:T(8,128)(2,1)S(1)}, bf16[384,256]{1,0:T(8,128)(2,1)S(1)}, u32[]{:S(2)}, u32[]{:S(2)}) collective-permute-start(bf16[384,256]{1,0:T(8,128)(2,1)S(1)} %collective-permute-done.16.rest_8_.rest_3_), channel_id=1, source_target_pairs={{0,1},{1,0},{2,3},{3,2},{4,5},{5,4},{6,7},{7,6},{8,9},{9,8},{10,11... | collective-permute-start | bytes 589832 | tf_op jit(solution)/shard_map/ppermute | solution.py:392
  68.8 3.9 %copy-start.8 = (bf16[240,512]{1,0:T(8,128)(2,1)S(1)}, bf16[240,512]{1,0:T(8,128)(2,1)}, u32[]{:S(2)}) copy-start(bf16[240,512]{1,0:T(8,128)(2,1)} %out_ref.3) | copy-start | bytes 737284
  71.7 24.9 %collective-permute-start.19 = (bf16[608,256]{1,0:T(8,128)(2,1)S(1)}, bf16[608,256]{1,0:T(8,128)(2,1)S(1)}, u32[]{:S(2)}, u32[]{:S(2)}) collective-permute-start(bf16[608,256]{1,0:T(8,128)(2,1)S(1)} %terms_rest.2), channel_id=1, source_target_pairs={{0,4},{1,5},{2,6},{3,7},{4,0},{5,1},{6,2},{7,3},{8,12},{9,13},{10,... | collective-permute-start | bytes 933896 | tf_op jit(solution)/shard_map/ppermute | solution.py:392
  74.2 5.0 %collective-permute-start.11 = (f32[1,512]{1,0:T(1,128)S(1)}, f32[1,512]{1,0:T(1,128)S(1)}, u32[]{:S(2)}, u32[]{:S(2)}) collective-permute-start(f32[1,512]{1,0:T(1,128)S(1)} %gather_wave.3), channel_id=1, source_target_pairs={{0,8},{8,0},{16,24},{24,16},{1,9},{9,1},{17,25},{25,17},{2,10},{10... | collective-permute-start | bytes 6152 | tf_op jit(solution)/shard_map/ppermute | solution.py:403
  77.3 19.3 %collective-permute-start.20 = (bf16[368,256]{1,0:T(8,128)(2,1)S(1)}, bf16[368,256]{1,0:T(8,128)(2,1)S(1)}, u32[]{:S(2)}, u32[]{:S(2)}) collective-permute-start(bf16[368,256]{1,0:T(8,128)(2,1)S(1)} %terms_rest.3), channel_id=1, source_target_pairs={{0,4},{1,5},{2,6},{3,7},{4,0},{5,1},{6,2},{7,3},{8,12},{9,13},{10,... | collective-permute-start | bytes 565256 | tf_op jit(solution)/shard_map/ppermute | solution.py:392
  79.2 3.7 %collective-permute-start.12 = (f32[2,512]{1,0:T(2,128)S(1)}, f32[2,512]{1,0:T(2,128)S(1)}, u32[]{:S(2)}, u32[]{:S(2)}) collective-permute-start(f32[2,512]{1,0:T(2,128)S(1)} %pad_maximum_fusion.1), channel_id=1, source_target_pairs={{0,16},{8,24},{16,0},{24,8},{1,17},{9,25},{17,1},{25,9},{2,18},{10... | collective-permute-start | bytes 12296 | tf_op jit(solution)/shard_map/ppermute | solution.py:403

commit v9 on v8

--- a/solution.py
+++ b/solution.py
@@ -473,7 +473,7 @@
     coded = code(x_t, width, cuts)
     across, same = swapped(coded, 2), swapped(coded, 1)
     waves = gather_wave(coded, wave_out, angle)
-    *across, waves, asked = once(*across, waves, asked)
+    *across, asked = once(*across, asked)
     asked = [requests_of(words) for words in asked]
     local = requests_of(message)
     beyond = swapped(across, 1)

time: 110 us -> 111 us (level)
  transfers between devices with their start and end apart: 21 -> 21, of which waited for: 7 -> 7; matrix products, arithmetic and copies ran while one was open for 14% -> 13% of each run, Pallas kernels for 29% -> 30%
where the time goes in v9:
time: 111 us; the launch traced here: 110 us
  Pallas kernels  38.8 us (35%)
  waiting for transfers between devices  22.9 us (21%)
  starting transfers between devices  20 us (18%)
  other arithmetic  11.9 us (11%)
  blocking collectives  10.3 us (9%)
  local copies, waits for them, and re-layouts  5.13 us (5%)
    pallas_call x7, Pallas kernels, terms(): pl.pallas_call(functools.partial(terms_kernel, kind, cut, segments, stand...  30.9 us
    ppermute x17, waiting for transfers between devices, flip(): lax.ppermute(block, 'grp', [(i, i ^ bits) for i in range(lax.axis_size('g...  20.8 us
    ppermute x17, starting transfers between devices, flip(): lax.ppermute(block, 'grp', [(i, i ^ bits) for i in range(lax.axis_size('g...  14.6 us
    all_to_all x1, blocking collectives, body(): sums = lax.all_to_all(sums, ('blk', 'grp'), 0, 0, tiled=True)  10.3 us
    sort x1, other arithmetic, body(): listed = jnp.sort(kind * rows + near_row[0] << bits | number)  5.75 us
    ppermute x4, starting transfers between devices, wave_swaps(): moved = lax.ppermute(waves, 'blk', [(i, i ^ bits) for i in range(blocks)])  5.4 us
    pallas_call x2, Pallas kernels, gather_wave(): pl.pallas_call(wave_kernel, out_shape=jax.ShapeDtypeStruct((1, samples),...  2.94 us
    pallas_call x3, Pallas kernels, join(): pl.pallas_call(functools.partial(join_kernel, cuts, len(served) // len(cu...  2.72 us
  transfers between devices with their start and end apart: 21, of which 7 were waited for; matrix products, arithmetic and copies ran while one was open for 13% of the time, Pallas kernels for 30%

profile of v9, /device:TPU:0, one launch (start us, length us, event | category | flops | bytes accessed | tf_op | source)
XLA Modules:
  0.0 109.9 jit_solution(2403843776848958377)
XLA Ops:
  0.7 1.2 %copy-done.2 = f32[1,1024,240]{1,2,0:T(8,128)S(1)} copy-done((f32[1,1024,240]{1,2,0:T(8,128)S(1)}, f32[1,1024,240]{1,2,0:T(8,128)}, u32[]{:S(2)}) %copy-start.2) | copy-done | bytes 983064
  2.1 3.1 %collective-permute-start.4 = (bf16[640,256]{1,0:T(8,128)(2,1)S(1)}, bf16[640,256]{1,0:T(8,128)(2,1)S(1)}, u32[]{:S(2)}, u32[]{:S(2)}) collective-permute-start(bf16[640,256]{1,0:T(8,128)(2,1)S(1)} %get-tuple-element.27.rest_0_.rest_3_), channel_id=1, source_target_pairs={{0,2},{1,3},{2,0},{3,1},{4,6},{5,7},{6,4},{7,5},{8,10},{9,11},{10,... | collective-permute-start | bytes 983048 | tf_op jit(solution)/shard_map/ppermute | solution.py:392
  5.7 0.7 broadcast_xor_fusion
  6.4 0.7 select_add_fusion
  7.3 5.8 %sort.15 = (s32[3072]{0:T(1024)S(1)}, s32[3072]{0:T(1024)}) sort(s32[3072]{0:T(1024)S(1)} %get-tuple-element.52, s32[3072]{0:T(1024)S(1)} %iota.24), dimensions={0}, to_apply=%region_0.1 | sort | flops 36864 | bytes 49152 | tf_op jit(solution)/shard_map/jit(sort)/sort | solution.py:437
  13.0 0.6 pad_add_fusion
  13.6 2.8 %collective-permute-start.6 = (s32[6161]{0:T(1024)}, s32[6161]{0:T(1024)}, u32[]{:S(2)}, u32[]{:S(2)}) collective-permute-start(s32[6161]{0:T(1024)} %pad_add_fusion), channel_id=1, source_target_pairs={{0,4},{1,5},{2,6},{3,7},{4,0},{5,1},{6,2},{7,3},{8,12},{9,13},{10,... | collective-permute-start | bytes 73940 | tf_op jit(solution)/shard_map/ppermute | solution.py:392
  16.4 0.6 convert_reduce_fusion.1
  17.1 0.9 copy-done.7
  18.0 1.5 %gather_wave.2 = f32[1,512]{1,0:T(1,128)S(1)} custom-call(bf16[240,512]{1,0:T(8,128)(2,1)S(1)} %copy-done.7, bf16[1024,512]{1,0:T(8,128)(2,1)S(1)} %bitcast.33, bf16[640,256]{1,0:T(8,128)(2,1)S(1)} %get-tuple-element.27.rest_0_.rest_3_, bf16[384,256]{1,0:T(8,128)(2,1)S(1)} %get-tuple-element.28.rest_1_.rest_4_), custom_call_target="tpu_custom_call" | custom-call | flops 1 | bytes 1 | tf_op jit(solution)/shard_map/gather_wave/pallas_call | solution.py:93
  19.5 1.5 %collective-permute-start = (f32[1,512]{1,0:T(1,128)S(1)}, f32[1,512]{1,0:T(1,128)S(1)}, u32[]{:S(2)}, u32[]{:S(2)}) collective-permute-start(f32[1,512]{1,0:T(1,128)S(1)} %gather_wave.2), channel_id=1, source_target_pairs={{0,8},{8,0},{16,24},{24,16},{1,9},{9,1},{17,25},{25,17},{2,10},{10... | collective-permute-start | bytes 6152 | tf_op jit(solution)/shard_map/ppermute | solution.py:403
  21.1 0.6 pad_clamp_fusion
  21.7 0.5 collective-permute-start.8
  22.2 0.7 slice_convert_fusion
  22.9 0.7 slice.11.bound_ref
  24.1 4.7 %terms_all.2 = bf16[608,256]{1,0:T(8,128)(2,1)} custom-call(s32[3072]{0:T(1024)S(1)} %get-tuple-element.50.source_ref, s32[3072]{0:T(1024)S(1)} %get-tuple-element.49.target_ref, s32[17]{0:T(128)S(1)} %slice.11.bound_ref, bf16[1024,3]{1,0:T(8,128)(2,1)S(1)} %convert_element_type.18.table_ref, bf16[8,240,240]{2,1,0:T(8,128)(2,1)S(1)} %copy-done.1, ...), custom_call_target="tpu_custom_call" | custom-call | flops 1 | bytes 1 | tf_op jit(solution)/shard_map/terms_all/pallas_call | solution.py:257
  28.8 2.1 %collective-permute-start.9 = (bf16[608,256]{1,0:T(8,128)(2,1)}, bf16[608,256]{1,0:T(8,128)(2,1)}, u32[]{:S(2)}, u32[]{:S(2)}) collective-permute-start(bf16[608,256]{1,0:T(8,128)(2,1)} %terms_all.2), channel_id=1, source_target_pairs={{0,4},{1,5},{2,6},{3,7},{4,0},{5,1},{6,2},{7,3},{8,12},{9,13},{10,... | collective-permute-start | bytes 933896 | tf_op jit(solution)/shard_map/ppermute | solution.py:392
  30.9 0.6 pad_maximum_fusion
  31.5 1.6 %collective-permute-start.1 = (f32[2,512]{1,0:T(2,128)}, f32[2,512]{1,0:T(2,128)}, u32[]{:S(2)}, u32[]{:S(2)}) collective-permute-start(f32[2,512]{1,0:T(2,128)} %pad_maximum_fusion), channel_id=1, source_target_pairs={{0,16},{8,24},{16,0},{24,8},{1,17},{9,25},{17,1},{25,9},{2,18},{10... | collective-permute-start | bytes 12296 | tf_op jit(solution)/shard_map/ppermute | solution.py:403
  33.1 0.5 iota_compare_fusion.2
  33.6 1.1 %convert_element_type.17.table_ref = bf16[1024,3]{1,0:T(8,128)(2,1)} reshape(bf16[3072]{0:T(1024)(128)(2,1)S(1)} %copy-done.11) | data formatting | bytes 12288 | tf_op jit(solution)/shard_map/convert_element_type | solution.py:444
  34.7 0.7 gather_fusion
  35.4 3.2 %terms_all.3 = bf16[368,256]{1,0:T(8,128)(2,1)S(1)} custom-call(s32[3072]{0:T(1024)S(1)} %get-tuple-element.50.source_ref, s32[3072]{0:T(1024)S(1)} %get-tuple-element.49.target_ref, s32[17]{0:T(128)S(1)} %slice.11.bound_ref, bf16[1024,3]{1,0:T(8,128)(2,1)S(1)} %convert_element_type.18.table_ref, bf16[8,240,240]{2,1,0:T(8,128)(2,1)S(1)} %copy-done.1, ...), custom_call_target="tpu_custom_call" | custom-call | flops 1 | bytes 1 | tf_op jit(solution)/shard_map/terms_all/pallas_call | solution.py:257
  38.7 0.8 collective-permute-start.10
  39.5 0.8 fusion.4
  40.3 7.0 %terms_near.2.base_ref = f32[1024,240]{1,0:T(8,128)S(1)} custom-call(s32[3072]{0:T(1024)S(1)} %get-tuple-element.54.source_ref, s32[3072]{0:T(1024)S(1)} %get-tuple-element.53.target_ref, s32[17]{0:T(128)S(1)} %convert_reduce_fusion.bound_ref, bf16[1024,3]{1,0:T(8,128)(2,1)S(1)} %copy-done.6, bf16[8,240,240]{2,1,0:T(8,128)(2,1)S(1)} %copy-done.1, ...), custom_call_target="tpu_custom_call" | custom-call | flops 1 | bytes 1 | tf_op jit(solution)/shard_map/terms_near/pallas_call | solution.py:257
  47.4 3.6 %collective-permute-done.9.rest_0_ = bf16[608,256]{1,0:T(8,128)(2,1)} collective-permute-done((bf16[608,256]{1,0:T(8,128)(2,1)}, bf16[608,256]{1,0:T(8,128)(2,1)}, u32[]{:S(2)}, u32[]{:S(2)}) %collective-permute-start.9) | collective-permute-done | bytes 311328 | tf_op jit(solution)/shard_map/ppermute | solution.py:392
  50.9 1.6 %join_first.2 = (f32[240,640]{1,0:T(8,128)S(1)}, bf16[640,256]{1,0:T(8,128)(2,1)S(1)}, f32[1,128]{1,0:T(1,128)S(1)}) custom-call(f32[1024,240]{1,0:T(8,128)S(1)} %terms_near.2.base_ref, f32[240,1024]{1,0:T(8,128)S(1)} %bitcast.37, f32[240,1024]{1,0:T(8,128)S(1)} %bitcast.29, f32[1,128]{1,0:T(1,128)S(1)} %broadcast_in_dim.44.sums_in_ref, ...), custom_call_target="tpu_custom_call" | custom-call | tf_op jit(solution)/shard_map/join_first/pallas_call | solution.py:317
  52.7 1.2 %collective-permute-done.10.rest_0_ = bf16[368,256]{1,0:T(8,128)(2,1)S(1)} collective-permute-done((bf16[368,256]{1,0:T(8,128)(2,1)S(1)}, bf16[368,256]{1,0:T(8,128)(2,1)S(1)}, u32[]{:S(2)}, u32[]{:S(2)}) %collective-permute-start.10) | collective-permute-done | bytes 188448 | tf_op jit(solution)/shard_map/ppermute | solution.py:392
  54.4 0.9 collective-permute-start.16
  55.3 0.5 collective-permute-done.14.rest_3_.rest_6_
  55.8 4.0 %terms_own.1 = (f32[1024,240]{1,0:T(8,128)S(1)}, f32[8,128]{1,0:T(8,128)S(1)}) custom-call(s32[3072]{0:T(1024)S(1)} %get-tuple-element.50.source_ref, s32[3072]{0:T(1024)S(1)} %get-tuple-element.49.target_ref, s32[17]{0:T(128)S(1)} %slice.11.bound_ref, bf16[1024,3]{1,0:T(8,128)(2,1)S(1)} %convert_element_type.18.table_ref, ...), custom_call_target="tpu_custom_call" | custom-call | flops 1 | bytes 1 | tf_op jit(solution)/shard_map/terms_own/pallas_call | solution.py:257
  59.9 7.1 %collective-permute-done.16.rest_8_.rest_3_ = bf16[384,256]{1,0:T(8,128)(2,1)S(1)} collective-permute-done((bf16[384,256]{1,0:T(8,128)(2,1)S(1)}, bf16[384,256]{1,0:T(8,128)(2,1)S(1)}, u32[]{:S(2)}, u32[]{:S(2)}) %collective-permute-start.16) | collective-permute-done | bytes 196640 | tf_op jit(solution)/shard_map/ppermute | solution.py:392
  67.0 0.5 collective-permute-start.18
  67.5 1.4 %collective-permute-done.18.rest_10_.rest_5_ = bf16[384,256]{1,0:T(8,128)(2,1)S(1)} collective-permute-done((bf16[384,256]{1,0:T(8,128)(2,1)S(1)}, bf16[384,256]{1,0:T(8,128)(2,1)S(1)}, u32[]{:S(2)}, u32[]{:S(2)}) %collective-permute-start.18) | collective-permute-done | bytes 196640 | tf_op jit(solution)/shard_map/ppermute | solution.py:392
  68.9 2.8 %terms_rest.2 = bf16[608,256]{1,0:T(8,128)(2,1)S(1)} custom-call(s32[3072]{0:T(1024)S(1)} %get-tuple-element.50.source_ref, s32[3072]{0:T(1024)S(1)} %get-tuple-element.49.target_ref, s32[17]{0:T(128)S(1)} %slice.11.bound_ref, bf16[1024,3]{1,0:T(8,128)(2,1)S(1)} %convert_element_type.18.table_ref, bf16[8,240,240]{2,1,0:T(8,128)(2,1)S(1)} %copy-done.1, ...), custom_call_target="tpu_custom_call" | custom-call | flops 1 | bytes 1 | tf_op jit(solution)/shard_map/terms_rest/pallas_call | solution.py:257
  71.7 1.2 %collective-permute-start.19 = (bf16[608,256]{1,0:T(8,128)(2,1)S(1)}, bf16[608,256]{1,0:T(8,128)(2,1)S(1)}, u32[]{:S(2)}, u32[]{:S(2)}) collective-permute-start(bf16[608,256]{1,0:T(8,128)(2,1)S(1)} %terms_rest.2), channel_id=1, source_target_pairs={{0,4},{1,5},{2,6},{3,7},{4,0},{5,1},{6,2},{7,3},{8,12},{9,13},{10,... | collective-permute-start | bytes 933896 | tf_op jit(solution)/shard_map/ppermute | solution.py:392
  72.9 1.5 %gather_wave.3 = f32[1,512]{1,0:T(1,128)S(1)} custom-call(bf16[240,512]{1,0:T(8,128)(2,1)S(1)} %copy-done.8, bf16[1024,512]{1,0:T(8,128)(2,1)S(1)} %bitcast.35, bf16[640,256]{1,0:T(8,128)(2,1)S(1)} %get-tuple-element.32.rest_0_.rest_3_, bf16[384,256]{1,0:T(8,128)(2,1)S(1)} %get-tuple-element.34.rest_1_.rest_4_), custom_call_target="tpu_custom_call" | custom-call | flops 1 | bytes 1 | tf_op jit(solution)/shard_map/gather_wave/pallas_call | solution.py:93
  74.3 0.6 collective-permute-start.11
  75.0 2.3 %terms_rest.3 = bf16[368,256]{1,0:T(8,128)(2,1)S(1)} custom-call(s32[3072]{0:T(1024)S(1)} %get-tuple-element.50.source_ref, s32[3072]{0:T(1024)S(1)} %get-tuple-element.49.target_ref, s32[17]{0:T(128)S(1)} %slice.11.bound_ref, bf16[1024,3]{1,0:T(8,128)(2,1)S(1)} %convert_element_type.18.table_ref, bf16[8,240,240]{2,1,0:T(8,128)(2,1)S(1)} %copy-done.1, ...), custom_call_target="tpu_custom_call" | custom-call | flops 1 | bytes 1 | tf_op jit(solution)/shard_map/terms_rest/pallas_call | solution.py:257
  77.3 1.9 %collective-permute-start.20 = (bf16[368,256]{1,0:T(8,128)(2,1)S(1)}, bf16[368,256]{1,0:T(8,128)(2,1)S(1)}, u32[]{:S(2)}, u32[]{:S(2)}) collective-permute-start(bf16[368,256]{1,0:T(8,128)(2,1)S(1)} %terms_rest.3), channel_id=1, source_target_pairs={{0,4},{1,5},{2,6},{3,7},{4,0},{5,1},{6,2},{7,3},{8,12},{9,13},{10,... | collective-permute-start | bytes 565256 | tf_op jit(solution)/shard_map/ppermute | solution.py:392
  79.3 1.7 %collective-permute-start.12 = (f32[2,512]{1,0:T(2,128)S(1)}, f32[2,512]{1,0:T(2,128)S(1)}, u32[]{:S(2)}, u32[]{:S(2)}) collective-permute-start(f32[2,512]{1,0:T(2,128)S(1)} %pad_maximum_fusion.1), channel_id=1, source_target_pairs={{0,16},{8,24},{16,0},{24,8},{1,17},{9,25},{17,1},{25,9},{2,18},{10... | collective-permute-start | bytes 12296 | tf_op jit(solution)/shard_map/ppermute | solution.py:403
  80.9 2.0 %collective-permute-done.12 = f32[2,512]{1,0:T(2,128)S(1)} collective-permute-done((f32[2,512]{1,0:T(2,128)S(1)}, f32[2,512]{1,0:T(2,128)S(1)}, u32[]{:S(2)}, u32[]{:S(2)}) %collective-permute-start.12) | collective-permute-done | bytes 4128 | tf_op jit(solution)/shard_map/ppermute | solution.py:403
  83.0 6.7 %terms_near.3.base_ref = f32[1024,240]{1,0:T(8,128)S(1)} custom-call(s32[3072]{0:T(1024)S(1)} %get-tuple-element.54.source_ref, s32[3072]{0:T(1024)S(1)} %get-tuple-element.53.target_ref, s32[17]{0:T(128)S(1)} %convert_reduce_fusion.bound_ref, bf16[1024,3]{1,0:T(8,128)(2,1)S(1)} %copy-done.6, bf16[8,240,240]{2,1,0:T(8,128)(2,1)S(1)} %copy-done.1, ...), custom_call_target="tpu_custom_call" | custom-call | flops 1 | bytes 1 | tf_op jit(solution)/shard_map/terms_near/pallas_call | solution.py:257
  89.7 7.0 %collective-permute-done.20.rest_1_ = bf16[368,256]{1,0:T(8,128)(2,1)S(1)} collective-permute-done((bf16[368,256]{1,0:T(8,128)(2,1)S(1)}, bf16[368,256]{1,0:T(8,128)(2,1)S(1)}, u32[]{:S(2)}, u32[]{:S(2)}) %collective-permute-start.20) | collective-permute-done | bytes 188448 | tf_op jit(solution)/shard_map/ppermute | solution.py:392
  96.8 0.7 join_second.1
  97.5 10.3 %all_to_all.11 = f32[32,1,128]{2,1,0:T(1,128)S(1)} all-to-all(f32[32,1,128]{2,1,0:T(1,128)S(1)} %bitcast.43), channel_id=1, replica_groups=mesh['blk'=4,'grp'=8] {'blk','grp'}, dimensions={0} | all-to-all | bytes 32768 | tf_op jit(solution)/shard_map/all_to_all | solution.py:541
  107.8 2.1 %finish.1 = (f32[240,1024]{1,0:T(8,128)}, f32[240,1024]{1,0:T(8,128)}, f32[2,3]{1,0:T(2,128)}) custom-call(f32[32,128]{1,0:T(8,128)S(1)} %bitcast.42, f32[240,1024]{1,0:T(8,128)S(1)} %bitcast.32, f32[240,1024]{1,0:T(8,128)S(1)} %get-tuple-element.44.c_ref, f32[240,640]{1,0:T(8,128)S(1)} %get-tuple-element.41.rest_2_.rest_0_, ...), custom_call_target="tpu_custom_call" | custom-call | tf_op jit(solution)/shard_map/finish/pallas_call | solution.py:381
  (56 shorter events, 2.1 us)
Async XLA Ops:
  0.6 34.1 %copy-start = (f32[1,1,4,512]{3,2,1,0:T(4,128)S(1)}, f32[1,1,4,512]{3,2,1,0:T(4,128)}, u32[]{:S(2)}) copy-start(f32[1,1,4,512]{3,2,1,0:T(4,128)} %param.19) | copy-start | bytes 24580
  0.6 1.2 %copy-start.2 = (f32[1,1024,240]{1,2,0:T(8,128)S(1)}, f32[1,1024,240]{1,2,0:T(8,128)}, u32[]{:S(2)}) copy-start(f32[1,1024,240]{1,2,0:T(8,128)} %param.10) | copy-start | bytes 2949124
  1.9 15.2 %copy-start.4 = (bf16[1,1024,512]{2,1,0:T(8,128)(2,1)S(1)}, bf16[1,1024,512]{2,1,0:T(8,128)(2,1)}, u32[]{:S(2)}) copy-start(bf16[1,1024,512]{2,1,0:T(8,128)(2,1)} %param.18) | copy-start | bytes 3145732
  2.1 19.0 %collective-permute-start.4 = (bf16[640,256]{1,0:T(8,128)(2,1)S(1)}, bf16[640,256]{1,0:T(8,128)(2,1)S(1)}, u32[]{:S(2)}, u32[]{:S(2)}) collective-permute-start(bf16[640,256]{1,0:T(8,128)(2,1)S(1)} %get-tuple-element.27.rest_0_.rest_3_), channel_id=1, source_target_pairs={{0,2},{1,3},{2,0},{3,1},{4,6},{5,7},{6,4},{7,5},{8,10},{9,11},{10,... | collective-permute-start | bytes 983048 | tf_op jit(solution)/shard_map/ppermute | solution.py:392
  5.2 18.9 %collective-permute-start.2 = (bf16[640,256]{1,0:T(8,128)(2,1)S(1)}, bf16[640,256]{1,0:T(8,128)(2,1)S(1)}, u32[]{:S(2)}, u32[]{:S(2)}) collective-permute-start(bf16[640,256]{1,0:T(8,128)(2,1)S(1)} %get-tuple-element.27.rest_0_.rest_3_), channel_id=1, source_target_pairs={{0,1},{1,0},{2,3},{3,2},{4,5},{5,4},{6,7},{7,6},{8,9},{9,8},{10,11... | collective-permute-start | bytes 983048 | tf_op jit(solution)/shard_map/ppermute | solution.py:392
  5.2 15.9 %collective-permute-start.5 = (bf16[384,256]{1,0:T(8,128)(2,1)S(1)}, bf16[384,256]{1,0:T(8,128)(2,1)}, u32[]{:S(2)}, u32[]{:S(2)}) collective-permute-start(bf16[384,256]{1,0:T(8,128)(2,1)S(1)} %get-tuple-element.28.rest_1_.rest_4_), channel_id=1, source_target_pairs={{0,2},{1,3},{2,0},{3,1},{4,6},{5,7},{6,4},{7,5},{8,10},{9,11},{10,... | collective-permute-start | bytes 589832 | tf_op jit(solution)/shard_map/ppermute | solution.py:392
  5.3 18.7 %collective-permute-start.3 = (bf16[384,256]{1,0:T(8,128)(2,1)S(1)}, bf16[384,256]{1,0:T(8,128)(2,1)}, u32[]{:S(2)}, u32[]{:S(2)}) collective-permute-start(bf16[384,256]{1,0:T(8,128)(2,1)S(1)} %get-tuple-element.28.rest_1_.rest_4_), channel_id=1, source_target_pairs={{0,1},{1,0},{2,3},{3,2},{4,5},{5,4},{6,7},{7,6},{8,9},{9,8},{10,11... | collective-permute-start | bytes 589832 | tf_op jit(solution)/shard_map/ppermute | solution.py:392
  7.3 5.8 %copy-start.10 = (s32[1,3072]{1,0:T(1,128)S(1)}, s32[1,3072]{1,0:T(1,128)}, u32[]{:S(2)}) copy-start(s32[1,3072]{1,0:T(1,128)} %param.14) | copy-start | bytes 36868
  13.6 5.8 %collective-permute-start.6 = (s32[6161]{0:T(1024)}, s32[6161]{0:T(1024)}, u32[]{:S(2)}, u32[]{:S(2)}) collective-permute-start(s32[6161]{0:T(1024)} %pad_add_fusion), channel_id=1, source_target_pairs={{0,4},{1,5},{2,6},{3,7},{4,0},{5,1},{6,2},{7,3},{8,12},{9,13},{10,... | collective-permute-start | bytes 73940 | tf_op jit(solution)/shard_map/ppermute | solution.py:392
  17.1 0.9 copy-start.7
  18.0 6.1 %copy-start.1 = (bf16[8,240,240]{2,1,0:T(8,128)(2,1)S(1)}, bf16[8,240,240]{2,1,0:T(8,128)(2,1)}, u32[]{:S(2)}) copy-start(bf16[8,240,240]{2,1,0:T(8,128)(2,1)} %tables_ref.13) | copy-start | bytes 2764804
  19.5 11.4 %collective-permute-start = (f32[1,512]{1,0:T(1,128)S(1)}, f32[1,512]{1,0:T(1,128)S(1)}, u32[]{:S(2)}, u32[]{:S(2)}) collective-permute-start(f32[1,512]{1,0:T(1,128)S(1)} %gather_wave.2), channel_id=1, source_target_pairs={{0,8},{8,0},{16,24},{24,16},{1,9},{9,1},{17,25},{25,17},{2,10},{10... | collective-permute-start | bytes 6152 | tf_op jit(solution)/shard_map/ppermute | solution.py:403
  21.0 3.0 %collective-permute-start.7 = (bf16[640,256]{1,0:T(8,128)(2,1)S(1)}, bf16[640,256]{1,0:T(8,128)(2,1)}, u32[]{:S(2)}, u32[]{:S(2)}) collective-permute-start(bf16[640,256]{1,0:T(8,128)(2,1)S(1)} %collective-permute-done.4.rest_7_.rest_4_), channel_id=1, source_target_pairs={{0,1},{1,0},{2,3},{3,2},{4,5},{5,4},{6,7},{7,6},{8,9},{9,8},{10,11... | collective-permute-start | bytes 983048 | tf_op jit(solution)/shard_map/ppermute | solution.py:392
  21.7 2.4 %collective-permute-start.8 = (bf16[384,256]{1,0:T(8,128)(2,1)}, bf16[384,256]{1,0:T(8,128)(2,1)}, u32[]{:S(2)}, u32[]{:S(2)}) collective-permute-start(bf16[384,256]{1,0:T(8,128)(2,1)} %collective-permute-done.5.rest_8_.rest_5_), channel_id=1, source_target_pairs={{0,1},{1,0},{2,3},{3,2},{4,5},{5,4},{6,7},{7,6},{8,9},{9,8},{10,11... | collective-permute-start | bytes 589832 | tf_op jit(solution)/shard_map/ppermute | solution.py:392
  28.8 4.8 %copy-start.11 = (bf16[3072]{0:T(1024)(128)(2,1)S(1)}, bf16[3072]{0:T(1024)(128)(2,1)}, u32[]{:S(2)}) copy-start(bf16[3072]{0:T(1024)(128)(2,1)} %convert_reduce_fusion.1) | copy-start | bytes 18436
  28.8 22.1 %collective-permute-start.9 = (bf16[608,256]{1,0:T(8,128)(2,1)}, bf16[608,256]{1,0:T(8,128)(2,1)}, u32[]{:S(2)}, u32[]{:S(2)}) collective-permute-start(bf16[608,256]{1,0:T(8,128)(2,1)} %terms_all.2), channel_id=1, source_target_pairs={{0,4},{1,5},{2,6},{3,7},{4,0},{5,1},{6,2},{7,3},{8,12},{9,13},{10,... | collective-permute-start | bytes 933896 | tf_op jit(solution)/shard_map/ppermute | solution.py:392
  31.5 8.0 %collective-permute-start.1 = (f32[2,512]{1,0:T(2,128)}, f32[2,512]{1,0:T(2,128)}, u32[]{:S(2)}, u32[]{:S(2)}) collective-permute-start(f32[2,512]{1,0:T(2,128)} %pad_maximum_fusion), channel_id=1, source_target_pairs={{0,16},{8,24},{16,0},{24,8},{1,17},{9,25},{17,1},{25,9},{2,18},{10... | collective-permute-start | bytes 12296 | tf_op jit(solution)/shard_map/ppermute | solution.py:403
  35.4 4.1 %copy-start.12 = (pred[4]{0:T(512)(128)(4,1)S(1)}, pred[4]{0:T(512)(128)(4,1)}, u32[]{:S(2)}) copy-start(pred[4]{0:T(512)(128)(4,1)} %iota_compare_fusion.2) | copy-start | bytes 16
  35.4 4.9 %copy-start.6 = (bf16[1024,3]{1,0:T(8,128)(2,1)S(1)}, bf16[1024,3]{1,0:T(8,128)(2,1)}, u32[]{:S(2)}) copy-start(bf16[1024,3]{1,0:T(8,128)(2,1)} %convert_element_type.17.table_ref) | copy-start | bytes 18436
  35.4 4.9 %copy-start.9 = (bf16[512,240]{0,1:T(8,128)(2,1)S(1)}, bf16[512,240]{0,1:T(8,128)(2,1)}, u32[]{:S(2)}) copy-start(bf16[512,240]{0,1:T(8,128)(2,1)} %param.17) | copy-start | bytes 737284
  38.7 15.2 %collective-permute-start.10 = (bf16[368,256]{1,0:T(8,128)(2,1)S(1)}, bf16[368,256]{1,0:T(8,128)(2,1)S(1)}, u32[]{:S(2)}, u32[]{:S(2)}) collective-permute-start(bf16[368,256]{1,0:T(8,128)(2,1)S(1)} %terms_all.3), channel_id=1, source_target_pairs={{0,4},{1,5},{2,6},{3,7},{4,0},{5,1},{6,2},{7,3},{8,12},{9,13},{10,... | collective-permute-start | bytes 565256 | tf_op jit(solution)/shard_map/ppermute | solution.py:392
  40.3 10.6 %copy-start.3 = (f32[1,1024,240]{1,2,0:T(8,128)S(1)}, f32[1,1024,240]{1,2,0:T(8,128)}, u32[]{:S(2)}) copy-start(f32[1,1024,240]{1,2,0:T(8,128)} %param.10) | copy-start | bytes 2949124
  40.3 10.6 %copy-start.5 = (f32[1,1024,240]{1,2,0:T(8,128)S(1)}, f32[1,1024,240]{1,2,0:T(8,128)}, u32[]{:S(2)}) copy-start(f32[1,1024,240]{1,2,0:T(8,128)} %param.11) | copy-start | bytes 2949124
  52.5 3.3 %collective-permute-start.13 = (bf16[640,256]{1,0:T(8,128)(2,1)S(1)}, bf16[640,256]{1,0:T(8,128)(2,1)S(1)}, u32[]{:S(2)}, u32[]{:S(2)}) collective-permute-start(bf16[640,256]{1,0:T(8,128)(2,1)S(1)} %get-tuple-element.32.rest_0_.rest_3_), channel_id=1, source_target_pairs={{0,1},{1,0},{2,3},{3,2},{4,5},{5,4},{6,7},{7,6},{8,9},{9,8},{10,11... | collective-permute-start | bytes 983048 | tf_op jit(solution)/shard_map/ppermute | solution.py:392
  52.6 14.3 %collective-permute-start.15 = (bf16[640,256]{1,0:T(8,128)(2,1)S(1)}, bf16[640,256]{1,0:T(8,128)(2,1)S(1)}, u32[]{:S(2)}, u32[]{:S(2)}) collective-permute-start(bf16[640,256]{1,0:T(8,128)(2,1)S(1)} %get-tuple-element.32.rest_0_.rest_3_), channel_id=1, source_target_pairs={{0,2},{1,3},{2,0},{3,1},{4,6},{5,7},{6,4},{7,5},{8,10},{9,11},{10,... | collective-permute-start | bytes 983048 | tf_op jit(solution)/shard_map/ppermute | solution.py:392
  54.3 1.5 %collective-permute-start.14 = (bf16[384,256]{1,0:T(8,128)(2,1)S(1)}, bf16[384,256]{1,0:T(8,128)(2,1)S(1)}, u32[]{:S(2)}, u32[]{:S(2)}) collective-permute-start(bf16[384,256]{1,0:T(8,128)(2,1)S(1)} %get-tuple-element.34.rest_1_.rest_4_), channel_id=1, source_target_pairs={{0,1},{1,0},{2,3},{3,2},{4,5},{5,4},{6,7},{7,6},{8,9},{9,8},{10,11... | collective-permute-start | bytes 589832 | tf_op jit(solution)/shard_map/ppermute | solution.py:392
  54.4 12.5 %collective-permute-start.16 = (bf16[384,256]{1,0:T(8,128)(2,1)S(1)}, bf16[384,256]{1,0:T(8,128)(2,1)S(1)}, u32[]{:S(2)}, u32[]{:S(2)}) collective-permute-start(bf16[384,256]{1,0:T(8,128)(2,1)S(1)} %get-tuple-element.34.rest_1_.rest_4_), channel_id=1, source_target_pairs={{0,2},{1,3},{2,0},{3,1},{4,6},{5,7},{6,4},{7,5},{8,10},{9,11},{10,... | collective-permute-start | bytes 589832 | tf_op jit(solution)/shard_map/ppermute | solution.py:392
  66.9 1.9 %collective-permute-start.17 = (bf16[640,256]{1,0:T(8,128)(2,1)S(1)}, bf16[640,256]{1,0:T(8,128)(2,1)S(1)}, u32[]{:S(2)}, u32[]{:S(2)}) collective-permute-start(bf16[640,256]{1,0:T(8,128)(2,1)S(1)} %collective-permute-done.15.rest_7_.rest_2_), channel_id=1, source_target_pairs={{0,1},{1,0},{2,3},{3,2},{4,5},{5,4},{6,7},{7,6},{8,9},{9,8},{10,11... | collective-permute-start | bytes 983048 | tf_op jit(solution)/shard_map/ppermute | solution.py:392
  67.0 1.9 %collective-permute-start.18 = (bf16[384,256]{1,0:T(8,128)(2,1)S(1)}, bf16[384,256]{1,0:T(8,128)(2,1)S(1)}, u32[]{:S(2)}, u32[]{:S(2)}) collective-permute-start(bf16[384,256]{1,0:T(8,128)(2,1)S(1)} %collective-permute-done.16.rest_8_.rest_3_), channel_id=1, source_target_pairs={{0,1},{1,0},{2,3},{3,2},{4,5},{5,4},{6,7},{7,6},{8,9},{9,8},{10,11... | collective-permute-start | bytes 589832 | tf_op jit(solution)/shard_map/ppermute | solution.py:392
  68.9 4.0 %copy-start.8 = (bf16[240,512]{1,0:T(8,128)(2,1)S(1)}, bf16[240,512]{1,0:T(8,128)(2,1)}, u32[]{:S(2)}) copy-start(bf16[240,512]{1,0:T(8,128)(2,1)} %out_ref.3) | copy-start | bytes 737284
  71.7 25.0 %collective-permute-start.19 = (bf16[608,256]{1,0:T(8,128)(2,1)S(1)}, bf16[608,256]{1,0:T(8,128)(2,1)S(1)}, u32[]{:S(2)}, u32[]{:S(2)}) collective-permute-start(bf16[608,256]{1,0:T(8,128)(2,1)S(1)} %terms_rest.2), channel_id=1, source_target_pairs={{0,4},{1,5},{2,6},{3,7},{4,0},{5,1},{6,2},{7,3},{8,12},{9,13},{10,... | collective-permute-start | bytes 933896 | tf_op jit(solution)/shard_map/ppermute | solution.py:392
  74.3 4.9 %collective-permute-start.11 = (f32[1,512]{1,0:T(1,128)S(1)}, f32[1,512]{1,0:T(1,128)S(1)}, u32[]{:S(2)}, u32[]{:S(2)}) collective-permute-start(f32[1,512]{1,0:T(1,128)S(1)} %gather_wave.3), channel_id=1, source_target_pairs={{0,8},{8,0},{16,24},{24,16},{1,9},{9,1},{17,25},{25,17},{2,10},{10... | collective-permute-start | bytes 6152 | tf_op jit(solution)/shard_map/ppermute | solution.py:403
  77.3 19.4 %collective-permute-start.20 = (bf16[368,256]{1,0:T(8,128)(2,1)S(1)}, bf16[368,256]{1,0:T(8,128)(2,1)S(1)}, u32[]{:S(2)}, u32[]{:S(2)}) collective-permute-start(bf16[368,256]{1,0:T(8,128)(2,1)S(1)} %terms_rest.3), channel_id=1, source_target_pairs={{0,4},{1,5},{2,6},{3,7},{4,0},{5,1},{6,2},{7,3},{8,12},{9,13},{10,... | collective-permute-start | bytes 565256 | tf_op jit(solution)/shard_map/ppermute | solution.py:392
  79.3 3.7 %collective-permute-start.12 = (f32[2,512]{1,0:T(2,128)S(1)}, f32[2,512]{1,0:T(2,128)S(1)}, u32[]{:S(2)}, u32[]{:S(2)}) collective-permute-start(f32[2,512]{1,0:T(2,128)S(1)} %pad_maximum_fusion.1), channel_id=1, source_target_pairs={{0,16},{8,24},{16,0},{24,8},{1,17},{9,25},{17,1},{25,9},{2,18},{10... | collective-permute-start | bytes 12296 | tf_op jit(solution)/shard_map/ppermute | solution.py:403
